TPU v7x, 32 devices: a whole 2x2x4 slice. The times are simulated.
32 devices in a mesh: ctx: 16 (over z, x, core), wt: 2 (over y).
Axes of the slice: x: 2, y: 2, z: 4, core: 2. Of those that a mesh axis runs over, the one named last changes fastest.
Arguments:
- tokens: bfloat16 [2, 4096, 1280], P('wt', 'ctx'), may hold values from -6 to 6
- cotangent: bfloat16 [2, 4096, 1280], P('wt', 'ctx'), may hold values from -6 to 6
- deal: int32 [2, 32], P('wt'), may hold values from 0 to 31, as said below
- lengths: int32 [2, 1], P('wt'), may hold values from 2048 to 4096, as said below
- gain_attn: bfloat16 [1280], P('wt'), may hold values from 0.5 to 1.5
- w_query: bfloat16 [1280, 1280], P('wt'), may hold values from -0.15625 to 0.15625
- w_key: bfloat16 [1280, 1280], P('wt'), may hold values from -0.15625 to 0.15625
- w_value: bfloat16 [1280, 1280], P('wt'), may hold values from -0.15625 to 0.15625
- w_output: bfloat16 [1280, 1280], P('wt'), may hold values from -4 to 4
- query_scale: float32 [80], replicated, may hold values from -1 to 1
- gain_mlp: bfloat16 [1280], P('wt'), may hold values from 0.5 to 1.5
- w_expand: bfloat16 [1280, 1280], P('wt'), may hold values from -0.15625 to 0.15625
- w_contract: bfloat16 [1280, 1280], P('wt'), may hold values from -0.15625 to 0.15625
Outputs:
- result: bfloat16 [2, 4096, 1280], P('wt', 'ctx')
- grad_inputs: bfloat16 [2, 4096, 1280], P('wt', 'ctx')
- grad_gain_attn: float32 [1280], P('wt')
- grad_query: float32 [1280, 1280], P('wt')
- grad_key: float32 [1280, 1280], P('wt')
- grad_value: float32 [1280, 1280], P('wt')
- grad_output: float32 [1280, 1280], P('wt')
- grad_scale: float32 [80], replicated
- grad_gain_mlp: float32 [1280], P('wt')
- grad_expand: float32 [1280, 1280], P('wt')
- grad_contract: float32 [1280, 1280], P('wt')
Inputs may be any that keep to these rules, and one draw needn't show every extreme that they name: `deal`: each group's row is a permutation of the span numbers 0 to 31; in each group one sequence, of length 4096, has its first span dealt to row 0 and its last span to row 31. `lengths`: in each group one sequence has length 4096.
All inputs are finite; a program needn't handle non-finite values.
Results may differ from a plain program's by a relative error of at most 0.023.
Values may be sent and summed in bfloat16 or wider, within the bound.
No kernel may reach another device: no remote copies, remote signals or barrier semaphores. Data moves between devices by JAX's collectives and lax.ppermute only.
A program may use at most 512 MiB of HBM per device.

v0:
```python
import math

import jax
import jax.numpy as jnp
from jax import lax
from jax.sharding import PartitionSpec as P

HEADS = 16
HEAD = 80
SPAN = 128
LONGEST = 4096


EPS = 1e-06
LOG2E = 1.442695041
NEG = -1e30


def normed(values, gain):
    return values * lax.rsqrt(jnp.mean(values * values, axis=-1, keepdims=True) + EPS) * gain


def locate(dealt_spans, seq_lengths, offset, count, slot_tokens):
    row_ids = offset + jnp.arange(count, dtype=jnp.int32)
    slot_ids = row_ids // SPAN
    matches = slot_ids[:, None] == jnp.arange(dealt_spans.shape[0], dtype=jnp.int32)[None, :]
    span_ids = jnp.sum(jnp.where(matches, dealt_spans[None, :], 0), axis=1)
    natural = span_ids * SPAN + row_ids % SPAN
    sequence = natural // slot_tokens
    position = natural % slot_tokens
    owners = sequence[:, None] == jnp.arange(seq_lengths.shape[0], dtype=jnp.int32)[None, :]
    limits = jnp.sum(jnp.where(owners, seq_lengths[None, :], 0), axis=1)
    return (sequence, position, position < limits)


def permitted(query_place, key_place):
    same_seq = query_place[0][:, None] == key_place[0][None, :]
    causal = key_place[1][None, :] <= query_place[1][:, None]
    return (same_seq & causal & key_place[2][None, :])[None]


def per_device(
    tokens,
    cotangent,
    deal,
    lengths,
    gain_attn,
    w_query,
    w_key,
    w_value,
    w_output,
    query_scale,
    gain_mlp,
    w_expand,
    w_contract,
):
    row_count = tokens.shape[1]
    feat_width = tokens.shape[2]
    group_rows = row_count * lax.axis_size("ctx")
    slot_tokens = min(LONGEST, group_rows)
    block_rows = min(512, group_rows)
    blocks = group_rows // block_rows
    dealt_spans = deal[0]
    seq_lengths = lengths[0]
    inputs = tokens[0].astype(jnp.float32)
    shards = (gain_attn, w_query, w_key, w_value, w_output, gain_mlp, w_expand, w_contract)
    gathered = (
        lax.all_gather(shards[0], "wt", axis=0, tiled=True),
        lax.all_gather(shards[1], "wt", axis=0, tiled=True),
        lax.all_gather(shards[2], "wt", axis=0, tiled=True),
        lax.all_gather(shards[3], "wt", axis=0, tiled=True),
        lax.all_gather(shards[4], "wt", axis=0, tiled=True),
        lax.all_gather(shards[5], "wt", axis=0, tiled=True),
        lax.all_gather(shards[6], "wt", axis=0, tiled=True),
        lax.all_gather(shards[7], "wt", axis=0, tiled=True),
    )
    gain_one = gathered[0].astype(jnp.float32)
    gain_two = gathered[5].astype(jnp.float32)
    query_place = locate(
        dealt_spans, seq_lengths, lax.axis_index("ctx") * row_count, row_count, slot_tokens
    )
    scale_row = LOG2E / math.sqrt(HEAD) * jax.nn.softplus(query_scale)
    attn_in = normed(inputs, gain_one).astype(jnp.bfloat16)
    query_lin = jnp.dot(attn_in, gathered[1], preferred_element_type=jnp.float32)
    queries = (query_lin.reshape(row_count, HEADS, HEAD) * scale_row).astype(jnp.bfloat16)
    key_own = jnp.dot(attn_in, gathered[2], preferred_element_type=jnp.float32).astype(jnp.bfloat16)
    value_own = jnp.dot(attn_in, gathered[3], preferred_element_type=jnp.float32).astype(
        jnp.bfloat16
    )
    portion = (
        lax.all_gather(key_own, "ctx", axis=0, tiled=True),
        lax.all_gather(value_own, "ctx", axis=0, tiled=True),
    )
    running = jnp.full((HEADS, row_count), NEG, jnp.float32)
    count = portion[0].shape[0]
    key_rows = portion[0].reshape(count, HEADS, HEAD)
    value_rows = portion[1].reshape(count, HEADS, HEAD)
    permit_mask = permitted(
        query_place, locate(dealt_spans, seq_lengths, jnp.int32(0), count, slot_tokens)
    )
    scores = jnp.einsum("qhd,khd->hqk", queries, key_rows, preferred_element_type=jnp.float32)
    scores = jnp.where(permit_mask, scores, NEG)
    newest = jnp.maximum(running, jnp.max(scores, axis=-1))
    weights = jnp.where(permit_mask, jnp.exp(scores - newest[..., None]), 0.0)
    running_total = jnp.sum(weights, axis=-1)
    update = jnp.einsum(
        "hqk,khd->qhd", weights.astype(jnp.bfloat16), value_rows, preferred_element_type=jnp.float32
    )
    summed = update
    running, running_total, summed = (newest, running_total, summed)
    log_norm = running + jnp.log(running_total)
    attended = summed / jnp.transpose(running_total)[:, :, None]
    attn_out = attended.reshape(row_count, feat_width).astype(jnp.bfloat16)
    mid = inputs + jnp.dot(attn_out, gathered[4], preferred_element_type=jnp.float32)
    mlp_in = normed(mid, gain_two).astype(jnp.bfloat16)
    expanded = jnp.dot(mlp_in, gathered[6], preferred_element_type=jnp.float32)
    activated = jax.nn.silu(expanded).astype(jnp.bfloat16)
    result = mid + jnp.dot(activated, gathered[7], preferred_element_type=jnp.float32)
    weights_back = (
        lax.all_gather(shards[0], "wt", axis=0, tiled=True),
        lax.all_gather(shards[1], "wt", axis=0, tiled=True),
        lax.all_gather(shards[2], "wt", axis=0, tiled=True),
        lax.all_gather(shards[3], "wt", axis=0, tiled=True),
        lax.all_gather(shards[4], "wt", axis=0, tiled=True),
        lax.all_gather(shards[5], "wt", axis=0, tiled=True),
        lax.all_gather(shards[6], "wt", axis=0, tiled=True),
        lax.all_gather(shards[7], "wt", axis=0, tiled=True),
    )
    whole_keys, whole_values = (
        lax.all_gather(key_own, "ctx", axis=0, tiled=True),
        lax.all_gather(value_own, "ctx", axis=0, tiled=True),
    )
    grad_result = cotangent[0].astype(jnp.float32)
    grad_branch = grad_result.astype(jnp.bfloat16)
    grad_contract = jnp.einsum(
        "tf,td->fd", activated, grad_branch, preferred_element_type=jnp.float32
    )
    grad_act = jnp.einsum(
        "td,fd->tf", grad_branch, weights_back[7], preferred_element_type=jnp.float32
    )
    sigmoid_gate = jax.nn.sigmoid(expanded)
    grad_expanded = (grad_act * sigmoid_gate * (1.0 + expanded * (1.0 - sigmoid_gate))).astype(
        jnp.bfloat16
    )
    grad_expand = jnp.einsum("td,tf->df", mlp_in, grad_expanded, preferred_element_type=jnp.float32)
    grad_mlp_in = jnp.einsum(
        "tf,df->td", grad_expanded, weights_back[6], preferred_element_type=jnp.float32
    )
    unused_two, pull_two = jax.vjp(normed, mid, gain_two)
    grad_mid_norm, grad_gain_two = pull_two(grad_mlp_in)
    grad_mid = grad_result + grad_mid_norm
    grad_mid_low = grad_mid.astype(jnp.bfloat16)
    grad_output_w = jnp.einsum(
        "td,te->de", attn_out, grad_mid_low, preferred_element_type=jnp.float32
    )
    grad_attended = jnp.einsum(
        "te,de->td", grad_mid_low, weights_back[4], preferred_element_type=jnp.float32
    ).astype(jnp.bfloat16)
    out_grad = grad_attended.reshape(row_count, HEADS, HEAD)
    delta = jnp.transpose(jnp.sum(out_grad.astype(jnp.float32) * attended, axis=-1))
    key_blocks = (
        jnp.arange(blocks, dtype=jnp.int32),
        whole_keys.reshape(blocks, block_rows, feat_width),
        whole_values.reshape(blocks, block_rows, feat_width),
    )
    query_zero = jnp.zeros((row_count, HEADS, HEAD), jnp.float32)

    def back_block(query_grad, block_in):
        offset = block_in[0] * block_rows
        key_rows = block_in[1].reshape(block_rows, HEADS, HEAD)
        value_rows = block_in[2].reshape(block_rows, HEADS, HEAD)
        permit_mask = permitted(
            query_place, locate(dealt_spans, seq_lengths, offset, block_rows, slot_tokens)
        )
        scores = jnp.einsum("qhd,khd->hqk", queries, key_rows, preferred_element_type=jnp.float32)
        probabilities = jnp.where(permit_mask, jnp.exp(scores - log_norm[..., None]), 0.0)
        value_grad = jnp.einsum(
            "hqk,qhd->khd",
            probabilities.astype(jnp.bfloat16),
            out_grad,
            preferred_element_type=jnp.float32,
        )
        prob_grad = jnp.einsum(
            "qhd,khd->hqk", out_grad, value_rows, preferred_element_type=jnp.float32
        )
        score_grad = (probabilities * (prob_grad - delta[..., None])).astype(jnp.bfloat16)
        query_grad = query_grad + jnp.einsum(
            "hqk,khd->qhd", score_grad, key_rows, preferred_element_type=jnp.float32
        )
        key_grad = jnp.einsum(
            "hqk,qhd->khd", score_grad, queries, preferred_element_type=jnp.float32
        )
        return (
            query_grad,
            (key_grad.reshape(block_rows, feat_width), value_grad.reshape(block_rows, feat_width)),
        )

    query_grad, key_terms = lax.scan(back_block, query_zero, key_blocks)
    key_sum, value_sum = (
        lax.psum_scatter(
            key_terms[0].reshape(group_rows, feat_width).astype(jnp.bfloat16),
            "ctx",
            scatter_dimension=0,
            tiled=True,
        ).astype(jnp.float32),
        lax.psum_scatter(
            key_terms[1].reshape(group_rows, feat_width).astype(jnp.bfloat16),
            "ctx",
            scatter_dimension=0,
            tiled=True,
        ).astype(jnp.float32),
    )
    grad_keys = key_sum.astype(jnp.bfloat16)
    grad_values = value_sum.astype(jnp.bfloat16)
    grad_query_lin = (query_grad * scale_row).reshape(row_count, feat_width).astype(jnp.bfloat16)
    grad_scale = (
        jnp.sum(query_grad * query_lin.reshape(row_count, HEADS, HEAD), axis=(0, 1))
        * (LOG2E / math.sqrt(HEAD))
        * jax.nn.sigmoid(query_scale)
    )
    grad_query_w = jnp.einsum(
        "td,te->de", attn_in, grad_query_lin, preferred_element_type=jnp.float32
    )
    grad_key_w = jnp.einsum("td,te->de", attn_in, grad_keys, preferred_element_type=jnp.float32)
    grad_value_w = jnp.einsum("td,te->de", attn_in, grad_values, preferred_element_type=jnp.float32)
    grad_attn_in = jnp.einsum(
        "te,de->td", grad_query_lin, weights_back[1], preferred_element_type=jnp.float32
    )
    grad_attn_in = grad_attn_in + jnp.einsum(
        "te,de->td", grad_keys, weights_back[2], preferred_element_type=jnp.float32
    )
    grad_attn_in = grad_attn_in + jnp.einsum(
        "te,de->td", grad_values, weights_back[3], preferred_element_type=jnp.float32
    )
    unused_one, pull_one = jax.vjp(normed, inputs, gain_one)
    grad_in_norm, grad_gain_one = pull_one(grad_attn_in)
    grad_inputs = (grad_mid + grad_in_norm).astype(jnp.bfloat16)
    terms = (
        grad_gain_one,
        grad_query_w,
        grad_key_w,
        grad_value_w,
        grad_output_w,
        jnp.tile(grad_scale, lax.axis_size("wt")),
        grad_gain_two,
        grad_expand,
        grad_contract,
    )
    shares = (
        lax.psum_scatter(
            terms[0].astype(jnp.bfloat16), "wt", scatter_dimension=0, tiled=True
        ).astype(jnp.float32),
        lax.psum_scatter(
            terms[1].astype(jnp.bfloat16), "wt", scatter_dimension=0, tiled=True
        ).astype(jnp.float32),
        lax.psum_scatter(
            terms[2].astype(jnp.bfloat16), "wt", scatter_dimension=0, tiled=True
        ).astype(jnp.float32),
        lax.psum_scatter(
            terms[3].astype(jnp.bfloat16), "wt", scatter_dimension=0, tiled=True
        ).astype(jnp.float32),
        lax.psum_scatter(
            terms[4].astype(jnp.bfloat16), "wt", scatter_dimension=0, tiled=True
        ).astype(jnp.float32),
        lax.psum_scatter(
            terms[5].astype(jnp.bfloat16), "wt", scatter_dimension=0, tiled=True
        ).astype(jnp.float32),
        lax.psum_scatter(
            terms[6].astype(jnp.bfloat16), "wt", scatter_dimension=0, tiled=True
        ).astype(jnp.float32),
        lax.psum_scatter(
            terms[7].astype(jnp.bfloat16), "wt", scatter_dimension=0, tiled=True
        ).astype(jnp.float32),
        lax.psum_scatter(
            terms[8].astype(jnp.bfloat16), "wt", scatter_dimension=0, tiled=True
        ).astype(jnp.float32),
    )
    totals = (
        lax.psum(shares[0].astype(jnp.bfloat16), "ctx").astype(jnp.float32),
        lax.psum(shares[1].astype(jnp.bfloat16), "ctx").astype(jnp.float32),
        lax.psum(shares[2].astype(jnp.bfloat16), "ctx").astype(jnp.float32),
        lax.psum(shares[3].astype(jnp.bfloat16), "ctx").astype(jnp.float32),
        lax.psum(shares[4].astype(jnp.bfloat16), "ctx").astype(jnp.float32),
        lax.psum(shares[5].astype(jnp.bfloat16), "ctx").astype(jnp.float32),
        lax.psum(shares[6].astype(jnp.bfloat16), "ctx").astype(jnp.float32),
        lax.psum(shares[7].astype(jnp.bfloat16), "ctx").astype(jnp.float32),
        lax.psum(shares[8].astype(jnp.bfloat16), "ctx").astype(jnp.float32),
    )
    return (
        result.astype(jnp.bfloat16)[None],
        grad_inputs[None],
        totals[0],
        totals[1],
        totals[2],
        totals[3],
        totals[4],
        totals[5],
        totals[6],
        totals[7],
        totals[8],
    )


def solution(mesh):
    in_specs = (
        P("wt", "ctx", None),
        P("wt", "ctx", None),
        P("wt", None),
        P("wt", None),
        P("wt"),
        P("wt", None),
        P("wt", None),
        P("wt", None),
        P("wt", None),
        P(),
        P("wt"),
        P("wt", None),
        P("wt", None),
    )
    out_specs = (
        P("wt", "ctx", None),
        P("wt", "ctx", None),
        P("wt"),
        P("wt", None),
        P("wt", None),
        P("wt", None),
        P("wt", None),
        P(),
        P("wt"),
        P("wt", None),
        P("wt", None),
    )
    return jax.shard_map(
        per_device, mesh=mesh, in_specs=in_specs, out_specs=out_specs, check_vma=False
    )
```

profile of v0, /device:TPU:0, one launch (start us, length us, event | category | flops | bytes accessed | tf_op | source)
XLA Modules:
  0.0 1535.2 jit_solution(627939134033975347)
XLA Ops:
  9.5 5.3 all-gather
  15.0 43.7 %all-gather.17.cloned.1.call-done = bf16[1280,1280]{1,0:T(8,128)(2,1)} async-done(((bf16[640,1280]{1,0:T(8,128)(2,1)}), bf16[1280,1280]{1,0:T(8,128)(2,1)}) %all-gather.17.cloned.1.call-update) | async-done | bytes 3276816 | tf_op jit(solution)/shard_map/all_gather | solution.py:70
  62.6 44.1 %all-gather.11.cloned.1.call-done = bf16[1280,1280]{1,0:T(8,128)(2,1)} async-done(((bf16[640,1280]{1,0:T(8,128)(2,1)}), bf16[1280,1280]{1,0:T(8,128)(2,1)}) %all-gather.11.cloned.1.call-update) | async-done | bytes 3276816 | tf_op jit(solution)/shard_map/all_gather | solution.py:71
  119.5 35.3 %all-gather.15.cloned.1.call-done = bf16[1280,1280]{1,0:T(8,128)(2,1)} async-done(((bf16[640,1280]{1,0:T(8,128)(2,1)}), bf16[1280,1280]{1,0:T(8,128)(2,1)}) %all-gather.15.cloned.1.call-update) | async-done | bytes 3276816 | tf_op jit(solution)/shard_map/all_gather | solution.py:69
  154.7 5.6 copy.59
  164.5 80.8 %all-gather.19.cloned.1.call-done = bf16[4096,1280]{1,0:T(8,128)(2,1)} async-done(((bf16[256,1280]{1,0:T(8,128)(2,1)}), bf16[4096,1280]{1,0:T(8,128)(2,1)}) %all-gather.19.cloned.1.call-update) | async-done | bytes 10485776 | tf_op jit(solution)/shard_map/all_gather | solution.py:91
  245.3 14.3 copy.60
  259.7 29.1 %select_reduce_fusion.1 = (f32[16,256]{1,0:T(8,128)S(1)}, f32[16,256,4096]{2,1,0:T(8,128)}) fusion(pred[256,4096]{1,0:T(8,128)(4,1)S(1)} %and_and_fusion.1, bf16[256,16,80]{0,2,1:T(8,128)(2,1)S(1)} %get-tuple-element.542, bf16[4096,16,80]{0,2,1:T(8,128)(2,1)} %bitcast.179), kind=kOutput, calls=%fused_computation.39 | convolution fusion | flops 2717904896 | bytes 79314944 | tf_op jit(solution)/shard_map/qhd,khd->hqk/dot_general | solution.py:101
  288.8 22.3 %fusion.14 = f32[16,256]{1,0:T(8,128)S(1)} fusion(f32[16,256,4096]{2,1,0:T(8,128)} %get-tuple-element.424, f32[16,256]{1,0:T(8,128)S(1)} %broadcast_maximum_fusion, pred[256,4096]{1,0:T(8,128)(4,1)S(1)} %and_and_fusion.1), kind=kLoop, calls=%fused_computation.40 | loop fusion | flops 67104768 | bytes 68190208 | tf_op jit(solution)/shard_map/reduce_sum | solution.py:105
  311.1 23.1 %all-gather.13.cloned.1.call-done = bf16[4096,1280]{1,0:T(8,128)(2,1)} async-done(((bf16[256,1280]{1,0:T(8,128)(2,1)}), bf16[4096,1280]{1,0:T(8,128)(2,1)}) %all-gather.13.cloned.1.call-update) | async-done | bytes 10485776 | tf_op jit(solution)/shard_map/all_gather | solution.py:92
  334.1 14.5 copy.58
  348.6 28.8 %fusion.78 = (bf16[256,16,80]{0,2,1:T(8,128)(2,1)S(1)}, f32[256,16,80]{0,2,1:T(8,128)}) fusion(f32[256,16]{0,1:T(8,128)S(1)} %bitcast.193, bf16[4096,16,80]{0,2,1:T(8,128)(2,1)} %bitcast.185, f32[16,256,4096]{2,1,0:T(8,128)} %get-tuple-element.424, f32[16,256]{1,0:T(8,128)S(1)} %broadcast_maximum_fusion, pred[256,4096]{1,0:T(8,128)(4,1)S(1)} %and_and_fusion.1), kind=kOutput, calls=%fused_computation.160 | convolution fusion | flops 2752118784 | bytes 80642048 | tf_op jit(solution)/shard_map/hqk,khd->qhd/dot_general | solution.py:106
  383.3 44.9 %all-gather.23.cloned.1.call-done = bf16[1280,1280]{1,0:T(8,128)(2,1)} async-done(((bf16[640,1280]{1,0:T(8,128)(2,1)}), bf16[1280,1280]{1,0:T(8,128)(2,1)}) %all-gather.23.cloned.1.call-update) | async-done | bytes 3276816 | tf_op jit(solution)/shard_map/all_gather | solution.py:74
  432.3 43.9 %all-gather.25.cloned.1.call-done = bf16[1280,1280]{1,0:T(8,128)(2,1)} async-done(((bf16[640,1280]{1,0:T(8,128)(2,1)}), bf16[1280,1280]{1,0:T(8,128)(2,1)}) %all-gather.25.cloned.1.call-update) | async-done | bytes 3276816 | tf_op jit(solution)/shard_map/all_gather | solution.py:75
  487.2 303.0 %while.18 = (s32[]{:T(128)}, f32[256,16,80]{0,2,1:T(8,128)}, bf16[8,512,1280]{2,1,0:T(8,128)(2,1)}, bf16[8,512,1280]{2,1,0:T(8,128)(2,1)}, bf16[8,512,1280]{2,1,...) while((s32[]{:T(128)}, f32[256,16,80]{0,2,1:T(8,128)}, ...), condition=%wide.region_10.11_spmd.clone, body=%wide.region_8.10_spmd.clone.sunk | while | flops 1695753728 | bytes 87756664 | solution.py:198
  500.2 5.0 fusion.142
  509.3 6.0 fusion.144
  529.1 4.6 fusion.141
  537.8 5.0 fusion.142
  546.8 6.0 fusion.144
  567.1 4.6 fusion.141
  575.7 5.0 fusion.142
  584.8 6.0 fusion.144
  605.0 4.6 fusion.141
  613.6 5.0 fusion.142
  622.7 6.0 fusion.144
  642.9 4.6 fusion.141
  651.5 5.0 fusion.142
  660.6 6.0 fusion.144
  680.8 4.6 fusion.141
  689.4 5.0 fusion.142
  698.5 6.0 fusion.144
  727.4 5.0 fusion.142
  736.4 6.0 fusion.144
  756.7 4.6 fusion.141
  765.3 5.0 fusion.142
  774.4 6.0 fusion.144
  812.2 97.3 %reduce-scatter.9.cloned.1.call-done = bf16[256,1280]{1,0:T(8,128)(2,1)} async-done(((bf16[4096,1280]{1,0:T(8,128)(2,1)}), bf16[256,1280]{1,0:T(8,128)(2,1)}) %reduce-scatter.9.cloned.1.call-update) | async-done | bytes 655376 | tf_op jit(solution)/shard_map/reduce_scatter | solution.py:200
  913.5 118.7 %reduce-scatter.11.cloned.1.call-done = bf16[256,1280]{1,0:T(8,128)(2,1)} async-done(((bf16[4096,1280]{1,0:T(8,128)(2,1)}), bf16[256,1280]{1,0:T(8,128)(2,1)}) %reduce-scatter.11.cloned.1.call-update) | async-done | bytes 655376 | tf_op jit(solution)/shard_map/reduce_scatter | solution.py:206
  1036.2 43.4 %reduce-scatter.21.cloned.1.call-done = bf16[640,1280]{1,0:T(8,128)(2,1)} async-done(((bf16[1280,1280]{1,0:T(8,128)(2,1)}), bf16[640,1280]{1,0:T(8,128)(2,1)}) %reduce-scatter.21.cloned.1.call-update) | async-done | bytes 1638416 | tf_op jit(solution)/shard_map/reduce_scatter | solution.py:271
  1079.6 47.6 %reduce-scatter.19.cloned.1.call-done = bf16[640,1280]{1,0:T(8,128)(2,1)} async-done(((bf16[1280,1280]{1,0:T(8,128)(2,1)}), bf16[640,1280]{1,0:T(8,128)(2,1)}) %reduce-scatter.19.cloned.1.call-update) | async-done | bytes 1638416 | tf_op jit(solution)/shard_map/reduce_scatter | solution.py:262
  1127.2 47.6 %reduce-scatter.13.cloned.1.call-done = bf16[640,1280]{1,0:T(8,128)(2,1)} async-done(((bf16[1280,1280]{1,0:T(8,128)(2,1)}), bf16[640,1280]{1,0:T(8,128)(2,1)}) %reduce-scatter.13.cloned.1.call-update) | async-done | bytes 1638416 | tf_op jit(solution)/shard_map/reduce_scatter | solution.py:253
  1174.8 47.6 %reduce-scatter.23.cloned.1.call-done = bf16[640,1280]{1,0:T(8,128)(2,1)} async-done(((bf16[1280,1280]{1,0:T(8,128)(2,1)}), bf16[640,1280]{1,0:T(8,128)(2,1)}) %reduce-scatter.23.cloned.1.call-update) | async-done | bytes 1638416 | tf_op jit(solution)/shard_map/reduce_scatter | solution.py:274
  1222.4 47.5 %reduce-scatter.15.cloned.1.call-done = bf16[640,1280]{1,0:T(8,128)(2,1)} async-done(((bf16[1280,1280]{1,0:T(8,128)(2,1)}), bf16[640,1280]{1,0:T(8,128)(2,1)}) %reduce-scatter.15.cloned.1.call-update) | async-done | bytes 1638416 | tf_op jit(solution)/shard_map/reduce_scatter | solution.py:256
  1269.9 47.6 %reduce-scatter.17.cloned.1.call-done = bf16[640,1280]{1,0:T(8,128)(2,1)} async-done(((bf16[1280,1280]{1,0:T(8,128)(2,1)}), bf16[640,1280]{1,0:T(8,128)(2,1)}) %reduce-scatter.17.cloned.1.call-update) | async-done | bytes 1638416 | tf_op jit(solution)/shard_map/reduce_scatter | solution.py:259
  1331.2 5.1 all-reduce.5
  1336.5 36.1 %all-reduce.3 = (bf16[640]{0:T(1024)(128)(2,1)S(1)}, bf16[80]{0:T(256)(128)(2,1)S(1)}, bf16[640]{0:T(1024)(128)(2,1)S(1)}) all-reduce(bf16[640]{0:T(1024)(128)(2,1)S(1)} %dynamic-slice.1, bf16[80]{0:T(256)(128)(2,1)S(1)} %dynamic-slice.3, bf16[640]{0:T(1024)(128)(2,1)S(1)} %dynamic-slice.5), channel_id=1, replica_groups=mesh['ctx'=16,'wt'=2] {'ctx'}, use_global_device_ids=true, to_apply=%region_16.17 | all-reduce | flops 1360 | bytes 5440 | tf_op jit(solution)/shard_map/psum | solution.py:279
  1375.6 139.4 %all-reduce.8.cloned.1.call-done = (bf16[640,1280]{1,0:T(8,128)(2,1)}, bf16[640,1280]{1,0:T(8,128)(2,1)}, bf16[640,1280]{1,0:T(8,128)(2,1)}, bf16[640,1280]{1,0:...) async-done(((bf16[640,1280]{1,0:T(8,128)(2,1)}, bf16[640,1280]{1,0:T(8,128)(2,1)}, bf16[640,1280]{1,0:T(8,128)(2,1)}, bf16[640,1280]{1,0:T(8,128)(2,1)}, ...) | async-done | bytes 9830416 | tf_op jit(solution)/shard_map/psum | solution.py:280
  (317 shorter events, 284.3 us)
Async XLA Ops:
  7.2 51.5 %all-gather.17.cloned.1.call-start = ((), (), s32[]{:S(2)}) async-start(), calls=%async_computation.11 | async-start | bytes 4915200 | tf_op jit(solution)/shard_map/all_gather | solution.py:70
  7.9 6.9 copy-start.2
  7.9 98.8 %all-gather.11.cloned.1.call-start = ((), (), s32[]{:S(2)}) async-start(), calls=%async_computation.8 | async-start | bytes 4915200 | tf_op jit(solution)/shard_map/all_gather | solution.py:71
  8.7 146.0 %all-gather.15.cloned.1.call-start = ((), (), s32[]{:S(2)}) async-start(), calls=%async_computation.10 | async-start | bytes 4915200 | tf_op jit(solution)/shard_map/all_gather | solution.py:69
  9.4 235.9 %all-gather.19.cloned.1.call-start = ((), (), s32[]{:S(2)}) async-start(), calls=%async_computation.12 | async-start | bytes 11141120 | tf_op jit(solution)/shard_map/all_gather | solution.py:91
  14.8 145.6 %copy-start.28 = (f32[1280]{0:T(1024)}, f32[1280]{0:T(1024)S(1)}, u32[]{:S(2)}) copy-start(f32[1280]{0:T(1024)S(1)} %reshape.514) | copy-start | bytes 15364
  15.0 47.5 %copy-start.33 = (f32[256]{0:T(256)}, f32[256]{0:T(256)S(1)}, u32[]{:S(2)}) copy-start(f32[256]{0:T(256)S(1)} %fusion.34) | copy-start | bytes 3076
  15.0 145.3 %copy-start.30 = (f32[256]{0:T(256)}, f32[256]{0:T(256)S(1)}, u32[]{:S(2)}) copy-start(f32[256]{0:T(256)S(1)} %fusion.66) | copy-start | bytes 3076
  62.6 271.6 %all-gather.13.cloned.1.call-start = ((), (), s32[]{:S(2)}) async-start(), calls=%async_computation.9 | async-start | bytes 11141120 | tf_op jit(solution)/shard_map/all_gather | solution.py:92
  110.5 269.6 %all-gather.21.cloned.1.call-start = ((), (), s32[]{:S(2)}) async-start(), calls=%async_computation.13 | async-start | bytes 4915200 | tf_op jit(solution)/shard_map/all_gather | solution.py:72
  111.1 2.6 copy-start.41
  111.2 2.6 copy-start.36
  111.2 317.0 %all-gather.23.cloned.1.call-start = ((), (), s32[]{:S(2)}) async-start(), calls=%async_computation.14 | async-start | bytes 4915200 | tf_op jit(solution)/shard_map/all_gather | solution.py:74
  111.9 364.2 %all-gather.25.cloned.1.call-start = ((), (), s32[]{:S(2)}) async-start(), calls=%async_computation.15 | async-start | bytes 4915200 | tf_op jit(solution)/shard_map/all_gather | solution.py:75
  112.7 796.8 %reduce-scatter.9.cloned.1.call-start = ((), (), s32[]{:S(2)}) async-start(), calls=%async_computation.16 | async-start | bytes 11141120 | tf_op jit(solution)/shard_map/reduce_scatter | solution.py:200
  113.8 46.6 %copy-start.37 = (f32[80]{0:T(128)}, f32[80]{0:T(128)S(1)}, u32[]{:S(2)}) copy-start(f32[80]{0:T(128)S(1)} %fusion.68) | copy-start | bytes 964
  377.4 5.8 copy-start.14
  383.2 97.7 %copy-start.6 = (f32[256,1280]{1,0:T(8,128)}, f32[256,1280]{1,0:T(8,128)S(1)}, u32[]{:S(2)}) copy-start(f32[256,1280]{1,0:T(8,128)S(1)} %get-tuple-element.428) | copy-start | bytes 3932164
  428.1 48.0 %copy-start.25 = (bf16[1,256,1280]{2,1,0:T(8,128)(2,1)S(1)}, bf16[1,256,1280]{2,1,0:T(8,128)(2,1)}, u32[]{:S(2)}) copy-start(bf16[1,256,1280]{2,1,0:T(8,128)(2,1)} %param.16) | copy-start | bytes 1966084
  476.1 3.5 copy-start.10
  505.2 2.5 copy-start
  542.8 2.5 copy-start
  580.7 2.5 copy-start
  618.6 2.5 copy-start
  656.5 2.5 copy-start
  694.4 2.5 copy-start
  732.3 2.5 copy-start
  770.3 2.5 copy-start
  790.2 242.0 %reduce-scatter.11.cloned.1.call-start = ((), (), s32[]{:S(2)}) async-start(), calls=%async_computation.17 | async-start | bytes 11141120 | tf_op jit(solution)/shard_map/reduce_scatter | solution.py:206
  790.8 288.8 %reduce-scatter.21.cloned.1.call-start = ((), (), s32[]{:S(2)}) async-start(), calls=%async_computation.22 | async-start | bytes 4915200 | tf_op jit(solution)/shard_map/reduce_scatter | solution.py:271
  794.7 332.5 %reduce-scatter.19.cloned.1.call-start = ((), (), s32[]{:S(2)}) async-start(), calls=%async_computation.21 | async-start | bytes 4915200 | tf_op jit(solution)/shard_map/reduce_scatter | solution.py:262
  799.3 375.5 %reduce-scatter.13.cloned.1.call-start = ((), (), s32[]{:S(2)}) async-start(), calls=%async_computation.18 | async-start | bytes 4915200 | tf_op jit(solution)/shard_map/reduce_scatter | solution.py:253
  800.7 2.7 copy-start.3
  800.7 2.7 copy-start.29
  800.7 2.7 copy-start.31
  806.4 416.0 %reduce-scatter.23.cloned.1.call-start = ((), (), s32[]{:S(2)}) async-start(), calls=%async_computation.23 | async-start | bytes 4915200 | tf_op jit(solution)/shard_map/reduce_scatter | solution.py:274
  812.0 457.9 %reduce-scatter.15.cloned.1.call-start = ((), (), s32[]{:S(2)}) async-start(), calls=%async_computation.19 | async-start | bytes 4915200 | tf_op jit(solution)/shard_map/reduce_scatter | solution.py:256
  913.5 404.0 %reduce-scatter.17.cloned.1.call-start = ((), (), s32[]{:S(2)}) async-start(), calls=%async_computation.20 | async-start | bytes 4915200 | tf_op jit(solution)/shard_map/reduce_scatter | solution.py:259
  1036.2 478.8 %all-reduce.8.cloned.1.call-start = ((), (), s32[]{:S(2)}) async-start(), calls=%async_computation.24 | async-start | bytes 19660800 | tf_op jit(solution)/shard_map/psum | solution.py:280
  1317.5 2.5 copy-start.42
  1317.5 2.7 copy-start.13
  1320.1 3.2 copy-start.8
  1320.1 3.2 copy-start.23
  1323.3 4.1 copy-start.9
  1323.3 4.1 copy-start.11
  1327.4 2.4 copy-start.39
  1329.9 44.5 %copy-start.34 = (f32[256]{0:T(256)S(1)}, f32[256]{0:T(256)}, u32[]{:S(2)}) copy-start(f32[256]{0:T(256)} %copy-done.33) | copy-start | bytes 3076
  1515.0 3.5 copy-start.20
  (20 other events, 30.7 us)
Sparse Core Ops, SparseCore 0:
  9.6 49.0 all-gather.16
  60.2 46.4 all-gather.10
  108.2 46.4 all-gather.14
  157.4 87.8 all-gather.18
  248.0 86.0 all-gather.12
  335.5 44.5 all-gather.20
  381.7 46.4 all-gather.22
  429.7 46.4 all-gather.24
  790.4 119.0 reduce-scatter.8
  913.4 118.7 reduce-scatter.10
  1035.0 44.5 reduce-scatter.20
  1082.4 44.7 reduce-scatter.18
  1130.0 44.7 reduce-scatter.12
  1177.6 44.7 reduce-scatter.22
  1225.0 44.7 reduce-scatter.14
  1272.6 44.7 reduce-scatter.16
  1321.7 193.2 all-reduce.7
where the time goes:
time: 1540 us
  waiting for transfers between devices  960 us (62%)
  matrix products  292 us (19%)
  local copies, waits for them, and re-layouts  158 us (10%)
  other arithmetic  52 us (3%)
  blocking collectives  51 us (3%)
  between operations  16.6 us (1%)
    psum x1, waiting for transfers between devices, per_device(): lax.psum(shares[1].astype(jnp.bfloat16), 'ctx').astype(jnp.float32)  139 us
    reduce_scatter x1, waiting for transfers between devices, per_device(): lax.psum_scatter(key_terms[1].reshape(group_rows, feat_width).astype(jnp....  119 us
    reduce_scatter x1, waiting for transfers between devices, per_device(): lax.psum_scatter(key_terms[0].reshape(group_rows, feat_width).astype(jnp....  97.3 us
    all_gather x1, waiting for transfers between devices, per_device(): lax.all_gather(key_own, 'ctx', axis=0, tiled=True)  80.8 us
    dynamic_update_slice x24, local copies, waits for them, and re-layouts, per_device(): query_grad, key_terms = lax.scan(back_block, query_zero, key_blocks)  56.3 us
    dynamic_slice x40, local copies, waits for them, and re-layouts, per_device(): query_grad, key_terms = lax.scan(back_block, query_zero, key_blocks)  53.6 us
    dot_general x8, matrix products, back_block(): jnp.einsum('hqk,qhd->khd', probabilities.astype(jnp.bfloat16), out_grad,...  48 us
    reduce_scatter x1, waiting for transfers between devices, per_device(): lax.psum_scatter(terms[1].astype(jnp.bfloat16), 'wt', scatter_dimension=0...  47.6 us
  transfers between devices with their start and end apart: 17, of which 17 were waited for; matrix products, arithmetic and copies ran while one was open for 11% of the time, Pallas kernels for 0%

commit v1 on v0

--- a/solution.py
+++ b/solution.py
@@ -1,8 +1,12 @@
+import functools
 import math
 
 import jax
 import jax.numpy as jnp
+import numpy as np
 from jax import lax
+from jax.experimental import pallas as pl
+from jax.experimental.pallas import tpu as pltpu
 from jax.sharding import PartitionSpec as P
 
 HEADS = 16
@@ -301,6 +305,622 @@
     )
 
 
+BF = jnp.bfloat16
+F32 = jnp.float32
+NN = (((1,), (0,)), ((), ()))
+NT = (((1,), (1,)), ((), ()))
+AXES = ("ctx", "wt")
+LIMIT = 56 * 1024 * 1024
+
+RING = ((0, 0), (1, 0), (2, 0), (3, 0), (3, 1), (2, 1), (1, 1), (0, 1))
+PLACE = {chip: at for at, chip in enumerate(RING)}
+OFFSETS = (0, -1, 1, -2, 2, -3, 3, 4)
+
+
+def flat(z, x, core, y):
+    return ((z * 2 + x) * 2 + core) * 2 + y
+
+
+def pairs(move):
+    return [
+        (flat(z, x, core, y), flat(*move(z, x, core, y)))
+        for z in range(4)
+        for x in range(2)
+        for core in range(2)
+        for y in range(2)
+    ]
+
+
+def turned(by):
+    def move(z, x, core, y):
+        return (*RING[(PLACE[(z, x)] + by) % 8], core, y)
+
+    return move
+
+
+CORE_SWAP = pairs(lambda z, x, core, y: (z, x, 1 - core, y))
+Y_SWAP = pairs(lambda z, x, core, y: (z, x, core, 1 - y))
+X_SWAP = pairs(lambda z, x, core, y: (z, 1 - x, core, y))
+NEAR_SWAP = pairs(lambda z, x, core, y: (z ^ 1, x, core, y))
+FAR_SWAP = pairs(lambda z, x, core, y: (z ^ 2, x, core, y))
+FORTH = pairs(turned(1))
+BACK = pairs(turned(-1))
+
+
+def slot_table():
+    rows = []
+    for c in range(16):
+        z, x, core = c // 4, (c // 2) % 2, c % 2
+        chips = [RING[(PLACE[(z, x)] + by) % 8] for by in OFFSETS]
+        own = [(a * 2 + b) * 2 + core for a, b in chips]
+        rows.append(own + [dev ^ 1 for dev in own])
+    return np.asarray(rows, np.int32)
+
+
+def send(value, moves):
+    return lax.ppermute(value, AXES, moves)
+
+
+def mm(left, right, dims=NN):
+    return lax.dot_general(left, right, dims, preferred_element_type=F32)
+
+
+def call(body, outs, args, smem=0, anys=0, scratch=(), cost=None, out_any=False):
+    whole = pl.BlockSpec(memory_space=pltpu.VMEM)
+    specs = [pl.BlockSpec(memory_space=pltpu.SMEM)] * smem
+    specs += [whole] * (len(args) - smem - anys)
+    specs += [pl.BlockSpec(memory_space=pl.ANY)] * anys
+    out_spec = pl.BlockSpec(memory_space=pl.ANY) if out_any else whole
+    estimate = None
+    if cost is not None:
+        estimate = pl.CostEstimate(flops=int(cost[0]), bytes_accessed=int(cost[1]), transcendentals=int(cost[2]))
+    return pl.pallas_call(
+        body,
+        out_shape=[jax.ShapeDtypeStruct(shape, kind) for shape, kind in outs],
+        in_specs=specs,
+        out_specs=[out_spec] * len(outs),
+        scratch_shapes=list(scratch),
+        cost_estimate=estimate,
+        compiler_params=pltpu.CompilerParams(vmem_limit_bytes=LIMIT),
+    )(*args)
+
+
+def half(y, width=640):
+    return pl.ds(pl.multiple_of(y * width, 128), width)
+
+
+def pick_kernel(info, wq, wk, wv, gain_a, gain_m, out):
+    chip = info[2]
+    cols = lax.broadcasted_iota(jnp.int32, (2 * HEAD, wq.shape[1]), 1)
+    rows = lax.broadcasted_iota(jnp.int32, (2 * HEAD, wq.shape[1]), 0)
+    chosen = jnp.where(cols == rows + chip * (2 * HEAD), 1.0, 0.0).astype(BF)
+    for at, ref in enumerate((wq, wk, wv)):
+        both = mm(chosen, ref[...], NT).astype(BF)
+        out[at * HEAD : (at + 1) * HEAD] = both[:HEAD]
+        out[3 * HEAD + at * HEAD : 3 * HEAD + (at + 1) * HEAD] = both[HEAD:]
+    line = lax.broadcasted_iota(jnp.int32, (16, gain_a.shape[1]), 0)
+    tail = jnp.where(line == 0, gain_a[...].astype(F32), 0.0)
+    tail = jnp.where(line == 1, gain_m[...].astype(F32), tail)
+    out[6 * HEAD :] = tail.astype(BF)
+
+
+def project_kernel(count, info, *refs):
+    xs = refs[:count]
+    own, other, scale, attn_in, mine, partner, weight, gain, lines = refs[count:]
+    y, core = info[0], info[1]
+    weight[:, half(y)] = own[: 6 * HEAD]
+    weight[:, half(1 - y)] = other[: 6 * HEAD]
+    gain[:, half(y)] = own[6 * HEAD :].astype(F32)
+    gain[:, half(1 - y)] = other[6 * HEAD :].astype(F32)
+    row = 0
+    for ref in xs:
+        values = ref[...].astype(F32)
+        scaled = values * lax.rsqrt(jnp.mean(values * values, axis=-1, keepdims=True) + EPS)
+        attn_in[row : row + ref.shape[0]] = (scaled * gain[0:1]).astype(BF)
+        row += ref.shape[0]
+    lin = mm(weight[...], attn_in[...], NT)
+    for head in range(2):
+        base = head * 3 * HEAD
+        lines[base : base + HEAD] = (lin[base : base + HEAD] * scale[...]).astype(BF)
+        lines[base + HEAD : base + 3 * HEAD] = lin[base + HEAD : base + 3 * HEAD].astype(BF)
+    mine[...] = lines[pl.ds(pl.multiple_of(core * 3 * HEAD, 16), 3 * HEAD)]
+    partner[...] = lines[pl.ds(pl.multiple_of((1 - core) * 3 * HEAD, 16), 3 * HEAD)]
+
+
+def span_slots(pieces):
+    return [(ref, col) for ref in pieces for col in range(0, ref.shape[1], SPAN)]
+
+
+def natural_span(info, deal, slot):
+    return deal[2 * info[4 + slot // 2] + slot % 2]
+
+
+def at_span(span):
+    return pl.ds(pl.multiple_of(span * SPAN, SPAN), SPAN)
+
+
+BLOCK = 512
+
+
+def forward_kernel(info, deal, *refs):
+    pieces = refs[:10]
+    out, lse, queries, keys, values, dealt = refs[10:]
+    total = queries.shape[1]
+    length = info[3]
+    spans = total // SPAN
+
+    @pl.loop(0, spans)
+    def _(at):
+        dealt[deal[at]] = at
+
+    line = lax.broadcasted_iota(jnp.int32, (16, total), 0)
+    values[HEAD:] = jnp.where(line == 0, 1.0, 0.0).astype(BF)
+    for slot, (ref, col) in enumerate(span_slots(pieces)):
+        where = at_span(natural_span(info, deal, slot))
+        queries[:, where] = ref[:HEAD, col : col + SPAN]
+        keys[where, :] = ref[HEAD : 2 * HEAD, col : col + SPAN].T
+        values[:HEAD, where] = ref[2 * HEAD :, col : col + SPAN]
+
+    key_at = lax.broadcasted_iota(jnp.int32, (BLOCK, BLOCK), 0)
+    query_at = lax.broadcasted_iota(jnp.int32, (BLOCK, BLOCK), 1)
+
+    @pl.loop(0, total // BLOCK)
+    def _(i):
+        here = pl.ds(pl.multiple_of(i * BLOCK, BLOCK), BLOCK)
+        query = queries[:, here]
+
+        def step(masked, j, carry):
+            peak, acc = carry
+            there = pl.ds(pl.multiple_of(j * BLOCK, BLOCK), BLOCK)
+            scores = mm(keys[there, :], query)
+            if masked:
+                key_pos = j * BLOCK + key_at
+                allowed = (key_pos <= i * BLOCK + query_at) & (key_pos < length)
+                scores = jnp.where(allowed, scores, NEG)
+            newest = jnp.maximum(peak, jnp.max(scores, axis=0, keepdims=True))
+            weights = jnp.exp(scores - newest)
+            acc = acc * jnp.exp(peak - newest) + mm(values[:, there], weights.astype(BF))
+            return newest, acc
+
+        carry = (jnp.full((1, BLOCK), NEG, F32), jnp.zeros((HEAD + 16, BLOCK), F32))
+        split = jnp.minimum(i, length // BLOCK)
+        carry = lax.fori_loop(0, split, functools.partial(step, False), carry)
+        peak, acc = lax.fori_loop(split, i + 1, functools.partial(step, True), carry)
+        norm = acc[HEAD : HEAD + 1]
+        lse[:, here] = peak + jnp.log(norm)
+        attended = (acc[:HEAD] / norm).astype(BF)
+        for part in range(BLOCK // SPAN):
+            row = dealt[i * (BLOCK // SPAN) + part]
+            out[row // 2, :, at_span(row % 2)] = attended[:, part * SPAN : (part + 1) * SPAN]
+
+
+def backward_kernel(info, deal, *refs):
+    pieces = refs[:10]
+    lse, attended, grad_out, scale, out = refs[10:15]
+    q_n, k_n, v_n, g_n, q_t, k_t, g_t, delta, dq_t, dk, dv, dealt = refs[15:]
+    total = q_t.shape[1]
+    length = info[3]
+    spans = total // SPAN
+    blocks = total // BLOCK
+
+    @pl.loop(0, spans)
+    def _(at):
+        dealt[deal[at]] = at
+
+    for slot, (ref, col) in enumerate(span_slots(pieces)):
+        where = at_span(natural_span(info, deal, slot))
+        cols = slice(col, col + SPAN)
+        q_t[:, where] = ref[:HEAD, cols]
+        k_t[:, where] = ref[HEAD : 2 * HEAD, cols]
+        q_n[where, :] = ref[:HEAD, cols].T
+        k_n[where, :] = ref[HEAD : 2 * HEAD, cols].T
+        v_n[where, :] = ref[2 * HEAD :, cols].T
+    for row in range(spans):
+        where = at_span(deal[row])
+        cols = slice(row % 2 * SPAN, row % 2 * SPAN + SPAN)
+        grad = grad_out[row // 2, :, cols]
+        g_t[:, where] = grad
+        g_n[where, :] = grad.T
+        product = grad.astype(F32) * attended[row // 2, :, cols].astype(F32)
+        delta[:, where] = jnp.sum(product, axis=0, keepdims=True)
+    dq_t[...] = jnp.zeros_like(dq_t)
+
+    key_at = lax.broadcasted_iota(jnp.int32, (BLOCK, BLOCK), 0)
+    query_at = lax.broadcasted_iota(jnp.int32, (BLOCK, BLOCK), 1)
+
+    @pl.loop(0, blocks)
+    def _(j):
+        there = pl.ds(pl.multiple_of(j * BLOCK, BLOCK), BLOCK)
+        dk[...] = jnp.zeros_like(dk)
+        dv[...] = jnp.zeros_like(dv)
+
+        def step(masked, i, carry):
+            here = pl.ds(pl.multiple_of(i * BLOCK, BLOCK), BLOCK)
+            scores = mm(k_n[there, :], q_t[:, here])
+            probs = jnp.exp(scores - lse[:, here])
+            if masked:
+                key_pos = j * BLOCK + key_at
+                allowed = (key_pos <= i * BLOCK + query_at) & (key_pos < length)
+                probs = jnp.where(allowed, probs, 0.0)
+            grad_probs = mm(v_n[there, :], g_t[:, here])
+            grad_scores = (probs * (grad_probs - delta[:, here])).astype(BF)
+            dv[...] += mm(probs.astype(BF), g_n[here, :])
+            dk[...] += mm(grad_scores, q_n[here, :])
+            dq_t[:, here] += mm(k_t[:, there], grad_scores)
+            return carry
+
+        split = jnp.where((j + 1) * BLOCK <= length, j + 1, blocks)
+        lax.fori_loop(j, split, functools.partial(step, True), 0)
+        lax.fori_loop(split, blocks, functools.partial(step, False), 0)
+        for part in range(BLOCK // SPAN):
+            row = dealt[j * (BLOCK // SPAN) + part]
+            rows = slice(part * SPAN, (part + 1) * SPAN)
+            out[row // 2, HEAD : 2 * HEAD, at_span(row % 2)] = dk[rows].T.astype(BF)
+            out[row // 2, 2 * HEAD :, at_span(row % 2)] = dv[rows].T.astype(BF)
+
+    for row in range(spans):
+        cols = slice(row % 2 * SPAN, row % 2 * SPAN + SPAN)
+        out[row // 2, :HEAD, cols] = (dq_t[:, at_span(deal[row])] * scale[...]).astype(BF)
+
+
+def load_weights(info, parts, wholes, sems):
+    y, core = info[0], info[1]
+    started = []
+    for at, whole in enumerate(wholes):
+        own, direct, passed = parts[3 * at : 3 * at + 3]
+        rows, part = own.shape[0], direct.shape[0]
+        far = (1 - y) * rows
+        places = ((own, y * rows), (direct, far + core * part), (passed, far + (1 - core) * part))
+        copies = []
+        for piece, (ref, start) in enumerate(places):
+            target = whole.at[pl.ds(pl.multiple_of(start, 64), ref.shape[0])]
+            copies.append(pltpu.make_async_copy(ref, target, sems.at[3 * at + piece]))
+            copies[-1].start()
+        started.append(copies)
+    return started
+
+
+def arrive(copies):
+    for copy in copies:
+        copy.wait()
+
+
+def mlp_kernel(info, tokens, cotangent, attn_t, own, other, *refs):
+    parts, outs = refs[:9], refs[9:16]
+    w_output, w_expand, w_contract, gain, sems = refs[16:]
+    result, grad_mid_out, grad_attended_t, act_out, mlp_in_out, grad_expanded_out, grad_mid_low_out = outs
+    y = info[0]
+    loads = load_weights(info, parts, (w_output, w_expand, w_contract), sems)
+    gain[:, half(y)] = own[6 * HEAD :].astype(F32)
+    gain[:, half(1 - y)] = other[6 * HEAD :].astype(F32)
+    gains = gain[1:2]
+    attn = attn_t[...].T
+    arrive(loads[0])
+    mid = tokens[...].astype(F32) + mm(attn, w_output[...])
+    rate = lax.rsqrt(jnp.mean(mid * mid, axis=-1, keepdims=True) + EPS)
+    mlp_in = (mid * rate * gains).astype(BF)
+    mlp_in_out[...] = mlp_in
+    arrive(loads[1])
+    expanded = mm(mlp_in, w_expand[...])
+    gate = jax.nn.sigmoid(expanded)
+    act = (expanded * gate).astype(BF)
+    act_out[...] = act
+    arrive(loads[2])
+    result[...] = (mid + mm(act, w_contract[...])).astype(BF)
+    grad_act = mm(cotangent[...], w_contract[...], NT)
+    grad_expanded = (grad_act * gate * (1.0 + expanded * (1.0 - gate))).astype(BF)
+    grad_expanded_out[...] = grad_expanded
+    grad_mlp_in = mm(grad_expanded, w_expand[...], NT) * gains
+    inner = jnp.mean(grad_mlp_in * mid, axis=-1, keepdims=True)
+    grad_mid = cotangent[...].astype(F32) + rate * grad_mlp_in - mid * (rate * rate * rate * inner)
+    grad_mid_out[...] = grad_mid
+    low = grad_mid.astype(BF)
+    grad_mid_low_out[...] = low
+    grad_attended_t[...] = mm(w_output[...], low, NT).astype(BF)
+
+
+def outer_kernel(info, act, cotangent, mlp_in, grad_expanded, attn_t, grad_mid_low, *outs):
+    core = info[1]
+    lefts = (act[...].T, mlp_in[...].T, attn_t[...])
+    for at, right in enumerate((cotangent, grad_expanded, grad_mid_low)):
+        outs[2 * at][...] = mm(lefts[at], right[:, half(core)]).astype(BF)
+        outs[2 * at + 1][...] = mm(lefts[at], right[:, half(1 - core)]).astype(BF)
+
+
+def row_sums(products):
+    ones = jnp.ones((16, products.shape[1]), BF)
+    high = products.astype(BF)
+    low = (products - high.astype(F32)).astype(BF)
+    return mm(ones, high, NT) + mm(ones, low, NT)
+
+
+def piece_rows(refs):
+    slots = []
+    for colour in range(2):
+        group = refs[9 * colour : 9 * colour + 9]
+        slots += [[(ref, 0)] for ref in group[:7]]
+        slots.append([(group[7], 0), (group[8], group[7].shape[0])])
+    return slots
+
+
+def spread_kernel(info, *refs):
+    pieces, (w_expand, gain) = refs[:18], refs[18:20]
+    outs, grad_gain, stage = refs[20:23], refs[23], refs[24]
+    for slot, parts in enumerate(piece_rows(pieces)):
+        dev = info[4 + slot]
+        block = ((dev // 2) % 2) * 4 + dev // 4
+        for ref, row in parts:
+            stage[slot, row : row + ref.shape[0]] = ref[...]
+        rows = pl.ds(pl.multiple_of(block * 80, 16), 80)
+        for at in range(3):
+            outs[at][rows, half(dev % 2)] = stage[slot, at * 80 : at * 80 + 80].astype(F32)
+    grad_gain[...] = row_sums(w_expand[...].astype(F32) * outs[1][...])[0:1] / gain[...].astype(F32)
+
+
+def weight_kernel(info, grads, own, other, *refs):
+    inputs = refs[:10]
+    keep, away, lines, weight, total = refs[10:]
+    y, core = info[0], info[1]
+    slot = 0
+    for ref in inputs:
+        for _ in range(0, ref.shape[0], 256):
+            lines[:, slot * 256 : slot * 256 + 256] = grads[info[4 + slot]]
+            slot += 1
+    weight[:, half(y)] = own[pl.ds(pl.multiple_of(core * 3 * HEAD, 16), HEAD)].astype(F32)
+    weight[:, half(1 - y)] = other[pl.ds(pl.multiple_of(core * 3 * HEAD, 16), HEAD)].astype(F32)
+    total[...] = jnp.zeros_like(total)
+    col = 0
+    for ref in inputs:
+        total[...] += mm(lines[:, col : col + ref.shape[0]], ref[...])
+        col += ref.shape[0]
+    keep[: 3 * HEAD] = total[:, half(y)]
+    away[: 3 * HEAD] = total[:, half(1 - y)].astype(BF)
+    sums = row_sums(weight[...] * total[:HEAD])
+    keep[3 * HEAD :] = jnp.zeros((16, keep.shape[1]), F32)
+    away[3 * HEAD :] = jnp.zeros((16, keep.shape[1]), BF)
+    keep[3 * HEAD :, :HEAD] = sums
+    away[3 * HEAD :, :HEAD] = sums.astype(BF)
+
+
+def finish_kernel(info, *refs):
+    pieces, (wq, wk, wv, gain, factor) = refs[:18], refs[18:23]
+    outs, grad_gain, grad_scale = refs[23:26], refs[26], refs[27]
+    stage, stacks = refs[28], refs[29:32]
+    scale_sum = jnp.zeros((1, HEAD), F32)
+    for slot, parts in enumerate(piece_rows(pieces)):
+        dev = info[4 + slot]
+        for ref, row in parts:
+            stage[slot, row : row + ref.shape[0]] = ref[...]
+        rows = pl.ds(pl.multiple_of(dev * HEAD, 16), HEAD)
+        for at in range(3):
+            stacks[at][rows] = stage[slot, at * HEAD : (at + 1) * HEAD]
+        scale_sum += stage[slot, 3 * HEAD :, :HEAD].astype(F32)[0:1]
+    grad_scale[...] = scale_sum * factor[...]
+    size = stage.shape[2]
+    same = lax.broadcasted_iota(jnp.int32, (size, size), 0) == lax.broadcasted_iota(jnp.int32, (size, size), 1)
+    unit = jnp.where(same, 1.0, 0.0).astype(BF)
+    sums = jnp.zeros((16, size), F32)
+    for at, own in enumerate((wq, wk, wv)):
+        turned_grad = mm(unit, stacks[at][...], NT)
+        outs[at][...] = turned_grad
+        sums += row_sums(own[...].astype(F32) * turned_grad)
+    grad_gain[...] = sums[0:1] / gain[...].astype(F32)
+
+
+def input_kernel(info, tokens, grads, grad_mid, own, other, *refs):
+    parts, out = refs[:9], refs[9]
+    weights, gain, sems = refs[10:13], refs[13], refs[14]
+    y = info[0]
+    loads = load_weights(info, parts, weights, sems)
+    gain[:, half(y)] = own[6 * HEAD :].astype(F32)
+    gain[:, half(1 - y)] = other[6 * HEAD :].astype(F32)
+    heads, width = grads.shape[0], grads.shape[2]
+    turned_grad = jnp.zeros((heads * HEAD, width), F32)
+    for at, ref in enumerate(weights):
+        part = grads[:, at * HEAD : (at + 1) * HEAD, :].reshape(heads * HEAD, width)
+        arrive(loads[at])
+        turned_grad += mm(ref[...], part)
+    grad = turned_grad.T * gain[0:1]
+    values = tokens[...].astype(F32)
+    rate = lax.rsqrt(jnp.mean(values * values, axis=-1, keepdims=True) + EPS)
+    inner = jnp.mean(grad * values, axis=-1, keepdims=True)
+    out[...] = (grad_mid[...] + rate * grad - values * (rate * rate * rate * inner)).astype(BF)
+
+
+def ring_gather(value, pieces_wanted=True):
+    forth, back = [value], [value]
+    for _ in range(3):
+        forth.append(send(forth[-1], FORTH))
+        back.append(send(back[-1], BACK))
+    cut = value.shape[0] // 32 * 16
+    last = (send(forth[-1][:cut], FORTH), send(back[-1][cut:], BACK))
+    return [value, forth[1], back[1], forth[2], back[2], forth[3], back[3], *last]
+
+
+def chip_gather(value):
+    mine = ring_gather(value)
+    return mine + [send(piece, CORE_SWAP) for piece in mine]
+
+
+def weight_parts(shards, core):
+    parts = []
+    for shard in shards:
+        size = shard.shape[0] // 2
+        direct = send(lax.dynamic_slice_in_dim(shard, core * size, size, 0), Y_SWAP)
+        parts += [shard, direct, send(direct, CORE_SWAP)]
+    return parts
+
+
+def halve(keep, away, where, moves, axis):
+    mine = lax.dynamic_index_in_dim(keep, where, axis, keepdims=False)
+    theirs = lax.dynamic_index_in_dim(keep, 1 - where, axis, keepdims=False)
+    return (mine.astype(F32) + send(theirs, moves).astype(F32)).astype(BF)
+
+
+def ring_device(
+    tokens, cotangent, deal, lengths, gain_attn, w_query, w_key, w_value, w_output, query_scale,
+    gain_mlp, w_expand, w_contract
+):
+    rows, width = tokens.shape[1:]
+    c, y = lax.axis_index("ctx"), lax.axis_index("wt")
+    core, x, z = c % 2, (c // 2) % 2, c // 4
+    table = lax.dynamic_index_in_dim(jnp.asarray(slot_table()), c, 0, keepdims=False)
+    info = jnp.concatenate([jnp.stack([y, core, c // 2, lengths[0, 0]]).astype(jnp.int32), table])
+    dealt = deal[0]
+    total = rows * 16
+    softplus = jax.nn.softplus(query_scale)
+    scale_col = (LOG2E / math.sqrt(HEAD) * softplus)[:, None]
+    factor = (jax.nn.sigmoid(query_scale) / softplus)[None, :]
+    inputs = tokens[0]
+    cot = cotangent[0]
+
+    arrived = ring_gather(inputs)
+    own = call(
+        pick_kernel,
+        [((6 * HEAD + 16, width // 2), BF)],
+        [info, w_query, w_key, w_value, gain_attn[None], gain_mlp[None]],
+        smem=1,
+        cost=(2 * 480 * 640 * 1280, 3 * 640 * 1280 * 2, 0),
+    )[0]
+    other = send(own, Y_SWAP)
+    mlp_weights = weight_parts((w_output, w_expand, w_contract), core)
+
+    attn_in, mine, partner = [], [], []
+    for group in (arrived[:1], arrived[1:3], arrived[3:5], arrived[5:7], arrived[7:]):
+        count = sum(part.shape[0] for part in group)
+        got = call(
+            functools.partial(project_kernel, len(group)),
+            [((count, width), BF), ((3 * HEAD, count), BF), ((3 * HEAD, count), BF)],
+            [info, *group, own, other, scale_col],
+            smem=1,
+            scratch=[
+                pltpu.VMEM((6 * HEAD, width), BF),
+                pltpu.VMEM((16, width), F32),
+                pltpu.VMEM((6 * HEAD, count), BF),
+            ],
+            cost=(2 * 480 * 1280 * count, 4 * 1280 * count, 0),
+        )
+        attn_in.append(got[0])
+        mine.append(got[1])
+        partner.append(send(got[2], CORE_SWAP))
+    spans = mine + partner
+
+    attended, lse = call(
+        forward_kernel,
+        [((16, HEAD, rows), BF), ((1, total), F32)],
+        [info, dealt, *spans],
+        smem=2,
+        scratch=[
+            pltpu.VMEM((HEAD, total), BF),
+            pltpu.VMEM((total, HEAD), BF),
+            pltpu.VMEM((HEAD + 16, total), BF),
+            pltpu.SMEM((total // SPAN,), jnp.int32),
+        ],
+        cost=(2 * total * total * 256, 3 * total * 160, total * total // 2),
+    )
+    attn_in += [send(piece, CORE_SWAP) for piece in attn_in]
+    back_weights = weight_parts((w_query, w_key, w_value), core)
+
+    attn_t = lax.all_to_all(attended, "ctx", 0, 0).reshape(width, rows)
+    whole_scratch = [pltpu.VMEM((width, width), BF)] * 3
+    whole_scratch += [pltpu.VMEM((16, width), F32), pltpu.SemaphoreType.DMA((9,))]
+    wide, low = ((rows, width), F32), ((rows, width), BF)
+    result, grad_mid, grad_attended_t, act, mlp_in, grad_expanded, grad_mid_low = call(
+        mlp_kernel,
+        [low, wide, ((width, rows), BF), low, low, low, low],
+        [info, inputs, cot, attn_t, own, other, *mlp_weights],
+        smem=1,
+        anys=9,
+        scratch=whole_scratch,
+        cost=(12 * rows * width * width, 6 * width * width, 0),
+    )
+    grad_out = lax.all_to_all(grad_attended_t.reshape(16, HEAD, rows), "ctx", 0, 0)
+
+    terms = call(
+        outer_kernel,
+        [((width, width // 2), BF)] * 6,
+        [info, act, cot, mlp_in, grad_expanded, attn_t, grad_mid_low],
+        smem=1,
+        cost=(6 * rows * width * width, 6 * width * width, 0),
+    )
+    bits = {"y": (y, Y_SWAP), "x": (x, X_SWAP), "far": (z // 2, FAR_SWAP), "near": (z % 2, NEAR_SWAP)}
+    orders = (("y", "x", "near", "far"), ("x", "y", "near", "far"), ("near", "y", "x", "far"))
+    pieces = []
+    for at, order in enumerate(orders):
+        held = (terms[2 * at].astype(F32) + send(terms[2 * at + 1], CORE_SWAP).astype(F32)).astype(BF)
+        held = held.reshape(2, 2, 2, 2, 80, width // 2)
+        left = ["y", "x", "far", "near"]
+        for name in order:
+            held = halve(held, None, bits[name][0], bits[name][1], left.index(name))
+            left.remove(name)
+        pieces.append(held)
+    spread = chip_gather(jnp.concatenate(pieces, axis=0))
+    shard = ((width // 2, width), F32)
+    line = ((1, width // 2), F32)
+    grad_contract, grad_expand, grad_output, grad_gain_mlp = call(
+        spread_kernel,
+        [shard, shard, shard, line],
+        [info, *spread, w_expand, gain_mlp[None]],
+        smem=1,
+        scratch=[pltpu.VMEM((16, 240, width // 2), BF)],
+        cost=(0, 3 * 640 * 1280 * 4, 0),
+    )
+
+    grads = call(
+        backward_kernel,
+        [((16, 3 * HEAD, rows), BF)],
+        [info, dealt, *spans, lse, attended, grad_out, scale_col],
+        smem=2,
+        scratch=[pltpu.VMEM((total, HEAD), BF)] * 4
+        + [pltpu.VMEM((HEAD, total), BF)] * 3
+        + [
+            pltpu.VMEM((1, total), F32),
+            pltpu.VMEM((HEAD, total), F32),
+            pltpu.VMEM((BLOCK, HEAD), F32),
+            pltpu.VMEM((BLOCK, HEAD), F32),
+            pltpu.SMEM((total // SPAN,), jnp.int32),
+        ],
+        cost=(5 * total * total * 256, 6 * total * 160, total * total // 2),
+    )[0]
+
+    keep, away = call(
+        weight_kernel,
+        [((256, width // 2), F32), ((256, width // 2), BF)],
+        [info, grads, own, other, *attn_in],
+        smem=1,
+        scratch=[
+            pltpu.VMEM((3 * HEAD, total), BF),
+            pltpu.VMEM((HEAD, width), F32),
+            pltpu.VMEM((3 * HEAD, width), F32),
+        ],
+        cost=(2 * 240 * total * width, 2 * total * width, 0),
+    )
+    summed = (keep + send(away, Y_SWAP).astype(F32)).astype(BF)
+    returned = lax.all_to_all(grads, "ctx", 0, 0)
+    grad_inputs = call(
+        input_kernel,
+        [low],
+        [info, inputs, returned, grad_mid, own, other, *back_weights],
+        smem=1,
+        anys=9,
+        scratch=whole_scratch,
+        cost=(6 * rows * width * width, 6 * width * width, 0),
+    )[0]
+    spread = chip_gather(summed)
+    grad_query, grad_key, grad_value, grad_gain_attn, grad_scale = call(
+        finish_kernel,
+        [shard, shard, shard, line, ((1, HEAD), F32)],
+        [info, *spread, w_query, w_key, w_value, gain_attn[None], factor],
+        smem=1,
+        scratch=[pltpu.VMEM((16, 256, width // 2), BF)] + [pltpu.VMEM((width, width // 2), BF)] * 3,
+        cost=(6 * 640 * 640 * 1280, 3 * 640 * 1280 * 4, 0),
+    )
+    return (
+        result[None], grad_inputs[None], grad_gain_attn[0], grad_query, grad_key, grad_value, grad_output,
+        grad_scale[0], grad_gain_mlp[0], grad_expand, grad_contract,
+    )
+
+
 def solution(mesh):
     in_specs = (
         P("wt", "ctx", None),
@@ -330,6 +950,7 @@
         P("wt", None),
         P("wt", None),
     )
+    body = ring_device if mesh.shape["ctx"] == HEADS and mesh.shape["wt"] == 2 else per_device
     return jax.shard_map(
-        per_device, mesh=mesh, in_specs=in_specs, out_specs=out_specs, check_vma=False
-    )
+        body, mesh=mesh, in_specs=in_specs, out_specs=out_specs, check_vma=False
+    )

time: 1540 us -> 455 us (0.30)
  waiting for transfers between devices: 960 us -> 199 us
  matrix products: 292 us -> 0 us
  Pallas kernels: 0 us -> 142 us
  local copies, waits for them, and re-layouts: 158 us -> 18 us
  starting transfers between devices: 0.85 us -> 76.2 us
  blocking collectives: 51 us -> 0 us
  other arithmetic: 52 us -> 8.52 us
    reduce_scatter x8 -> x0, waiting for transfers between devices: 497 us -> none  [the longest x1 119 us: per_device(): lax.psum_scatter(key_terms[1].reshape(group_rows, feat_width).astype(jnp....]
    all_gather x8 -> x0, waiting for transfers between devices: 318 us -> none  [the longest x1 80.8 us: per_device(): lax.all_gather(key_own, 'ctx', axis=0, tiled=True)]
    dot_general x60 -> x0, matrix products: 292 us -> none  [the longest x8 48 us: back_block(): jnp.einsum('hqk,qhd->khd', probabilities.astype(jnp.bfloat16), out_grad,...]
    ppermute x0 -> x81, waiting for transfers between devices: none -> 194 us  [send(): return lax.ppermute(value, AXES, moves)]
    pallas_call x0 -> x14, Pallas kernels: none -> 142 us  [call(): pl.pallas_call(body, out_shape=[jax.ShapeDtypeStruct(shape, kind) for sha...]
    psum x1 -> x0, waiting for transfers between devices: 139 us -> none  [per_device(): lax.psum(shares[1].astype(jnp.bfloat16), 'ctx').astype(jnp.float32)]
    ppermute x0 -> x81, starting transfers between devices: none -> 59.1 us  [send(): return lax.ppermute(value, AXES, moves)]
    dynamic_update_slice x24 -> x0, local copies, waits for them, and re-layouts: 56.3 us -> none  [per_device(): query_grad, key_terms = lax.scan(back_block, query_zero, key_blocks)]
  transfers between devices with their start and end apart: 17 -> 84, of which waited for: 17 -> 30; matrix products, arithmetic and copies ran while one was open for 11% -> 4% of each run, Pallas kernels for 0% -> 29%
where the time goes in v1:
time: 455 us; the launch traced here: 447 us
  waiting for transfers between devices  199 us (44%)
  Pallas kernels  142 us (31%)
  starting transfers between devices  76.2 us (17%)
  local copies, waits for them, and re-layouts  18 us (4%)
  other arithmetic  8.52 us (2%)
    ppermute x81, waiting for transfers between devices, send(): return lax.ppermute(value, AXES, moves)  194 us
    pallas_call x14, Pallas kernels, call(): pl.pallas_call(body, out_shape=[jax.ShapeDtypeStruct(shape, kind) for sha...  142 us
    ppermute x81, starting transfers between devices, send(): return lax.ppermute(value, AXES, moves)  59.1 us
  transfers between devices with their start and end apart: 84, of which 30 were waited for; matrix products, arithmetic and copies ran while one was open for 4% of the time, Pallas kernels for 29%

profile of v1, /device:TPU:0, one launch (start us, length us, event | category | flops | bytes accessed | tf_op | source)
XLA Modules:
  0.0 447.3 jit_solution(7733882843160359255)
XLA Ops:
  0.6 3.1 collective-permute-start.1
  3.7 14.9 %collective-permute-done.1.refs_0_ = bf16[256,1280]{1,0:T(8,128)(2,1)S(1)} collective-permute-done((bf16[256,1280]{1,0:T(8,128)(2,1)}, bf16[256,1280]{1,0:T(8,128)(2,1)S(1)}, u32[]{:S(2)}, u32[]{:S(2)}) %collective-permute-start.1) | collective-permute-done | bytes 655392 | tf_op jit(solution)/shard_map/ppermute | solution.py:361
  25.2 5.0 %shard_map.221.refs_1_.refs_2_.own = bf16[496,640]{1,0:T(8,128)(2,1)} custom-call(s32[20]{0:T(128)} %concatenate.6.info, bf16[640,1280]{1,0:T(8,128)(2,1)} %refs_18_.2, bf16[640,1280]{1,0:T(8,128)(2,1)} %refs_19_.1, bf16[640,1280]{1,0:T(8,128)(2,1)} %refs_20_.1, bf16[1,640]{1,0:T(2,128)(2,1)} %broadcast_in_dim.20.gain_a.refs_21_, ...), custom_call_target="tpu_custom_call" | custom-call | flops 786432000 | bytes 4915200 | tf_op jit(solution)/shard_map/pallas_call | solution.py:377
  32.0 2.7 collective-permute-done.3.refs_0_
  36.7 2.1 constant_dynamic-slice_fusion.9
  40.3 9.7 %collective-permute-done.5.refs_0_ = bf16[256,1280]{1,0:T(8,128)(2,1)S(1)} collective-permute-done((bf16[256,1280]{1,0:T(8,128)(2,1)}, bf16[256,1280]{1,0:T(8,128)(2,1)S(1)}, u32[]{:S(2)}, u32[]{:S(2)}) %collective-permute-start.5) | collective-permute-done | bytes 655392 | tf_op jit(solution)/shard_map/ppermute | solution.py:361
  54.6 2.9 shard_map.222
  57.6 3.7 shard_map.223
  61.8 3.7 shard_map.224
  65.5 3.7 shard_map.225
  70.6 2.9 shard_map.226
  78.2 26.2 %shard_map.227 = (bf16[16,80,256]{2,1,0:T(8,128)(2,1)}, f32[1,4096]{1,0:T(1,128)}) custom-call(s32[20]{0:T(128)} %concatenate.6.info, s32[32]{0:T(128)} %bitcast.107, bf16[240,256]{1,0:T(8,128)(2,1)} %get-tuple-element.52.refs_0_, bf16[240,512]{1,0:T(8,128)(2,1)} %get-tuple-element.53.refs_1_, bf16[240,512]{1,0:T(8,128)(2,1)} %get-tuple-element.54.refs_2_, ...), custom_call_target="tpu_custom_call" | custom-call | flops 8589934592 | bytes 1966080 | tf_op jit(solution)/shard_map/pallas_call | solution.py:377
  104.4 6.1 %all-to-all-start = ((bf16[16,80,256]{2,1,0:T(8,128)(2,1)}), bf16[16,80,256]{2,1,0:T(8,128)(2,1)S(1)}, u32[]{:S(2)}, u32[]{:S(2)}) async-start(bf16[16,80,256]{2,1,0:T(8,128)(2,1)} %get-tuple-element.62.refs_11_), calls=%async_computation | async-start | bytes 1310720 | tf_op jit(solution)/shard_map/all_to_all | solution.py:824
  113.0 16.6 %collective-permute-done.18.refs_7_ = bf16[320,1280]{1,0:T(8,128)(2,1)} collective-permute-done((bf16[320,1280]{1,0:T(8,128)(2,1)S(1)}, bf16[320,1280]{1,0:T(8,128)(2,1)}, u32[]{:S(2)}, u32[]{:S(2)}) %collective-permute-start.18) | collective-permute-done | bytes 819232 | tf_op jit(solution)/shard_map/ppermute | solution.py:361
  130.1 3.1 collective-permute-done.19.refs_8_
  134.4 11.8 %shard_map.228 = (bf16[256,1280]{1,0:T(8,128)(2,1)}, f32[256,1280]{1,0:T(8,128)}, bf16[1280,256]{1,0:T(8,128)(2,1)}, bf16[256,1280]{1,0:T(8,128)(2,1)}, bf16[256...) custom-call(s32[20]{0:T(128)} %concatenate.6.info, bf16[256,1280]{1,0:T(8,128)(2,1)} %bitcast.97, ...), custom_call_target="tpu_custom_call" | custom-call | flops 5033164800 | bytes 9830400 | tf_op jit(solution)/shard_map/pallas_call | solution.py:377
  146.2 6.0 %all-to-all-start.1 = ((bf16[16,80,256]{2,1,0:T(8,128)(2,1)}), bf16[16,80,256]{2,1,0:T(8,128)(2,1)}, u32[]{:S(2)}, u32[]{:S(2)}) async-start(bf16[16,80,256]{2,1,0:T(8,128)(2,1)} %bitcast.104), calls=%async_computation.1 | async-start | bytes 1310720 | tf_op jit(solution)/shard_map/all_to_all | solution.py:837
  156.2 6.7 %shard_map.233 = (bf16[1280,640]{1,0:T(8,128)(2,1)}, bf16[1280,640]{1,0:T(8,128)(2,1)}, bf16[1280,640]{1,0:T(8,128)(2,1)}, bf16[1280,640]{1,0:T(8,128)(2,1)}, bf...) custom-call(s32[20]{0:T(128)} %concatenate.6.info, bf16[256,1280]{1,0:T(8,128)(2,1)} %get-tuple-element.78.act, ...), custom_call_target="tpu_custom_call" | custom-call | flops 2516582400 | bytes 9830400 | tf_op jit(solution)/shard_map/pallas_call | solution.py:377
  163.5 5.3 %all-to-all-done.1.refs_12_ = bf16[16,80,256]{2,1,0:T(8,128)(2,1)} async-done(((bf16[16,80,256]{2,1,0:T(8,128)(2,1)}), bf16[16,80,256]{2,1,0:T(8,128)(2,1)}, u32[]{:S(2)}, u32[]{:S(2)}) %all-to-all-start.1) | async-done | bytes 655392 | tf_op jit(solution)/shard_map/all_to_all | solution.py:837
  168.8 35.0 %shard_map.229.grads = bf16[16,240,256]{2,1,0:T(8,128)(2,1)} custom-call(s32[20]{0:T(128)} %concatenate.6.info, s32[32]{0:T(128)} %bitcast.108, bf16[240,256]{1,0:T(8,128)(2,1)} %get-tuple-element.52.refs_0_, bf16[240,512]{1,0:T(8,128)(2,1)} %get-tuple-element.53.refs_1_, bf16[240,512]{1,0:T(8,128)(2,1)} %get-tuple-element.54.refs_2_, ...), custom_call_target="tpu_custom_call" | custom-call | flops 21474836480 | bytes 3932160 | tf_op jit(solution)/shard_map/pallas_call | solution.py:377
  203.9 5.0 %all-to-all-start.2 = ((bf16[16,240,256]{2,1,0:T(8,128)(2,1)}), bf16[16,240,256]{2,1,0:T(8,128)(2,1)S(1)}, u32[]{:S(2)}, u32[]{:S(2)}) async-start(bf16[16,240,256]{2,1,0:T(8,128)(2,1)} %shard_map.229.grads), calls=%async_computation.2 | async-start | bytes 3932160 | tf_op jit(solution)/shard_map/all_to_all | solution.py:899
  211.0 9.1 %shard_map.231 = (f32[256,640]{1,0:T(8,128)}, bf16[256,640]{1,0:T(8,128)(2,1)}) custom-call(s32[20]{0:T(128)} %concatenate.6.info, bf16[16,240,256]{2,1,0:T(8,128)(2,1)} %shard_map.229.grads, bf16[496,640]{1,0:T(8,128)(2,1)} %shard_map.221.refs_1_.refs_2_.own, bf16[496,640]{1,0:T(8,128)(2,1)} %copy-done, bf16[256,1280]{1,0:T(8,128)(2,1)} %get-tuple-element.67.refs_0_, ...), custom_call_target="tpu_custom_call" | custom-call | flops 2516582400 | bytes 10485760 | tf_op jit(solution)/shard_map/pallas_call | solution.py:377
  223.7 2.1 collective-permute-start.60
  230.1 24.3 %collective-permute-done.31 = bf16[256,640]{1,0:T(8,128)(2,1)S(1)} collective-permute-done((bf16[256,640]{1,0:T(8,128)(2,1)}, bf16[256,640]{1,0:T(8,128)(2,1)S(1)}, u32[]{:S(2)}, u32[]{:S(2)}) %collective-permute-start.31) | collective-permute-done | bytes 327712 | tf_op jit(solution)/shard_map/ppermute | solution.py:361
  256.0 5.2 %collective-permute-done.60 = bf16[2,2,2,80,640]{4,3,2,1,0:T(8,128)(2,1)S(1)} collective-permute-done((bf16[2,2,2,80,640]{4,3,2,1,0:T(8,128)(2,1)S(1)}, bf16[2,2,2,80,640]{4,3,2,1,0:T(8,128)(2,1)S(1)}, u32[]{:S(2)}, u32[]{:S(2)}) %collective-permute-start.60) | collective-permute-done | bytes 819232 | tf_op jit(solution)/shard_map/ppermute | solution.py:361
  263.8 11.7 %collective-permute-done.50 = bf16[2,2,2,80,640]{4,3,1,2,0:T(8,128)(2,1)S(1)} collective-permute-done((bf16[2,2,2,80,640]{4,3,1,2,0:T(8,128)(2,1)S(1)}, bf16[2,2,2,80,640]{4,3,1,2,0:T(8,128)(2,1)S(1)}, u32[]{:S(2)}, u32[]{:S(2)}) %collective-permute-start.50) | collective-permute-done | bytes 819232 | tf_op jit(solution)/shard_map/ppermute | solution.py:361
  277.3 24.5 %collective-permute-done.61 = bf16[2,2,80,640]{3,2,1,0:T(8,128)(2,1)S(1)} collective-permute-done((bf16[2,2,80,640]{3,2,1,0:T(8,128)(2,1)S(1)}, bf16[2,2,80,640]{3,2,1,0:T(8,128)(2,1)S(1)}, u32[]{:S(2)}, u32[]{:S(2)}) %collective-permute-start.61) | collective-permute-done | bytes 409632 | tf_op jit(solution)/shard_map/ppermute | solution.py:361
  303.7 5.6 %collective-permute-done.56 = bf16[2,2,80,640]{3,2,0,1:T(8,128)(2,1)S(1)} collective-permute-done((bf16[2,2,80,640]{3,2,0,1:T(8,128)(2,1)S(1)}, bf16[2,2,80,640]{3,2,0,1:T(8,128)(2,1)S(1)}, u32[]{:S(2)}, u32[]{:S(2)}) %collective-permute-start.56) | collective-permute-done | bytes 409632 | tf_op jit(solution)/shard_map/ppermute | solution.py:361
  311.8 10.4 %collective-permute-done.62 = bf16[2,80,640]{2,1,0:T(8,128)(2,1)S(1)} collective-permute-done((bf16[2,80,640]{2,1,0:T(8,128)(2,1)S(1)}, bf16[2,80,640]{2,1,0:T(8,128)(2,1)S(1)}, u32[]{:S(2)}, u32[]{:S(2)}) %collective-permute-start.62) | collective-permute-done | bytes 204832 | tf_op jit(solution)/shard_map/ppermute | solution.py:361
  322.3 6.3 %collective-permute-done.57 = bf16[2,80,640]{2,1,0:T(8,128)(2,1)S(1)} collective-permute-done((bf16[2,80,640]{2,1,0:T(8,128)(2,1)S(1)}, bf16[2,80,640]{2,1,0:T(8,128)(2,1)S(1)}, u32[]{:S(2)}, u32[]{:S(2)}) %collective-permute-start.57) | collective-permute-done | bytes 204832 | tf_op jit(solution)/shard_map/ppermute | solution.py:361
  328.7 8.5 %collective-permute-done.52 = bf16[2,80,640]{2,1,0:T(8,128)(2,1)S(1)} collective-permute-done((bf16[2,80,640]{2,1,0:T(8,128)(2,1)S(1)}, bf16[2,80,640]{2,1,0:T(8,128)(2,1)S(1)}, u32[]{:S(2)}, u32[]{:S(2)}) %collective-permute-start.52) | collective-permute-done | bytes 204832 | tf_op jit(solution)/shard_map/ppermute | solution.py:361
  339.8 7.1 %collective-permute-done.33.refs_2_ = bf16[256,640]{1,0:T(8,128)(2,1)S(1)} collective-permute-done((bf16[256,640]{1,0:T(8,128)(2,1)S(1)}, bf16[256,640]{1,0:T(8,128)(2,1)S(1)}, u32[]{:S(2)}, u32[]{:S(2)}) %collective-permute-start.33) | collective-permute-done | bytes 327712 | tf_op jit(solution)/shard_map/ppermute | solution.py:361
  347.9 11.0 %collective-permute-done.58 = bf16[80,640]{1,0:T(8,128)(2,1)S(1)} collective-permute-done((bf16[80,640]{1,0:T(8,128)(2,1)S(1)}, bf16[80,640]{1,0:T(8,128)(2,1)S(1)}, u32[]{:S(2)}, u32[]{:S(2)}) %collective-permute-start.58) | collective-permute-done | bytes 102432 | tf_op jit(solution)/shard_map/ppermute | solution.py:361
  361.3 3.2 collective-permute-done.53
  365.4 4.3 collective-permute-done.36.refs_5_
  369.7 3.7 collective-permute-start.65
  374.1 5.2 %collective-permute-done.38.refs_7_ = bf16[128,640]{1,0:T(8,128)(2,1)S(1)} collective-permute-done((bf16[128,640]{1,0:T(8,128)(2,1)S(1)}, bf16[128,640]{1,0:T(8,128)(2,1)S(1)}, u32[]{:S(2)}, u32[]{:S(2)}) %collective-permute-start.38) | collective-permute-done | bytes 163872 | tf_op jit(solution)/shard_map/ppermute | solution.py:361
  379.3 3.9 collective-permute-start.39
  383.3 2.1 collective-permute-start.67
  385.3 2.5 collective-permute-done.39.refs_8_
  390.2 2.0 collective-permute-done.66.refs_3_
  393.2 2.5 collective-permute-start.69
  396.5 3.9 collective-permute-done.68.refs_5_
  402.4 2.1 collective-permute-start.71
  404.5 3.9 collective-permute-done.70.refs_7_
  411.3 13.2 %shard_map.232 = (f32[640,1280]{1,0:T(8,128)}, f32[640,1280]{1,0:T(8,128)}, f32[640,1280]{1,0:T(8,128)}, f32[1,640]{1,0:T(1,128)}, f32[1,80]{1,0:T(1,128)}) custom-call(s32[20]{0:T(128)} %concatenate.6.info, bf16[256,640]{1,0:T(8,128)(2,1)} %copy-done.23, bf16[256,640]{1,0:T(8,128)(2,1)} %copy-done.43, bf16[256,640]{1,0:T(8,128)(2,1)} %copy-done.44, ...), custom_call_target="tpu_custom_call" | custom-call | flops 3145728000 | bytes 9830400 | tf_op jit(solution)/shard_map/pallas_call | solution.py:377
  426.0 7.3 %shard_map.234 = (f32[640,1280]{1,0:T(8,128)}, f32[640,1280]{1,0:T(8,128)}, f32[640,1280]{1,0:T(8,128)}, f32[1,640]{1,0:T(1,128)}) custom-call(s32[20]{0:T(128)} %concatenate.6.info, bf16[240,640]{1,0:T(8,128)(2,1)} %copy-done.12, bf16[240,640]{1,0:T(8,128)(2,1)} %copy-done.26, bf16[240,640]{1,0:T(8,128)(2,1)} %copy-done.27, bf16[240,640]{1,0:T(8,128)(2,1)} %copy-done.28, ...), custom_call_target="tpu_custom_call" | custom-call | bytes 9830400 | tf_op jit(solution)/shard_map/pallas_call | solution.py:377
  435.9 11.2 %shard_map.230 = bf16[256,1280]{1,0:T(8,128)(2,1)} custom-call(s32[20]{0:T(128)} %concatenate.6.info, bf16[256,1280]{1,0:T(8,128)(2,1)} %bitcast.98, bf16[16,240,256]{2,1,0:T(8,128)(2,1)} %copy-done.4, f32[256,1280]{1,0:T(8,128)} %get-tuple-element.66.grad_mid, bf16[496,640]{1,0:T(8,128)(2,1)} %shard_map.221.refs_1_.refs_2_.own, bf16[496,640]{1,0:T(8,128)(2,1)} %copy-done, ...), custom_call_target="tpu_custom_call" | custom-call | flops 2516582400 | bytes 9830400 | tf_op jit(solution)/shard_map/pallas_call | solution.py:377
  (312 shorter events, 71.8 us)
Async XLA Ops:
  0.6 17.9 %collective-permute-start.1 = (bf16[256,1280]{1,0:T(8,128)(2,1)}, bf16[256,1280]{1,0:T(8,128)(2,1)S(1)}, u32[]{:S(2)}, u32[]{:S(2)}) collective-permute-start(bf16[256,1280]{1,0:T(8,128)(2,1)} %bitcast.94), channel_id=1, source_target_pairs={{0,8},{1,9},{2,10},{3,11},{4,0},{5,1},{6,2},{7,3},{8,16},{9,17},{1... | collective-permute-start | bytes 1966088 | tf_op jit(solution)/shard_map/ppermute | solution.py:361
  3.7 16.7 %collective-permute-start.2 = (bf16[256,1280]{1,0:T(8,128)(2,1)}, bf16[256,1280]{1,0:T(8,128)(2,1)}, u32[]{:S(2)}, u32[]{:S(2)}) collective-permute-start(bf16[256,1280]{1,0:T(8,128)(2,1)} %bitcast.95), channel_id=1, source_target_pairs={{0,4},{1,5},{2,6},{3,7},{4,12},{5,13},{6,14},{7,15},{8,0},{9,1},{1... | collective-permute-start | bytes 1966088 | tf_op jit(solution)/shard_map/ppermute | solution.py:361
  18.6 16.1 %collective-permute-start.3 = (bf16[256,1280]{1,0:T(8,128)(2,1)S(1)}, bf16[256,1280]{1,0:T(8,128)(2,1)}, u32[]{:S(2)}, u32[]{:S(2)}) collective-permute-start(bf16[256,1280]{1,0:T(8,128)(2,1)S(1)} %collective-permute-done.1.refs_0_), channel_id=1, source_target_pairs={{0,8},{1,9},{2,10},{3,11},{4,0},{5,1},{6,2},{7,3},{8,16},{9,17},{1... | collective-permute-start | bytes 1966088 | tf_op jit(solution)/shard_map/ppermute | solution.py:361
  20.4 15.8 %collective-permute-start.4 = (bf16[256,1280]{1,0:T(8,128)(2,1)}, bf16[256,1280]{1,0:T(8,128)(2,1)}, u32[]{:S(2)}, u32[]{:S(2)}) collective-permute-start(bf16[256,1280]{1,0:T(8,128)(2,1)} %collective-permute-done.2.refs_1_), channel_id=1, source_target_pairs={{0,4},{1,5},{2,6},{3,7},{4,12},{5,13},{6,14},{7,15},{8,0},{9,1},{1... | collective-permute-start | bytes 1966088 | tf_op jit(solution)/shard_map/ppermute | solution.py:361
  30.2 23.6 %collective-permute-start = (bf16[496,640]{1,0:T(8,128)(2,1)}, bf16[496,640]{1,0:T(8,128)(2,1)S(1)}, u32[]{:S(2)}, u32[]{:S(2)}) collective-permute-start(bf16[496,640]{1,0:T(8,128)(2,1)} %shard_map.221.refs_1_.refs_2_.own), channel_id=1, source_target_pairs={{0,1},{1,0},{2,3},{3,2},{4,5},{5,4},{6,7},{7,6},{8,9},{9,8},{10,11... | collective-permute-start | bytes 1904648 | tf_op jit(solution)/shard_map/ppermute | solution.py:361
  34.7 15.3 %collective-permute-start.5 = (bf16[256,1280]{1,0:T(8,128)(2,1)}, bf16[256,1280]{1,0:T(8,128)(2,1)S(1)}, u32[]{:S(2)}, u32[]{:S(2)}) collective-permute-start(bf16[256,1280]{1,0:T(8,128)(2,1)} %collective-permute-done.3.refs_0_), channel_id=1, source_target_pairs={{0,8},{1,9},{2,10},{3,11},{4,0},{5,1},{6,2},{7,3},{8,16},{9,17},{1... | collective-permute-start | bytes 1966088 | tf_op jit(solution)/shard_map/ppermute | solution.py:361
  36.2 15.1 %collective-permute-start.6 = (bf16[256,1280]{1,0:T(8,128)(2,1)}, bf16[256,1280]{1,0:T(8,128)(2,1)S(1)}, u32[]{:S(2)}, u32[]{:S(2)}) collective-permute-start(bf16[256,1280]{1,0:T(8,128)(2,1)} %collective-permute-done.4.refs_1_), channel_id=1, source_target_pairs={{0,4},{1,5},{2,6},{3,7},{4,12},{5,13},{6,14},{7,15},{8,0},{9,1},{1... | collective-permute-start | bytes 1966088 | tf_op jit(solution)/shard_map/ppermute | solution.py:361
  50.1 19.1 %collective-permute-start.7 = (bf16[128,1280]{1,0:T(8,128)(2,1)S(1)}, bf16[128,1280]{1,0:T(8,128)(2,1)S(1)}, u32[]{:S(2)}, u32[]{:S(2)}) collective-permute-start(bf16[128,1280]{1,0:T(8,128)(2,1)S(1)} %slice.24), channel_id=1, source_target_pairs={{0,8},{1,9},{2,10},{3,11},{4,0},{5,1},{6,2},{7,3},{8,16},{9,17},{1... | collective-permute-start | bytes 983048 | tf_op jit(solution)/shard_map/ppermute | solution.py:361
  52.2 17.6 %collective-permute-start.8 = (bf16[128,1280]{1,0:T(8,128)(2,1)S(1)}, bf16[128,1280]{1,0:T(8,128)(2,1)S(1)}, u32[]{:S(2)}, u32[]{:S(2)}) collective-permute-start(bf16[128,1280]{1,0:T(8,128)(2,1)S(1)} %slice.25), channel_id=1, source_target_pairs={{0,4},{1,5},{2,6},{3,7},{4,12},{5,13},{6,14},{7,15},{8,0},{9,1},{1... | collective-permute-start | bytes 983048 | tf_op jit(solution)/shard_map/ppermute | solution.py:361
  57.6 16.5 %collective-permute-start.9 = (bf16[240,256]{1,0:T(8,128)(2,1)}, bf16[240,256]{1,0:T(8,128)(2,1)S(1)}, u32[]{:S(2)}, u32[]{:S(2)}) collective-permute-start(bf16[240,256]{1,0:T(8,128)(2,1)} %get-tuple-element.57), channel_id=1, source_target_pairs={{0,2},{1,3},{2,0},{3,1},{4,6},{5,7},{6,4},{7,5},{8,10},{9,11},{10,... | collective-permute-start | bytes 368648 | tf_op jit(solution)/shard_map/ppermute | solution.py:361
  61.3 14.1 %collective-permute-start.10 = (bf16[240,512]{1,0:T(8,128)(2,1)}, bf16[240,512]{1,0:T(8,128)(2,1)S(1)}, u32[]{:S(2)}, u32[]{:S(2)}) collective-permute-start(bf16[240,512]{1,0:T(8,128)(2,1)} %get-tuple-element.58), channel_id=1, source_target_pairs={{0,2},{1,3},{2,0},{3,1},{4,6},{5,7},{6,4},{7,5},{8,10},{9,11},{10,... | collective-permute-start | bytes 737288 | tf_op jit(solution)/shard_map/ppermute | solution.py:361
  74.1 36.3 %collective-permute-start.14 = (bf16[320,1280]{1,0:T(8,128)(2,1)S(1)}, bf16[320,1280]{1,0:T(8,128)(2,1)}, u32[]{:S(2)}, u32[]{:S(2)}) collective-permute-start(bf16[320,1280]{1,0:T(8,128)(2,1)S(1)} %copy-done.15), channel_id=1, source_target_pairs={{0,1},{1,0},{2,3},{3,2},{4,5},{5,4},{6,7},{7,6},{8,9},{9,8},{10,11... | collective-permute-start | bytes 2457608 | tf_op jit(solution)/shard_map/ppermute | solution.py:361
  75.4 37.6 %collective-permute-start.16 = (bf16[320,1280]{1,0:T(8,128)(2,1)S(1)}, bf16[320,1280]{1,0:T(8,128)(2,1)}, u32[]{:S(2)}, u32[]{:S(2)}) collective-permute-start(bf16[320,1280]{1,0:T(8,128)(2,1)S(1)} %copy-done.14), channel_id=1, source_target_pairs={{0,1},{1,0},{2,3},{3,2},{4,5},{5,4},{6,7},{7,6},{8,9},{9,8},{10,11... | collective-permute-start | bytes 2457608 | tf_op jit(solution)/shard_map/ppermute | solution.py:361
  76.3 53.3 %collective-permute-start.18 = (bf16[320,1280]{1,0:T(8,128)(2,1)S(1)}, bf16[320,1280]{1,0:T(8,128)(2,1)}, u32[]{:S(2)}, u32[]{:S(2)}) collective-permute-start(bf16[320,1280]{1,0:T(8,128)(2,1)S(1)} %constant_dynamic-slice_fusion.7), channel_id=1, source_target_pairs={{0,1},{1,0},{2,3},{3,2},{4,5},{5,4},{6,7},{7,6},{8,9},{9,8},{10,11... | collective-permute-start | bytes 2457608 | tf_op jit(solution)/shard_map/ppermute | solution.py:361
  104.4 28.9 %all-to-all-start = ((bf16[16,80,256]{2,1,0:T(8,128)(2,1)}), bf16[16,80,256]{2,1,0:T(8,128)(2,1)S(1)}, u32[]{:S(2)}, u32[]{:S(2)}) async-start(bf16[16,80,256]{2,1,0:T(8,128)(2,1)} %get-tuple-element.62.refs_11_), calls=%async_computation | async-start | bytes 1310720 | tf_op jit(solution)/shard_map/all_to_all | solution.py:824
  110.5 19.6 %collective-permute-start.15 = (bf16[320,1280]{1,0:T(8,128)(2,1)}, bf16[320,1280]{1,0:T(8,128)(2,1)S(1)}, u32[]{:S(2)}, u32[]{:S(2)}) collective-permute-start(bf16[320,1280]{1,0:T(8,128)(2,1)} %collective-permute-done.14.refs_1_), channel_id=1, source_target_pairs={{0,2},{1,3},{2,0},{3,1},{4,6},{5,7},{6,4},{7,5},{8,10},{9,11},{10,... | collective-permute-start | bytes 2457608 | tf_op jit(solution)/shard_map/ppermute | solution.py:361
  113.0 17.1 %collective-permute-start.17 = (bf16[320,1280]{1,0:T(8,128)(2,1)}, bf16[320,1280]{1,0:T(8,128)(2,1)S(1)}, u32[]{:S(2)}, u32[]{:S(2)}) collective-permute-start(bf16[320,1280]{1,0:T(8,128)(2,1)} %collective-permute-done.16.refs_4_), channel_id=1, source_target_pairs={{0,2},{1,3},{2,0},{3,1},{4,6},{5,7},{6,4},{7,5},{8,10},{9,11},{10,... | collective-permute-start | bytes 2457608 | tf_op jit(solution)/shard_map/ppermute | solution.py:361
  129.6 33.9 %collective-permute-start.27 = (bf16[512,1280]{1,0:T(8,128)(2,1)}, bf16[512,1280]{1,0:T(8,128)(2,1)}, u32[]{:S(2)}, u32[]{:S(2)}) collective-permute-start(bf16[512,1280]{1,0:T(8,128)(2,1)} %get-tuple-element.68.refs_1_), channel_id=1, source_target_pairs={{0,2},{1,3},{2,0},{3,1},{4,6},{5,7},{6,4},{7,5},{8,10},{9,11},{10,... | collective-permute-start | bytes 3932168 | tf_op jit(solution)/shard_map/ppermute | solution.py:361
  146.2 22.6 %all-to-all-start.1 = ((bf16[16,80,256]{2,1,0:T(8,128)(2,1)}), bf16[16,80,256]{2,1,0:T(8,128)(2,1)}, u32[]{:S(2)}, u32[]{:S(2)}) async-start(bf16[16,80,256]{2,1,0:T(8,128)(2,1)} %bitcast.104), calls=%async_computation.1 | async-start | bytes 1310720 | tf_op jit(solution)/shard_map/all_to_all | solution.py:837
  155.7 53.2 %collective-permute-start.28 = (bf16[512,1280]{1,0:T(8,128)(2,1)S(1)}, bf16[512,1280]{1,0:T(8,128)(2,1)}, u32[]{:S(2)}, u32[]{:S(2)}) collective-permute-start(bf16[512,1280]{1,0:T(8,128)(2,1)S(1)} %copy-done.11), channel_id=1, source_target_pairs={{0,2},{1,3},{2,0},{3,1},{4,6},{5,7},{6,4},{7,5},{8,10},{9,11},{10,... | collective-permute-start | bytes 3932168 | tf_op jit(solution)/shard_map/ppermute | solution.py:361
  155.7 55.3 %collective-permute-start.29 = (bf16[512,1280]{1,0:T(8,128)(2,1)}, bf16[512,1280]{1,0:T(8,128)(2,1)}, u32[]{:S(2)}, u32[]{:S(2)}) collective-permute-start(bf16[512,1280]{1,0:T(8,128)(2,1)} %get-tuple-element.70.refs_3_), channel_id=1, source_target_pairs={{0,2},{1,3},{2,0},{3,1},{4,6},{5,7},{6,4},{7,5},{8,10},{9,11},{10,... | collective-permute-start | bytes 3932168 | tf_op jit(solution)/shard_map/ppermute | solution.py:361
  156.2 54.3 %collective-permute-start.30 = (bf16[256,1280]{1,0:T(8,128)(2,1)}, bf16[256,1280]{1,0:T(8,128)(2,1)}, u32[]{:S(2)}, u32[]{:S(2)}) collective-permute-start(bf16[256,1280]{1,0:T(8,128)(2,1)} %get-tuple-element.71.refs_4_), channel_id=1, source_target_pairs={{0,2},{1,3},{2,0},{3,1},{4,6},{5,7},{6,4},{7,5},{8,10},{9,11},{10,... | collective-permute-start | bytes 1966088 | tf_op jit(solution)/shard_map/ppermute | solution.py:361
  162.9 57.1 %collective-permute-start.59 = (bf16[1280,640]{1,0:T(8,128)(2,1)}, bf16[1280,640]{1,0:T(8,128)(2,1)}, u32[]{:S(2)}, u32[]{:S(2)}) collective-permute-start(bf16[1280,640]{1,0:T(8,128)(2,1)} %get-tuple-element.87), channel_id=1, source_target_pairs={{0,2},{1,3},{2,0},{3,1},{4,6},{5,7},{6,4},{7,5},{8,10},{9,11},{10,... | collective-permute-start | bytes 4915208 | tf_op jit(solution)/shard_map/ppermute | solution.py:361
  163.4 60.2 %collective-permute-start.54 = (bf16[1280,640]{1,0:T(8,128)(2,1)}, bf16[1280,640]{1,0:T(8,128)(2,1)}, u32[]{:S(2)}, u32[]{:S(2)}) collective-permute-start(bf16[1280,640]{1,0:T(8,128)(2,1)} %get-tuple-element.85), channel_id=1, source_target_pairs={{0,2},{1,3},{2,0},{3,1},{4,6},{5,7},{6,4},{7,5},{8,10},{9,11},{10,... | collective-permute-start | bytes 4915208 | tf_op jit(solution)/shard_map/ppermute | solution.py:361
  203.9 230.7 %all-to-all-start.2 = ((bf16[16,240,256]{2,1,0:T(8,128)(2,1)}), bf16[16,240,256]{2,1,0:T(8,128)(2,1)S(1)}, u32[]{:S(2)}, u32[]{:S(2)}) async-start(bf16[16,240,256]{2,1,0:T(8,128)(2,1)} %shard_map.229.grads), calls=%async_computation.2 | async-start | bytes 3932160 | tf_op jit(solution)/shard_map/all_to_all | solution.py:899
  208.9 128.4 %collective-permute-start.20 = (bf16[320,1280]{1,0:T(8,128)(2,1)}, bf16[320,1280]{1,0:T(8,128)(2,1)S(1)}, u32[]{:S(2)}, u32[]{:S(2)}) collective-permute-start(bf16[320,1280]{1,0:T(8,128)(2,1)} %constant_dynamic-slice_fusion.6), channel_id=1, source_target_pairs={{0,1},{1,0},{2,3},{3,2},{4,5},{5,4},{6,7},{7,6},{8,9},{9,8},{10,11... | collective-permute-start | bytes 2457608 | tf_op jit(solution)/shard_map/ppermute | solution.py:361
  210.5 127.7 %collective-permute-start.22 = (bf16[320,1280]{1,0:T(8,128)(2,1)}, bf16[320,1280]{1,0:T(8,128)(2,1)}, u32[]{:S(2)}, u32[]{:S(2)}) collective-permute-start(bf16[320,1280]{1,0:T(8,128)(2,1)} %constant_dynamic-slice_fusion.5), channel_id=1, source_target_pairs={{0,1},{1,0},{2,3},{3,2},{4,5},{5,4},{6,7},{7,6},{8,9},{9,8},{10,11... | collective-permute-start | bytes 2457608 | tf_op jit(solution)/shard_map/ppermute | solution.py:361
  211.0 16.9 %collective-permute-start.49 = (bf16[1280,640]{1,0:T(8,128)(2,1)}, bf16[1280,640]{1,0:T(8,128)(2,1)S(1)}, u32[]{:S(2)}, u32[]{:S(2)}) collective-permute-start(bf16[1280,640]{1,0:T(8,128)(2,1)} %get-tuple-element.83), channel_id=1, source_target_pairs={{0,2},{1,3},{2,0},{3,1},{4,6},{5,7},{6,4},{7,5},{8,10},{9,11},{10,... | collective-permute-start | bytes 4915208 | tf_op jit(solution)/shard_map/ppermute | solution.py:361
  220.1 34.3 %collective-permute-start.31 = (bf16[256,640]{1,0:T(8,128)(2,1)}, bf16[256,640]{1,0:T(8,128)(2,1)S(1)}, u32[]{:S(2)}, u32[]{:S(2)}) collective-permute-start(bf16[256,640]{1,0:T(8,128)(2,1)} %get-tuple-element.73), channel_id=1, source_target_pairs={{0,1},{1,0},{2,3},{3,2},{4,5},{5,4},{6,7},{7,6},{8,9},{9,8},{10,11... | collective-permute-start | bytes 983048 | tf_op jit(solution)/shard_map/ppermute | solution.py:361
  223.7 37.5 %collective-permute-start.60 = (bf16[2,2,2,80,640]{4,3,2,1,0:T(8,128)(2,1)S(1)}, bf16[2,2,2,80,640]{4,3,2,1,0:T(8,128)(2,1)S(1)}, u32[]{:S(2)}, u32[]{:S(2)}) collective-permute-start(bf16[2,2,2,80,640]{4,3,2,1,0:T(8,128)(2,1)S(1)} %dynamic-slice_bitcast_fusion), channel_id=1, source_target_pairs={{0,8},{1,9},{2,10},{3,11},{4,12},{5,13},{6,14},{7,15},{8,0},{9,1},... | collective-permute-start | bytes 2457608 | tf_op jit(solution)/shard_map/ppermute | solution.py:361
  227.9 35.1 %collective-permute-start.55 = (bf16[2,2,2,80,640]{4,3,1,2,0:T(8,128)(2,1)S(1)}, bf16[2,2,2,80,640]{4,3,1,2,0:T(8,128)(2,1)S(1)}, u32[]{:S(2)}, u32[]{:S(2)}) collective-permute-start(bf16[2,2,2,80,640]{4,3,1,2,0:T(8,128)(2,1)S(1)} %bitcast.99), channel_id=1, source_target_pairs={{0,4},{1,5},{2,6},{3,7},{4,0},{5,1},{6,2},{7,3},{8,12},{9,13},{10,... | collective-permute-start | bytes 2457608 | tf_op jit(solution)/shard_map/ppermute | solution.py:361
  254.4 21.1 %collective-permute-start.50 = (bf16[2,2,2,80,640]{4,3,1,2,0:T(8,128)(2,1)S(1)}, bf16[2,2,2,80,640]{4,3,1,2,0:T(8,128)(2,1)S(1)}, u32[]{:S(2)}, u32[]{:S(2)}) collective-permute-start(bf16[2,2,2,80,640]{4,3,1,2,0:T(8,128)(2,1)S(1)} %bitcast.100), channel_id=1, source_target_pairs={{0,1},{1,0},{2,3},{3,2},{4,5},{5,4},{6,7},{7,6},{8,9},{9,8},{10,11... | collective-permute-start | bytes 2457608 | tf_op jit(solution)/shard_map/ppermute | solution.py:361
  261.2 78.4 %collective-permute-start.24 = (bf16[320,1280]{1,0:T(8,128)(2,1)S(1)}, bf16[320,1280]{1,0:T(8,128)(2,1)}, u32[]{:S(2)}, u32[]{:S(2)}) collective-permute-start(bf16[320,1280]{1,0:T(8,128)(2,1)S(1)} %copy-done.13), channel_id=1, source_target_pairs={{0,1},{1,0},{2,3},{3,2},{4,5},{5,4},{6,7},{7,6},{8,9},{9,8},{10,11... | collective-permute-start | bytes 2457608 | tf_op jit(solution)/shard_map/ppermute | solution.py:361
  263.0 38.9 %collective-permute-start.61 = (bf16[2,2,80,640]{3,2,1,0:T(8,128)(2,1)S(1)}, bf16[2,2,80,640]{3,2,1,0:T(8,128)(2,1)S(1)}, u32[]{:S(2)}, u32[]{:S(2)}) collective-permute-start(bf16[2,2,80,640]{3,2,1,0:T(8,128)(2,1)S(1)} %dynamic-slice_bitcast_fusion.1), channel_id=1, source_target_pairs={{0,1},{1,0},{2,3},{3,2},{4,5},{5,4},{6,7},{7,6},{8,9},{9,8},{10,11... | collective-permute-start | bytes 1228808 | tf_op jit(solution)/shard_map/ppermute | solution.py:361
  275.6 33.8 %collective-permute-start.56 = (bf16[2,2,80,640]{3,2,0,1:T(8,128)(2,1)S(1)}, bf16[2,2,80,640]{3,2,0,1:T(8,128)(2,1)S(1)}, u32[]{:S(2)}, u32[]{:S(2)}) collective-permute-start(bf16[2,2,80,640]{3,2,0,1:T(8,128)(2,1)S(1)} %dynamic-slice_bitcast_fusion.2), channel_id=1, source_target_pairs={{0,1},{1,0},{2,3},{3,2},{4,5},{5,4},{6,7},{7,6},{8,9},{9,8},{10,11... | collective-permute-start | bytes 1228808 | tf_op jit(solution)/shard_map/ppermute | solution.py:361
  309.4 28.9 %collective-permute-start.32 = (bf16[256,640]{1,0:T(8,128)(2,1)S(1)}, bf16[256,640]{1,0:T(8,128)(2,1)S(1)}, u32[]{:S(2)}, u32[]{:S(2)}) collective-permute-start(bf16[256,640]{1,0:T(8,128)(2,1)S(1)} %add_convert_fusion.3.refs_0_), channel_id=1, source_target_pairs={{0,8},{1,9},{2,10},{3,11},{4,0},{5,1},{6,2},{7,3},{8,16},{9,17},{1... | collective-permute-start | bytes 983048 | tf_op jit(solution)/shard_map/ppermute | solution.py:361
  338.3 20.7 %collective-permute-start.40 = (bf16[256,640]{1,0:T(8,128)(2,1)S(1)}, bf16[256,640]{1,0:T(8,128)(2,1)S(1)}, u32[]{:S(2)}, u32[]{:S(2)}) collective-permute-start(bf16[256,640]{1,0:T(8,128)(2,1)S(1)} %add_convert_fusion.3.refs_0_), channel_id=1, source_target_pairs={{0,2},{1,3},{2,0},{3,1},{4,6},{5,7},{6,4},{7,5},{8,10},{9,11},{10,... | collective-permute-start | bytes 983048 | tf_op jit(solution)/shard_map/ppermute | solution.py:361
  338.4 20.7 %collective-permute-start.34 = (bf16[256,640]{1,0:T(8,128)(2,1)S(1)}, bf16[256,640]{1,0:T(8,128)(2,1)S(1)}, u32[]{:S(2)}, u32[]{:S(2)}) collective-permute-start(bf16[256,640]{1,0:T(8,128)(2,1)S(1)} %collective-permute-done.32.refs_1_), channel_id=1, source_target_pairs={{0,8},{1,9},{2,10},{3,11},{4,0},{5,1},{6,2},{7,3},{8,16},{9,17},{1... | collective-permute-start | bytes 983048 | tf_op jit(solution)/shard_map/ppermute | solution.py:361
  339.6 20.1 %collective-permute-start.41 = (bf16[256,640]{1,0:T(8,128)(2,1)S(1)}, bf16[256,640]{1,0:T(8,128)(2,1)}, u32[]{:S(2)}, u32[]{:S(2)}) collective-permute-start(bf16[256,640]{1,0:T(8,128)(2,1)S(1)} %collective-permute-done.32.refs_1_), channel_id=1, source_target_pairs={{0,2},{1,3},{2,0},{3,1},{4,6},{5,7},{6,4},{7,5},{8,10},{9,11},{10,... | collective-permute-start | bytes 983048 | tf_op jit(solution)/shard_map/ppermute | solution.py:361
  359.2 14.3 %collective-permute-start.43 = (bf16[256,640]{1,0:T(8,128)(2,1)S(1)}, bf16[256,640]{1,0:T(8,128)(2,1)S(1)}, u32[]{:S(2)}, u32[]{:S(2)}) collective-permute-start(bf16[256,640]{1,0:T(8,128)(2,1)S(1)} %collective-permute-done.34.refs_3_), channel_id=1, source_target_pairs={{0,2},{1,3},{2,0},{3,1},{4,6},{5,7},{6,4},{7,5},{8,10},{9,11},{10,... | collective-permute-start | bytes 983048 | tf_op jit(solution)/shard_map/ppermute | solution.py:361
  364.6 18.5 %collective-permute-start.64 = (bf16[240,640]{1,0:T(8,128)(2,1)S(1)}, bf16[240,640]{1,0:T(8,128)(2,1)S(1)}, u32[]{:S(2)}, u32[]{:S(2)}) collective-permute-start(bf16[240,640]{1,0:T(8,128)(2,1)S(1)} %pad_maximum_fusion.refs_0_), channel_id=1, source_target_pairs={{0,8},{1,9},{2,10},{3,11},{4,0},{5,1},{6,2},{7,3},{8,16},{9,17},{1... | collective-permute-start | bytes 921608 | tf_op jit(solution)/shard_map/ppermute | solution.py:361
  373.5 14.3 %collective-permute-start.45 = (bf16[256,640]{1,0:T(8,128)(2,1)S(1)}, bf16[256,640]{1,0:T(8,128)(2,1)S(1)}, u32[]{:S(2)}, u32[]{:S(2)}) collective-permute-start(bf16[256,640]{1,0:T(8,128)(2,1)S(1)} %collective-permute-done.36.refs_5_), channel_id=1, source_target_pairs={{0,2},{1,3},{2,0},{3,1},{4,6},{5,7},{6,4},{7,5},{8,10},{9,11},{10,... | collective-permute-start | bytes 983048 | tf_op jit(solution)/shard_map/ppermute | solution.py:361
  373.6 14.8 %collective-permute-start.46 = (bf16[256,640]{1,0:T(8,128)(2,1)S(1)}, bf16[256,640]{1,0:T(8,128)(2,1)S(1)}, u32[]{:S(2)}, u32[]{:S(2)}) collective-permute-start(bf16[256,640]{1,0:T(8,128)(2,1)S(1)} %collective-permute-done.37.refs_6_), channel_id=1, source_target_pairs={{0,2},{1,3},{2,0},{3,1},{4,6},{5,7},{6,4},{7,5},{8,10},{9,11},{10,... | collective-permute-start | bytes 983048 | tf_op jit(solution)/shard_map/ppermute | solution.py:361
  396.4 38.2 %collective-permute-start.21 = (bf16[320,1280]{1,0:T(8,128)(2,1)S(1)}, bf16[320,1280]{1,0:T(8,128)(2,1)}, u32[]{:S(2)}, u32[]{:S(2)}) collective-permute-start(bf16[320,1280]{1,0:T(8,128)(2,1)S(1)} %collective-permute-done.20.refs_1_), channel_id=1, source_target_pairs={{0,2},{1,3},{2,0},{3,1},{4,6},{5,7},{6,4},{7,5},{8,10},{9,11},{10,... | collective-permute-start | bytes 2457608 | tf_op jit(solution)/shard_map/ppermute | solution.py:361
  400.3 34.2 %collective-permute-start.23 = (bf16[320,1280]{1,0:T(8,128)(2,1)}, bf16[320,1280]{1,0:T(8,128)(2,1)}, u32[]{:S(2)}, u32[]{:S(2)}) collective-permute-start(bf16[320,1280]{1,0:T(8,128)(2,1)} %collective-permute-done.22.refs_4_), channel_id=1, source_target_pairs={{0,2},{1,3},{2,0},{3,1},{4,6},{5,7},{6,4},{7,5},{8,10},{9,11},{10,... | collective-permute-start | bytes 2457608 | tf_op jit(solution)/shard_map/ppermute | solution.py:361
  401.4 33.2 %collective-permute-start.25 = (bf16[320,1280]{1,0:T(8,128)(2,1)}, bf16[320,1280]{1,0:T(8,128)(2,1)}, u32[]{:S(2)}, u32[]{:S(2)}) collective-permute-start(bf16[320,1280]{1,0:T(8,128)(2,1)} %collective-permute-done.24.refs_7_), channel_id=1, source_target_pairs={{0,2},{1,3},{2,0},{3,1},{4,6},{5,7},{6,4},{7,5},{8,10},{9,11},{10,... | collective-permute-start | bytes 2457608 | tf_op jit(solution)/shard_map/ppermute | solution.py:361
  410.7 15.2 %collective-permute-start.78 = (bf16[240,640]{1,0:T(8,128)(2,1)S(1)}, bf16[240,640]{1,0:T(8,128)(2,1)}, u32[]{:S(2)}, u32[]{:S(2)}) collective-permute-start(bf16[240,640]{1,0:T(8,128)(2,1)S(1)} %collective-permute-done.69.refs_6_), channel_id=1, source_target_pairs={{0,2},{1,3},{2,0},{3,1},{4,6},{5,7},{6,4},{7,5},{8,10},{9,11},{10,... | collective-permute-start | bytes 921608 | tf_op jit(solution)/shard_map/ppermute | solution.py:361
  410.9 15.1 %collective-permute-start.80 = (bf16[128,640]{1,0:T(8,128)(2,1)}, bf16[128,640]{1,0:T(8,128)(2,1)}, u32[]{:S(2)}, u32[]{:S(2)}) collective-permute-start(bf16[128,640]{1,0:T(8,128)(2,1)} %collective-permute-done.71.refs_8_), channel_id=1, source_target_pairs={{0,2},{1,3},{2,0},{3,1},{4,6},{5,7},{6,4},{7,5},{8,10},{9,11},{10,... | collective-permute-start | bytes 491528 | tf_op jit(solution)/shard_map/ppermute | solution.py:361
  (99 other events, 1420.3 us)

commit v2 on v1

--- a/solution.py
+++ b/solution.py
@@ -365,12 +365,10 @@
     return lax.dot_general(left, right, dims, preferred_element_type=F32)
 
 
-def call(body, outs, args, smem=0, anys=0, scratch=(), cost=None, out_any=False):
-    whole = pl.BlockSpec(memory_space=pltpu.VMEM)
+def call(body, outs, args, smem=0, anys=(), scratch=(), cost=None, out_anys=(), aliases=None):
+    whole, anywhere = pl.BlockSpec(memory_space=pltpu.VMEM), pl.BlockSpec(memory_space=pl.ANY)
     specs = [pl.BlockSpec(memory_space=pltpu.SMEM)] * smem
-    specs += [whole] * (len(args) - smem - anys)
-    specs += [pl.BlockSpec(memory_space=pl.ANY)] * anys
-    out_spec = pl.BlockSpec(memory_space=pl.ANY) if out_any else whole
+    specs += [anywhere if at in anys else whole for at in range(smem, len(args))]
     estimate = None
     if cost is not None:
         estimate = pl.CostEstimate(flops=int(cost[0]), bytes_accessed=int(cost[1]), transcendentals=int(cost[2]))
@@ -378,8 +376,9 @@
         body,
         out_shape=[jax.ShapeDtypeStruct(shape, kind) for shape, kind in outs],
         in_specs=specs,
-        out_specs=[out_spec] * len(outs),
+        out_specs=[anywhere if at in out_anys else whole for at in range(len(outs))],
         scratch_shapes=list(scratch),
+        input_output_aliases=aliases or {},
         cost_estimate=estimate,
         compiler_params=pltpu.CompilerParams(vmem_limit_bytes=LIMIT),
     )(*args)
@@ -404,9 +403,10 @@
     out[6 * HEAD :] = tail.astype(BF)
 
 
-def project_kernel(count, info, *refs):
+def project_kernel(count, start, info, *refs):
     xs = refs[:count]
-    own, other, scale, attn_in, mine, partner, weight, gain, lines = refs[count:]
+    own, other, scale = refs[count : count + 3]
+    whole, mine, partner, attn_in, weight, gain, lines, sem = refs[-8:]
     y, core = info[0], info[1]
     weight[:, half(y)] = own[: 6 * HEAD]
     weight[:, half(1 - y)] = other[: 6 * HEAD]
@@ -418,6 +418,8 @@
         scaled = values * lax.rsqrt(jnp.mean(values * values, axis=-1, keepdims=True) + EPS)
         attn_in[row : row + ref.shape[0]] = (scaled * gain[0:1]).astype(BF)
         row += ref.shape[0]
+    copy = pltpu.make_async_copy(attn_in, whole.at[pl.ds(start, row)], sem)
+    copy.start()
     lin = mm(weight[...], attn_in[...], NT)
     for head in range(2):
         base = head * 3 * HEAD
@@ -425,6 +427,7 @@
         lines[base + HEAD : base + 3 * HEAD] = lin[base + HEAD : base + 3 * HEAD].astype(BF)
     mine[...] = lines[pl.ds(pl.multiple_of(core * 3 * HEAD, 16), 3 * HEAD)]
     partner[...] = lines[pl.ds(pl.multiple_of((1 - core) * 3 * HEAD, 16), 3 * HEAD)]
+    copy.wait()
 
 
 def span_slots(pieces):
@@ -439,15 +442,37 @@
     return pl.ds(pl.multiple_of(span * SPAN, SPAN), SPAN)
 
 
-BLOCK = 512
+BLOCK = 1024
+WIDE = 128
+
+
+def block_at(at):
+    return pl.ds(pl.multiple_of(at * BLOCK, BLOCK), BLOCK)
+
+
+def in_parts(line):
+    high = line.astype(BF)
+    rest = line - high.astype(F32)
+    middle = rest.astype(BF)
+    low = (rest - middle.astype(F32)).astype(BF)
+    at = lax.broadcasted_iota(jnp.int32, (16, line.shape[1]), 0)
+    rows = jnp.where(at == 0, high.astype(F32), 0.0)
+    rows = jnp.where(at == 1, middle.astype(F32), rows)
+    return jnp.where(at == 2, low.astype(F32), rows).astype(BF)
+
+
+def ones_behind(ref):
+    at = lax.broadcasted_iota(jnp.int32, ref.shape, 1)
+    ref[...] = jnp.where((at >= HEAD) & (at < HEAD + 3), 1.0, 0.0).astype(BF)
 
 
 def forward_kernel(info, deal, *refs):
     pieces = refs[:10]
-    out, lse, queries, keys, values, dealt = refs[10:]
+    out, q_out, k_out, queries, keys, values, lse, dealt = refs[10:]
     total = queries.shape[1]
     length = info[3]
     spans = total // SPAN
+    blocks = total // BLOCK
 
     @pl.loop(0, spans)
     def _(at):
@@ -455,49 +480,95 @@
 
     line = lax.broadcasted_iota(jnp.int32, (16, total), 0)
     values[HEAD:] = jnp.where(line == 0, 1.0, 0.0).astype(BF)
+    queries[HEAD:] = jnp.zeros((WIDE - HEAD, total), BF)
+    ones_behind(keys)
+    longest = jnp.zeros((1, SPAN), F32)
     for slot, (ref, col) in enumerate(span_slots(pieces)):
         where = at_span(natural_span(info, deal, slot))
-        queries[:, where] = ref[:HEAD, col : col + SPAN]
-        keys[where, :] = ref[HEAD : 2 * HEAD, col : col + SPAN].T
+        key = ref[HEAD : 2 * HEAD, col : col + SPAN]
+        queries[:HEAD, where] = ref[:HEAD, col : col + SPAN]
+        keys[where, :HEAD] = key.T
         values[:HEAD, where] = ref[2 * HEAD :, col : col + SPAN]
+        sizes = key.astype(F32)
+        longest = jnp.maximum(longest, jnp.sum(sizes * sizes, axis=0, keepdims=True))
+    longest = jnp.max(longest, axis=1, keepdims=True)
 
     key_at = lax.broadcasted_iota(jnp.int32, (BLOCK, BLOCK), 0)
     query_at = lax.broadcasted_iota(jnp.int32, (BLOCK, BLOCK), 1)
 
-    @pl.loop(0, total // BLOCK)
-    def _(i):
-        here = pl.ds(pl.multiple_of(i * BLOCK, BLOCK), BLOCK)
-        query = queries[:, here]
-
-        def step(masked, j, carry):
-            peak, acc = carry
-            there = pl.ds(pl.multiple_of(j * BLOCK, BLOCK), BLOCK)
-            scores = mm(keys[there, :], query)
-            if masked:
-                key_pos = j * BLOCK + key_at
-                allowed = (key_pos <= i * BLOCK + query_at) & (key_pos < length)
-                scores = jnp.where(allowed, scores, NEG)
-            newest = jnp.maximum(peak, jnp.max(scores, axis=0, keepdims=True))
-            weights = jnp.exp(scores - newest)
-            acc = acc * jnp.exp(peak - newest) + mm(values[:, there], weights.astype(BF))
-            return newest, acc
-
-        carry = (jnp.full((1, BLOCK), NEG, F32), jnp.zeros((HEAD + 16, BLOCK), F32))
-        split = jnp.minimum(i, length // BLOCK)
-        carry = lax.fori_loop(0, split, functools.partial(step, False), carry)
-        peak, acc = lax.fori_loop(split, i + 1, functools.partial(step, True), carry)
+    def scores_of(masked, i, j):
+        scores = mm(keys[block_at(j), :], queries[:, block_at(i)])
+        if masked:
+            key_pos = j * BLOCK + key_at
+            allowed = (key_pos <= i * BLOCK + query_at) & (key_pos < length)
+            scores = jnp.where(allowed, scores, NEG)
+        return scores
+
+    def finish(i, peak, acc):
+        here = block_at(i)
         norm = acc[HEAD : HEAD + 1]
         lse[:, here] = peak + jnp.log(norm)
         attended = (acc[:HEAD] / norm).astype(BF)
         for part in range(BLOCK // SPAN):
             row = dealt[i * (BLOCK // SPAN) + part]
             out[row // 2, :, at_span(row % 2)] = attended[:, part * SPAN : (part + 1) * SPAN]
+        return jnp.min(norm)
+
+    def bounded(i, least):
+        here = block_at(i)
+        query = queries[:HEAD, here].astype(F32)
+        bound = jnp.sqrt(jnp.sum(query * query, axis=0, keepdims=True) * longest) - 40.0
+        shift = in_parts(-bound)
+        queries[HEAD : HEAD + 16, here] = shift
+
+        def step(masked, j, acc):
+            weights = jnp.exp(scores_of(masked, i, j)).astype(BF)
+            return acc + mm(values[:, block_at(j)], weights)
+
+        split = jnp.minimum(i, length // BLOCK)
+        acc = lax.fori_loop(0, split, functools.partial(step, False), jnp.zeros((HEAD + 16, BLOCK), F32))
+        acc = lax.fori_loop(split, i + 1, functools.partial(step, True), acc)
+        exact = jnp.sum(shift.astype(F32), axis=0, keepdims=True)
+        return jnp.minimum(least, finish(i, -exact, acc))
+
+    least = lax.fori_loop(0, blocks, bounded, jnp.float32(1.0))
+
+    @pl.when(jnp.logical_not(least > 1e-26))
+    def _():
+        queries[HEAD:] = jnp.zeros((WIDE - HEAD, total), BF)
+
+        @pl.loop(0, blocks)
+        def _(i):
+            def step(j, carry):
+                peak, acc = carry
+                scores = scores_of(True, i, j)
+                newest = jnp.maximum(peak, jnp.max(scores, axis=0, keepdims=True))
+                weights = jnp.exp(scores - newest).astype(BF)
+                return newest, acc * jnp.exp(peak - newest) + mm(values[:, block_at(j)], weights)
+
+            start = (jnp.full((1, BLOCK), NEG, F32), jnp.zeros((HEAD + 16, BLOCK), F32))
+            finish(i, *lax.fori_loop(0, i + 1, step, start))
+
+    q_out[:HEAD] = queries[:HEAD]
+    q_out[HEAD : HEAD + 16] = in_parts(-lse[...])
+    q_out[HEAD + 16 :] = jnp.zeros((WIDE - HEAD - 16, total), BF)
+    k_out[...] = keys[...]
+
+
+def turn_kernel(info, deal, *refs):
+    pieces, (k_t, q_n, v_n) = refs[:10], refs[10:]
+    q_n[...] = jnp.zeros_like(q_n)
+    ones_behind(v_n)
+    for slot, (ref, col) in enumerate(span_slots(pieces)):
+        where = at_span(natural_span(info, deal, slot))
+        cols = slice(col, col + SPAN)
+        k_t[:, where] = ref[HEAD : 2 * HEAD, cols]
+        q_n[where, :HEAD] = ref[:HEAD, cols].T
+        v_n[where, :HEAD] = ref[2 * HEAD :, cols].T
 
 
 def backward_kernel(info, deal, *refs):
-    pieces = refs[:10]
-    lse, attended, grad_out, scale, out = refs[10:15]
-    q_n, k_n, v_n, g_n, q_t, k_t, g_t, delta, dq_t, dk, dv, dealt = refs[15:]
+    q_t, k_n, k_t, q_n, v_n, attended, grad_out, scale, out, g_t, g_n, delta, dq_t, dk, dv, dealt = refs
     total = q_t.shape[1]
     length = info[3]
     spans = total // SPAN
@@ -507,22 +578,17 @@
     def _(at):
         dealt[deal[at]] = at
 
-    for slot, (ref, col) in enumerate(span_slots(pieces)):
-        where = at_span(natural_span(info, deal, slot))
-        cols = slice(col, col + SPAN)
-        q_t[:, where] = ref[:HEAD, cols]
-        k_t[:, where] = ref[HEAD : 2 * HEAD, cols]
-        q_n[where, :] = ref[:HEAD, cols].T
-        k_n[where, :] = ref[HEAD : 2 * HEAD, cols].T
-        v_n[where, :] = ref[2 * HEAD :, cols].T
+    g_n[...] = jnp.zeros_like(g_n)
+    g_t[HEAD:] = jnp.zeros((WIDE - HEAD, total), BF)
     for row in range(spans):
         where = at_span(deal[row])
         cols = slice(row % 2 * SPAN, row % 2 * SPAN + SPAN)
         grad = grad_out[row // 2, :, cols]
-        g_t[:, where] = grad
-        g_n[where, :] = grad.T
+        g_t[:HEAD, where] = grad
+        g_n[where, :HEAD] = grad.T
         product = grad.astype(F32) * attended[row // 2, :, cols].astype(F32)
         delta[:, where] = jnp.sum(product, axis=0, keepdims=True)
+    g_t[HEAD : HEAD + 16] = in_parts(-delta[...])
     dq_t[...] = jnp.zeros_like(dq_t)
 
     key_at = lax.broadcasted_iota(jnp.int32, (BLOCK, BLOCK), 0)
@@ -530,20 +596,18 @@
 
     @pl.loop(0, blocks)
     def _(j):
-        there = pl.ds(pl.multiple_of(j * BLOCK, BLOCK), BLOCK)
+        there = block_at(j)
         dk[...] = jnp.zeros_like(dk)
         dv[...] = jnp.zeros_like(dv)
 
         def step(masked, i, carry):
-            here = pl.ds(pl.multiple_of(i * BLOCK, BLOCK), BLOCK)
-            scores = mm(k_n[there, :], q_t[:, here])
-            probs = jnp.exp(scores - lse[:, here])
+            here = block_at(i)
+            probs = jnp.exp(mm(k_n[there, :], q_t[:, here]))
             if masked:
                 key_pos = j * BLOCK + key_at
                 allowed = (key_pos <= i * BLOCK + query_at) & (key_pos < length)
                 probs = jnp.where(allowed, probs, 0.0)
-            grad_probs = mm(v_n[there, :], g_t[:, here])
-            grad_scores = (probs * (grad_probs - delta[:, here])).astype(BF)
+            grad_scores = (probs * mm(v_n[there, :], g_t[:, here])).astype(BF)
             dv[...] += mm(probs.astype(BF), g_n[here, :])
             dk[...] += mm(grad_scores, q_n[here, :])
             dq_t[:, here] += mm(k_t[:, there], grad_scores)
@@ -555,27 +619,35 @@
         for part in range(BLOCK // SPAN):
             row = dealt[j * (BLOCK // SPAN) + part]
             rows = slice(part * SPAN, (part + 1) * SPAN)
-            out[row // 2, HEAD : 2 * HEAD, at_span(row % 2)] = dk[rows].T.astype(BF)
-            out[row // 2, 2 * HEAD :, at_span(row % 2)] = dv[rows].T.astype(BF)
+            out[row // 2, HEAD : 2 * HEAD, at_span(row % 2)] = dk[rows].T[:HEAD].astype(BF)
+            out[row // 2, 2 * HEAD :, at_span(row % 2)] = dv[rows].T[:HEAD].astype(BF)
 
     for row in range(spans):
         cols = slice(row % 2 * SPAN, row % 2 * SPAN + SPAN)
         out[row // 2, :HEAD, cols] = (dq_t[:, at_span(deal[row])] * scale[...]).astype(BF)
 
 
-def load_weights(info, parts, wholes, sems):
+def load_weights(info, own, direct, passed, wholes, sems):
     y, core = info[0], info[1]
     started = []
+    count = 0
     for at, whole in enumerate(wholes):
-        own, direct, passed = parts[3 * at : 3 * at + 3]
-        rows, part = own.shape[0], direct.shape[0]
+        rows, part = own[at].shape[0], own[at].shape[0] // 2
         far = (1 - y) * rows
-        places = ((own, y * rows), (direct, far + core * part), (passed, far + (1 - core) * part))
+        places = [(own[at], y * rows)]
+        for chunks, base in ((direct, far + core * part), (passed, far + (1 - core) * part)):
+            start = 0
+            for chunk in chunks:
+                low, high = max(start, at * part), min(start + chunk.shape[0], at * part + part)
+                if low < high:
+                    places.append((chunk.at[pl.ds(low - start, high - low)], base + low - at * part))
+                start += chunk.shape[0]
         copies = []
-        for piece, (ref, start) in enumerate(places):
-            target = whole.at[pl.ds(pl.multiple_of(start, 64), ref.shape[0])]
-            copies.append(pltpu.make_async_copy(ref, target, sems.at[3 * at + piece]))
+        for ref, start in places:
+            target = whole.at[pl.ds(pl.multiple_of(start, 16), ref.shape[0])]
+            copies.append(pltpu.make_async_copy(ref, target, sems.at[count]))
             copies[-1].start()
+            count += 1
         started.append(copies)
     return started
 
@@ -585,12 +657,14 @@
         copy.wait()
 
 
-def mlp_kernel(info, tokens, cotangent, attn_t, own, other, *refs):
-    parts, outs = refs[:9], refs[9:16]
-    w_output, w_expand, w_contract, gain, sems = refs[16:]
-    result, grad_mid_out, grad_attended_t, act_out, mlp_in_out, grad_expanded_out, grad_mid_low_out = outs
-    y = info[0]
-    loads = load_weights(info, parts, (w_output, w_expand, w_contract), sems)
+def mlp_kernel(chunks, info, tokens, cotangent, attn_t, own, other, *refs):
+    shards, direct, passed = refs[:3], refs[3 : 3 + chunks], refs[3 + chunks : 3 + 2 * chunks]
+    refs = refs[3 + 2 * chunks :]
+    outs = refs[:5]
+    w_output, w_expand, w_contract, gain, right, sems = refs[5:]
+    result, grad_mid_out, grad_attended_t, away, rights = outs
+    y, core = info[0], info[1]
+    loads = load_weights(info, shards, direct, passed, (w_output, w_expand, w_contract), sems)
     gain[:, half(y)] = own[6 * HEAD :].astype(F32)
     gain[:, half(1 - y)] = other[6 * HEAD :].astype(F32)
     gains = gain[1:2]
@@ -599,32 +673,93 @@
     mid = tokens[...].astype(F32) + mm(attn, w_output[...])
     rate = lax.rsqrt(jnp.mean(mid * mid, axis=-1, keepdims=True) + EPS)
     mlp_in = (mid * rate * gains).astype(BF)
-    mlp_in_out[...] = mlp_in
+    away[1] = mlp_in
     arrive(loads[1])
     expanded = mm(mlp_in, w_expand[...])
     gate = jax.nn.sigmoid(expanded)
     act = (expanded * gate).astype(BF)
-    act_out[...] = act
+    away[0] = act
     arrive(loads[2])
     result[...] = (mid + mm(act, w_contract[...])).astype(BF)
     grad_act = mm(cotangent[...], w_contract[...], NT)
     grad_expanded = (grad_act * gate * (1.0 + expanded * (1.0 - gate))).astype(BF)
-    grad_expanded_out[...] = grad_expanded
+    right[0] = grad_expanded
     grad_mlp_in = mm(grad_expanded, w_expand[...], NT) * gains
     inner = jnp.mean(grad_mlp_in * mid, axis=-1, keepdims=True)
     grad_mid = cotangent[...].astype(F32) + rate * grad_mlp_in - mid * (rate * rate * rate * inner)
     grad_mid_out[...] = grad_mid
     low = grad_mid.astype(BF)
-    grad_mid_low_out[...] = low
+    right[1] = low
     grad_attended_t[...] = mm(w_output[...], low, NT).astype(BF)
-
-
-def outer_kernel(info, act, cotangent, mlp_in, grad_expanded, attn_t, grad_mid_low, *outs):
+    for at in range(2):
+        rights[:, at * 640 : at * 640 + 640] = right[at, :, half(core)]
+        away[2, :, at * 640 : at * 640 + 640] = right[at, :, half(1 - core)]
+
+
+BITS = ("y", "x", "far", "near")
+ORDERS = (("y", "x", "near", "far"), ("x", "near", "y", "far"), ("near", "y", "x", "far"))
+BIT_AT = {"y": 0, "x": 20, "near": 21, "far": 22}
+PART = 80
+
+
+def left_bits(order, done):
+    return [name for name in BITS if name not in order[:done]]
+
+
+def halves(info, order, done):
+    left = left_bits(order, done)
+    name = order[done]
+    bit = info[BIT_AT[name]]
+    stride = 1 << (len(left) - 1 - left.index(name))
+    count = 1 << len(left)
+    bases = [block for block in range(count) if block & stride == 0]
+    return [(base + bit * stride, base + (1 - bit) * stride) for base in bases]
+
+
+def rows_of(block):
+    start = block * PART
+    return pl.ds(start if isinstance(block, int) else pl.multiple_of(start, 16), PART)
+
+
+def outer_kernel(info, own, rights, partner, attn_t, attn_t_partner, cot, cot_partner, *refs):
+    outs, (left, right, full) = refs[:6], refs[6:]
     core = info[1]
-    lefts = (act[...].T, mlp_in[...].T, attn_t[...])
-    for at, right in enumerate((cotangent, grad_expanded, grad_mid_low)):
-        outs[2 * at][...] = mm(lefts[at], right[:, half(core)]).astype(BF)
-        outs[2 * at + 1][...] = mm(lefts[at], right[:, half(1 - core)]).astype(BF)
+    rows = cot.shape[0]
+    for at in range(3):
+        if at < 2:
+            left[:, :rows] = own[at].T
+            left[:, rows:] = partner[at].T
+        else:
+            left[:, :rows] = attn_t[...]
+            left[:, rows:] = attn_t_partner[...]
+        if at == 0:
+            right[:rows] = cot[:, half(core)]
+            right[rows:] = cot_partner[:, half(core)]
+        else:
+            cols = slice((at - 1) * 640, at * 640)
+            right[:rows] = rights[:, cols]
+            right[rows:] = partner[2, :, cols]
+        full[...] = mm(left[...], right[...]).astype(BF)
+        for to, (kept, sent) in enumerate(halves(info, ORDERS[at], 0)):
+            outs[at][rows_of(to)] = full[rows_of(kept)]
+            outs[3 + at][rows_of(to)] = full[rows_of(sent)]
+
+
+def round_kernel(done, info, *refs):
+    kept, came, outs = refs[:3], refs[3:6], refs[6:]
+    for at in range(3):
+        for to, (mine, theirs) in enumerate(halves(info, ORDERS[at], done)):
+            if len(outs) == 6:
+                stay, away, target = outs[at], outs[3 + at], rows_of(to)
+            else:
+                stay, away, target = outs[0], outs[1], rows_of(at)
+            for out, block in ((stay, mine), (away, theirs)):
+                total = kept[at][rows_of(block)].astype(F32) + came[at][rows_of(block)].astype(F32)
+                out[target] = total.astype(BF)
+
+
+def folded(products):
+    return sum(products[:, at : at + 128] for at in range(0, products.shape[1], 128))
 
 
 def row_sums(products):
@@ -634,45 +769,79 @@
     return mm(ones, high, NT) + mm(ones, low, NT)
 
 
-def piece_rows(refs):
-    slots = []
+def stack_kernel(*refs):
+    for at, ref in enumerate(refs[:-1]):
+        refs[-1][at] = ref[...]
+
+
+def joined(pieces, last):
+    count = len(pieces) // 2
+    ready = []
     for colour in range(2):
-        group = refs[9 * colour : 9 * colour + 9]
-        slots += [[(ref, 0)] for ref in group[:7]]
-        slots.append([(group[7], 0), (group[8], group[7].shape[0])])
-    return slots
-
-
-def spread_kernel(info, *refs):
-    pieces, (w_expand, gain) = refs[:18], refs[18:20]
-    outs, grad_gain, stage = refs[20:23], refs[23], refs[24]
-    for slot, parts in enumerate(piece_rows(pieces)):
-        dev = info[4 + slot]
+        group = pieces[colour * count : colour * count + count]
+        cut = group[-2].shape[0]
+        last[colour, :cut] = group[-2][...]
+        last[colour, cut:] = group[-1][...]
+        ready += [*group[:-2], last.at[colour]]
+    return ready
+
+
+def slot_of(at, count, first):
+    return first + at if at < count else 8 + first + at - count
+
+
+def scatter(info, refs, first, blocks, sems, outs, expand, sums):
+    copies = []
+    for at, ref in enumerate(refs):
+        dev = info[4 + slot_of(at, len(refs) // 2, first)]
         block = ((dev // 2) % 2) * 4 + dev // 4
-        for ref, row in parts:
-            stage[slot, row : row + ref.shape[0]] = ref[...]
-        rows = pl.ds(pl.multiple_of(block * 80, 16), 80)
-        for at in range(3):
-            outs[at][rows, half(dev % 2)] = stage[slot, at * 80 : at * 80 + 80].astype(F32)
-    grad_gain[...] = row_sums(w_expand[...].astype(F32) * outs[1][...])[0:1] / gain[...].astype(F32)
+        rows = pl.ds(pl.multiple_of(block * PART, 16), PART)
+        for way in range(3):
+            blocks[3 * at + way] = ref[way * PART : (way + 1) * PART].astype(F32)
+            target = outs[way].at[rows, half(dev % 2)]
+            copies.append(pltpu.make_async_copy(blocks.at[3 * at + way], target, sems.at[3 * at + way]))
+            copies[-1].start()
+        sums[rows] += folded(blocks[3 * at + 1] * expand[rows, half(dev % 2)].astype(F32))
+    return copies
+
+
+def spread_kernel(info, near, near_partner, expand, sums, *refs):
+    outs, (blocks, sems) = refs[:3], refs[3:]
+    pieces = [stack.at[at] for stack in (near, near_partner) for at in range(5)]
+    sums[...] = jnp.zeros_like(sums)
+    arrive(scatter(info, pieces, 0, blocks, sems, outs, expand, sums))
+
+
+def spread_last_kernel(info, *refs):
+    pieces, (before, gain, expand), (*outs, grad_gain), refs = refs[:8], refs[8:11], refs[14:18], refs[18:]
+    blocks, last, sums, sems = refs
+    sums[...] = before[...]
+    copies = scatter(info, joined(pieces, last), 5, blocks, sems, outs, expand, sums)
+    size = sums.shape[0]
+    grad_gain[...] = (row_sums(sums[...])[0:1] / gain[...].astype(F32)).reshape(size)
+    arrive(copies)
 
 
 def weight_kernel(info, grads, own, other, *refs):
-    inputs = refs[:10]
-    keep, away, lines, weight, total = refs[10:]
+    inputs = refs[:2]
+    keep, away, lines, weight, total, attn_in, sems = refs[2:]
     y, core = info[0], info[1]
-    slot = 0
-    for ref in inputs:
-        for _ in range(0, ref.shape[0], 256):
-            lines[:, slot * 256 : slot * 256 + 256] = grads[info[4 + slot]]
-            slot += 1
+    rows = attn_in.shape[0] // 8
+    loads = []
+    for at in range(8):
+        source = inputs[at // 4].at[pl.ds(at % 4 * rows, rows)]
+        loads.append(pltpu.make_async_copy(source, attn_in.at[pl.ds(at * rows, rows)], sems.at[at]))
+        loads[-1].start()
+    for slot in range(16):
+        lines[:, slot * 256 : slot * 256 + 256] = grads[info[4 + slot]]
     weight[:, half(y)] = own[pl.ds(pl.multiple_of(core * 3 * HEAD, 16), HEAD)].astype(F32)
     weight[:, half(1 - y)] = other[pl.ds(pl.multiple_of(core * 3 * HEAD, 16), HEAD)].astype(F32)
     total[...] = jnp.zeros_like(total)
-    col = 0
-    for ref in inputs:
-        total[...] += mm(lines[:, col : col + ref.shape[0]], ref[...])
-        col += ref.shape[0]
+    for at in range(4):
+        loads[2 * at].wait()
+        loads[2 * at + 1].wait()
+        part = slice(2 * at * rows, 2 * (at + 1) * rows)
+        total[...] += mm(lines[:, part], attn_in[part])
     keep[: 3 * HEAD] = total[:, half(y)]
     away[: 3 * HEAD] = total[:, half(1 - y)].astype(BF)
     sums = row_sums(weight[...] * total[:HEAD])
@@ -682,36 +851,41 @@
     away[3 * HEAD :, :HEAD] = sums.astype(BF)
 
 
-def finish_kernel(info, *refs):
-    pieces, (wq, wk, wv, gain, factor) = refs[:18], refs[18:23]
-    outs, grad_gain, grad_scale = refs[23:26], refs[26], refs[27]
-    stage, stacks = refs[28], refs[29:32]
+def finish_kernel(info, near, near_partner, *refs):
+    pieces, shards, (gain, factor), refs = refs[:8], refs[8:11], refs[11:13], refs[13:]
+    outs, (grad_gain, grad_scale), (stacks, weights, last, turned, sems) = refs[:3], refs[3:5], refs[5:]
+    loads = [pltpu.make_async_copy(ref, weights.at[at], sems.at[at]) for at, ref in enumerate(shards)]
+    for load in loads:
+        load.start()
     scale_sum = jnp.zeros((1, HEAD), F32)
-    for slot, parts in enumerate(piece_rows(pieces)):
-        dev = info[4 + slot]
-        for ref, row in parts:
-            stage[slot, row : row + ref.shape[0]] = ref[...]
-        rows = pl.ds(pl.multiple_of(dev * HEAD, 16), HEAD)
-        for at in range(3):
-            stacks[at][rows] = stage[slot, at * HEAD : (at + 1) * HEAD]
-        scale_sum += stage[slot, 3 * HEAD :, :HEAD].astype(F32)[0:1]
+    early = [stack.at[at] for stack in (near, near_partner) for at in range(5)]
+    for first, group in ((0, early), (5, joined(pieces, last))):
+        for at, ref in enumerate(group):
+            rows = pl.ds(pl.multiple_of(info[4 + slot_of(at, len(group) // 2, first)] * HEAD, 16), HEAD)
+            for way in range(3):
+                stacks[way, rows] = ref[way * HEAD : (way + 1) * HEAD]
+            scale_sum += ref[3 * HEAD :, :HEAD].astype(F32)[0:1]
     grad_scale[...] = scale_sum * factor[...]
-    size = stage.shape[2]
+    size = turned.shape[1]
     same = lax.broadcasted_iota(jnp.int32, (size, size), 0) == lax.broadcasted_iota(jnp.int32, (size, size), 1)
     unit = jnp.where(same, 1.0, 0.0).astype(BF)
-    sums = jnp.zeros((16, size), F32)
-    for at, own in enumerate((wq, wk, wv)):
-        turned_grad = mm(unit, stacks[at][...], NT)
-        outs[at][...] = turned_grad
-        sums += row_sums(own[...].astype(F32) * turned_grad)
-    grad_gain[...] = sums[0:1] / gain[...].astype(F32)
-
-
-def input_kernel(info, tokens, grads, grad_mid, own, other, *refs):
-    parts, out = refs[:9], refs[9]
-    weights, gain, sems = refs[10:13], refs[13], refs[14]
+    copies = []
+    sums = jnp.zeros((size, 128), F32)
+    for at, out in enumerate(outs):
+        turned[at] = mm(unit, stacks[at], NT)
+        copies.append(pltpu.make_async_copy(turned.at[at], out, sems.at[3 + at]))
+        copies[-1].start()
+        loads[at].wait()
+        sums += folded(weights[at].astype(F32) * turned[at])
+    grad_gain[...] = (row_sums(sums)[0:1] / gain[...].astype(F32)).reshape(size)
+    arrive(copies)
+
+
+def input_kernel(chunks, info, tokens, grads, grad_mid, own, other, *refs):
+    shards, direct, passed = refs[:3], refs[3 : 3 + chunks], refs[3 + chunks : 3 + 2 * chunks]
+    out, *weights, gain, sems = refs[3 + 2 * chunks :]
     y = info[0]
-    loads = load_weights(info, parts, weights, sems)
+    loads = load_weights(info, shards, direct, passed, weights, sems)
     gain[:, half(y)] = own[6 * HEAD :].astype(F32)
     gain[:, half(1 - y)] = other[6 * HEAD :].astype(F32)
     heads, width = grads.shape[0], grads.shape[2]
@@ -727,34 +901,13 @@
     out[...] = (grad_mid[...] + rate * grad - values * (rate * rate * rate * inner)).astype(BF)
 
 
-def ring_gather(value, pieces_wanted=True):
-    forth, back = [value], [value]
-    for _ in range(3):
-        forth.append(send(forth[-1], FORTH))
-        back.append(send(back[-1], BACK))
-    cut = value.shape[0] // 32 * 16
-    last = (send(forth[-1][:cut], FORTH), send(back[-1][cut:], BACK))
-    return [value, forth[1], back[1], forth[2], back[2], forth[3], back[3], *last]
-
-
-def chip_gather(value):
-    mine = ring_gather(value)
-    return mine + [send(piece, CORE_SWAP) for piece in mine]
-
-
-def weight_parts(shards, core):
-    parts = []
-    for shard in shards:
-        size = shard.shape[0] // 2
-        direct = send(lax.dynamic_slice_in_dim(shard, core * size, size, 0), Y_SWAP)
-        parts += [shard, direct, send(direct, CORE_SWAP)]
-    return parts
-
-
-def halve(keep, away, where, moves, axis):
-    mine = lax.dynamic_index_in_dim(keep, where, axis, keepdims=False)
-    theirs = lax.dynamic_index_in_dim(keep, 1 - where, axis, keepdims=False)
-    return (mine.astype(F32) + send(theirs, moves).astype(F32)).astype(BF)
+def after(values, *others):
+    return lax.optimization_barrier((tuple(values), others))[0]
+
+
+def weight_rows(shards, core):
+    size = shards[0].shape[0] // 2
+    return jnp.concatenate([lax.dynamic_slice_in_dim(shard, core * size, size, 0) for shard in shards], axis=0)
 
 
 def ring_device(
@@ -765,7 +918,8 @@
     c, y = lax.axis_index("ctx"), lax.axis_index("wt")
     core, x, z = c % 2, (c // 2) % 2, c // 4
     table = lax.dynamic_index_in_dim(jnp.asarray(slot_table()), c, 0, keepdims=False)
-    info = jnp.concatenate([jnp.stack([y, core, c // 2, lengths[0, 0]]).astype(jnp.int32), table])
+    head = jnp.stack([y, core, c // 2, lengths[0, 0]]).astype(jnp.int32)
+    info = jnp.concatenate([head, table, jnp.stack([x, z % 2, z // 2]).astype(jnp.int32)])
     dealt = deal[0]
     total = rows * 16
     softplus = jax.nn.softplus(query_scale)
@@ -773,8 +927,39 @@
     factor = (jax.nn.sigmoid(query_scale) / softplus)[None, :]
     inputs = tokens[0]
     cot = cotangent[0]
-
-    arrived = ring_gather(inputs)
+    cut = rows // 2
+    mine, partner, gathered = [], [], []
+
+    def project(*group):
+        count = sum(part.shape[0] for part in group)
+        start = sum(piece.shape[1] for piece in mine)
+        args = [info, *group, own, other, scale_col]
+        got = call(
+            functools.partial(project_kernel, len(group), start),
+            [((8 * rows, width), BF), ((3 * HEAD, count), BF), ((3 * HEAD, count), BF)],
+            args + gathered[-1:],
+            smem=1,
+            anys=range(len(args), len(args) + 1),
+            out_anys=(0,),
+            aliases={len(args): 0} if gathered else None,
+            scratch=[
+                pltpu.VMEM((count, width), BF),
+                pltpu.VMEM((6 * HEAD, width), BF),
+                pltpu.VMEM((16, width), F32),
+                pltpu.VMEM((6 * HEAD, count), BF),
+                pltpu.SemaphoreType.DMA,
+            ],
+            cost=(2 * 480 * 1280 * count, 4 * 1280 * count, 0),
+        )
+        gathered.append(got[0])
+        mine.append(got[1])
+        partner.append(send(got[2], CORE_SWAP))
+        return got[1]
+
+    forth1, back1 = send(inputs, FORTH), send(inputs, BACK)
+    size = width // 4
+    first_rows = lax.dynamic_slice_in_dim(w_output, core * size, 128, 0)
+    direct, passed = [send(first_rows, Y_SWAP)], []
     own = call(
         pick_kernel,
         [((6 * HEAD + 16, width // 2), BF)],
@@ -783,141 +968,245 @@
         cost=(2 * 480 * 640 * 1280, 3 * 640 * 1280 * 2, 0),
     )[0]
     other = send(own, Y_SWAP)
-    mlp_weights = weight_parts((w_output, w_expand, w_contract), core)
-
-    attn_in, mine, partner = [], [], []
-    for group in (arrived[:1], arrived[1:3], arrived[3:5], arrived[5:7], arrived[7:]):
-        count = sum(part.shape[0] for part in group)
-        got = call(
-            functools.partial(project_kernel, len(group)),
-            [((count, width), BF), ((3 * HEAD, count), BF), ((3 * HEAD, count), BF)],
-            [info, *group, own, other, scale_col],
-            smem=1,
-            scratch=[
-                pltpu.VMEM((6 * HEAD, width), BF),
-                pltpu.VMEM((16, width), F32),
-                pltpu.VMEM((6 * HEAD, count), BF),
-            ],
-            cost=(2 * 480 * 1280 * count, 4 * 1280 * count, 0),
-        )
-        attn_in.append(got[0])
-        mine.append(got[1])
-        partner.append(send(got[2], CORE_SWAP))
-    spans = mine + partner
-
-    attended, lse = call(
+    rows_out = weight_rows(after((w_output, w_expand, w_contract), own), core)
+    rows_back = weight_rows(after((w_query, w_key, w_value), own), core)
+    chunks = [rows_out[128:256], rows_out[256:512], rows_out[512:640], rows_out[640:], rows_back[:288]]
+    chunks += [rows_back[288:448], rows_back[448:704], rows_back[704:]]
+    forth1, back1, direct[0], *chunks = after((forth1, back1, direct[0], *chunks))
+
+    forth2, back2 = send(forth1, FORTH), send(back1, BACK)
+    passed.append(send(direct[0], CORE_SWAP))
+    direct.append(send(after(chunks[:1], direct[0])[0], Y_SWAP))
+    done = project(inputs)
+    forth2, back2, direct[1], passed[0] = after((forth2, back2, direct[1], passed[0]), done)
+
+    forth3, back3 = send(forth2, FORTH), send(back2, BACK)
+    passed.append(send(direct[1], CORE_SWAP))
+    direct.append(send(after(chunks[1:2], direct[1])[0], Y_SWAP))
+    done = project(forth1, back1)
+    forth3, back3, direct[2], passed[1] = after((forth3, back3, direct[2], passed[1]), done)
+
+    forth4, back4 = send(forth3[:cut], FORTH), send(back3[cut:], BACK)
+    passed.append(send(direct[2], CORE_SWAP))
+    direct.append(send(after(chunks[2:3], direct[2])[0], Y_SWAP))
+    done2 = project(forth2, back2)
+    done3 = project(forth3, back3)
+    forth4, back4, direct[3], passed[2] = after((forth4, back4, direct[3], passed[2]), done2, done3)
+    passed.append(send(direct[3], CORE_SWAP))
+    project(forth4, back4)
+    *spans, passed[3] = after((*mine, *partner, passed[3]))
+    direct.append(send(after(chunks[3:4], spans[0])[0], Y_SWAP))
+
+    tall, flat_t = ((total, WIDE), BF), ((WIDE, total), BF)
+    attended, q_t, k_n = call(
         forward_kernel,
-        [((16, HEAD, rows), BF), ((1, total), F32)],
+        [((16, HEAD, rows), BF), flat_t, tall],
         [info, dealt, *spans],
         smem=2,
         scratch=[
-            pltpu.VMEM((HEAD, total), BF),
-            pltpu.VMEM((total, HEAD), BF),
+            pltpu.VMEM((WIDE, total), BF),
+            pltpu.VMEM((total, WIDE), BF),
             pltpu.VMEM((HEAD + 16, total), BF),
+            pltpu.VMEM((1, total), F32),
             pltpu.SMEM((total // SPAN,), jnp.int32),
         ],
         cost=(2 * total * total * 256, 3 * total * 160, total * total // 2),
     )
-    attn_in += [send(piece, CORE_SWAP) for piece in attn_in]
-    back_weights = weight_parts((w_query, w_key, w_value), core)
-
+    attended, direct[4] = after((attended, direct[4]))
+    passed.append(send(direct[4], CORE_SWAP))
+    direct_back = [send(after(chunks[4:5], direct[4])[0], Y_SWAP)]
+    attn_in = gathered[-1]
+    attn_in_partner, cot_partner = (send(value, CORE_SWAP) for value in after((attn_in, cot), attended))
     attn_t = lax.all_to_all(attended, "ctx", 0, 0).reshape(width, rows)
-    whole_scratch = [pltpu.VMEM((width, width), BF)] * 3
-    whole_scratch += [pltpu.VMEM((16, width), F32), pltpu.SemaphoreType.DMA((9,))]
+    k_t, q_n, v_n = call(
+        turn_kernel,
+        [((HEAD, total), BF), tall, tall],
+        [info, dealt, *after(spans, attended)],
+        smem=2,
+        cost=(0, 6 * total * 256, 0),
+    )
+    attn_t, passed[4], attn_in_partner, cot_partner, direct_back[0] = after(
+        (attn_t, passed[4], attn_in_partner, cot_partner, direct_back[0]), k_t
+    )
+    direct_back.append(send(after(chunks[5:6], attn_t)[0], Y_SWAP))
+    whole_scratch = [pltpu.VMEM((width, width), BF)] * 3 + [pltpu.VMEM((16, width), F32)]
     wide, low = ((rows, width), F32), ((rows, width), BF)
-    result, grad_mid, grad_attended_t, act, mlp_in, grad_expanded, grad_mid_low = call(
-        mlp_kernel,
-        [low, wide, ((width, rows), BF), low, low, low, low],
-        [info, inputs, cot, attn_t, own, other, *mlp_weights],
+    result, grad_mid, grad_attended_t, packed, rights = call(
+        functools.partial(mlp_kernel, 5),
+        [low, wide, ((width, rows), BF), ((3, rows, width), BF), low],
+        [info, inputs, cot, attn_t, own, other, w_output, w_expand, w_contract, *direct, *passed],
         smem=1,
-        anys=9,
-        scratch=whole_scratch,
+        anys=range(6, 19),
+        scratch=whole_scratch + [pltpu.VMEM((2, rows, width), BF), pltpu.SemaphoreType.DMA((24,))],
         cost=(12 * rows * width * width, 6 * width * width, 0),
     )
+    grad_attended_t, packed, direct_back[1] = after((grad_attended_t, packed, direct_back[1]))
     grad_out = lax.all_to_all(grad_attended_t.reshape(16, HEAD, rows), "ctx", 0, 0)
-
+    packed_partner = send(packed, CORE_SWAP)
+    direct_back.append(send(after(chunks[6:7], packed)[0], Y_SWAP))
+    attn_t_partner = send(attn_t, CORE_SWAP)
+
+    half_width = width // 2
     terms = call(
         outer_kernel,
-        [((width, width // 2), BF)] * 6,
-        [info, act, cot, mlp_in, grad_expanded, attn_t, grad_mid_low],
+        [((half_width, half_width), BF)] * 6,
+        [info, packed, rights, packed_partner, attn_t, attn_t_partner, cot, cot_partner],
         smem=1,
+        scratch=[
+            pltpu.VMEM((width, 2 * rows), BF),
+            pltpu.VMEM((2 * rows, half_width), BF),
+            pltpu.VMEM((width, half_width), BF),
+        ],
         cost=(6 * rows * width * width, 6 * width * width, 0),
     )
-    bits = {"y": (y, Y_SWAP), "x": (x, X_SWAP), "far": (z // 2, FAR_SWAP), "near": (z % 2, NEAR_SWAP)}
-    orders = (("y", "x", "near", "far"), ("x", "y", "near", "far"), ("near", "y", "x", "far"))
-    pieces = []
-    for at, order in enumerate(orders):
-        held = (terms[2 * at].astype(F32) + send(terms[2 * at + 1], CORE_SWAP).astype(F32)).astype(BF)
-        held = held.reshape(2, 2, 2, 2, 80, width // 2)
-        left = ["y", "x", "far", "near"]
-        for name in order:
-            held = halve(held, None, bits[name][0], bits[name][1], left.index(name))
-            left.remove(name)
-        pieces.append(held)
-    spread = chip_gather(jnp.concatenate(pieces, axis=0))
-    shard = ((width // 2, width), F32)
-    line = ((1, width // 2), F32)
-    grad_contract, grad_expand, grad_output, grad_gain_mlp = call(
-        spread_kernel,
-        [shard, shard, shard, line],
-        [info, *spread, w_expand, gain_mlp[None]],
-        smem=1,
-        scratch=[pltpu.VMEM((16, 240, width // 2), BF)],
-        cost=(0, 3 * 640 * 1280 * 4, 0),
-    )
-
+    moves = {"y": Y_SWAP, "x": X_SWAP, "near": NEAR_SWAP, "far": FAR_SWAP}
+
+    def travel(values, done):
+        return [send(value, moves[order[done]]) for value, order in zip(values, ORDERS)]
+
+    def halving(kept, came, done):
+        size = half_width >> done
+        shapes = [((size, half_width), BF)] * 6 if done < 3 else [((3 * PART, half_width), BF)] * 2
+        return call(
+            functools.partial(round_kernel, done),
+            shapes,
+            [info, *kept, *came],
+            smem=1,
+            cost=(0, 12 * size * half_width, 0),
+        )
+
+    came = travel(terms[3:], 0)
+    kept = terms[:3]
+    grad_out, direct_back[2] = after((grad_out, direct_back[2]), kept[0])
+    direct_back.append(send(after(chunks[7:], kept[0])[0], Y_SWAP))
     grads = call(
         backward_kernel,
         [((16, 3 * HEAD, rows), BF)],
-        [info, dealt, *spans, lse, attended, grad_out, scale_col],
+        [info, dealt, q_t, k_n, k_t, q_n, v_n, attended, grad_out, scale_col],
         smem=2,
-        scratch=[pltpu.VMEM((total, HEAD), BF)] * 4
-        + [pltpu.VMEM((HEAD, total), BF)] * 3
-        + [
+        scratch=[
+            pltpu.VMEM((WIDE, total), BF),
+            pltpu.VMEM((total, WIDE), BF),
             pltpu.VMEM((1, total), F32),
             pltpu.VMEM((HEAD, total), F32),
-            pltpu.VMEM((BLOCK, HEAD), F32),
-            pltpu.VMEM((BLOCK, HEAD), F32),
+            pltpu.VMEM((BLOCK, WIDE), F32),
+            pltpu.VMEM((BLOCK, WIDE), F32),
             pltpu.SMEM((total // SPAN,), jnp.int32),
         ],
         cost=(5 * total * total * 256, 6 * total * 160, total * total // 2),
     )[0]
-
+    grads, direct_back[3], *came = after((grads, direct_back[3], *came))
+    returned = lax.all_to_all(grads, "ctx", 0, 0)
     keep, away = call(
         weight_kernel,
-        [((256, width // 2), F32), ((256, width // 2), BF)],
-        [info, grads, own, other, *attn_in],
+        [((256, half_width), F32), ((256, half_width), BF)],
+        [info, grads, own, other, attn_in, attn_in_partner],
         smem=1,
+        anys=(4, 5),
         scratch=[
             pltpu.VMEM((3 * HEAD, total), BF),
             pltpu.VMEM((HEAD, width), F32),
             pltpu.VMEM((3 * HEAD, width), F32),
+            pltpu.VMEM((total, width), BF),
+            pltpu.SemaphoreType.DMA((8,)),
         ],
         cost=(2 * 240 * total * width, 2 * total * width, 0),
     )
-    summed = (keep + send(away, Y_SWAP).astype(F32)).astype(BF)
-    returned = lax.all_to_all(grads, "ctx", 0, 0)
+    from_pair = send(away, Y_SWAP)
+    terms = halving(kept, after(came, keep), 1)
+    kept, came = terms[:3], travel(terms[3:], 1)
+    keep = after((keep,), kept[0])[0]
+    summed = (keep + from_pair.astype(F32)).astype(BF)
+    passed_back = [send(value, CORE_SWAP) for value in after(direct_back, summed)]
+
+    shard = ((half_width, width), F32)
+    line = ((half_width,), F32)
+
+    def stacked(values):
+        stack = call(stack_kernel, [((len(values), *values[0].shape), BF)], values)[0]
+        return stack, send(stack, CORE_SWAP)
+
+    forth1, back1 = send(summed, FORTH), send(summed, BACK)
+    forth2, back2 = send(forth1, FORTH), send(back1, BACK)
+    terms = halving(kept, after(came, forth1), 2)
+    kept, came = terms[:3], travel(terms[3:], 2)
+    forth2, back2 = after((forth2, back2), kept[0], returned, *passed_back)
+    forth3, back3 = send(forth2, FORTH), send(back2, BACK)
+    near, near_partner = stacked([summed, forth1, back1, forth2, back2])
+    terms = halving(kept, came, 3)
+    far = send(terms[1], FAR_SWAP)
+    forth3, back3, near_partner = after((forth3, back3, near_partner), terms[0])
+    last = [send(forth3[:128], FORTH), send(back3[128:], BACK)]
+    beyond = [send(value, CORE_SWAP) for value in (forth3, back3)]
+    piece = (terms[0].astype(F32) + far.astype(F32)).astype(BF)
+    *last, piece = after((*last, piece), *beyond)
+    query_pieces = [near, near_partner, forth3, back3, *last, *beyond, *(send(value, CORE_SWAP) for value in last)]
+
+    forth1, back1 = send(piece, FORTH), send(piece, BACK)
+    grad_query, grad_key, grad_value, grad_gain_attn, grad_scale = call(
+        finish_kernel,
+        [shard] * 3 + [line, ((1, HEAD), F32)],
+        [info, *query_pieces, w_query, w_key, w_value, gain_attn[None], factor],
+        smem=1,
+        anys=range(11, 14),
+        out_anys=range(3),
+        scratch=[
+            pltpu.VMEM((3, width, half_width), BF),
+            pltpu.VMEM((3, half_width, width), BF),
+            pltpu.VMEM((2, 256, half_width), BF),
+            pltpu.VMEM((3, half_width, width), F32),
+            pltpu.SemaphoreType.DMA((6,)),
+        ],
+        cost=(6 * 640 * 640 * 1280, 3 * 640 * 1280 * 4, 0),
+    )
+    forth1, back1 = after((forth1, back1), grad_query)
+    forth2, back2 = send(forth1, FORTH), send(back1, BACK)
     grad_inputs = call(
-        input_kernel,
+        functools.partial(input_kernel, 4),
         [low],
-        [info, inputs, returned, grad_mid, own, other, *back_weights],
+        [info, inputs, returned, grad_mid, own, other, w_query, w_key, w_value, *direct_back, *passed_back],
         smem=1,
-        anys=9,
-        scratch=whole_scratch,
+        anys=range(6, 17),
+        scratch=whole_scratch + [pltpu.SemaphoreType.DMA((24,))],
         cost=(6 * rows * width * width, 6 * width * width, 0),
     )[0]
-    spread = chip_gather(summed)
-    grad_query, grad_key, grad_value, grad_gain_attn, grad_scale = call(
-        finish_kernel,
-        [shard, shard, shard, line, ((1, HEAD), F32)],
-        [info, *spread, w_query, w_key, w_value, gain_attn[None], factor],
+    forth2, back2 = after((forth2, back2), grad_inputs)
+    forth3, back3 = send(forth2, FORTH), send(back2, BACK)
+    near, near_partner = stacked([piece, forth1, back1, forth2, back2])
+    forth3, back3, near_partner = after((forth3, back3, near_partner))
+    last = [send(forth3[:112], FORTH), send(back3[112:], BACK)]
+    beyond = [send(value, CORE_SWAP) for value in (forth3, back3)]
+    partial_out = call(
+        spread_kernel,
+        [((half_width, 128), F32), shard, shard, shard],
+        [info, near, near_partner, w_expand],
         smem=1,
-        scratch=[pltpu.VMEM((16, 256, width // 2), BF)] + [pltpu.VMEM((width, width // 2), BF)] * 3,
-        cost=(6 * 640 * 640 * 1280, 3 * 640 * 1280 * 4, 0),
+        out_anys=(1, 2, 3),
+        scratch=[pltpu.VMEM((30, PART, half_width), F32), pltpu.SemaphoreType.DMA((30,))],
+        cost=(0, 3 * 640 * 1280 * 4, 0),
+    )
+    last = after(last, partial_out[0], *beyond)
+    args = [info, forth3, back3, *last, *beyond, *(send(value, CORE_SWAP) for value in last)]
+    args += [partial_out[0], gain_mlp[None], w_expand, *partial_out[1:]]
+    grad_contract, grad_expand, grad_output, grad_gain_mlp = call(
+        spread_last_kernel,
+        [shard] * 3 + [line],
+        args,
+        smem=1,
+        anys=range(len(args) - 3, len(args)),
+        out_anys=range(3),
+        aliases={len(args) - 3 + at: at for at in range(3)},
+        scratch=[
+            pltpu.VMEM((18, PART, half_width), F32),
+            pltpu.VMEM((2, *piece.shape), BF),
+            pltpu.VMEM((half_width, 128), F32),
+            pltpu.SemaphoreType.DMA((18,)),
+        ],
+        cost=(0, 3 * 640 * 1280 * 4, 0),
     )
     return (
-        result[None], grad_inputs[None], grad_gain_attn[0], grad_query, grad_key, grad_value, grad_output,
-        grad_scale[0], grad_gain_mlp[0], grad_expand, grad_contract,
+        result[None], grad_inputs[None], grad_gain_attn, grad_query, grad_key, grad_value, grad_output,
+        grad_scale[0], grad_gain_mlp, grad_expand, grad_contract,
     )
 
 

time: 455 us -> 371 us (0.82)
  waiting for transfers between devices: 199 us -> 99.8 us
  Pallas kernels: 142 us -> 159 us
  other arithmetic: 8.52 us -> 2.57 us
    ppermute x81 -> x73, waiting for transfers between devices: 194 us -> 99.7 us  [send(): return lax.ppermute(value, AXES, moves)]
    pallas_call x14 -> x21, Pallas kernels: 142 us -> 159 us  [call(): pl.pallas_call(body, out_shape=[jax.ShapeDtypeStruct(shape, kind) for sha...]
    ppermute x81 -> x73, starting transfers between devices: 59.1 us -> 65.7 us  [send(): return lax.ppermute(value, AXES, moves)]
    all_to_all x1, waiting for transfers between devices: 5.29 us -> 0.01 us  [ring_device(): lax.all_to_all(grad_attended_t.reshape(16, HEAD, rows), 'ctx', 0, 0)]
    unnamed x126 -> x164, local copies, waits for them, and re-layouts: 6.57 us -> 11.7 us
  transfers between devices with their start and end apart: 84 -> 76, of which waited for: 30 -> 30; matrix products, arithmetic and copies ran while one was open for 4% -> 3% of each run, Pallas kernels for 29% -> 40%
where the time goes in v2:
time: 371 us; the launch traced here: 366 us
  Pallas kernels  159 us (43%)
  waiting for transfers between devices  99.8 us (27%)
  starting transfers between devices  80.5 us (22%)
  local copies, waits for them, and re-layouts  21.8 us (6%)
    pallas_call x21, Pallas kernels, call(): pl.pallas_call(body, out_shape=[jax.ShapeDtypeStruct(shape, kind) for sha...  159 us
    ppermute x73, waiting for transfers between devices, send(): return lax.ppermute(value, AXES, moves)  99.7 us
    ppermute x73, starting transfers between devices, send(): return lax.ppermute(value, AXES, moves)  65.7 us
    unnamed x164, local copies, waits for them, and re-layouts  11.7 us
  transfers between devices with their start and end apart: 76, of which 30 were waited for; matrix products, arithmetic and copies ran while one was open for 3% of the time, Pallas kernels for 40%

profile of v2, /device:TPU:0, one launch (start us, length us, event | category | flops | bytes accessed | tf_op | source)
XLA Modules:
  0.0 366.0 jit_solution(15721898321158663062)
XLA Ops:
  0.6 3.0 collective-permute-start.2
  4.8 2.0 collective-permute-start.3
  11.3 5.1 %shard_map.221.refs_1_.refs_2_.own = bf16[496,640]{1,0:T(8,128)(2,1)} custom-call(s32[23]{0:T(128)} %concatenate.13.info, bf16[640,1280]{1,0:T(8,128)(2,1)} %refs_8_.1, bf16[640,1280]{1,0:T(8,128)(2,1)} %refs_9_.1, bf16[640,1280]{1,0:T(8,128)(2,1)} %refs_10_.2, bf16[1,640]{1,0:T(2,128)(2,1)} %broadcast_in_dim.20.gain_a.refs_11_, ...), custom_call_target="tpu_custom_call" | custom-call | flops 786432000 | bytes 4915200 | tf_op jit(solution)/shard_map/pallas_call | solution.py:375
  23.8 2.0 collective-permute-start.4
  25.9 1.9 collective-permute-start.6
  29.1 4.7 %collective-permute-done.refs_2_.refs_3_.other = bf16[496,640]{1,0:T(8,128)(2,1)S(1)} collective-permute-done((bf16[496,640]{1,0:T(8,128)(2,1)}, bf16[496,640]{1,0:T(8,128)(2,1)S(1)}, u32[]{:S(2)}, u32[]{:S(2)}) %collective-permute-start) | collective-permute-done | bytes 634912 | tf_op jit(solution)/shard_map/ppermute | solution.py:361
  34.6 3.5 shard_map.222
  44.8 4.3 %shard_map.223 = (bf16[2048,1280]{1,0:T(8,128)(2,1)}, bf16[240,512]{1,0:T(8,128)(2,1)}, bf16[240,512]{1,0:T(8,128)(2,1)}) custom-call(s32[23]{0:T(128)} %concatenate.13.info, bf16[256,1280]{1,0:T(8,128)(2,1)} %collective-permute-done.1.refs_0_, bf16[256,1280]{1,0:T(8,128)(2,1)} %collective-permute-done.2.refs_1_, ...), custom_call_target="tpu_custom_call", output_to_operand_aliasing={{0}: (6, {})} | custom-call | flops 629145600 | bytes 2621440 | tf_op jit(solution)/shard_map/pallas_call | solution.py:375
  49.1 6.3 %collective-permute-done.10.refs_5_ = bf16[256,1280]{1,0:T(8,128)(2,1)S(1)} collective-permute-done((bf16[256,1280]{1,0:T(8,128)(2,1)S(1)}, bf16[256,1280]{1,0:T(8,128)(2,1)S(1)}, u32[]{:S(2)}, u32[]{:S(2)}) %collective-permute-start.10) | collective-permute-done | bytes 655392 | tf_op jit(solution)/shard_map/ppermute | solution.py:361
  58.7 1.8 collective-permute-start.12
  61.0 4.2 %shard_map.224 = (bf16[2048,1280]{1,0:T(8,128)(2,1)}, bf16[240,512]{1,0:T(8,128)(2,1)}, bf16[240,512]{1,0:T(8,128)(2,1)}) custom-call(s32[23]{0:T(128)} %concatenate.13.info, bf16[256,1280]{1,0:T(8,128)(2,1)} %collective-permute-done.4.refs_0_, bf16[256,1280]{1,0:T(8,128)(2,1)} %collective-permute-done.5.refs_1_, ...), custom_call_target="tpu_custom_call", output_to_operand_aliasing={{0}: (6, {})} | custom-call | flops 629145600 | bytes 2621440 | tf_op jit(solution)/shard_map/pallas_call | solution.py:375
  65.3 4.3 %shard_map.225 = (bf16[2048,1280]{1,0:T(8,128)(2,1)}, bf16[240,512]{1,0:T(8,128)(2,1)}, bf16[240,512]{1,0:T(8,128)(2,1)}) custom-call(s32[23]{0:T(128)} %concatenate.13.info, bf16[256,1280]{1,0:T(8,128)(2,1)} %copy-done.7, bf16[256,1280]{1,0:T(8,128)(2,1)} %copy-done.8, ...), custom_call_target="tpu_custom_call", output_to_operand_aliasing={{0}: (6, {})} | custom-call | flops 629145600 | bytes 2621440 | tf_op jit(solution)/shard_map/pallas_call | solution.py:375
  71.3 3.4 shard_map.226
  77.7 17.5 %shard_map.227 = (bf16[16,80,256]{2,1,0:T(8,128)(2,1)}, bf16[128,4096]{1,0:T(8,128)(2,1)}, bf16[4096,128]{1,0:T(8,128)(2,1)}) custom-call(s32[23]{0:T(128)} %concatenate.13.info, s32[32]{0:T(128)} %bitcast.32, bf16[240,256]{1,0:T(8,128)(2,1)} %get-tuple-element.235.refs_0_, bf16[240,512]{1,0:T(8,128)(2,1)} %get-tuple-element.236.refs_1_, ...), custom_call_target="tpu_custom_call" | custom-call | flops 8589934592 | bytes 1966080 | tf_op jit(solution)/shard_map/pallas_call | solution.py:375
  97.9 4.5 %all-to-all-start = ((bf16[16,80,256]{2,1,0:T(8,128)(2,1)}), bf16[16,80,256]{2,1,0:T(8,128)(2,1)S(1)}, u32[]{:S(2)}, u32[]{:S(2)}) async-start(bf16[16,80,256]{2,1,0:T(8,128)(2,1)} %get-tuple-element.228.refs_5_), calls=%async_computation | async-start | bytes 1310720 | tf_op jit(solution)/shard_map/all_to_all | solution.py:1020
  104.1 4.0 %shard_map.228 = (bf16[80,4096]{1,0:T(8,128)(2,1)}, bf16[4096,128]{1,0:T(8,128)(2,1)}, bf16[4096,128]{1,0:T(8,128)(2,1)}) custom-call(s32[23]{0:T(128)} %concatenate.13.info, s32[32]{0:T(128)} %bitcast.33, bf16[240,256]{1,0:T(8,128)(2,1)} %get-tuple-element.235.refs_0_, bf16[240,512]{1,0:T(8,128)(2,1)} %get-tuple-element.236.refs_1_, ...), custom_call_target="tpu_custom_call" | custom-call | bytes 6291456 | tf_op jit(solution)/shard_map/pallas_call | solution.py:375
  108.8 12.7 %collective-permute-done.26.refs_3_ = bf16[288,1280]{1,0:T(8,128)(2,1)S(1)} collective-permute-done((bf16[288,1280]{1,0:T(8,128)(2,1)S(1)}, bf16[288,1280]{1,0:T(8,128)(2,1)S(1)}, u32[]{:S(2)}, u32[]{:S(2)}) %collective-permute-start.26) | collective-permute-done | bytes 737312 | tf_op jit(solution)/shard_map/ppermute | solution.py:361
  122.7 12.0 %shard_map.229 = (bf16[256,1280]{1,0:T(8,128)(2,1)}, f32[256,1280]{1,0:T(8,128)}, bf16[1280,256]{1,0:T(8,128)(2,1)}, bf16[3,256,1280]{2,1,0:T(8,128)(2,1)}, bf16[256,1280]{1,0:T(8,128)(2,1)}) custom-call(s32[23]{0:T(128)} %concatenate.13.info, bf16[256,1280]{1,0:T(8,128)(2,1)} %bitcast.25, bf16[256,1280]{1,0:T(8,128)(2,1)} %bitcast.36, ...), custom_call_target="tpu_custom_call" | custom-call | flops 5033164800 | bytes 9830400 | tf_op jit(solution)/shard_map/pallas_call | solution.py:375
  134.9 6.3 %all-to-all-start.1 = ((bf16[16,80,256]{2,1,0:T(8,128)(2,1)}), bf16[16,80,256]{2,1,0:T(8,128)(2,1)S(1)}, u32[]{:S(2)}, u32[]{:S(2)}) async-start(bf16[16,80,256]{2,1,0:T(8,128)(2,1)} %bitcast.31), calls=%async_computation.1 | async-start | bytes 1310720 | tf_op jit(solution)/shard_map/all_to_all | solution.py:1044
  144.5 8.2 %shard_map.230 = (bf16[640,640]{1,0:T(8,128)(2,1)}, bf16[640,640]{1,0:T(8,128)(2,1)}, bf16[640,640]{1,0:T(8,128)(2,1)}, bf16[640,640]{1,0:T(8,128)(2,1)}, bf16[6...) custom-call(s32[23]{0:T(128)} %concatenate.13.info, bf16[3,256,1280]{2,1,0:T(8,128)(2,1)} %get-tuple-element.263.own, ...), custom_call_target="tpu_custom_call" | custom-call | flops 2516582400 | bytes 9830400 | tf_op jit(solution)/shard_map/pallas_call | solution.py:375
  152.7 5.9 %collective-permute-done.28.refs_5_ = bf16[256,1280]{1,0:T(8,128)(2,1)} collective-permute-done((bf16[256,1280]{1,0:T(8,128)(2,1)S(1)}, bf16[256,1280]{1,0:T(8,128)(2,1)}, u32[]{:S(2)}, u32[]{:S(2)}) %collective-permute-start.28) | collective-permute-done | bytes 655392 | tf_op jit(solution)/shard_map/ppermute | solution.py:361
  160.7 1.9 collective-permute-start.33
  164.1 34.8 %shard_map.231.grads = bf16[16,240,256]{2,1,0:T(8,128)(2,1)} custom-call(s32[23]{0:T(128)} %concatenate.13.info, s32[32]{0:T(128)} %bitcast.34, bf16[128,4096]{1,0:T(8,128)(2,1)} %get-tuple-element.253.refs_0_, bf16[4096,128]{1,0:T(8,128)(2,1)} %get-tuple-element.254.refs_1_, bf16[80,4096]{1,0:T(8,128)(2,1)} %get-tuple-element.245.refs_2_, ...), custom_call_target="tpu_custom_call" | custom-call | flops 21474836480 | bytes 3932160 | tf_op jit(solution)/shard_map/pallas_call | solution.py:375
  200.7 4.0 %all-to-all-start.2 = ((bf16[16,240,256]{2,1,0:T(8,128)(2,1)}), bf16[16,240,256]{2,1,0:T(8,128)(2,1)S(1)}, u32[]{:S(2)}, u32[]{:S(2)}) async-start(bf16[16,240,256]{2,1,0:T(8,128)(2,1)} %shard_map.231.grads), calls=%async_computation.2 | async-start | bytes 3932160 | tf_op jit(solution)/shard_map/all_to_all | solution.py:1099
  204.7 8.4 %shard_map.232 = (f32[256,640]{1,0:T(8,128)}, bf16[256,640]{1,0:T(8,128)(2,1)}) custom-call(s32[23]{0:T(128)} %concatenate.13.info, bf16[16,240,256]{2,1,0:T(8,128)(2,1)} %shard_map.231.grads, bf16[496,640]{1,0:T(8,128)(2,1)} %shard_map.221.refs_1_.refs_2_.own, bf16[496,640]{1,0:T(8,128)(2,1)} %copy-done, bf16[2048,1280]{1,0:T(8,128)(2,1)} %get-tuple-element.231.refs_0_, ...), custom_call_target="tpu_custom_call" | custom-call | flops 2516582400 | bytes 10485760 | tf_op jit(solution)/shard_map/pallas_call | solution.py:375
  214.0 4.4 %shard_map.233 = (bf16[320,640]{1,0:T(8,128)(2,1)}, bf16[320,640]{1,0:T(8,128)(2,1)}, bf16[320,640]{1,0:T(8,128)(2,1)}, bf16[320,640]{1,0:T(8,128)(2,1)}, bf16[3...) custom-call(s32[23]{0:T(128)} %concatenate.13.info, bf16[640,640]{1,0:T(8,128)(2,1)} %get-tuple-element.267.refs_0_, ...), custom_call_target="tpu_custom_call" | custom-call | bytes 2457600 | tf_op jit(solution)/shard_map/pallas_call | solution.py:375
  218.5 2.0 collective-permute-start.44
  223.5 2.1 collective-permute-start.41
  225.6 12.3 %collective-permute-done.44.refs_3_ = bf16[320,640]{1,0:T(8,128)(2,1)S(1)} collective-permute-done((bf16[320,640]{1,0:T(8,128)(2,1)}, bf16[320,640]{1,0:T(8,128)(2,1)S(1)}, u32[]{:S(2)}, u32[]{:S(2)}) %collective-permute-start.44) | collective-permute-done | bytes 409632 | tf_op jit(solution)/shard_map/ppermute | solution.py:361
  237.9 10.8 %collective-permute-done.45.refs_4_ = bf16[320,640]{1,0:T(8,128)(2,1)S(1)} collective-permute-done((bf16[320,640]{1,0:T(8,128)(2,1)}, bf16[320,640]{1,0:T(8,128)(2,1)S(1)}, u32[]{:S(2)}, u32[]{:S(2)}) %collective-permute-start.45) | collective-permute-done | bytes 409632 | tf_op jit(solution)/shard_map/ppermute | solution.py:361
  248.9 6.4 %collective-permute-done.41.refs_2_ = bf16[256,640]{1,0:T(8,128)(2,1)S(1)} collective-permute-done((bf16[256,640]{1,0:T(8,128)(2,1)S(1)}, bf16[256,640]{1,0:T(8,128)(2,1)S(1)}, u32[]{:S(2)}, u32[]{:S(2)}) %collective-permute-start.41) | collective-permute-done | bytes 327712 | tf_op jit(solution)/shard_map/ppermute | solution.py:361
  255.2 2.2 collective-permute-done.40.refs_1_
  259.5 2.8 shard_map.235
  262.3 4.6 %collective-permute-done.43.refs_4_ = bf16[256,640]{1,0:T(8,128)(2,1)S(1)} collective-permute-done((bf16[256,640]{1,0:T(8,128)(2,1)S(1)}, bf16[256,640]{1,0:T(8,128)(2,1)S(1)}, u32[]{:S(2)}, u32[]{:S(2)}) %collective-permute-start.43) | collective-permute-done | bytes 327712 | tf_op jit(solution)/shard_map/ppermute | solution.py:361
  268.9 3.4 shard_map.236.near
  277.0 2.9 collective-permute-done.50.refs_3_
  279.9 2.0 collective-permute-start.48
  283.8 2.3 shard_map.237
  286.6 2.4 collective-permute-done.47.refs_0_
  291.9 8.1 %collective-permute-start.53 = (bf16[128,640]{1,0:T(8,128)(2,1)S(1)}, bf16[128,640]{1,0:T(8,128)(2,1)S(1)}, u32[]{:S(2)}, u32[]{:S(2)}) collective-permute-start(bf16[128,640]{1,0:T(8,128)(2,1)S(1)} %slice.50), channel_id=1, source_target_pairs={{0,8},{1,9},{2,10},{3,11},{4,0},{5,1},{6,2},{7,3},{8,16},{9,17},{1... | collective-permute-start | bytes 491528 | tf_op jit(solution)/shard_map/ppermute | solution.py:361
  300.0 4.8 %collective-permute-done.55 = bf16[240,640]{1,0:T(8,128)(2,1)S(1)} collective-permute-done((bf16[240,640]{1,0:T(8,128)(2,1)}, bf16[240,640]{1,0:T(8,128)(2,1)S(1)}, u32[]{:S(2)}, u32[]{:S(2)}) %collective-permute-start.55) | collective-permute-done | bytes 307232 | tf_op jit(solution)/shard_map/ppermute | solution.py:361
  307.6 2.3 collective-permute-start.60
  310.6 11.5 %shard_map.238 = (f32[640,1280]{1,0:T(8,128)}, f32[640,1280]{1,0:T(8,128)}, f32[640,1280]{1,0:T(8,128)}, f32[640]{0:T(1024)}, f32[1,80]{1,0:T(1,128)}) custom-call(s32[23]{0:T(128)} %concatenate.13.info, bf16[5,256,640]{2,1,0:T(8,128)(2,1)} %shard_map.236.near, bf16[5,256,640]{2,1,0:T(8,128)(2,1)} %copy-done.59, bf16[256,640]{1,0:T(8,128)(2,1)} %copy-done.57, ...), custom_call_target="tpu_custom_call" | custom-call | flops 3145728000 | bytes 9830400 | tf_op jit(solution)/shard_map/pallas_call | solution.py:375
  324.2 11.3 %shard_map.234 = bf16[256,1280]{1,0:T(8,128)(2,1)} custom-call(s32[23]{0:T(128)} %concatenate.13.info, bf16[256,1280]{1,0:T(8,128)(2,1)} %bitcast.26, bf16[16,240,256]{2,1,0:T(8,128)(2,1)} %copy-done.5, f32[256,1280]{1,0:T(8,128)} %get-tuple-element.275.grad_mid, bf16[496,640]{1,0:T(8,128)(2,1)} %shard_map.221.refs_1_.refs_2_.own, bf16[496,640]{1,0:T(8,128)(2,1)} %copy-done, ...), custom_call_target="tpu_custom_call" | custom-call | flops 2516582400 | bytes 9830400 | tf_op jit(solution)/shard_map/pallas_call | solution.py:375
  336.9 2.6 shard_map.239.near
  341.6 7.9 %collective-permute-done.64.refs_0_ = bf16[240,640]{1,0:T(8,128)(2,1)S(1)} collective-permute-done((bf16[240,640]{1,0:T(8,128)(2,1)}, bf16[240,640]{1,0:T(8,128)(2,1)S(1)}, u32[]{:S(2)}, u32[]{:S(2)}) %collective-permute-start.64) | collective-permute-done | bytes 307232 | tf_op jit(solution)/shard_map/ppermute | solution.py:361
  352.5 6.0 %shard_map.240 = (f32[640,128]{1,0:T(8,128)}, f32[640,1280]{1,0:T(8,128)}, f32[640,1280]{1,0:T(8,128)}, f32[640,1280]{1,0:T(8,128)}) custom-call(s32[23]{0:T(128)} %concatenate.13.info, bf16[5,240,640]{2,1,0:T(8,128)(2,1)} %shard_map.239.near, bf16[5,240,640]{2,1,0:T(8,128)(2,1)} %copy-done.6, bf16[640,1280]{1,0:T(8,128)(2,1)} %refs_10_.3), custom_call_target="tpu_custom_call" | custom-call | bytes 9830400 | tf_op jit(solution)/shard_map/pallas_call | solution.py:375
  360.9 4.8 %shard_map.241 = (f32[640,1280]{1,0:T(8,128)}, f32[640,1280]{1,0:T(8,128)}, f32[640,1280]{1,0:T(8,128)}, f32[640]{0:T(1024)}) custom-call(s32[23]{0:T(128)} %concatenate.13.info, bf16[240,640]{1,0:T(8,128)(2,1)} %copy-done.16, bf16[240,640]{1,0:T(8,128)(2,1)} %copy-done.15, ...), custom_call_target="tpu_custom_call", output_to_operand_aliasing={{0}: (12, {}), {1}: (13, {}), {2}: (14, {})} | custom-call | bytes 9830400 | tf_op jit(solution)/shard_map/pallas_call | solution.py:375
  (314 shorter events, 77.0 us)
Async XLA Ops:
  0.6 23.2 %collective-permute-start.2 = (bf16[256,1280]{1,0:T(8,128)(2,1)}, bf16[256,1280]{1,0:T(8,128)(2,1)}, u32[]{:S(2)}, u32[]{:S(2)}) collective-permute-start(bf16[256,1280]{1,0:T(8,128)(2,1)} %bitcast.22), channel_id=1, source_target_pairs={{0,4},{1,5},{2,6},{3,7},{4,12},{5,13},{6,14},{7,15},{8,0},{9,1},{1... | collective-permute-start | bytes 1966088 | tf_op jit(solution)/shard_map/ppermute | solution.py:361
  3.6 20.2 %collective-permute-start.1 = (bf16[256,1280]{1,0:T(8,128)(2,1)}, bf16[256,1280]{1,0:T(8,128)(2,1)}, u32[]{:S(2)}, u32[]{:S(2)}) collective-permute-start(bf16[256,1280]{1,0:T(8,128)(2,1)} %bitcast.23), channel_id=1, source_target_pairs={{0,8},{1,9},{2,10},{3,11},{4,0},{5,1},{6,2},{7,3},{8,16},{9,17},{1... | collective-permute-start | bytes 1966088 | tf_op jit(solution)/shard_map/ppermute | solution.py:361
  4.8 19.0 %collective-permute-start.3 = (bf16[128,1280]{1,0:T(8,128)(2,1)S(1)}, bf16[128,1280]{1,0:T(8,128)(2,1)}, u32[]{:S(2)}, u32[]{:S(2)}) collective-permute-start(bf16[128,1280]{1,0:T(8,128)(2,1)S(1)} %constant_dynamic-slice_fusion.10), channel_id=1, source_target_pairs={{0,1},{1,0},{2,3},{3,2},{4,5},{5,4},{6,7},{7,6},{8,9},{9,8},{10,11... | collective-permute-start | bytes 983048 | tf_op jit(solution)/shard_map/ppermute | solution.py:361
  16.4 17.4 %collective-permute-start = (bf16[496,640]{1,0:T(8,128)(2,1)}, bf16[496,640]{1,0:T(8,128)(2,1)S(1)}, u32[]{:S(2)}, u32[]{:S(2)}) collective-permute-start(bf16[496,640]{1,0:T(8,128)(2,1)} %shard_map.221.refs_1_.refs_2_.own), channel_id=1, source_target_pairs={{0,1},{1,0},{2,3},{3,2},{4,5},{5,4},{6,7},{7,6},{8,9},{9,8},{10,11... | collective-permute-start | bytes 1904648 | tf_op jit(solution)/shard_map/ppermute | solution.py:361
  23.8 16.0 %collective-permute-start.4 = (bf16[256,1280]{1,0:T(8,128)(2,1)}, bf16[256,1280]{1,0:T(8,128)(2,1)}, u32[]{:S(2)}, u32[]{:S(2)}) collective-permute-start(bf16[256,1280]{1,0:T(8,128)(2,1)} %collective-permute-done.1.refs_0_), channel_id=1, source_target_pairs={{0,8},{1,9},{2,10},{3,11},{4,0},{5,1},{6,2},{7,3},{8,16},{9,17},{1... | collective-permute-start | bytes 1966088 | tf_op jit(solution)/shard_map/ppermute | solution.py:361
  25.8 15.4 %collective-permute-start.5 = (bf16[256,1280]{1,0:T(8,128)(2,1)}, bf16[256,1280]{1,0:T(8,128)(2,1)}, u32[]{:S(2)}, u32[]{:S(2)}) collective-permute-start(bf16[256,1280]{1,0:T(8,128)(2,1)} %collective-permute-done.2.refs_1_), channel_id=1, source_target_pairs={{0,4},{1,5},{2,6},{3,7},{4,12},{5,13},{6,14},{7,15},{8,0},{9,1},{1... | collective-permute-start | bytes 1966088 | tf_op jit(solution)/shard_map/ppermute | solution.py:361
  25.9 13.0 %collective-permute-start.7 = (bf16[128,1280]{1,0:T(8,128)(2,1)}, bf16[128,1280]{1,0:T(8,128)(2,1)S(1)}, u32[]{:S(2)}, u32[]{:S(2)}) collective-permute-start(bf16[128,1280]{1,0:T(8,128)(2,1)} %collective-permute-done.3.refs_3_), channel_id=1, source_target_pairs={{0,2},{1,3},{2,0},{3,1},{4,6},{5,7},{6,4},{7,5},{8,10},{9,11},{10,... | collective-permute-start | bytes 983048 | tf_op jit(solution)/shard_map/ppermute | solution.py:361
  25.9 13.0 %collective-permute-start.6 = (bf16[128,1280]{1,0:T(8,128)(2,1)}, bf16[128,1280]{1,0:T(8,128)(2,1)}, u32[]{:S(2)}, u32[]{:S(2)}) collective-permute-start(bf16[128,1280]{1,0:T(8,128)(2,1)} %get-tuple-element.190), channel_id=1, source_target_pairs={{0,1},{1,0},{2,3},{3,2},{4,5},{5,4},{6,7},{7,6},{8,9},{9,8},{10,11... | collective-permute-start | bytes 983048 | tf_op jit(solution)/shard_map/ppermute | solution.py:361
  41.2 14.1 %collective-permute-start.10 = (bf16[256,1280]{1,0:T(8,128)(2,1)S(1)}, bf16[256,1280]{1,0:T(8,128)(2,1)S(1)}, u32[]{:S(2)}, u32[]{:S(2)}) collective-permute-start(bf16[256,1280]{1,0:T(8,128)(2,1)S(1)} %pad_maximum_fusion.1), channel_id=1, source_target_pairs={{0,1},{1,0},{2,3},{3,2},{4,5},{5,4},{6,7},{7,6},{8,9},{9,8},{10,11... | collective-permute-start | bytes 1966088 | tf_op jit(solution)/shard_map/ppermute | solution.py:361
  42.7 14.1 %collective-permute-start.8 = (bf16[256,1280]{1,0:T(8,128)(2,1)}, bf16[256,1280]{1,0:T(8,128)(2,1)S(1)}, u32[]{:S(2)}, u32[]{:S(2)}) collective-permute-start(bf16[256,1280]{1,0:T(8,128)(2,1)} %collective-permute-done.4.refs_0_), channel_id=1, source_target_pairs={{0,8},{1,9},{2,10},{3,11},{4,0},{5,1},{6,2},{7,3},{8,16},{9,17},{1... | collective-permute-start | bytes 1966088 | tf_op jit(solution)/shard_map/ppermute | solution.py:361
  44.3 13.8 %collective-permute-start.9 = (bf16[256,1280]{1,0:T(8,128)(2,1)}, bf16[256,1280]{1,0:T(8,128)(2,1)S(1)}, u32[]{:S(2)}, u32[]{:S(2)}) collective-permute-start(bf16[256,1280]{1,0:T(8,128)(2,1)} %collective-permute-done.5.refs_1_), channel_id=1, source_target_pairs={{0,4},{1,5},{2,6},{3,7},{4,12},{5,13},{6,14},{7,15},{8,0},{9,1},{1... | collective-permute-start | bytes 1966088 | tf_op jit(solution)/shard_map/ppermute | solution.py:361
  58.1 12.0 %collective-permute-start.15 = (bf16[256,1280]{1,0:T(8,128)(2,1)S(1)}, bf16[256,1280]{1,0:T(8,128)(2,1)S(1)}, u32[]{:S(2)}, u32[]{:S(2)}) collective-permute-start(bf16[256,1280]{1,0:T(8,128)(2,1)S(1)} %collective-permute-done.10.refs_5_), channel_id=1, source_target_pairs={{0,2},{1,3},{2,0},{3,1},{4,6},{5,7},{6,4},{7,5},{8,10},{9,11},{10,... | collective-permute-start | bytes 1966088 | tf_op jit(solution)/shard_map/ppermute | solution.py:361
  58.2 11.4 %collective-permute-start.13 = (bf16[128,1280]{1,0:T(8,128)(2,1)S(1)}, bf16[128,1280]{1,0:T(8,128)(2,1)S(1)}, u32[]{:S(2)}, u32[]{:S(2)}) collective-permute-start(bf16[128,1280]{1,0:T(8,128)(2,1)S(1)} %slice.49), channel_id=1, source_target_pairs={{0,4},{1,5},{2,6},{3,7},{4,12},{5,13},{6,14},{7,15},{8,0},{9,1},{1... | collective-permute-start | bytes 983048 | tf_op jit(solution)/shard_map/ppermute | solution.py:361
  58.7 10.9 %collective-permute-start.12 = (bf16[128,1280]{1,0:T(8,128)(2,1)S(1)}, bf16[128,1280]{1,0:T(8,128)(2,1)S(1)}, u32[]{:S(2)}, u32[]{:S(2)}) collective-permute-start(bf16[128,1280]{1,0:T(8,128)(2,1)S(1)} %slice.48), channel_id=1, source_target_pairs={{0,8},{1,9},{2,10},{3,11},{4,0},{5,1},{6,2},{7,3},{8,16},{9,17},{1... | collective-permute-start | bytes 983048 | tf_op jit(solution)/shard_map/ppermute | solution.py:361
  76.5 20.6 %collective-permute-start.22 = (bf16[320,1280]{1,0:T(8,128)(2,1)S(1)}, bf16[320,1280]{1,0:T(8,128)(2,1)S(1)}, u32[]{:S(2)}, u32[]{:S(2)}) collective-permute-start(bf16[320,1280]{1,0:T(8,128)(2,1)S(1)} %get-tuple-element.227), channel_id=1, source_target_pairs={{0,1},{1,0},{2,3},{3,2},{4,5},{5,4},{6,7},{7,6},{8,9},{9,8},{10,11... | collective-permute-start | bytes 2457608 | tf_op jit(solution)/shard_map/ppermute | solution.py:361
  97.9 23.6 %collective-permute-start.24 = (bf16[2048,1280]{1,0:T(8,128)(2,1)}, bf16[2048,1280]{1,0:T(8,128)(2,1)}, u32[]{:S(2)}, u32[]{:S(2)}) collective-permute-start(bf16[2048,1280]{1,0:T(8,128)(2,1)} %get-tuple-element.231.refs_0_), channel_id=1, source_target_pairs={{0,2},{1,3},{2,0},{3,1},{4,6},{5,7},{6,4},{7,5},{8,10},{9,11},{10,... | collective-permute-start | bytes 15728648 | tf_op jit(solution)/shard_map/ppermute | solution.py:361
  97.9 23.6 %all-to-all-start = ((bf16[16,80,256]{2,1,0:T(8,128)(2,1)}), bf16[16,80,256]{2,1,0:T(8,128)(2,1)S(1)}, u32[]{:S(2)}, u32[]{:S(2)}) async-start(bf16[16,80,256]{2,1,0:T(8,128)(2,1)} %get-tuple-element.228.refs_5_), calls=%async_computation | async-start | bytes 1310720 | tf_op jit(solution)/shard_map/all_to_all | solution.py:1020
  102.5 19.1 %collective-permute-start.23 = (bf16[320,1280]{1,0:T(8,128)(2,1)}, bf16[320,1280]{1,0:T(8,128)(2,1)}, u32[]{:S(2)}, u32[]{:S(2)}) collective-permute-start(bf16[320,1280]{1,0:T(8,128)(2,1)} %copy-done.60), channel_id=1, source_target_pairs={{0,2},{1,3},{2,0},{3,1},{4,6},{5,7},{6,4},{7,5},{8,10},{9,11},{10,... | collective-permute-start | bytes 2457608 | tf_op jit(solution)/shard_map/ppermute | solution.py:361
  103.0 18.5 %collective-permute-start.26 = (bf16[288,1280]{1,0:T(8,128)(2,1)S(1)}, bf16[288,1280]{1,0:T(8,128)(2,1)S(1)}, u32[]{:S(2)}, u32[]{:S(2)}) collective-permute-start(bf16[288,1280]{1,0:T(8,128)(2,1)S(1)} %copy-done.14), channel_id=1, source_target_pairs={{0,1},{1,0},{2,3},{3,2},{4,5},{5,4},{6,7},{7,6},{8,9},{9,8},{10,11... | collective-permute-start | bytes 2211848 | tf_op jit(solution)/shard_map/ppermute | solution.py:361
  121.6 13.2 %collective-permute-start.27 = (bf16[160,1280]{1,0:T(8,128)(2,1)}, bf16[160,1280]{1,0:T(8,128)(2,1)S(1)}, u32[]{:S(2)}, u32[]{:S(2)}) collective-permute-start(bf16[160,1280]{1,0:T(8,128)(2,1)} %pad_maximum_fusion.2), channel_id=1, source_target_pairs={{0,1},{1,0},{2,3},{3,2},{4,5},{5,4},{6,7},{7,6},{8,9},{9,8},{10,11... | collective-permute-start | bytes 1228808 | tf_op jit(solution)/shard_map/ppermute | solution.py:361
  134.9 23.7 %all-to-all-start.1 = ((bf16[16,80,256]{2,1,0:T(8,128)(2,1)}), bf16[16,80,256]{2,1,0:T(8,128)(2,1)S(1)}, u32[]{:S(2)}, u32[]{:S(2)}) async-start(bf16[16,80,256]{2,1,0:T(8,128)(2,1)} %bitcast.31), calls=%async_computation.1 | async-start | bytes 1310720 | tf_op jit(solution)/shard_map/all_to_all | solution.py:1044
  141.7 16.8 %collective-permute-start.28 = (bf16[256,1280]{1,0:T(8,128)(2,1)S(1)}, bf16[256,1280]{1,0:T(8,128)(2,1)}, u32[]{:S(2)}, u32[]{:S(2)}) collective-permute-start(bf16[256,1280]{1,0:T(8,128)(2,1)S(1)} %pad_maximum_fusion), channel_id=1, source_target_pairs={{0,1},{1,0},{2,3},{3,2},{4,5},{5,4},{6,7},{7,6},{8,9},{9,8},{10,11... | collective-permute-start | bytes 1966088 | tf_op jit(solution)/shard_map/ppermute | solution.py:361
  158.6 40.3 %collective-permute-start.31 = (bf16[256,1280]{1,0:T(8,128)(2,1)S(1)}, bf16[256,1280]{1,0:T(8,128)(2,1)S(1)}, u32[]{:S(2)}, u32[]{:S(2)}) collective-permute-start(bf16[256,1280]{1,0:T(8,128)(2,1)S(1)} %copy-done.21), channel_id=1, source_target_pairs={{0,1},{1,0},{2,3},{3,2},{4,5},{5,4},{6,7},{7,6},{8,9},{9,8},{10,11... | collective-permute-start | bytes 1966088 | tf_op jit(solution)/shard_map/ppermute | solution.py:361
  159.6 39.4 %collective-permute-start.32 = (bf16[640,640]{1,0:T(8,128)(2,1)}, bf16[640,640]{1,0:T(8,128)(2,1)S(1)}, u32[]{:S(2)}, u32[]{:S(2)}) collective-permute-start(bf16[640,640]{1,0:T(8,128)(2,1)} %get-tuple-element.271), channel_id=1, source_target_pairs={{0,1},{1,0},{2,3},{3,2},{4,5},{5,4},{6,7},{7,6},{8,9},{9,8},{10,11... | collective-permute-start | bytes 2457608 | tf_op jit(solution)/shard_map/ppermute | solution.py:361
  160.7 39.1 %collective-permute-start.33 = (bf16[640,640]{1,0:T(8,128)(2,1)}, bf16[640,640]{1,0:T(8,128)(2,1)}, u32[]{:S(2)}, u32[]{:S(2)}) collective-permute-start(bf16[640,640]{1,0:T(8,128)(2,1)} %get-tuple-element.272), channel_id=1, source_target_pairs={{0,4},{1,5},{2,6},{3,7},{4,0},{5,1},{6,2},{7,3},{8,12},{9,13},{10,... | collective-permute-start | bytes 2457608 | tf_op jit(solution)/shard_map/ppermute | solution.py:361
  162.6 37.2 %collective-permute-start.34 = (bf16[640,640]{1,0:T(8,128)(2,1)}, bf16[640,640]{1,0:T(8,128)(2,1)}, u32[]{:S(2)}, u32[]{:S(2)}) collective-permute-start(bf16[640,640]{1,0:T(8,128)(2,1)} %get-tuple-element.273), channel_id=1, source_target_pairs={{0,8},{1,9},{2,10},{3,11},{4,12},{5,13},{6,14},{7,15},{8,0},{9,1},... | collective-permute-start | bytes 2457608 | tf_op jit(solution)/shard_map/ppermute | solution.py:361
  200.7 68.2 %all-to-all-start.2 = ((bf16[16,240,256]{2,1,0:T(8,128)(2,1)}), bf16[16,240,256]{2,1,0:T(8,128)(2,1)S(1)}, u32[]{:S(2)}, u32[]{:S(2)}) async-start(bf16[16,240,256]{2,1,0:T(8,128)(2,1)} %shard_map.231.grads), calls=%async_computation.2 | async-start | bytes 3932160 | tf_op jit(solution)/shard_map/all_to_all | solution.py:1099
  213.0 10.4 %collective-permute-start.35 = (bf16[256,640]{1,0:T(8,128)(2,1)}, bf16[256,640]{1,0:T(8,128)(2,1)S(1)}, u32[]{:S(2)}, u32[]{:S(2)}) collective-permute-start(bf16[256,640]{1,0:T(8,128)(2,1)} %get-tuple-element.292), channel_id=1, source_target_pairs={{0,1},{1,0},{2,3},{3,2},{4,5},{5,4},{6,7},{7,6},{8,9},{9,8},{10,11... | collective-permute-start | bytes 983048 | tf_op jit(solution)/shard_map/ppermute | solution.py:361
  218.5 19.4 %collective-permute-start.44 = (bf16[320,640]{1,0:T(8,128)(2,1)}, bf16[320,640]{1,0:T(8,128)(2,1)S(1)}, u32[]{:S(2)}, u32[]{:S(2)}) collective-permute-start(bf16[320,640]{1,0:T(8,128)(2,1)} %get-tuple-element.299), channel_id=1, source_target_pairs={{0,4},{1,5},{2,6},{3,7},{4,0},{5,1},{6,2},{7,3},{8,12},{9,13},{10,... | collective-permute-start | bytes 1228808 | tf_op jit(solution)/shard_map/ppermute | solution.py:361
  220.5 28.2 %collective-permute-start.45 = (bf16[320,640]{1,0:T(8,128)(2,1)}, bf16[320,640]{1,0:T(8,128)(2,1)S(1)}, u32[]{:S(2)}, u32[]{:S(2)}) collective-permute-start(bf16[320,640]{1,0:T(8,128)(2,1)} %get-tuple-element.300), channel_id=1, source_target_pairs={{0,8},{1,9},{2,10},{3,11},{4,12},{5,13},{6,14},{7,15},{8,0},{9,1},... | collective-permute-start | bytes 1228808 | tf_op jit(solution)/shard_map/ppermute | solution.py:361
  222.0 26.9 %collective-permute-start.46 = (bf16[320,640]{1,0:T(8,128)(2,1)}, bf16[320,640]{1,0:T(8,128)(2,1)S(1)}, u32[]{:S(2)}, u32[]{:S(2)}) collective-permute-start(bf16[320,640]{1,0:T(8,128)(2,1)} %get-tuple-element.301), channel_id=1, source_target_pairs={{0,1},{1,0},{2,3},{3,2},{4,5},{5,4},{6,7},{7,6},{8,9},{9,8},{10,11... | collective-permute-start | bytes 1228808 | tf_op jit(solution)/shard_map/ppermute | solution.py:361
  223.5 31.7 %collective-permute-start.41 = (bf16[256,640]{1,0:T(8,128)(2,1)S(1)}, bf16[256,640]{1,0:T(8,128)(2,1)S(1)}, u32[]{:S(2)}, u32[]{:S(2)}) collective-permute-start(bf16[256,640]{1,0:T(8,128)(2,1)S(1)} %add_convert_fusion.refs_0_), channel_id=1, source_target_pairs={{0,4},{1,5},{2,6},{3,7},{4,12},{5,13},{6,14},{7,15},{8,0},{9,1},{1... | collective-permute-start | bytes 983048 | tf_op jit(solution)/shard_map/ppermute | solution.py:361
  225.6 33.4 %collective-permute-start.37 = (bf16[160,1280]{1,0:T(8,128)(2,1)S(1)}, bf16[160,1280]{1,0:T(8,128)(2,1)S(1)}, u32[]{:S(2)}, u32[]{:S(2)}) collective-permute-start(bf16[160,1280]{1,0:T(8,128)(2,1)S(1)} %copy-done.26), channel_id=1, source_target_pairs={{0,2},{1,3},{2,0},{3,1},{4,6},{5,7},{6,4},{7,5},{8,10},{9,11},{10,... | collective-permute-start | bytes 1228808 | tf_op jit(solution)/shard_map/ppermute | solution.py:361
  237.9 31.0 %collective-permute-start.36 = (bf16[288,1280]{1,0:T(8,128)(2,1)S(1)}, bf16[288,1280]{1,0:T(8,128)(2,1)}, u32[]{:S(2)}, u32[]{:S(2)}) collective-permute-start(bf16[288,1280]{1,0:T(8,128)(2,1)S(1)} %collective-permute-done.26.refs_3_), channel_id=1, source_target_pairs={{0,2},{1,3},{2,0},{3,1},{4,6},{5,7},{6,4},{7,5},{8,10},{9,11},{10,... | collective-permute-start | bytes 2211848 | tf_op jit(solution)/shard_map/ppermute | solution.py:361
  248.9 18.2 %collective-permute-start.38 = (bf16[256,1280]{1,0:T(8,128)(2,1)}, bf16[256,1280]{1,0:T(8,128)(2,1)S(1)}, u32[]{:S(2)}, u32[]{:S(2)}) collective-permute-start(bf16[256,1280]{1,0:T(8,128)(2,1)} %collective-permute-done.28.refs_5_), channel_id=1, source_target_pairs={{0,2},{1,3},{2,0},{3,1},{4,6},{5,7},{6,4},{7,5},{8,10},{9,11},{10,... | collective-permute-start | bytes 1966088 | tf_op jit(solution)/shard_map/ppermute | solution.py:361
  255.2 11.9 %collective-permute-start.39 = (bf16[256,1280]{1,0:T(8,128)(2,1)S(1)}, bf16[256,1280]{1,0:T(8,128)(2,1)S(1)}, u32[]{:S(2)}, u32[]{:S(2)}) collective-permute-start(bf16[256,1280]{1,0:T(8,128)(2,1)S(1)} %copy-done.18), channel_id=1, source_target_pairs={{0,2},{1,3},{2,0},{3,1},{4,6},{5,7},{6,4},{7,5},{8,10},{9,11},{10,... | collective-permute-start | bytes 1966088 | tf_op jit(solution)/shard_map/ppermute | solution.py:361
  272.4 17.5 %collective-permute-start.49 = (bf16[5,256,640]{2,1,0:T(8,128)(2,1)}, bf16[5,256,640]{2,1,0:T(8,128)(2,1)S(1)}, u32[]{:S(2)}, u32[]{:S(2)}) collective-permute-start(bf16[5,256,640]{2,1,0:T(8,128)(2,1)} %shard_map.236.near), channel_id=1, source_target_pairs={{0,2},{1,3},{2,0},{3,1},{4,6},{5,7},{6,4},{7,5},{8,10},{9,11},{10,... | collective-permute-start | bytes 4915208 | tf_op jit(solution)/shard_map/ppermute | solution.py:361
  276.7 12.3 %collective-permute-start.47 = (bf16[256,640]{1,0:T(8,128)(2,1)}, bf16[256,640]{1,0:T(8,128)(2,1)S(1)}, u32[]{:S(2)}, u32[]{:S(2)}) collective-permute-start(bf16[256,640]{1,0:T(8,128)(2,1)} %copy-done.35), channel_id=1, source_target_pairs={{0,8},{1,9},{2,10},{3,11},{4,0},{5,1},{6,2},{7,3},{8,16},{9,17},{1... | collective-permute-start | bytes 983048 | tf_op jit(solution)/shard_map/ppermute | solution.py:361
  286.1 18.7 %collective-permute-start.55 = (bf16[240,640]{1,0:T(8,128)(2,1)}, bf16[240,640]{1,0:T(8,128)(2,1)S(1)}, u32[]{:S(2)}, u32[]{:S(2)}) collective-permute-start(bf16[240,640]{1,0:T(8,128)(2,1)} %get-tuple-element.317), channel_id=1, source_target_pairs={{0,16},{1,17},{2,18},{3,19},{4,20},{5,21},{6,22},{7,23},{8,24},{9,... | collective-permute-start | bytes 921608 | tf_op jit(solution)/shard_map/ppermute | solution.py:361
  289.8 17.2 %collective-permute-start.56 = (bf16[256,640]{1,0:T(8,128)(2,1)S(1)}, bf16[256,640]{1,0:T(8,128)(2,1)S(1)}, u32[]{:S(2)}, u32[]{:S(2)}) collective-permute-start(bf16[256,640]{1,0:T(8,128)(2,1)S(1)} %collective-permute-done.47.refs_0_), channel_id=1, source_target_pairs={{0,2},{1,3},{2,0},{3,1},{4,6},{5,7},{6,4},{7,5},{8,10},{9,11},{10,... | collective-permute-start | bytes 983048 | tf_op jit(solution)/shard_map/ppermute | solution.py:361
  289.9 17.1 %collective-permute-start.57 = (bf16[256,640]{1,0:T(8,128)(2,1)S(1)}, bf16[256,640]{1,0:T(8,128)(2,1)S(1)}, u32[]{:S(2)}, u32[]{:S(2)}) collective-permute-start(bf16[256,640]{1,0:T(8,128)(2,1)S(1)} %collective-permute-done.48.refs_1_), channel_id=1, source_target_pairs={{0,2},{1,3},{2,0},{3,1},{4,6},{5,7},{6,4},{7,5},{8,10},{9,11},{10,... | collective-permute-start | bytes 983048 | tf_op jit(solution)/shard_map/ppermute | solution.py:361
  290.4 16.5 %collective-permute-start.54 = (bf16[128,640]{1,0:T(8,128)(2,1)S(1)}, bf16[128,640]{1,0:T(8,128)(2,1)S(1)}, u32[]{:S(2)}, u32[]{:S(2)}) collective-permute-start(bf16[128,640]{1,0:T(8,128)(2,1)S(1)} %slice.51), channel_id=1, source_target_pairs={{0,4},{1,5},{2,6},{3,7},{4,12},{5,13},{6,14},{7,15},{8,0},{9,1},{1... | collective-permute-start | bytes 491528 | tf_op jit(solution)/shard_map/ppermute | solution.py:361
  291.9 15.0 %collective-permute-start.53 = (bf16[128,640]{1,0:T(8,128)(2,1)S(1)}, bf16[128,640]{1,0:T(8,128)(2,1)S(1)}, u32[]{:S(2)}, u32[]{:S(2)}) collective-permute-start(bf16[128,640]{1,0:T(8,128)(2,1)S(1)} %slice.50), channel_id=1, source_target_pairs={{0,8},{1,9},{2,10},{3,11},{4,0},{5,1},{6,2},{7,3},{8,16},{9,17},{1... | collective-permute-start | bytes 491528 | tf_op jit(solution)/shard_map/ppermute | solution.py:361
  307.6 14.5 %collective-permute-start.61 = (bf16[240,640]{1,0:T(8,128)(2,1)S(1)}, bf16[240,640]{1,0:T(8,128)(2,1)S(1)}, u32[]{:S(2)}, u32[]{:S(2)}) collective-permute-start(bf16[240,640]{1,0:T(8,128)(2,1)S(1)} %add_convert_fusion.1.refs_0_), channel_id=1, source_target_pairs={{0,4},{1,5},{2,6},{3,7},{4,12},{5,13},{6,14},{7,15},{8,0},{9,1},{1... | collective-permute-start | bytes 921608 | tf_op jit(solution)/shard_map/ppermute | solution.py:361
  307.6 14.5 %collective-permute-start.60 = (bf16[240,640]{1,0:T(8,128)(2,1)S(1)}, bf16[240,640]{1,0:T(8,128)(2,1)S(1)}, u32[]{:S(2)}, u32[]{:S(2)}) collective-permute-start(bf16[240,640]{1,0:T(8,128)(2,1)S(1)} %add_convert_fusion.1.refs_0_), channel_id=1, source_target_pairs={{0,8},{1,9},{2,10},{3,11},{4,0},{5,1},{6,2},{7,3},{8,16},{9,17},{1... | collective-permute-start | bytes 921608 | tf_op jit(solution)/shard_map/ppermute | solution.py:361
  322.1 13.4 %collective-permute-start.62 = (bf16[240,640]{1,0:T(8,128)(2,1)S(1)}, bf16[240,640]{1,0:T(8,128)(2,1)S(1)}, u32[]{:S(2)}, u32[]{:S(2)}) collective-permute-start(bf16[240,640]{1,0:T(8,128)(2,1)S(1)} %collective-permute-done.60.refs_1_), channel_id=1, source_target_pairs={{0,8},{1,9},{2,10},{3,11},{4,0},{5,1},{6,2},{7,3},{8,16},{9,17},{1... | collective-permute-start | bytes 921608 | tf_op jit(solution)/shard_map/ppermute | solution.py:361
  322.7 12.8 %collective-permute-start.63 = (bf16[240,640]{1,0:T(8,128)(2,1)S(1)}, bf16[240,640]{1,0:T(8,128)(2,1)S(1)}, u32[]{:S(2)}, u32[]{:S(2)}) collective-permute-start(bf16[240,640]{1,0:T(8,128)(2,1)S(1)} %collective-permute-done.61.refs_2_), channel_id=1, source_target_pairs={{0,4},{1,5},{2,6},{3,7},{4,12},{5,13},{6,14},{7,15},{8,0},{9,1},{1... | collective-permute-start | bytes 921608 | tf_op jit(solution)/shard_map/ppermute | solution.py:361
  339.5 10.2 %collective-permute-start.66 = (bf16[5,240,640]{2,1,0:T(8,128)(2,1)}, bf16[5,240,640]{2,1,0:T(8,128)(2,1)S(1)}, u32[]{:S(2)}, u32[]{:S(2)}) collective-permute-start(bf16[5,240,640]{2,1,0:T(8,128)(2,1)} %shard_map.239.near), channel_id=1, source_target_pairs={{0,2},{1,3},{2,0},{3,1},{4,6},{5,7},{6,4},{7,5},{8,10},{9,11},{10,... | collective-permute-start | bytes 4608008 | tf_op jit(solution)/shard_map/ppermute | solution.py:361
  (110 other events, 858.5 us)

commit v3 on v2

--- a/solution.py
+++ b/solution.py
@@ -468,7 +468,7 @@
 
 def forward_kernel(info, deal, *refs):
     pieces = refs[:10]
-    out, q_out, k_out, queries, keys, values, lse, dealt = refs[10:]
+    out, queries, keys, values, lse, dealt = refs[10:]
     total = queries.shape[1]
     length = info[3]
     spans = total // SPAN
@@ -549,10 +549,7 @@
             start = (jnp.full((1, BLOCK), NEG, F32), jnp.zeros((HEAD + 16, BLOCK), F32))
             finish(i, *lax.fori_loop(0, i + 1, step, start))
 
-    q_out[:HEAD] = queries[:HEAD]
-    q_out[HEAD : HEAD + 16] = in_parts(-lse[...])
-    q_out[HEAD + 16 :] = jnp.zeros((WIDE - HEAD - 16, total), BF)
-    k_out[...] = keys[...]
+    queries[HEAD : HEAD + 16] = in_parts(-lse[...])
 
 
 def turn_kernel(info, deal, *refs):
@@ -607,8 +604,9 @@
                 key_pos = j * BLOCK + key_at
                 allowed = (key_pos <= i * BLOCK + query_at) & (key_pos < length)
                 probs = jnp.where(allowed, probs, 0.0)
-            grad_scores = (probs * mm(v_n[there, :], g_t[:, here])).astype(BF)
-            dv[...] += mm(probs.astype(BF), g_n[here, :])
+            probs = probs.astype(BF)
+            grad_scores = probs * mm(v_n[there, :], g_t[:, here]).astype(BF)
+            dv[...] += mm(probs, g_n[here, :])
             dk[...] += mm(grad_scores, q_n[here, :])
             dq_t[:, here] += mm(k_t[:, there], grad_scores)
             return carry
@@ -824,7 +822,7 @@
 
 def weight_kernel(info, grads, own, other, *refs):
     inputs = refs[:2]
-    keep, away, lines, weight, total, attn_in, sems = refs[2:]
+    keep, away, lines, weight, total, gain_sums, attn_in, sems = refs[2:]
     y, core = info[0], info[1]
     rows = attn_in.shape[0] // 8
     loads = []
@@ -834,8 +832,9 @@
         loads[-1].start()
     for slot in range(16):
         lines[:, slot * 256 : slot * 256 + 256] = grads[info[4 + slot]]
-    weight[:, half(y)] = own[pl.ds(pl.multiple_of(core * 3 * HEAD, 16), HEAD)].astype(F32)
-    weight[:, half(1 - y)] = other[pl.ds(pl.multiple_of(core * 3 * HEAD, 16), HEAD)].astype(F32)
+    mine = pl.ds(pl.multiple_of(core * 3 * HEAD, 16), 3 * HEAD)
+    weight[:, half(y)] = own[mine].astype(F32)
+    weight[:, half(1 - y)] = other[mine].astype(F32)
     total[...] = jnp.zeros_like(total)
     for at in range(4):
         loads[2 * at].wait()
@@ -844,40 +843,39 @@
         total[...] += mm(lines[:, part], attn_in[part])
     keep[: 3 * HEAD] = total[:, half(y)]
     away[: 3 * HEAD] = total[:, half(1 - y)].astype(BF)
-    sums = row_sums(weight[...] * total[:HEAD])
-    keep[3 * HEAD :] = jnp.zeros((16, keep.shape[1]), F32)
-    away[3 * HEAD :] = jnp.zeros((16, keep.shape[1]), BF)
-    keep[3 * HEAD :, :HEAD] = sums
-    away[3 * HEAD :, :HEAD] = sums.astype(BF)
+    weight[...] *= total[...]
+    scale_sums = row_sums(weight[:HEAD])[0:1]
+    gain_sums[...] = jnp.sum(weight[...], axis=0, keepdims=True)
+    line = lax.broadcasted_iota(jnp.int32, (16, keep.shape[1]), 0)
+    keep[3 * HEAD :] = jnp.where(line == 1, gain_sums[:, half(y)], 0.0)
+    away[3 * HEAD :] = jnp.where(line == 1, gain_sums[:, half(1 - y)], 0.0).astype(BF)
+    keep[3 * HEAD : 3 * HEAD + 1, :HEAD] = scale_sums
+    first = lax.broadcasted_iota(jnp.int32, (16, HEAD), 0) == 0
+    behind = jnp.where(line == 1, gain_sums[:, half(1 - y)], 0.0)[:, :HEAD]
+    away[3 * HEAD :, :HEAD] = jnp.where(first, scale_sums, behind).astype(BF)
 
 
 def finish_kernel(info, near, near_partner, *refs):
-    pieces, shards, (gain, factor), refs = refs[:8], refs[8:11], refs[11:13], refs[13:]
-    outs, (grad_gain, grad_scale), (stacks, weights, last, turned, sems) = refs[:3], refs[3:5], refs[5:]
-    loads = [pltpu.make_async_copy(ref, weights.at[at], sems.at[at]) for at, ref in enumerate(shards)]
-    for load in loads:
-        load.start()
-    scale_sum = jnp.zeros((1, HEAD), F32)
+    pieces, (gain, factor), outs, refs = refs[:8], refs[8:10], refs[10:13], refs[13:]
+    grad_gain, grad_scale, stacks, last, turned, sems = refs
+    extra = jnp.zeros((16, last.shape[2]), F32)
     early = [stack.at[at] for stack in (near, near_partner) for at in range(5)]
     for first, group in ((0, early), (5, joined(pieces, last))):
         for at, ref in enumerate(group):
             rows = pl.ds(pl.multiple_of(info[4 + slot_of(at, len(group) // 2, first)] * HEAD, 16), HEAD)
             for way in range(3):
                 stacks[way, rows] = ref[way * HEAD : (way + 1) * HEAD]
-            scale_sum += ref[3 * HEAD :, :HEAD].astype(F32)[0:1]
-    grad_scale[...] = scale_sum * factor[...]
+            extra += ref[3 * HEAD :].astype(F32)
+    grad_scale[...] = extra[0:1, :HEAD] * factor[...]
     size = turned.shape[1]
+    grad_gain[...] = (extra[1:2] / gain[...].astype(F32)).reshape(size)
     same = lax.broadcasted_iota(jnp.int32, (size, size), 0) == lax.broadcasted_iota(jnp.int32, (size, size), 1)
     unit = jnp.where(same, 1.0, 0.0).astype(BF)
     copies = []
-    sums = jnp.zeros((size, 128), F32)
     for at, out in enumerate(outs):
         turned[at] = mm(unit, stacks[at], NT)
-        copies.append(pltpu.make_async_copy(turned.at[at], out, sems.at[3 + at]))
+        copies.append(pltpu.make_async_copy(turned.at[at], out, sems.at[at]))
         copies[-1].start()
-        loads[at].wait()
-        sums += folded(weights[at].astype(F32) * turned[at])
-    grad_gain[...] = (row_sums(sums)[0:1] / gain[...].astype(F32)).reshape(size)
     arrive(copies)
 
 
@@ -889,14 +887,15 @@
     gain[:, half(y)] = own[6 * HEAD :].astype(F32)
     gain[:, half(1 - y)] = other[6 * HEAD :].astype(F32)
     heads, width = grads.shape[0], grads.shape[2]
-    turned_grad = jnp.zeros((heads * HEAD, width), F32)
+    values = tokens[...].astype(F32)
+    rate = lax.rsqrt(jnp.mean(values * values, axis=-1, keepdims=True) + EPS)
+    turned_grad = None
     for at, ref in enumerate(weights):
         part = grads[:, at * HEAD : (at + 1) * HEAD, :].reshape(heads * HEAD, width)
         arrive(loads[at])
-        turned_grad += mm(ref[...], part)
+        product = mm(ref[...], part)
+        turned_grad = product if turned_grad is None else turned_grad + product
     grad = turned_grad.T * gain[0:1]
-    values = tokens[...].astype(F32)
-    rate = lax.rsqrt(jnp.mean(values * values, axis=-1, keepdims=True) + EPS)
     inner = jnp.mean(grad * values, axis=-1, keepdims=True)
     out[...] = (grad_mid[...] + rate * grad - values * (rate * rate * rate * inner)).astype(BF)
 
@@ -930,7 +929,7 @@
     cut = rows // 2
     mine, partner, gathered = [], [], []
 
-    def project(*group):
+    def project(other, *group):
         count = sum(part.shape[0] for part in group)
         start = sum(piece.shape[1] for piece in mine)
         args = [info, *group, own, other, scale_col]
@@ -968,34 +967,32 @@
         cost=(2 * 480 * 640 * 1280, 3 * 640 * 1280 * 2, 0),
     )[0]
     other = send(own, Y_SWAP)
-    rows_out = weight_rows(after((w_output, w_expand, w_contract), own), core)
-    rows_back = weight_rows(after((w_query, w_key, w_value), own), core)
-    chunks = [rows_out[128:256], rows_out[256:512], rows_out[512:640], rows_out[640:], rows_back[:288]]
-    chunks += [rows_back[288:448], rows_back[448:704], rows_back[704:]]
-    forth1, back1, direct[0], *chunks = after((forth1, back1, direct[0], *chunks))
+    forth1, back1, direct[0] = after((forth1, back1, direct[0]), own)
 
     forth2, back2 = send(forth1, FORTH), send(back1, BACK)
+    rows_out = weight_rows(after((w_output, w_expand, w_contract), forth1), core)
+    rows_back = weight_rows(after((w_query, w_key, w_value), forth1), core)
+    chunks = [rows_out[128:416], rows_out[416:576], rows_out[576:]]
+    chunks += [rows_back[:224], rows_back[224:384], rows_back[384:608], rows_back[608:]]
     passed.append(send(direct[0], CORE_SWAP))
-    direct.append(send(after(chunks[:1], direct[0])[0], Y_SWAP))
-    done = project(inputs)
-    forth2, back2, direct[1], passed[0] = after((forth2, back2, direct[1], passed[0]), done)
+    forth2, back2, other, passed[0], *chunks = after((forth2, back2, other, passed[0], *chunks))
 
     forth3, back3 = send(forth2, FORTH), send(back2, BACK)
+    direct.append(send(after(chunks[:1], passed[0])[0], Y_SWAP))
+    done = project(other, inputs)
+    done = project(other, forth1, back1), done
+    done = project(other, forth2, back2), done
+    forth3, back3, direct[1] = after((forth3, back3, direct[1]), done)
+
+    forth4, back4 = send(forth3[:cut], FORTH), send(back3[cut:], BACK)
     passed.append(send(direct[1], CORE_SWAP))
     direct.append(send(after(chunks[1:2], direct[1])[0], Y_SWAP))
-    done = project(forth1, back1)
-    forth3, back3, direct[2], passed[1] = after((forth3, back3, direct[2], passed[1]), done)
-
-    forth4, back4 = send(forth3[:cut], FORTH), send(back3[cut:], BACK)
+    done = project(other, forth3, back3)
+    forth4, back4, direct[2], passed[1] = after((forth4, back4, direct[2], passed[1]), done)
     passed.append(send(direct[2], CORE_SWAP))
     direct.append(send(after(chunks[2:3], direct[2])[0], Y_SWAP))
-    done2 = project(forth2, back2)
-    done3 = project(forth3, back3)
-    forth4, back4, direct[3], passed[2] = after((forth4, back4, direct[3], passed[2]), done2, done3)
-    passed.append(send(direct[3], CORE_SWAP))
-    project(forth4, back4)
-    *spans, passed[3] = after((*mine, *partner, passed[3]))
-    direct.append(send(after(chunks[3:4], spans[0])[0], Y_SWAP))
+    project(other, forth4, back4)
+    *spans, passed[2] = after((*mine, *partner, passed[2]))
 
     tall, flat_t = ((total, WIDE), BF), ((WIDE, total), BF)
     attended, q_t, k_n = call(
@@ -1004,17 +1001,15 @@
         [info, dealt, *spans],
         smem=2,
         scratch=[
-            pltpu.VMEM((WIDE, total), BF),
-            pltpu.VMEM((total, WIDE), BF),
             pltpu.VMEM((HEAD + 16, total), BF),
             pltpu.VMEM((1, total), F32),
             pltpu.SMEM((total // SPAN,), jnp.int32),
         ],
         cost=(2 * total * total * 256, 3 * total * 160, total * total // 2),
     )
-    attended, direct[4] = after((attended, direct[4]))
-    passed.append(send(direct[4], CORE_SWAP))
-    direct_back = [send(after(chunks[4:5], direct[4])[0], Y_SWAP)]
+    attended, direct[3] = after((attended, direct[3]))
+    passed.append(send(direct[3], CORE_SWAP))
+    direct_back = [send(after(chunks[3:4], direct[3])[0], Y_SWAP)]
     attn_in = gathered[-1]
     attn_in_partner, cot_partner = (send(value, CORE_SWAP) for value in after((attn_in, cot), attended))
     attn_t = lax.all_to_all(attended, "ctx", 0, 0).reshape(width, rows)
@@ -1025,25 +1020,25 @@
         smem=2,
         cost=(0, 6 * total * 256, 0),
     )
-    attn_t, passed[4], attn_in_partner, cot_partner, direct_back[0] = after(
-        (attn_t, passed[4], attn_in_partner, cot_partner, direct_back[0]), k_t
-    )
-    direct_back.append(send(after(chunks[5:6], attn_t)[0], Y_SWAP))
+    attn_t, passed[3], attn_in_partner, cot_partner, direct_back[0] = after(
+        (attn_t, passed[3], attn_in_partner, cot_partner, direct_back[0]), k_t
+    )
+    direct_back.append(send(after(chunks[4:5], attn_t)[0], Y_SWAP))
     whole_scratch = [pltpu.VMEM((width, width), BF)] * 3 + [pltpu.VMEM((16, width), F32)]
     wide, low = ((rows, width), F32), ((rows, width), BF)
     result, grad_mid, grad_attended_t, packed, rights = call(
-        functools.partial(mlp_kernel, 5),
+        functools.partial(mlp_kernel, 4),
         [low, wide, ((width, rows), BF), ((3, rows, width), BF), low],
         [info, inputs, cot, attn_t, own, other, w_output, w_expand, w_contract, *direct, *passed],
         smem=1,
-        anys=range(6, 19),
+        anys=range(6, 17),
         scratch=whole_scratch + [pltpu.VMEM((2, rows, width), BF), pltpu.SemaphoreType.DMA((24,))],
         cost=(12 * rows * width * width, 6 * width * width, 0),
     )
     grad_attended_t, packed, direct_back[1] = after((grad_attended_t, packed, direct_back[1]))
     grad_out = lax.all_to_all(grad_attended_t.reshape(16, HEAD, rows), "ctx", 0, 0)
     packed_partner = send(packed, CORE_SWAP)
-    direct_back.append(send(after(chunks[6:7], packed)[0], Y_SWAP))
+    direct_back.append(send(after(chunks[5:6], packed)[0], Y_SWAP))
     attn_t_partner = send(attn_t, CORE_SWAP)
 
     half_width = width // 2
@@ -1078,7 +1073,7 @@
     came = travel(terms[3:], 0)
     kept = terms[:3]
     grad_out, direct_back[2] = after((grad_out, direct_back[2]), kept[0])
-    direct_back.append(send(after(chunks[7:], kept[0])[0], Y_SWAP))
+    direct_back.append(send(after(chunks[6:], kept[0])[0], Y_SWAP))
     grads = call(
         backward_kernel,
         [((16, 3 * HEAD, rows), BF)],
@@ -1105,8 +1100,9 @@
         anys=(4, 5),
         scratch=[
             pltpu.VMEM((3 * HEAD, total), BF),
-            pltpu.VMEM((HEAD, width), F32),
             pltpu.VMEM((3 * HEAD, width), F32),
+            pltpu.VMEM((3 * HEAD, width), F32),
+            pltpu.VMEM((1, width), F32),
             pltpu.VMEM((total, width), BF),
             pltpu.SemaphoreType.DMA((8,)),
         ],
@@ -1135,32 +1131,10 @@
     near, near_partner = stacked([summed, forth1, back1, forth2, back2])
     terms = halving(kept, came, 3)
     far = send(terms[1], FAR_SWAP)
-    forth3, back3, near_partner = after((forth3, back3, near_partner), terms[0])
+    forth3, back3 = after((forth3, back3), terms[0])
     last = [send(forth3[:128], FORTH), send(back3[128:], BACK)]
     beyond = [send(value, CORE_SWAP) for value in (forth3, back3)]
     piece = (terms[0].astype(F32) + far.astype(F32)).astype(BF)
-    *last, piece = after((*last, piece), *beyond)
-    query_pieces = [near, near_partner, forth3, back3, *last, *beyond, *(send(value, CORE_SWAP) for value in last)]
-
-    forth1, back1 = send(piece, FORTH), send(piece, BACK)
-    grad_query, grad_key, grad_value, grad_gain_attn, grad_scale = call(
-        finish_kernel,
-        [shard] * 3 + [line, ((1, HEAD), F32)],
-        [info, *query_pieces, w_query, w_key, w_value, gain_attn[None], factor],
-        smem=1,
-        anys=range(11, 14),
-        out_anys=range(3),
-        scratch=[
-            pltpu.VMEM((3, width, half_width), BF),
-            pltpu.VMEM((3, half_width, width), BF),
-            pltpu.VMEM((2, 256, half_width), BF),
-            pltpu.VMEM((3, half_width, width), F32),
-            pltpu.SemaphoreType.DMA((6,)),
-        ],
-        cost=(6 * 640 * 640 * 1280, 3 * 640 * 1280 * 4, 0),
-    )
-    forth1, back1 = after((forth1, back1), grad_query)
-    forth2, back2 = send(forth1, FORTH), send(back1, BACK)
     grad_inputs = call(
         functools.partial(input_kernel, 4),
         [low],
@@ -1170,12 +1144,29 @@
         scratch=whole_scratch + [pltpu.SemaphoreType.DMA((24,))],
         cost=(6 * rows * width * width, 6 * width * width, 0),
     )[0]
-    forth2, back2 = after((forth2, back2), grad_inputs)
+    last = after(last, *beyond, grad_inputs, near_partner)
+    piece = after((piece,), last[0])[0]
+    query_pieces = [near, near_partner, forth3, back3, *last, *beyond, *(send(value, CORE_SWAP) for value in last)]
+
+    forth1, back1 = send(piece, FORTH), send(piece, BACK)
+    grad_query, grad_key, grad_value, grad_gain_attn, grad_scale = call(
+        finish_kernel,
+        [shard] * 3 + [line, ((1, HEAD), F32)],
+        [info, *query_pieces, gain_attn[None], factor],
+        smem=1,
+        out_anys=range(3),
+        scratch=[
+            pltpu.VMEM((3, width, half_width), BF),
+            pltpu.VMEM((2, 256, half_width), BF),
+            pltpu.VMEM((3, half_width, width), F32),
+            pltpu.SemaphoreType.DMA((3,)),
+        ],
+        cost=(6 * 640 * 640 * 1280, 3 * 640 * 1280 * 4, 0),
+    )
+    forth1, back1 = after((forth1, back1), grad_query)
+    forth2, back2 = send(forth1, FORTH), send(back1, BACK)
     forth3, back3 = send(forth2, FORTH), send(back2, BACK)
     near, near_partner = stacked([piece, forth1, back1, forth2, back2])
-    forth3, back3, near_partner = after((forth3, back3, near_partner))
-    last = [send(forth3[:112], FORTH), send(back3[112:], BACK)]
-    beyond = [send(value, CORE_SWAP) for value in (forth3, back3)]
     partial_out = call(
         spread_kernel,
         [((half_width, 128), F32), shard, shard, shard],
@@ -1185,7 +1176,10 @@
         scratch=[pltpu.VMEM((30, PART, half_width), F32), pltpu.SemaphoreType.DMA((30,))],
         cost=(0, 3 * 640 * 1280 * 4, 0),
     )
-    last = after(last, partial_out[0], *beyond)
+    forth3, back3 = after((forth3, back3), partial_out[0])
+    last = [send(forth3[:112], FORTH), send(back3[112:], BACK)]
+    beyond = [send(value, CORE_SWAP) for value in (forth3, back3)]
+    last = after(last, *beyond)
     args = [info, forth3, back3, *last, *beyond, *(send(value, CORE_SWAP) for value in last)]
     args += [partial_out[0], gain_mlp[None], w_expand, *partial_out[1:]]
     grad_contract, grad_expand, grad_output, grad_gain_mlp = call(

time: 371 us -> 367 us (0.989)
  starting transfers between devices: 80.5 us -> 71.7 us
    ppermute x73 -> x71, starting transfers between devices: 65.7 us -> 54.8 us  [send(): return lax.ppermute(value, AXES, moves)]
    unnamed x164 -> x168, local copies, waits for them, and re-layouts: 11.7 us -> 14.4 us
    ppermute x73 -> x71, waiting for transfers between devices: 99.7 us -> 102 us  [send(): return lax.ppermute(value, AXES, moves)]
  transfers between devices with their start and end apart: 76 -> 74, of which waited for: 30 -> 31; matrix products, arithmetic and copies ran while one was open for 3% -> 4% of each run, Pallas kernels for 40% -> 40%
where the time goes in v3:
time: 367 us; the launch traced here: 361 us
  Pallas kernels  156 us (43%)
  waiting for transfers between devices  103 us (28%)
  starting transfers between devices  71.7 us (20%)
  local copies, waits for them, and re-layouts  24.4 us (7%)
    pallas_call x21, Pallas kernels, call(): pl.pallas_call(body, out_shape=[jax.ShapeDtypeStruct(shape, kind) for sha...  156 us
    ppermute x71, waiting for transfers between devices, send(): return lax.ppermute(value, AXES, moves)  102 us
    ppermute x71, starting transfers between devices, send(): return lax.ppermute(value, AXES, moves)  54.8 us
    unnamed x168, local copies, waits for them, and re-layouts  14.4 us
  transfers between devices with their start and end apart: 74, of which 31 were waited for; matrix products, arithmetic and copies ran while one was open for 4% of the time, Pallas kernels for 40%

profile of v3, /device:TPU:0, one launch (start us, length us, event | category | flops | bytes accessed | tf_op | source)
XLA Modules:
  0.0 360.9 jit_solution(3129631804194809577)
XLA Ops:
  0.6 3.0 collective-permute-start.1
  4.8 2.0 collective-permute-start.2
  11.2 5.2 %shard_map.221.refs_1_.refs_2_.own = bf16[496,640]{1,0:T(8,128)(2,1)} custom-call(s32[23]{0:T(128)} %concatenate.17.info, bf16[640,1280]{1,0:T(8,128)(2,1)} %refs_0_.3, bf16[640,1280]{1,0:T(8,128)(2,1)} %refs_1_.3, bf16[640,1280]{1,0:T(8,128)(2,1)} %refs_2_.3, bf16[1,640]{1,0:T(2,128)(2,1)} %broadcast_in_dim.20.gain_a.refs_8_, ...), custom_call_target="tpu_custom_call" | custom-call | flops 786432000 | bytes 4915200 | tf_op jit(solution)/shard_map/pallas_call | solution.py:375
  16.5 2.3 collective-permute-done.1.refs_1_
  28.4 1.8 constant_dynamic-slice_fusion.2
  31.9 6.1 %collective-permute-done.4.refs_1_ = bf16[256,1280]{1,0:T(8,128)(2,1)} collective-permute-done((bf16[256,1280]{1,0:T(8,128)(2,1)}, bf16[256,1280]{1,0:T(8,128)(2,1)}, u32[]{:S(2)}, u32[]{:S(2)}) %collective-permute-start.4) | collective-permute-done | bytes 655392 | tf_op jit(solution)/shard_map/ppermute | solution.py:361
  43.0 3.5 shard_map.222
  46.4 4.2 %shard_map.223 = (bf16[2048,1280]{1,0:T(8,128)(2,1)}, bf16[240,512]{1,0:T(8,128)(2,1)}, bf16[240,512]{1,0:T(8,128)(2,1)}) custom-call(s32[23]{0:T(128)} %concatenate.17.info, bf16[256,1280]{1,0:T(8,128)(2,1)} %collective-permute-done.refs_0_, bf16[256,1280]{1,0:T(8,128)(2,1)} %collective-permute-done.1.refs_1_, ...), custom_call_target="tpu_custom_call", output_to_operand_aliasing={{0}: (6, {})} | custom-call | flops 629145600 | bytes 2621440 | tf_op jit(solution)/shard_map/pallas_call | solution.py:375
  50.7 4.2 %shard_map.224 = (bf16[2048,1280]{1,0:T(8,128)(2,1)}, bf16[240,512]{1,0:T(8,128)(2,1)}, bf16[240,512]{1,0:T(8,128)(2,1)}) custom-call(s32[23]{0:T(128)} %concatenate.17.info, bf16[256,1280]{1,0:T(8,128)(2,1)} %collective-permute-done.3.refs_0_, bf16[256,1280]{1,0:T(8,128)(2,1)} %collective-permute-done.4.refs_1_, ...), custom_call_target="tpu_custom_call", output_to_operand_aliasing={{0}: (6, {})} | custom-call | flops 629145600 | bytes 2621440 | tf_op jit(solution)/shard_map/pallas_call | solution.py:375
  60.5 4.3 %shard_map.225 = (bf16[2048,1280]{1,0:T(8,128)(2,1)}, bf16[240,512]{1,0:T(8,128)(2,1)}, bf16[240,512]{1,0:T(8,128)(2,1)}) custom-call(s32[23]{0:T(128)} %concatenate.17.info, bf16[256,1280]{1,0:T(8,128)(2,1)} %copy-done.7, bf16[256,1280]{1,0:T(8,128)(2,1)} %copy-done.8, ...), custom_call_target="tpu_custom_call", output_to_operand_aliasing={{0}: (6, {})} | custom-call | flops 629145600 | bytes 2621440 | tf_op jit(solution)/shard_map/pallas_call | solution.py:375
  64.7 3.3 collective-permute-done.11.refs_1_
  72.3 3.5 shard_map.226
  78.1 17.5 %shard_map.227 = (bf16[16,80,256]{2,1,0:T(8,128)(2,1)}, bf16[128,4096]{1,0:T(8,128)(2,1)}, bf16[4096,128]{1,0:T(8,128)(2,1)}) custom-call(s32[23]{0:T(128)} %concatenate.17.info, s32[32]{0:T(128)} %bitcast.32, bf16[240,256]{1,0:T(8,128)(2,1)} %get-tuple-element.227.refs_0_, bf16[240,512]{1,0:T(8,128)(2,1)} %get-tuple-element.228.refs_1_, ...), custom_call_target="tpu_custom_call" | custom-call | flops 8589934592 | bytes 1966080 | tf_op jit(solution)/shard_map/pallas_call | solution.py:375
  96.7 6.2 %all-to-all-start = ((bf16[16,80,256]{2,1,0:T(8,128)(2,1)}), bf16[16,80,256]{2,1,0:T(8,128)(2,1)S(1)}, u32[]{:S(2)}, u32[]{:S(2)}) async-start(bf16[16,80,256]{2,1,0:T(8,128)(2,1)} %get-tuple-element.220.refs_5_), calls=%async_computation | async-start | bytes 1310720 | tf_op jit(solution)/shard_map/all_to_all | solution.py:1015
  104.2 4.0 %shard_map.228 = (bf16[80,4096]{1,0:T(8,128)(2,1)}, bf16[4096,128]{1,0:T(8,128)(2,1)}, bf16[4096,128]{1,0:T(8,128)(2,1)}) custom-call(s32[23]{0:T(128)} %concatenate.17.info, s32[32]{0:T(128)} %bitcast.33, bf16[240,256]{1,0:T(8,128)(2,1)} %get-tuple-element.227.refs_0_, bf16[240,512]{1,0:T(8,128)(2,1)} %get-tuple-element.228.refs_1_, ...), custom_call_target="tpu_custom_call" | custom-call | bytes 6291456 | tf_op jit(solution)/shard_map/pallas_call | solution.py:375
  108.2 10.7 %collective-permute-done.24.refs_3_ = bf16[224,1280]{1,0:T(8,128)(2,1)S(1)} collective-permute-done((bf16[224,1280]{1,0:T(8,128)(2,1)S(1)}, bf16[224,1280]{1,0:T(8,128)(2,1)S(1)}, u32[]{:S(2)}, u32[]{:S(2)}) %collective-permute-start.24) | collective-permute-done | bytes 573472 | tf_op jit(solution)/shard_map/ppermute | solution.py:361
  121.4 12.0 %shard_map.229 = (bf16[256,1280]{1,0:T(8,128)(2,1)}, f32[256,1280]{1,0:T(8,128)}, bf16[1280,256]{1,0:T(8,128)(2,1)}, bf16[3,256,1280]{2,1,0:T(8,128)(2,1)}, bf16[256,1280]{1,0:T(8,128)(2,1)}) custom-call(s32[23]{0:T(128)} %concatenate.17.info, bf16[256,1280]{1,0:T(8,128)(2,1)} %bitcast.25, bf16[256,1280]{1,0:T(8,128)(2,1)} %bitcast.36, ...), custom_call_target="tpu_custom_call" | custom-call | flops 5033164800 | bytes 9830400 | tf_op jit(solution)/shard_map/pallas_call | solution.py:375
  133.6 6.3 %all-to-all-start.1 = ((bf16[16,80,256]{2,1,0:T(8,128)(2,1)}), bf16[16,80,256]{2,1,0:T(8,128)(2,1)S(1)}, u32[]{:S(2)}, u32[]{:S(2)}) async-start(bf16[16,80,256]{2,1,0:T(8,128)(2,1)} %bitcast.31), calls=%async_computation.1 | async-start | bytes 1310720 | tf_op jit(solution)/shard_map/all_to_all | solution.py:1039
  143.2 8.1 %shard_map.230 = (bf16[640,640]{1,0:T(8,128)(2,1)}, bf16[640,640]{1,0:T(8,128)(2,1)}, bf16[640,640]{1,0:T(8,128)(2,1)}, bf16[640,640]{1,0:T(8,128)(2,1)}, bf16[6...) custom-call(s32[23]{0:T(128)} %concatenate.17.info, bf16[3,256,1280]{2,1,0:T(8,128)(2,1)} %get-tuple-element.253.own, ...), custom_call_target="tpu_custom_call" | custom-call | flops 2516582400 | bytes 9830400 | tf_op jit(solution)/shard_map/pallas_call | solution.py:375
  151.4 4.1 %collective-permute-done.26.refs_5_ = bf16[224,1280]{1,0:T(8,128)(2,1)} collective-permute-done((bf16[224,1280]{1,0:T(8,128)(2,1)S(1)}, bf16[224,1280]{1,0:T(8,128)(2,1)}, u32[]{:S(2)}, u32[]{:S(2)}) %collective-permute-start.26) | collective-permute-done | bytes 573472 | tf_op jit(solution)/shard_map/ppermute | solution.py:361
  159.6 2.1 collective-permute-start.32
  162.4 34.4 %shard_map.231.grads = bf16[16,240,256]{2,1,0:T(8,128)(2,1)} custom-call(s32[23]{0:T(128)} %concatenate.17.info, s32[32]{0:T(128)} %bitcast.34, bf16[128,4096]{1,0:T(8,128)(2,1)} %get-tuple-element.243.refs_0_, bf16[4096,128]{1,0:T(8,128)(2,1)} %get-tuple-element.244.refs_1_, bf16[80,4096]{1,0:T(8,128)(2,1)} %get-tuple-element.237.refs_2_, ...), custom_call_target="tpu_custom_call" | custom-call | flops 21474836480 | bytes 3932160 | tf_op jit(solution)/shard_map/pallas_call | solution.py:375
  198.6 4.3 %all-to-all-start.2 = ((bf16[16,240,256]{2,1,0:T(8,128)(2,1)}), bf16[16,240,256]{2,1,0:T(8,128)(2,1)S(1)}, u32[]{:S(2)}, u32[]{:S(2)}) async-start(bf16[16,240,256]{2,1,0:T(8,128)(2,1)} %shard_map.231.grads), calls=%async_computation.2 | async-start | bytes 3932160 | tf_op jit(solution)/shard_map/all_to_all | solution.py:1094
  203.0 8.4 %shard_map.232 = (f32[256,640]{1,0:T(8,128)}, bf16[256,640]{1,0:T(8,128)(2,1)}) custom-call(s32[23]{0:T(128)} %concatenate.17.info, bf16[16,240,256]{2,1,0:T(8,128)(2,1)} %shard_map.231.grads, bf16[496,640]{1,0:T(8,128)(2,1)} %shard_map.221.refs_1_.refs_2_.own, bf16[496,640]{1,0:T(8,128)(2,1)} %copy-done, bf16[2048,1280]{1,0:T(8,128)(2,1)} %get-tuple-element.223.refs_0_, ...), custom_call_target="tpu_custom_call" | custom-call | flops 2516582400 | bytes 10485760 | tf_op jit(solution)/shard_map/pallas_call | solution.py:375
  212.8 4.4 %shard_map.233 = (bf16[320,640]{1,0:T(8,128)(2,1)}, bf16[320,640]{1,0:T(8,128)(2,1)}, bf16[320,640]{1,0:T(8,128)(2,1)}, bf16[320,640]{1,0:T(8,128)(2,1)}, bf16[3...) custom-call(s32[23]{0:T(128)} %concatenate.17.info, bf16[640,640]{1,0:T(8,128)(2,1)} %get-tuple-element.257.refs_0_, ...), custom_call_target="tpu_custom_call" | custom-call | bytes 2457600 | tf_op jit(solution)/shard_map/pallas_call | solution.py:375
  217.1 2.0 collective-permute-start.42
  221.9 1.8 collective-permute-start.39
  223.7 12.4 %collective-permute-done.42.refs_3_ = bf16[320,640]{1,0:T(8,128)(2,1)S(1)} collective-permute-done((bf16[320,640]{1,0:T(8,128)(2,1)}, bf16[320,640]{1,0:T(8,128)(2,1)S(1)}, u32[]{:S(2)}, u32[]{:S(2)}) %collective-permute-start.42) | collective-permute-done | bytes 409632 | tf_op jit(solution)/shard_map/ppermute | solution.py:361
  236.2 10.8 %collective-permute-done.43.refs_4_ = bf16[320,640]{1,0:T(8,128)(2,1)S(1)} collective-permute-done((bf16[320,640]{1,0:T(8,128)(2,1)}, bf16[320,640]{1,0:T(8,128)(2,1)S(1)}, u32[]{:S(2)}, u32[]{:S(2)}) %collective-permute-start.43) | collective-permute-done | bytes 409632 | tf_op jit(solution)/shard_map/ppermute | solution.py:361
  247.2 6.3 %collective-permute-done.39.refs_2_ = bf16[256,640]{1,0:T(8,128)(2,1)S(1)} collective-permute-done((bf16[256,640]{1,0:T(8,128)(2,1)S(1)}, bf16[256,640]{1,0:T(8,128)(2,1)S(1)}, u32[]{:S(2)}, u32[]{:S(2)}) %collective-permute-start.39) | collective-permute-done | bytes 327712 | tf_op jit(solution)/shard_map/ppermute | solution.py:361
  253.5 2.2 collective-permute-done.38.refs_1_
  257.8 2.8 shard_map.235
  260.6 4.6 %collective-permute-done.41.refs_4_ = bf16[256,640]{1,0:T(8,128)(2,1)S(1)} collective-permute-done((bf16[256,640]{1,0:T(8,128)(2,1)S(1)}, bf16[256,640]{1,0:T(8,128)(2,1)S(1)}, u32[]{:S(2)}, u32[]{:S(2)}) %collective-permute-start.41) | collective-permute-done | bytes 327712 | tf_op jit(solution)/shard_map/ppermute | solution.py:361
  266.2 3.4 shard_map.236.near
  274.6 2.9 collective-permute-done.48.refs_3_
  280.0 5.5 %collective-permute-done.50.refs_5_ = bf16[160,640]{1,0:T(8,128)(2,1)S(1)} collective-permute-done((bf16[160,640]{1,0:T(8,128)(2,1)S(1)}, bf16[160,640]{1,0:T(8,128)(2,1)S(1)}, u32[]{:S(2)}, u32[]{:S(2)}) %collective-permute-start.50) | collective-permute-done | bytes 204832 | tf_op jit(solution)/shard_map/ppermute | solution.py:361
  286.3 2.4 shard_map.237
  288.7 2.0 collective-permute-start.52
  291.2 3.0 collective-permute-done.52.refs_3_
  294.3 11.3 %shard_map.234 = bf16[256,1280]{1,0:T(8,128)(2,1)} custom-call(s32[23]{0:T(128)} %concatenate.17.info, bf16[256,1280]{1,0:T(8,128)(2,1)} %bitcast.26, bf16[16,240,256]{2,1,0:T(8,128)(2,1)} %copy-done.5, f32[256,1280]{1,0:T(8,128)} %get-tuple-element.265.grad_mid, bf16[496,640]{1,0:T(8,128)(2,1)} %shard_map.221.refs_1_.refs_2_.own, bf16[496,640]{1,0:T(8,128)(2,1)} %copy-done, ...), custom_call_target="tpu_custom_call" | custom-call | flops 2516582400 | bytes 9830400 | tf_op jit(solution)/shard_map/pallas_call | solution.py:375
  308.5 2.3 collective-permute-start.58
  311.5 9.3 %shard_map.238 = (f32[640,1280]{1,0:T(8,128)}, f32[640,1280]{1,0:T(8,128)}, f32[640,1280]{1,0:T(8,128)}, f32[640]{0:T(1024)}, f32[1,80]{1,0:T(1,128)}) custom-call(s32[23]{0:T(128)} %concatenate.17.info, bf16[5,256,640]{2,1,0:T(8,128)(2,1)} %shard_map.236.near, bf16[5,256,640]{2,1,0:T(8,128)(2,1)} %copy-done.63, bf16[256,640]{1,0:T(8,128)(2,1)} %copy-done.61, ...), custom_call_target="tpu_custom_call" | custom-call | flops 3145728000 | bytes 9830400 | tf_op jit(solution)/shard_map/pallas_call | solution.py:375
  320.9 2.5 collective-permute-start.60
  323.5 7.2 %collective-permute-done.60.refs_3_ = bf16[240,640]{1,0:T(8,128)(2,1)S(1)} collective-permute-done((bf16[240,640]{1,0:T(8,128)(2,1)S(1)}, bf16[240,640]{1,0:T(8,128)(2,1)S(1)}, u32[]{:S(2)}, u32[]{:S(2)}) %collective-permute-start.60) | collective-permute-done | bytes 307232 | tf_op jit(solution)/shard_map/ppermute | solution.py:361
  332.8 2.6 shard_map.239.near
  340.2 6.0 %shard_map.240 = (f32[640,128]{1,0:T(8,128)}, f32[640,1280]{1,0:T(8,128)}, f32[640,1280]{1,0:T(8,128)}, f32[640,1280]{1,0:T(8,128)}) custom-call(s32[23]{0:T(128)} %concatenate.17.info, bf16[5,240,640]{2,1,0:T(8,128)(2,1)} %shard_map.239.near, bf16[5,240,640]{2,1,0:T(8,128)(2,1)} %copy-done.6, bf16[640,1280]{1,0:T(8,128)(2,1)} %refs_10_.1), custom_call_target="tpu_custom_call" | custom-call | bytes 9830400 | tf_op jit(solution)/shard_map/pallas_call | solution.py:375
  349.4 4.0 %collective-permute-done.65.refs_2_ = bf16[112,640]{1,0:T(8,128)(2,1)S(1)} collective-permute-done((bf16[112,640]{1,0:T(8,128)(2,1)S(1)}, bf16[112,640]{1,0:T(8,128)(2,1)S(1)}, u32[]{:S(2)}, u32[]{:S(2)}) %collective-permute-start.65) | collective-permute-done | bytes 143392 | tf_op jit(solution)/shard_map/ppermute | solution.py:361
  355.9 4.8 %shard_map.241 = (f32[640,1280]{1,0:T(8,128)}, f32[640,1280]{1,0:T(8,128)}, f32[640,1280]{1,0:T(8,128)}, f32[640]{0:T(1024)}) custom-call(s32[23]{0:T(128)} %concatenate.17.info, bf16[240,640]{1,0:T(8,128)(2,1)} %copy-done.17, bf16[240,640]{1,0:T(8,128)(2,1)} %copy-done.16, ...), custom_call_target="tpu_custom_call", output_to_operand_aliasing={{0}: (12, {}), {1}: (13, {}), {2}: (14, {})} | custom-call | bytes 9830400 | tf_op jit(solution)/shard_map/pallas_call | solution.py:375
  (314 shorter events, 80.3 us)
Async XLA Ops:
  0.6 18.1 %collective-permute-start.1 = (bf16[256,1280]{1,0:T(8,128)(2,1)}, bf16[256,1280]{1,0:T(8,128)(2,1)}, u32[]{:S(2)}, u32[]{:S(2)}) collective-permute-start(bf16[256,1280]{1,0:T(8,128)(2,1)} %bitcast.22), channel_id=1, source_target_pairs={{0,4},{1,5},{2,6},{3,7},{4,12},{5,13},{6,14},{7,15},{8,0},{9,1},{1... | collective-permute-start | bytes 1966088 | tf_op jit(solution)/shard_map/ppermute | solution.py:361
  3.6 16.5 %collective-permute-start = (bf16[256,1280]{1,0:T(8,128)(2,1)}, bf16[256,1280]{1,0:T(8,128)(2,1)}, u32[]{:S(2)}, u32[]{:S(2)}) collective-permute-start(bf16[256,1280]{1,0:T(8,128)(2,1)} %bitcast.23), channel_id=1, source_target_pairs={{0,8},{1,9},{2,10},{3,11},{4,0},{5,1},{6,2},{7,3},{8,16},{9,17},{1... | collective-permute-start | bytes 1966088 | tf_op jit(solution)/shard_map/ppermute | solution.py:361
  4.8 11.7 %collective-permute-start.2 = (bf16[128,1280]{1,0:T(8,128)(2,1)S(1)}, bf16[128,1280]{1,0:T(8,128)(2,1)}, u32[]{:S(2)}, u32[]{:S(2)}) collective-permute-start(bf16[128,1280]{1,0:T(8,128)(2,1)S(1)} %constant_dynamic-slice_fusion.9), channel_id=1, source_target_pairs={{0,1},{1,0},{2,3},{3,2},{4,5},{5,4},{6,7},{7,6},{8,9},{9,8},{10,11... | collective-permute-start | bytes 983048 | tf_op jit(solution)/shard_map/ppermute | solution.py:361
  16.4 15.5 %collective-permute-start.5 = (bf16[496,640]{1,0:T(8,128)(2,1)}, bf16[496,640]{1,0:T(8,128)(2,1)S(1)}, u32[]{:S(2)}, u32[]{:S(2)}) collective-permute-start(bf16[496,640]{1,0:T(8,128)(2,1)} %shard_map.221.refs_1_.refs_2_.own), channel_id=1, source_target_pairs={{0,1},{1,0},{2,3},{3,2},{4,5},{5,4},{6,7},{7,6},{8,9},{9,8},{10,11... | collective-permute-start | bytes 1904648 | tf_op jit(solution)/shard_map/ppermute | solution.py:361
  20.1 17.9 %collective-permute-start.3 = (bf16[256,1280]{1,0:T(8,128)(2,1)}, bf16[256,1280]{1,0:T(8,128)(2,1)}, u32[]{:S(2)}, u32[]{:S(2)}) collective-permute-start(bf16[256,1280]{1,0:T(8,128)(2,1)} %collective-permute-done.refs_0_), channel_id=1, source_target_pairs={{0,8},{1,9},{2,10},{3,11},{4,0},{5,1},{6,2},{7,3},{8,16},{9,17},{1... | collective-permute-start | bytes 1966088 | tf_op jit(solution)/shard_map/ppermute | solution.py:361
  20.6 11.3 %collective-permute-start.6 = (bf16[128,1280]{1,0:T(8,128)(2,1)}, bf16[128,1280]{1,0:T(8,128)(2,1)S(1)}, u32[]{:S(2)}, u32[]{:S(2)}) collective-permute-start(bf16[128,1280]{1,0:T(8,128)(2,1)} %collective-permute-done.2.refs_3_), channel_id=1, source_target_pairs={{0,2},{1,3},{2,0},{3,1},{4,6},{5,7},{6,4},{7,5},{8,10},{9,11},{10,... | collective-permute-start | bytes 983048 | tf_op jit(solution)/shard_map/ppermute | solution.py:361
  20.6 17.5 %collective-permute-start.4 = (bf16[256,1280]{1,0:T(8,128)(2,1)}, bf16[256,1280]{1,0:T(8,128)(2,1)}, u32[]{:S(2)}, u32[]{:S(2)}) collective-permute-start(bf16[256,1280]{1,0:T(8,128)(2,1)} %collective-permute-done.1.refs_1_), channel_id=1, source_target_pairs={{0,4},{1,5},{2,6},{3,7},{4,12},{5,13},{6,14},{7,15},{8,0},{9,1},{1... | collective-permute-start | bytes 1966088 | tf_op jit(solution)/shard_map/ppermute | solution.py:361
  38.0 19.2 %collective-permute-start.9 = (bf16[288,1280]{1,0:T(8,128)(2,1)}, bf16[288,1280]{1,0:T(8,128)(2,1)}, u32[]{:S(2)}, u32[]{:S(2)}) collective-permute-start(bf16[288,1280]{1,0:T(8,128)(2,1)} %pad_maximum_fusion.2), channel_id=1, source_target_pairs={{0,1},{1,0},{2,3},{3,2},{4,5},{5,4},{6,7},{7,6},{8,9},{9,8},{10,11... | collective-permute-start | bytes 2211848 | tf_op jit(solution)/shard_map/ppermute | solution.py:361
  39.7 16.3 %collective-permute-start.7 = (bf16[256,1280]{1,0:T(8,128)(2,1)}, bf16[256,1280]{1,0:T(8,128)(2,1)S(1)}, u32[]{:S(2)}, u32[]{:S(2)}) collective-permute-start(bf16[256,1280]{1,0:T(8,128)(2,1)} %collective-permute-done.3.refs_0_), channel_id=1, source_target_pairs={{0,8},{1,9},{2,10},{3,11},{4,0},{5,1},{6,2},{7,3},{8,16},{9,17},{1... | collective-permute-start | bytes 1966088 | tf_op jit(solution)/shard_map/ppermute | solution.py:361
  41.2 16.0 %collective-permute-start.8 = (bf16[256,1280]{1,0:T(8,128)(2,1)}, bf16[256,1280]{1,0:T(8,128)(2,1)S(1)}, u32[]{:S(2)}, u32[]{:S(2)}) collective-permute-start(bf16[256,1280]{1,0:T(8,128)(2,1)} %collective-permute-done.4.refs_1_), channel_id=1, source_target_pairs={{0,4},{1,5},{2,6},{3,7},{4,12},{5,13},{6,14},{7,15},{8,0},{9,1},{1... | collective-permute-start | bytes 1966088 | tf_op jit(solution)/shard_map/ppermute | solution.py:361
  57.3 12.2 %collective-permute-start.13 = (bf16[288,1280]{1,0:T(8,128)(2,1)}, bf16[288,1280]{1,0:T(8,128)(2,1)S(1)}, u32[]{:S(2)}, u32[]{:S(2)}) collective-permute-start(bf16[288,1280]{1,0:T(8,128)(2,1)} %collective-permute-done.9.refs_4_), channel_id=1, source_target_pairs={{0,2},{1,3},{2,0},{3,1},{4,6},{5,7},{6,4},{7,5},{8,10},{9,11},{10,... | collective-permute-start | bytes 2211848 | tf_op jit(solution)/shard_map/ppermute | solution.py:361
  57.3 12.2 %collective-permute-start.12 = (bf16[160,1280]{1,0:T(8,128)(2,1)S(1)}, bf16[160,1280]{1,0:T(8,128)(2,1)S(1)}, u32[]{:S(2)}, u32[]{:S(2)}) collective-permute-start(bf16[160,1280]{1,0:T(8,128)(2,1)S(1)} %copy-done.30), channel_id=1, source_target_pairs={{0,1},{1,0},{2,3},{3,2},{4,5},{5,4},{6,7},{7,6},{8,9},{9,8},{10,11... | collective-permute-start | bytes 1228808 | tf_op jit(solution)/shard_map/ppermute | solution.py:361
  58.2 9.9 %collective-permute-start.11 = (bf16[128,1280]{1,0:T(8,128)(2,1)S(1)}, bf16[128,1280]{1,0:T(8,128)(2,1)S(1)}, u32[]{:S(2)}, u32[]{:S(2)}) collective-permute-start(bf16[128,1280]{1,0:T(8,128)(2,1)S(1)} %slice.51), channel_id=1, source_target_pairs={{0,4},{1,5},{2,6},{3,7},{4,12},{5,13},{6,14},{7,15},{8,0},{9,1},{1... | collective-permute-start | bytes 983048 | tf_op jit(solution)/shard_map/ppermute | solution.py:361
  59.7 9.8 %collective-permute-start.10 = (bf16[128,1280]{1,0:T(8,128)(2,1)S(1)}, bf16[128,1280]{1,0:T(8,128)(2,1)S(1)}, u32[]{:S(2)}, u32[]{:S(2)}) collective-permute-start(bf16[128,1280]{1,0:T(8,128)(2,1)S(1)} %slice.50), channel_id=1, source_target_pairs={{0,8},{1,9},{2,10},{3,11},{4,0},{5,1},{6,2},{7,3},{8,16},{9,17},{1... | collective-permute-start | bytes 983048 | tf_op jit(solution)/shard_map/ppermute | solution.py:361
  71.8 23.8 %collective-permute-start.20 = (bf16[384,1280]{1,0:T(8,128)(2,1)S(1)}, bf16[384,1280]{1,0:T(8,128)(2,1)S(1)}, u32[]{:S(2)}, u32[]{:S(2)}) collective-permute-start(bf16[384,1280]{1,0:T(8,128)(2,1)S(1)} %pad_maximum_fusion), channel_id=1, source_target_pairs={{0,1},{1,0},{2,3},{3,2},{4,5},{5,4},{6,7},{7,6},{8,9},{9,8},{10,11... | collective-permute-start | bytes 2949128 | tf_op jit(solution)/shard_map/ppermute | solution.py:361
  96.6 24.0 %collective-permute-start.22 = (bf16[2048,1280]{1,0:T(8,128)(2,1)}, bf16[2048,1280]{1,0:T(8,128)(2,1)}, u32[]{:S(2)}, u32[]{:S(2)}) collective-permute-start(bf16[2048,1280]{1,0:T(8,128)(2,1)} %get-tuple-element.223.refs_0_), channel_id=1, source_target_pairs={{0,2},{1,3},{2,0},{3,1},{4,6},{5,7},{6,4},{7,5},{8,10},{9,11},{10,... | collective-permute-start | bytes 15728648 | tf_op jit(solution)/shard_map/ppermute | solution.py:361
  96.7 23.8 %all-to-all-start = ((bf16[16,80,256]{2,1,0:T(8,128)(2,1)}), bf16[16,80,256]{2,1,0:T(8,128)(2,1)S(1)}, u32[]{:S(2)}, u32[]{:S(2)}) async-start(bf16[16,80,256]{2,1,0:T(8,128)(2,1)} %get-tuple-element.220.refs_5_), calls=%async_computation | async-start | bytes 1310720 | tf_op jit(solution)/shard_map/all_to_all | solution.py:1015
  102.9 17.6 %collective-permute-start.21 = (bf16[384,1280]{1,0:T(8,128)(2,1)}, bf16[384,1280]{1,0:T(8,128)(2,1)}, u32[]{:S(2)}, u32[]{:S(2)}) collective-permute-start(bf16[384,1280]{1,0:T(8,128)(2,1)} %copy-done.64), channel_id=1, source_target_pairs={{0,2},{1,3},{2,0},{3,1},{4,6},{5,7},{6,4},{7,5},{8,10},{9,11},{10,... | collective-permute-start | bytes 2949128 | tf_op jit(solution)/shard_map/ppermute | solution.py:361
  103.5 15.4 %collective-permute-start.23 = (bf16[256,1280]{1,0:T(8,128)(2,1)}, bf16[256,1280]{1,0:T(8,128)(2,1)S(1)}, u32[]{:S(2)}, u32[]{:S(2)}) collective-permute-start(bf16[256,1280]{1,0:T(8,128)(2,1)} %bitcast.35), channel_id=1, source_target_pairs={{0,2},{1,3},{2,0},{3,1},{4,6},{5,7},{6,4},{7,5},{8,10},{9,11},{10,... | collective-permute-start | bytes 1966088 | tf_op jit(solution)/shard_map/ppermute | solution.py:361
  103.6 15.3 %collective-permute-start.24 = (bf16[224,1280]{1,0:T(8,128)(2,1)S(1)}, bf16[224,1280]{1,0:T(8,128)(2,1)S(1)}, u32[]{:S(2)}, u32[]{:S(2)}) collective-permute-start(bf16[224,1280]{1,0:T(8,128)(2,1)S(1)} %copy-done.25), channel_id=1, source_target_pairs={{0,1},{1,0},{2,3},{3,2},{4,5},{5,4},{6,7},{7,6},{8,9},{9,8},{10,11... | collective-permute-start | bytes 1720328 | tf_op jit(solution)/shard_map/ppermute | solution.py:361
  120.6 12.9 %collective-permute-start.25 = (bf16[160,1280]{1,0:T(8,128)(2,1)S(1)}, bf16[160,1280]{1,0:T(8,128)(2,1)S(1)}, u32[]{:S(2)}, u32[]{:S(2)}) collective-permute-start(bf16[160,1280]{1,0:T(8,128)(2,1)S(1)} %copy-done.31), channel_id=1, source_target_pairs={{0,1},{1,0},{2,3},{3,2},{4,5},{5,4},{6,7},{7,6},{8,9},{9,8},{10,11... | collective-permute-start | bytes 1228808 | tf_op jit(solution)/shard_map/ppermute | solution.py:361
  133.6 22.9 %all-to-all-start.1 = ((bf16[16,80,256]{2,1,0:T(8,128)(2,1)}), bf16[16,80,256]{2,1,0:T(8,128)(2,1)S(1)}, u32[]{:S(2)}, u32[]{:S(2)}) async-start(bf16[16,80,256]{2,1,0:T(8,128)(2,1)} %bitcast.31), calls=%async_computation.1 | async-start | bytes 1310720 | tf_op jit(solution)/shard_map/all_to_all | solution.py:1039
  140.4 15.1 %collective-permute-start.26 = (bf16[224,1280]{1,0:T(8,128)(2,1)S(1)}, bf16[224,1280]{1,0:T(8,128)(2,1)}, u32[]{:S(2)}, u32[]{:S(2)}) collective-permute-start(bf16[224,1280]{1,0:T(8,128)(2,1)S(1)} %get-tuple-element.254), channel_id=1, source_target_pairs={{0,1},{1,0},{2,3},{3,2},{4,5},{5,4},{6,7},{7,6},{8,9},{9,8},{10,11... | collective-permute-start | bytes 1720328 | tf_op jit(solution)/shard_map/ppermute | solution.py:361
  157.3 39.5 %collective-permute-start.30 = (bf16[640,640]{1,0:T(8,128)(2,1)}, bf16[640,640]{1,0:T(8,128)(2,1)S(1)}, u32[]{:S(2)}, u32[]{:S(2)}) collective-permute-start(bf16[640,640]{1,0:T(8,128)(2,1)} %get-tuple-element.261), channel_id=1, source_target_pairs={{0,1},{1,0},{2,3},{3,2},{4,5},{5,4},{6,7},{7,6},{8,9},{9,8},{10,11... | collective-permute-start | bytes 2457608 | tf_op jit(solution)/shard_map/ppermute | solution.py:361
  158.6 38.2 %collective-permute-start.31 = (bf16[640,640]{1,0:T(8,128)(2,1)}, bf16[640,640]{1,0:T(8,128)(2,1)S(1)}, u32[]{:S(2)}, u32[]{:S(2)}) collective-permute-start(bf16[640,640]{1,0:T(8,128)(2,1)} %get-tuple-element.262), channel_id=1, source_target_pairs={{0,4},{1,5},{2,6},{3,7},{4,0},{5,1},{6,2},{7,3},{8,12},{9,13},{10,... | collective-permute-start | bytes 2457608 | tf_op jit(solution)/shard_map/ppermute | solution.py:361
  159.6 38.1 %collective-permute-start.32 = (bf16[640,640]{1,0:T(8,128)(2,1)}, bf16[640,640]{1,0:T(8,128)(2,1)S(1)}, u32[]{:S(2)}, u32[]{:S(2)}) collective-permute-start(bf16[640,640]{1,0:T(8,128)(2,1)} %get-tuple-element.263), channel_id=1, source_target_pairs={{0,8},{1,9},{2,10},{3,11},{4,12},{5,13},{6,14},{7,15},{8,0},{9,1},... | collective-permute-start | bytes 2457608 | tf_op jit(solution)/shard_map/ppermute | solution.py:361
  161.7 37.0 %collective-permute-start.29 = (bf16[352,1280]{1,0:T(8,128)(2,1)S(1)}, bf16[352,1280]{1,0:T(8,128)(2,1)S(1)}, u32[]{:S(2)}, u32[]{:S(2)}) collective-permute-start(bf16[352,1280]{1,0:T(8,128)(2,1)S(1)} %copy-done.12), channel_id=1, source_target_pairs={{0,1},{1,0},{2,3},{3,2},{4,5},{5,4},{6,7},{7,6},{8,9},{9,8},{10,11... | collective-permute-start | bytes 2703368 | tf_op jit(solution)/shard_map/ppermute | solution.py:361
  198.6 67.5 %all-to-all-start.2 = ((bf16[16,240,256]{2,1,0:T(8,128)(2,1)}), bf16[16,240,256]{2,1,0:T(8,128)(2,1)S(1)}, u32[]{:S(2)}, u32[]{:S(2)}) async-start(bf16[16,240,256]{2,1,0:T(8,128)(2,1)} %shard_map.231.grads), calls=%async_computation.2 | async-start | bytes 3932160 | tf_op jit(solution)/shard_map/all_to_all | solution.py:1094
  211.4 10.4 %collective-permute-start.33 = (bf16[256,640]{1,0:T(8,128)(2,1)}, bf16[256,640]{1,0:T(8,128)(2,1)S(1)}, u32[]{:S(2)}, u32[]{:S(2)}) collective-permute-start(bf16[256,640]{1,0:T(8,128)(2,1)} %get-tuple-element.282), channel_id=1, source_target_pairs={{0,1},{1,0},{2,3},{3,2},{4,5},{5,4},{6,7},{7,6},{8,9},{9,8},{10,11... | collective-permute-start | bytes 983048 | tf_op jit(solution)/shard_map/ppermute | solution.py:361
  217.1 19.0 %collective-permute-start.42 = (bf16[320,640]{1,0:T(8,128)(2,1)}, bf16[320,640]{1,0:T(8,128)(2,1)S(1)}, u32[]{:S(2)}, u32[]{:S(2)}) collective-permute-start(bf16[320,640]{1,0:T(8,128)(2,1)} %get-tuple-element.289), channel_id=1, source_target_pairs={{0,4},{1,5},{2,6},{3,7},{4,0},{5,1},{6,2},{7,3},{8,12},{9,13},{10,... | collective-permute-start | bytes 1228808 | tf_op jit(solution)/shard_map/ppermute | solution.py:361
  219.2 27.8 %collective-permute-start.43 = (bf16[320,640]{1,0:T(8,128)(2,1)}, bf16[320,640]{1,0:T(8,128)(2,1)S(1)}, u32[]{:S(2)}, u32[]{:S(2)}) collective-permute-start(bf16[320,640]{1,0:T(8,128)(2,1)} %get-tuple-element.290), channel_id=1, source_target_pairs={{0,8},{1,9},{2,10},{3,11},{4,12},{5,13},{6,14},{7,15},{8,0},{9,1},... | collective-permute-start | bytes 1228808 | tf_op jit(solution)/shard_map/ppermute | solution.py:361
  220.6 26.5 %collective-permute-start.44 = (bf16[320,640]{1,0:T(8,128)(2,1)}, bf16[320,640]{1,0:T(8,128)(2,1)S(1)}, u32[]{:S(2)}, u32[]{:S(2)}) collective-permute-start(bf16[320,640]{1,0:T(8,128)(2,1)} %get-tuple-element.291), channel_id=1, source_target_pairs={{0,1},{1,0},{2,3},{3,2},{4,5},{5,4},{6,7},{7,6},{8,9},{9,8},{10,11... | collective-permute-start | bytes 1228808 | tf_op jit(solution)/shard_map/ppermute | solution.py:361
  221.9 31.6 %collective-permute-start.39 = (bf16[256,640]{1,0:T(8,128)(2,1)S(1)}, bf16[256,640]{1,0:T(8,128)(2,1)S(1)}, u32[]{:S(2)}, u32[]{:S(2)}) collective-permute-start(bf16[256,640]{1,0:T(8,128)(2,1)S(1)} %add_convert_fusion.refs_0_), channel_id=1, source_target_pairs={{0,4},{1,5},{2,6},{3,7},{4,12},{5,13},{6,14},{7,15},{8,0},{9,1},{1... | collective-permute-start | bytes 983048 | tf_op jit(solution)/shard_map/ppermute | solution.py:361
  223.7 42.4 %collective-permute-start.37 = (bf16[352,1280]{1,0:T(8,128)(2,1)S(1)}, bf16[352,1280]{1,0:T(8,128)(2,1)}, u32[]{:S(2)}, u32[]{:S(2)}) collective-permute-start(bf16[352,1280]{1,0:T(8,128)(2,1)S(1)} %collective-permute-done.29.refs_6_), channel_id=1, source_target_pairs={{0,2},{1,3},{2,0},{3,1},{4,6},{5,7},{6,4},{7,5},{8,10},{9,11},{10,... | collective-permute-start | bytes 2703368 | tf_op jit(solution)/shard_map/ppermute | solution.py:361
  236.2 21.1 %collective-permute-start.35 = (bf16[160,1280]{1,0:T(8,128)(2,1)S(1)}, bf16[160,1280]{1,0:T(8,128)(2,1)S(1)}, u32[]{:S(2)}, u32[]{:S(2)}) collective-permute-start(bf16[160,1280]{1,0:T(8,128)(2,1)S(1)} %copy-done.27), channel_id=1, source_target_pairs={{0,2},{1,3},{2,0},{3,1},{4,6},{5,7},{6,4},{7,5},{8,10},{9,11},{10,... | collective-permute-start | bytes 1228808 | tf_op jit(solution)/shard_map/ppermute | solution.py:361
  247.2 13.4 %collective-permute-start.34 = (bf16[224,1280]{1,0:T(8,128)(2,1)S(1)}, bf16[224,1280]{1,0:T(8,128)(2,1)S(1)}, u32[]{:S(2)}, u32[]{:S(2)}) collective-permute-start(bf16[224,1280]{1,0:T(8,128)(2,1)S(1)} %copy-done.22), channel_id=1, source_target_pairs={{0,2},{1,3},{2,0},{3,1},{4,6},{5,7},{6,4},{7,5},{8,10},{9,11},{10,... | collective-permute-start | bytes 1720328 | tf_op jit(solution)/shard_map/ppermute | solution.py:361
  269.6 36.0 %collective-permute-start.45 = (bf16[5,256,640]{2,1,0:T(8,128)(2,1)}, bf16[5,256,640]{2,1,0:T(8,128)(2,1)S(1)}, u32[]{:S(2)}, u32[]{:S(2)}) collective-permute-start(bf16[5,256,640]{2,1,0:T(8,128)(2,1)} %shard_map.236.near), channel_id=1, source_target_pairs={{0,2},{1,3},{2,0},{3,1},{4,6},{5,7},{6,4},{7,5},{8,10},{9,11},{10,... | collective-permute-start | bytes 4915208 | tf_op jit(solution)/shard_map/ppermute | solution.py:361
  271.3 17.3 %collective-permute-start.46 = (bf16[256,640]{1,0:T(8,128)(2,1)S(1)}, bf16[256,640]{1,0:T(8,128)(2,1)S(1)}, u32[]{:S(2)}, u32[]{:S(2)}) collective-permute-start(bf16[256,640]{1,0:T(8,128)(2,1)S(1)} %copy-done.40), channel_id=1, source_target_pairs={{0,8},{1,9},{2,10},{3,11},{4,0},{5,1},{6,2},{7,3},{8,16},{9,17},{1... | collective-permute-start | bytes 983048 | tf_op jit(solution)/shard_map/ppermute | solution.py:361
  271.7 17.0 %collective-permute-start.47 = (bf16[256,640]{1,0:T(8,128)(2,1)}, bf16[256,640]{1,0:T(8,128)(2,1)S(1)}, u32[]{:S(2)}, u32[]{:S(2)}) collective-permute-start(bf16[256,640]{1,0:T(8,128)(2,1)} %copy-done.37), channel_id=1, source_target_pairs={{0,4},{1,5},{2,6},{3,7},{4,12},{5,13},{6,14},{7,15},{8,0},{9,1},{1... | collective-permute-start | bytes 983048 | tf_op jit(solution)/shard_map/ppermute | solution.py:361
  290.7 14.9 %collective-permute-start.53 = (bf16[256,640]{1,0:T(8,128)(2,1)S(1)}, bf16[256,640]{1,0:T(8,128)(2,1)S(1)}, u32[]{:S(2)}, u32[]{:S(2)}) collective-permute-start(bf16[256,640]{1,0:T(8,128)(2,1)S(1)} %collective-permute-done.46.refs_0_), channel_id=1, source_target_pairs={{0,2},{1,3},{2,0},{3,1},{4,6},{5,7},{6,4},{7,5},{8,10},{9,11},{10,... | collective-permute-start | bytes 983048 | tf_op jit(solution)/shard_map/ppermute | solution.py:361
  290.7 14.9 %collective-permute-start.54 = (bf16[256,640]{1,0:T(8,128)(2,1)S(1)}, bf16[256,640]{1,0:T(8,128)(2,1)S(1)}, u32[]{:S(2)}, u32[]{:S(2)}) collective-permute-start(bf16[256,640]{1,0:T(8,128)(2,1)S(1)} %collective-permute-done.47.refs_1_), channel_id=1, source_target_pairs={{0,2},{1,3},{2,0},{3,1},{4,6},{5,7},{6,4},{7,5},{8,10},{9,11},{10,... | collective-permute-start | bytes 983048 | tf_op jit(solution)/shard_map/ppermute | solution.py:361
  291.2 16.6 %collective-permute-start.57 = (bf16[240,640]{1,0:T(8,128)(2,1)}, bf16[240,640]{1,0:T(8,128)(2,1)S(1)}, u32[]{:S(2)}, u32[]{:S(2)}) collective-permute-start(bf16[240,640]{1,0:T(8,128)(2,1)} %get-tuple-element.312), channel_id=1, source_target_pairs={{0,16},{1,17},{2,18},{3,19},{4,20},{5,21},{6,22},{7,23},{8,24},{9,... | collective-permute-start | bytes 921608 | tf_op jit(solution)/shard_map/ppermute | solution.py:361
  294.2 11.3 %collective-permute-start.51 = (bf16[128,640]{1,0:T(8,128)(2,1)S(1)}, bf16[128,640]{1,0:T(8,128)(2,1)S(1)}, u32[]{:S(2)}, u32[]{:S(2)}) collective-permute-start(bf16[128,640]{1,0:T(8,128)(2,1)S(1)} %slice.52), channel_id=1, source_target_pairs={{0,8},{1,9},{2,10},{3,11},{4,0},{5,1},{6,2},{7,3},{8,16},{9,17},{1... | collective-permute-start | bytes 491528 | tf_op jit(solution)/shard_map/ppermute | solution.py:361
  307.9 12.9 %collective-permute-start.59 = (bf16[240,640]{1,0:T(8,128)(2,1)S(1)}, bf16[240,640]{1,0:T(8,128)(2,1)S(1)}, u32[]{:S(2)}, u32[]{:S(2)}) collective-permute-start(bf16[240,640]{1,0:T(8,128)(2,1)S(1)} %add_convert_fusion.1.refs_0_), channel_id=1, source_target_pairs={{0,4},{1,5},{2,6},{3,7},{4,12},{5,13},{6,14},{7,15},{8,0},{9,1},{1... | collective-permute-start | bytes 921608 | tf_op jit(solution)/shard_map/ppermute | solution.py:361
  308.5 12.3 %collective-permute-start.58 = (bf16[240,640]{1,0:T(8,128)(2,1)S(1)}, bf16[240,640]{1,0:T(8,128)(2,1)S(1)}, u32[]{:S(2)}, u32[]{:S(2)}) collective-permute-start(bf16[240,640]{1,0:T(8,128)(2,1)S(1)} %add_convert_fusion.1.refs_0_), channel_id=1, source_target_pairs={{0,8},{1,9},{2,10},{3,11},{4,0},{5,1},{6,2},{7,3},{8,16},{9,17},{1... | collective-permute-start | bytes 921608 | tf_op jit(solution)/shard_map/ppermute | solution.py:361
  320.9 9.8 %collective-permute-start.60 = (bf16[240,640]{1,0:T(8,128)(2,1)S(1)}, bf16[240,640]{1,0:T(8,128)(2,1)S(1)}, u32[]{:S(2)}, u32[]{:S(2)}) collective-permute-start(bf16[240,640]{1,0:T(8,128)(2,1)S(1)} %collective-permute-done.58.refs_1_), channel_id=1, source_target_pairs={{0,8},{1,9},{2,10},{3,11},{4,0},{5,1},{6,2},{7,3},{8,16},{9,17},{1... | collective-permute-start | bytes 921608 | tf_op jit(solution)/shard_map/ppermute | solution.py:361
  335.4 10.7 %collective-permute-start.61 = (bf16[240,640]{1,0:T(8,128)(2,1)}, bf16[240,640]{1,0:T(8,128)(2,1)S(1)}, u32[]{:S(2)}, u32[]{:S(2)}) collective-permute-start(bf16[240,640]{1,0:T(8,128)(2,1)} %copy-done.45), channel_id=1, source_target_pairs={{0,8},{1,9},{2,10},{3,11},{4,0},{5,1},{6,2},{7,3},{8,16},{9,17},{1... | collective-permute-start | bytes 921608 | tf_op jit(solution)/shard_map/ppermute | solution.py:361
  337.1 9.6 %collective-permute-start.63 = (bf16[240,640]{1,0:T(8,128)(2,1)}, bf16[240,640]{1,0:T(8,128)(2,1)S(1)}, u32[]{:S(2)}, u32[]{:S(2)}) collective-permute-start(bf16[240,640]{1,0:T(8,128)(2,1)} %copy-done.46), channel_id=1, source_target_pairs={{0,4},{1,5},{2,6},{3,7},{4,12},{5,13},{6,14},{7,15},{8,0},{9,1},{1... | collective-permute-start | bytes 921608 | tf_op jit(solution)/shard_map/ppermute | solution.py:361
  (110 other events, 833.1 us)

commit v4 on v3

--- a/solution.py
+++ b/solution.py
@@ -525,9 +525,21 @@
             weights = jnp.exp(scores_of(masked, i, j)).astype(BF)
             return acc + mm(values[:, block_at(j)], weights)
 
+        def tile(low, first):
+            keys_at = pl.ds(pl.multiple_of(i * BLOCK + low, BLOCK // 2), BLOCK // 2)
+            queries_at = pl.ds(pl.multiple_of(i * BLOCK + first, BLOCK // 2), BLOCK - first)
+            scores = mm(keys[keys_at, :], queries[:, queries_at])
+            local = key_at[: BLOCK // 2, first:] + low
+            allowed = (local <= query_at[: BLOCK // 2, first:]) & (i * BLOCK + local < length)
+            weights = jnp.exp(jnp.where(allowed, scores, NEG)).astype(BF)
+            return mm(values[:, keys_at], weights)
+
         split = jnp.minimum(i, length // BLOCK)
         acc = lax.fori_loop(0, split, functools.partial(step, False), jnp.zeros((HEAD + 16, BLOCK), F32))
-        acc = lax.fori_loop(split, i + 1, functools.partial(step, True), acc)
+        acc = lax.fori_loop(split, i, functools.partial(step, True), acc)
+        acc += tile(0, 0)
+        later = acc[:, BLOCK // 2 :] + tile(BLOCK // 2, BLOCK // 2)
+        acc = jnp.concatenate([acc[:, : BLOCK // 2], later], axis=1)
         exact = jnp.sum(shift.astype(F32), axis=0, keepdims=True)
         return jnp.minimum(least, finish(i, -exact, acc))
 
@@ -597,22 +609,29 @@
         dk[...] = jnp.zeros_like(dk)
         dv[...] = jnp.zeros_like(dv)
 
-        def step(masked, i, carry):
-            here = block_at(i)
-            probs = jnp.exp(mm(k_n[there, :], q_t[:, here]))
+        def tile(masked, i, low, first, size):
+            keys = pl.ds(pl.multiple_of(j * BLOCK + low, BLOCK // 2), size)
+            here = pl.ds(pl.multiple_of(i * BLOCK + first, BLOCK // 2), BLOCK - first)
+            probs = jnp.exp(mm(k_n[keys, :], q_t[:, here]))
             if masked:
-                key_pos = j * BLOCK + key_at
-                allowed = (key_pos <= i * BLOCK + query_at) & (key_pos < length)
+                key_pos = j * BLOCK + low + key_at[:size, first:]
+                allowed = (key_pos <= i * BLOCK + query_at[:size, first:]) & (key_pos < length)
                 probs = jnp.where(allowed, probs, 0.0)
             probs = probs.astype(BF)
-            grad_scores = probs * mm(v_n[there, :], g_t[:, here]).astype(BF)
-            dv[...] += mm(probs, g_n[here, :])
-            dk[...] += mm(grad_scores, q_n[here, :])
-            dq_t[:, here] += mm(k_t[:, there], grad_scores)
+            grad_scores = probs * mm(v_n[keys, :], g_t[:, here]).astype(BF)
+            rows = slice(low, low + size)
+            dv[rows] += mm(probs, g_n[here, :])
+            dk[rows] += mm(grad_scores, q_n[here, :])
+            dq_t[:, here] += mm(k_t[:, keys], grad_scores)
+
+        def step(masked, i, carry):
+            tile(masked, i, 0, 0, BLOCK)
             return carry
 
+        tile(True, j, 0, 0, BLOCK // 2)
+        tile(True, j, BLOCK // 2, BLOCK // 2, BLOCK // 2)
         split = jnp.where((j + 1) * BLOCK <= length, j + 1, blocks)
-        lax.fori_loop(j, split, functools.partial(step, True), 0)
+        lax.fori_loop(j + 1, split, functools.partial(step, True), 0)
         lax.fori_loop(split, blocks, functools.partial(step, False), 0)
         for part in range(BLOCK // SPAN):
             row = dealt[j * (BLOCK // SPAN) + part]
@@ -972,7 +991,7 @@
     forth2, back2 = send(forth1, FORTH), send(back1, BACK)
     rows_out = weight_rows(after((w_output, w_expand, w_contract), forth1), core)
     rows_back = weight_rows(after((w_query, w_key, w_value), forth1), core)
-    chunks = [rows_out[128:416], rows_out[416:576], rows_out[576:]]
+    chunks = [rows_out[128:448], rows_out[448:624], rows_out[624:]]
     chunks += [rows_back[:224], rows_back[224:384], rows_back[384:608], rows_back[608:]]
     passed.append(send(direct[0], CORE_SWAP))
     forth2, back2, other, passed[0], *chunks = after((forth2, back2, other, passed[0], *chunks))
@@ -1090,7 +1109,7 @@
         ],
         cost=(5 * total * total * 256, 6 * total * 160, total * total // 2),
     )[0]
-    grads, direct_back[3], *came = after((grads, direct_back[3], *came))
+    grads, *came = after((grads, *came))
     returned = lax.all_to_all(grads, "ctx", 0, 0)
     keep, away = call(
         weight_kernel,

time: 367 us -> 362 us (0.986)
  Pallas kernels: 156 us -> 151 us
    pallas_call x21, Pallas kernels: 156 us -> 151 us  [call(): pl.pallas_call(body, out_shape=[jax.ShapeDtypeStruct(shape, kind) for sha...]
    unnamed x168 -> x164, local copies, waits for them, and re-layouts: 14.4 us -> 12.3 us
  transfers between devices with their start and end apart: 74 -> 74, of which waited for: 31 -> 31; matrix products, arithmetic and copies ran while one was open for 4% -> 4% of each run, Pallas kernels for 40% -> 39%
where the time goes in v4:
time: 362 us; the launch traced here: 356 us
  Pallas kernels  151 us (42%)
  waiting for transfers between devices  102 us (28%)
  starting transfers between devices  74.8 us (21%)
  local copies, waits for them, and re-layouts  22.5 us (6%)
    pallas_call x21, Pallas kernels, call(): pl.pallas_call(body, out_shape=[jax.ShapeDtypeStruct(shape, kind) for sha...  151 us
    ppermute x71, waiting for transfers between devices, send(): return lax.ppermute(value, AXES, moves)  101 us
    ppermute x71, starting transfers between devices, send(): return lax.ppermute(value, AXES, moves)  58.3 us
    unnamed x164, local copies, waits for them, and re-layouts  12.3 us
  transfers between devices with their start and end apart: 74, of which 31 were waited for; matrix products, arithmetic and copies ran while one was open for 4% of the time, Pallas kernels for 39%

profile of v4, /device:TPU:0, one launch (start us, length us, event | category | flops | bytes accessed | tf_op | source)
XLA Modules:
  0.0 356.5 jit_solution(6397804463444453317)
XLA Ops:
  0.6 3.0 collective-permute-start.1
  4.8 2.0 collective-permute-start.2
  11.3 5.1 %shard_map.221.refs_1_.refs_2_.own = bf16[496,640]{1,0:T(8,128)(2,1)} custom-call(s32[23]{0:T(128)} %concatenate.17.info, bf16[640,1280]{1,0:T(8,128)(2,1)} %refs_0_.3, bf16[640,1280]{1,0:T(8,128)(2,1)} %refs_1_.3, bf16[640,1280]{1,0:T(8,128)(2,1)} %refs_2_.3, bf16[1,640]{1,0:T(2,128)(2,1)} %broadcast_in_dim.20.gain_a.refs_8_, ...), custom_call_target="tpu_custom_call" | custom-call | flops 786432000 | bytes 4915200 | tf_op jit(solution)/shard_map/pallas_call | solution.py:375
  16.6 2.1 collective-permute-done.1.refs_1_
  32.2 5.6 %collective-permute-done.4.refs_1_ = bf16[256,1280]{1,0:T(8,128)(2,1)} collective-permute-done((bf16[256,1280]{1,0:T(8,128)(2,1)S(1)}, bf16[256,1280]{1,0:T(8,128)(2,1)}, u32[]{:S(2)}, u32[]{:S(2)}) %collective-permute-start.4) | collective-permute-done | bytes 655392 | tf_op jit(solution)/shard_map/ppermute | solution.py:361
  42.8 3.5 shard_map.222
  46.3 4.3 %shard_map.223 = (bf16[2048,1280]{1,0:T(8,128)(2,1)}, bf16[240,512]{1,0:T(8,128)(2,1)}, bf16[240,512]{1,0:T(8,128)(2,1)}) custom-call(s32[23]{0:T(128)} %concatenate.17.info, bf16[256,1280]{1,0:T(8,128)(2,1)} %collective-permute-done.refs_0_, bf16[256,1280]{1,0:T(8,128)(2,1)} %copy-done.17, ...), custom_call_target="tpu_custom_call", output_to_operand_aliasing={{0}: (6, {})} | custom-call | flops 629145600 | bytes 2621440 | tf_op jit(solution)/shard_map/pallas_call | solution.py:375
  50.6 4.2 %shard_map.224 = (bf16[2048,1280]{1,0:T(8,128)(2,1)}, bf16[240,512]{1,0:T(8,128)(2,1)}, bf16[240,512]{1,0:T(8,128)(2,1)}) custom-call(s32[23]{0:T(128)} %concatenate.17.info, bf16[256,1280]{1,0:T(8,128)(2,1)} %collective-permute-done.3.refs_0_, bf16[256,1280]{1,0:T(8,128)(2,1)} %collective-permute-done.4.refs_1_, ...), custom_call_target="tpu_custom_call", output_to_operand_aliasing={{0}: (6, {})} | custom-call | flops 629145600 | bytes 2621440 | tf_op jit(solution)/shard_map/pallas_call | solution.py:375
  62.1 4.3 %shard_map.225 = (bf16[2048,1280]{1,0:T(8,128)(2,1)}, bf16[240,512]{1,0:T(8,128)(2,1)}, bf16[240,512]{1,0:T(8,128)(2,1)}) custom-call(s32[23]{0:T(128)} %concatenate.17.info, bf16[256,1280]{1,0:T(8,128)(2,1)} %copy-done.7, bf16[256,1280]{1,0:T(8,128)(2,1)} %copy-done.8, ...), custom_call_target="tpu_custom_call", output_to_operand_aliasing={{0}: (6, {})} | custom-call | flops 629145600 | bytes 2621440 | tf_op jit(solution)/shard_map/pallas_call | solution.py:375
  66.4 3.2 collective-permute-done.11.refs_1_
  72.3 3.4 shard_map.226
  78.4 15.3 %shard_map.227 = (bf16[16,80,256]{2,1,0:T(8,128)(2,1)}, bf16[128,4096]{1,0:T(8,128)(2,1)}, bf16[4096,128]{1,0:T(8,128)(2,1)}) custom-call(s32[23]{0:T(128)} %concatenate.17.info, s32[32]{0:T(128)} %bitcast.32, bf16[240,256]{1,0:T(8,128)(2,1)} %get-tuple-element.226.refs_0_, bf16[240,512]{1,0:T(8,128)(2,1)} %get-tuple-element.227.refs_1_, ...), custom_call_target="tpu_custom_call" | custom-call | flops 8589934592 | bytes 1966080 | tf_op jit(solution)/shard_map/pallas_call | solution.py:375
  93.7 3.7 %collective-permute-done.20.refs_6_ = bf16[336,1280]{1,0:T(8,128)(2,1)S(1)} collective-permute-done((bf16[336,1280]{1,0:T(8,128)(2,1)S(1)}, bf16[336,1280]{1,0:T(8,128)(2,1)S(1)}, u32[]{:S(2)}, u32[]{:S(2)}) %collective-permute-start.20) | collective-permute-done | bytes 860192 | tf_op jit(solution)/shard_map/ppermute | solution.py:361
  98.3 6.3 %all-to-all-start = ((bf16[16,80,256]{2,1,0:T(8,128)(2,1)}), bf16[16,80,256]{2,1,0:T(8,128)(2,1)S(1)}, u32[]{:S(2)}, u32[]{:S(2)}) async-start(bf16[16,80,256]{2,1,0:T(8,128)(2,1)} %get-tuple-element.219.refs_5_), calls=%async_computation | async-start | bytes 1310720 | tf_op jit(solution)/shard_map/all_to_all | solution.py:1034
  106.8 4.0 %shard_map.228 = (bf16[80,4096]{1,0:T(8,128)(2,1)}, bf16[4096,128]{1,0:T(8,128)(2,1)}, bf16[4096,128]{1,0:T(8,128)(2,1)}) custom-call(s32[23]{0:T(128)} %concatenate.17.info, s32[32]{0:T(128)} %bitcast.33, bf16[240,256]{1,0:T(8,128)(2,1)} %get-tuple-element.226.refs_0_, bf16[240,512]{1,0:T(8,128)(2,1)} %get-tuple-element.227.refs_1_, ...), custom_call_target="tpu_custom_call" | custom-call | bytes 6291456 | tf_op jit(solution)/shard_map/pallas_call | solution.py:375
  110.8 9.8 %collective-permute-done.24.refs_3_ = bf16[224,1280]{1,0:T(8,128)(2,1)S(1)} collective-permute-done((bf16[224,1280]{1,0:T(8,128)(2,1)S(1)}, bf16[224,1280]{1,0:T(8,128)(2,1)S(1)}, u32[]{:S(2)}, u32[]{:S(2)}) %collective-permute-start.24) | collective-permute-done | bytes 573472 | tf_op jit(solution)/shard_map/ppermute | solution.py:361
  124.0 12.1 %shard_map.229 = (bf16[256,1280]{1,0:T(8,128)(2,1)}, f32[256,1280]{1,0:T(8,128)}, bf16[1280,256]{1,0:T(8,128)(2,1)}, bf16[3,256,1280]{2,1,0:T(8,128)(2,1)}, bf16[256,1280]{1,0:T(8,128)(2,1)}) custom-call(s32[23]{0:T(128)} %concatenate.17.info, bf16[256,1280]{1,0:T(8,128)(2,1)} %bitcast.25, bf16[256,1280]{1,0:T(8,128)(2,1)} %bitcast.36, ...), custom_call_target="tpu_custom_call" | custom-call | flops 5033164800 | bytes 9830400 | tf_op jit(solution)/shard_map/pallas_call | solution.py:375
  136.1 6.0 %all-to-all-start.1 = ((bf16[16,80,256]{2,1,0:T(8,128)(2,1)}), bf16[16,80,256]{2,1,0:T(8,128)(2,1)S(1)}, u32[]{:S(2)}, u32[]{:S(2)}) async-start(bf16[16,80,256]{2,1,0:T(8,128)(2,1)} %bitcast.31), calls=%async_computation.1 | async-start | bytes 1310720 | tf_op jit(solution)/shard_map/all_to_all | solution.py:1058
  146.1 8.1 %shard_map.230 = (bf16[640,640]{1,0:T(8,128)(2,1)}, bf16[640,640]{1,0:T(8,128)(2,1)}, bf16[640,640]{1,0:T(8,128)(2,1)}, bf16[640,640]{1,0:T(8,128)(2,1)}, bf16[6...) custom-call(s32[23]{0:T(128)} %concatenate.17.info, bf16[3,256,1280]{2,1,0:T(8,128)(2,1)} %get-tuple-element.252.own, ...), custom_call_target="tpu_custom_call" | custom-call | flops 2516582400 | bytes 9830400 | tf_op jit(solution)/shard_map/pallas_call | solution.py:375
  154.2 3.6 %collective-permute-done.26.refs_5_ = bf16[224,1280]{1,0:T(8,128)(2,1)} collective-permute-done((bf16[224,1280]{1,0:T(8,128)(2,1)S(1)}, bf16[224,1280]{1,0:T(8,128)(2,1)}, u32[]{:S(2)}, u32[]{:S(2)}) %collective-permute-start.26) | collective-permute-done | bytes 573472 | tf_op jit(solution)/shard_map/ppermute | solution.py:361
  160.8 2.1 collective-permute-start.31
  162.9 31.4 %shard_map.231.grads = bf16[16,240,256]{2,1,0:T(8,128)(2,1)} custom-call(s32[23]{0:T(128)} %concatenate.17.info, s32[32]{0:T(128)} %bitcast.34, bf16[128,4096]{1,0:T(8,128)(2,1)} %get-tuple-element.242.refs_0_, bf16[4096,128]{1,0:T(8,128)(2,1)} %get-tuple-element.243.refs_1_, bf16[80,4096]{1,0:T(8,128)(2,1)} %get-tuple-element.236.refs_2_, ...), custom_call_target="tpu_custom_call" | custom-call | flops 21474836480 | bytes 3932160 | tf_op jit(solution)/shard_map/pallas_call | solution.py:375
  194.3 4.2 %all-to-all-start.2 = ((bf16[16,240,256]{2,1,0:T(8,128)(2,1)}), bf16[16,240,256]{2,1,0:T(8,128)(2,1)S(1)}, u32[]{:S(2)}, u32[]{:S(2)}) async-start(bf16[16,240,256]{2,1,0:T(8,128)(2,1)} %shard_map.231.grads), calls=%async_computation.2 | async-start | bytes 3932160 | tf_op jit(solution)/shard_map/all_to_all | solution.py:1113
  199.5 8.4 %shard_map.232 = (f32[256,640]{1,0:T(8,128)}, bf16[256,640]{1,0:T(8,128)(2,1)}) custom-call(s32[23]{0:T(128)} %concatenate.17.info, bf16[16,240,256]{2,1,0:T(8,128)(2,1)} %shard_map.231.grads, bf16[496,640]{1,0:T(8,128)(2,1)} %shard_map.221.refs_1_.refs_2_.own, bf16[496,640]{1,0:T(8,128)(2,1)} %copy-done, bf16[2048,1280]{1,0:T(8,128)(2,1)} %get-tuple-element.222.refs_0_, ...), custom_call_target="tpu_custom_call" | custom-call | flops 2516582400 | bytes 10485760 | tf_op jit(solution)/shard_map/pallas_call | solution.py:375
  209.1 4.4 %shard_map.233 = (bf16[320,640]{1,0:T(8,128)(2,1)}, bf16[320,640]{1,0:T(8,128)(2,1)}, bf16[320,640]{1,0:T(8,128)(2,1)}, bf16[320,640]{1,0:T(8,128)(2,1)}, bf16[3...) custom-call(s32[23]{0:T(128)} %concatenate.17.info, bf16[640,640]{1,0:T(8,128)(2,1)} %get-tuple-element.256.refs_0_, ...), custom_call_target="tpu_custom_call" | custom-call | bytes 2457600 | tf_op jit(solution)/shard_map/pallas_call | solution.py:375
  213.4 1.9 collective-permute-start.42
  217.7 10.9 %collective-permute-done.33 = bf16[256,640]{1,0:T(8,128)(2,1)S(1)} collective-permute-done((bf16[256,640]{1,0:T(8,128)(2,1)}, bf16[256,640]{1,0:T(8,128)(2,1)S(1)}, u32[]{:S(2)}, u32[]{:S(2)}) %collective-permute-start.33) | collective-permute-done | bytes 327712 | tf_op jit(solution)/shard_map/ppermute | solution.py:361
  228.7 1.9 collective-permute-start.39
  231.7 10.8 %collective-permute-done.43.refs_4_ = bf16[320,640]{1,0:T(8,128)(2,1)S(1)} collective-permute-done((bf16[320,640]{1,0:T(8,128)(2,1)}, bf16[320,640]{1,0:T(8,128)(2,1)S(1)}, u32[]{:S(2)}, u32[]{:S(2)}) %collective-permute-start.43) | collective-permute-done | bytes 409632 | tf_op jit(solution)/shard_map/ppermute | solution.py:361
  242.7 6.3 %collective-permute-done.39.refs_2_ = bf16[256,640]{1,0:T(8,128)(2,1)S(1)} collective-permute-done((bf16[256,640]{1,0:T(8,128)(2,1)S(1)}, bf16[256,640]{1,0:T(8,128)(2,1)S(1)}, u32[]{:S(2)}, u32[]{:S(2)}) %collective-permute-start.39) | collective-permute-done | bytes 327712 | tf_op jit(solution)/shard_map/ppermute | solution.py:361
  249.0 2.2 collective-permute-done.38.refs_1_
  253.3 2.8 shard_map.235
  256.1 4.7 %collective-permute-done.41.refs_4_ = bf16[256,640]{1,0:T(8,128)(2,1)S(1)} collective-permute-done((bf16[256,640]{1,0:T(8,128)(2,1)S(1)}, bf16[256,640]{1,0:T(8,128)(2,1)S(1)}, u32[]{:S(2)}, u32[]{:S(2)}) %collective-permute-start.41) | collective-permute-done | bytes 327712 | tf_op jit(solution)/shard_map/ppermute | solution.py:361
  261.7 3.4 shard_map.236.near
  269.9 3.2 collective-permute-done.48.refs_3_
  275.5 5.5 %collective-permute-done.50.refs_5_ = bf16[160,640]{1,0:T(8,128)(2,1)S(1)} collective-permute-done((bf16[160,640]{1,0:T(8,128)(2,1)S(1)}, bf16[160,640]{1,0:T(8,128)(2,1)S(1)}, u32[]{:S(2)}, u32[]{:S(2)}) %collective-permute-start.50) | collective-permute-done | bytes 204832 | tf_op jit(solution)/shard_map/ppermute | solution.py:361
  281.8 2.3 shard_map.237
  284.2 2.0 collective-permute-start.52
  286.7 2.9 collective-permute-done.52.refs_3_
  289.7 11.3 %shard_map.234 = bf16[256,1280]{1,0:T(8,128)(2,1)} custom-call(s32[23]{0:T(128)} %concatenate.17.info, bf16[256,1280]{1,0:T(8,128)(2,1)} %bitcast.26, bf16[16,240,256]{2,1,0:T(8,128)(2,1)} %copy-done.5, f32[256,1280]{1,0:T(8,128)} %get-tuple-element.262.grad_mid, bf16[496,640]{1,0:T(8,128)(2,1)} %shard_map.221.refs_1_.refs_2_.own, bf16[496,640]{1,0:T(8,128)(2,1)} %copy-done, ...), custom_call_target="tpu_custom_call" | custom-call | flops 2516582400 | bytes 9830400 | tf_op jit(solution)/shard_map/pallas_call | solution.py:375
  304.0 2.3 collective-permute-start.58
  307.1 9.3 %shard_map.238 = (f32[640,1280]{1,0:T(8,128)}, f32[640,1280]{1,0:T(8,128)}, f32[640,1280]{1,0:T(8,128)}, f32[640]{0:T(1024)}, f32[1,80]{1,0:T(1,128)}) custom-call(s32[23]{0:T(128)} %concatenate.17.info, bf16[5,256,640]{2,1,0:T(8,128)(2,1)} %shard_map.236.near, bf16[5,256,640]{2,1,0:T(8,128)(2,1)} %copy-done.60, bf16[256,640]{1,0:T(8,128)(2,1)} %copy-done.57, ...), custom_call_target="tpu_custom_call" | custom-call | flops 3145728000 | bytes 9830400 | tf_op jit(solution)/shard_map/pallas_call | solution.py:375
  316.4 2.5 collective-permute-start.60
  319.0 7.2 %collective-permute-done.60.refs_3_ = bf16[240,640]{1,0:T(8,128)(2,1)S(1)} collective-permute-done((bf16[240,640]{1,0:T(8,128)(2,1)S(1)}, bf16[240,640]{1,0:T(8,128)(2,1)S(1)}, u32[]{:S(2)}, u32[]{:S(2)}) %collective-permute-start.60) | collective-permute-done | bytes 307232 | tf_op jit(solution)/shard_map/ppermute | solution.py:361
  328.4 2.6 shard_map.239.near
  335.8 6.0 %shard_map.240 = (f32[640,128]{1,0:T(8,128)}, f32[640,1280]{1,0:T(8,128)}, f32[640,1280]{1,0:T(8,128)}, f32[640,1280]{1,0:T(8,128)}) custom-call(s32[23]{0:T(128)} %concatenate.17.info, bf16[5,240,640]{2,1,0:T(8,128)(2,1)} %shard_map.239.near, bf16[5,240,640]{2,1,0:T(8,128)(2,1)} %copy-done.6, bf16[640,1280]{1,0:T(8,128)(2,1)} %refs_10_.1), custom_call_target="tpu_custom_call" | custom-call | bytes 9830400 | tf_op jit(solution)/shard_map/pallas_call | solution.py:375
  345.0 4.0 %collective-permute-done.65.refs_2_ = bf16[112,640]{1,0:T(8,128)(2,1)S(1)} collective-permute-done((bf16[112,640]{1,0:T(8,128)(2,1)S(1)}, bf16[112,640]{1,0:T(8,128)(2,1)S(1)}, u32[]{:S(2)}, u32[]{:S(2)}) %collective-permute-start.65) | collective-permute-done | bytes 143392 | tf_op jit(solution)/shard_map/ppermute | solution.py:361
  351.4 4.8 %shard_map.241 = (f32[640,1280]{1,0:T(8,128)}, f32[640,1280]{1,0:T(8,128)}, f32[640,1280]{1,0:T(8,128)}, f32[640]{0:T(1024)}) custom-call(s32[23]{0:T(128)} %concatenate.17.info, bf16[240,640]{1,0:T(8,128)(2,1)} %copy-done.13, bf16[240,640]{1,0:T(8,128)(2,1)} %copy-done.12, ...), custom_call_target="tpu_custom_call", output_to_operand_aliasing={{0}: (12, {}), {1}: (13, {}), {2}: (14, {})} | custom-call | bytes 9830400 | tf_op jit(solution)/shard_map/pallas_call | solution.py:375
  (310 shorter events, 83.0 us)
Async XLA Ops:
  0.6 18.0 %collective-permute-start.1 = (bf16[256,1280]{1,0:T(8,128)(2,1)}, bf16[256,1280]{1,0:T(8,128)(2,1)S(1)}, u32[]{:S(2)}, u32[]{:S(2)}) collective-permute-start(bf16[256,1280]{1,0:T(8,128)(2,1)} %bitcast.22), channel_id=1, source_target_pairs={{0,4},{1,5},{2,6},{3,7},{4,12},{5,13},{6,14},{7,15},{8,0},{9,1},{1... | collective-permute-start | bytes 1966088 | tf_op jit(solution)/shard_map/ppermute | solution.py:361
  3.6 16.5 %collective-permute-start = (bf16[256,1280]{1,0:T(8,128)(2,1)}, bf16[256,1280]{1,0:T(8,128)(2,1)}, u32[]{:S(2)}, u32[]{:S(2)}) collective-permute-start(bf16[256,1280]{1,0:T(8,128)(2,1)} %bitcast.23), channel_id=1, source_target_pairs={{0,8},{1,9},{2,10},{3,11},{4,0},{5,1},{6,2},{7,3},{8,16},{9,17},{1... | collective-permute-start | bytes 1966088 | tf_op jit(solution)/shard_map/ppermute | solution.py:361
  4.8 11.8 %collective-permute-start.2 = (bf16[128,1280]{1,0:T(8,128)(2,1)S(1)}, bf16[128,1280]{1,0:T(8,128)(2,1)}, u32[]{:S(2)}, u32[]{:S(2)}) collective-permute-start(bf16[128,1280]{1,0:T(8,128)(2,1)S(1)} %constant_dynamic-slice_fusion.9), channel_id=1, source_target_pairs={{0,1},{1,0},{2,3},{3,2},{4,5},{5,4},{6,7},{7,6},{8,9},{9,8},{10,11... | collective-permute-start | bytes 983048 | tf_op jit(solution)/shard_map/ppermute | solution.py:361
  16.4 15.7 %collective-permute-start.5 = (bf16[496,640]{1,0:T(8,128)(2,1)}, bf16[496,640]{1,0:T(8,128)(2,1)S(1)}, u32[]{:S(2)}, u32[]{:S(2)}) collective-permute-start(bf16[496,640]{1,0:T(8,128)(2,1)} %shard_map.221.refs_1_.refs_2_.own), channel_id=1, source_target_pairs={{0,1},{1,0},{2,3},{3,2},{4,5},{5,4},{6,7},{7,6},{8,9},{9,8},{10,11... | collective-permute-start | bytes 1904648 | tf_op jit(solution)/shard_map/ppermute | solution.py:361
  20.1 17.7 %collective-permute-start.3 = (bf16[256,1280]{1,0:T(8,128)(2,1)}, bf16[256,1280]{1,0:T(8,128)(2,1)}, u32[]{:S(2)}, u32[]{:S(2)}) collective-permute-start(bf16[256,1280]{1,0:T(8,128)(2,1)} %collective-permute-done.refs_0_), channel_id=1, source_target_pairs={{0,8},{1,9},{2,10},{3,11},{4,0},{5,1},{6,2},{7,3},{8,16},{9,17},{1... | collective-permute-start | bytes 1966088 | tf_op jit(solution)/shard_map/ppermute | solution.py:361
  20.6 11.6 %collective-permute-start.6 = (bf16[128,1280]{1,0:T(8,128)(2,1)}, bf16[128,1280]{1,0:T(8,128)(2,1)S(1)}, u32[]{:S(2)}, u32[]{:S(2)}) collective-permute-start(bf16[128,1280]{1,0:T(8,128)(2,1)} %collective-permute-done.2.refs_3_), channel_id=1, source_target_pairs={{0,2},{1,3},{2,0},{3,1},{4,6},{5,7},{6,4},{7,5},{8,10},{9,11},{10,... | collective-permute-start | bytes 983048 | tf_op jit(solution)/shard_map/ppermute | solution.py:361
  20.6 17.3 %collective-permute-start.4 = (bf16[256,1280]{1,0:T(8,128)(2,1)S(1)}, bf16[256,1280]{1,0:T(8,128)(2,1)}, u32[]{:S(2)}, u32[]{:S(2)}) collective-permute-start(bf16[256,1280]{1,0:T(8,128)(2,1)S(1)} %collective-permute-done.1.refs_1_), channel_id=1, source_target_pairs={{0,4},{1,5},{2,6},{3,7},{4,12},{5,13},{6,14},{7,15},{8,0},{9,1},{1... | collective-permute-start | bytes 1966088 | tf_op jit(solution)/shard_map/ppermute | solution.py:361
  37.8 20.2 %collective-permute-start.9 = (bf16[320,1280]{1,0:T(8,128)(2,1)}, bf16[320,1280]{1,0:T(8,128)(2,1)}, u32[]{:S(2)}, u32[]{:S(2)}) collective-permute-start(bf16[320,1280]{1,0:T(8,128)(2,1)} %pad_maximum_fusion.2), channel_id=1, source_target_pairs={{0,1},{1,0},{2,3},{3,2},{4,5},{5,4},{6,7},{7,6},{8,9},{9,8},{10,11... | collective-permute-start | bytes 2457608 | tf_op jit(solution)/shard_map/ppermute | solution.py:361
  39.5 16.3 %collective-permute-start.7 = (bf16[256,1280]{1,0:T(8,128)(2,1)}, bf16[256,1280]{1,0:T(8,128)(2,1)S(1)}, u32[]{:S(2)}, u32[]{:S(2)}) collective-permute-start(bf16[256,1280]{1,0:T(8,128)(2,1)} %collective-permute-done.3.refs_0_), channel_id=1, source_target_pairs={{0,8},{1,9},{2,10},{3,11},{4,0},{5,1},{6,2},{7,3},{8,16},{9,17},{1... | collective-permute-start | bytes 1966088 | tf_op jit(solution)/shard_map/ppermute | solution.py:361
  41.0 16.0 %collective-permute-start.8 = (bf16[256,1280]{1,0:T(8,128)(2,1)}, bf16[256,1280]{1,0:T(8,128)(2,1)S(1)}, u32[]{:S(2)}, u32[]{:S(2)}) collective-permute-start(bf16[256,1280]{1,0:T(8,128)(2,1)} %collective-permute-done.4.refs_1_), channel_id=1, source_target_pairs={{0,4},{1,5},{2,6},{3,7},{4,12},{5,13},{6,14},{7,15},{8,0},{9,1},{1... | collective-permute-start | bytes 1966088 | tf_op jit(solution)/shard_map/ppermute | solution.py:361
  58.0 13.1 %collective-permute-start.13 = (bf16[320,1280]{1,0:T(8,128)(2,1)}, bf16[320,1280]{1,0:T(8,128)(2,1)S(1)}, u32[]{:S(2)}, u32[]{:S(2)}) collective-permute-start(bf16[320,1280]{1,0:T(8,128)(2,1)} %collective-permute-done.9.refs_4_), channel_id=1, source_target_pairs={{0,2},{1,3},{2,0},{3,1},{4,6},{5,7},{6,4},{7,5},{8,10},{9,11},{10,... | collective-permute-start | bytes 2457608 | tf_op jit(solution)/shard_map/ppermute | solution.py:361
  58.0 13.1 %collective-permute-start.12 = (bf16[176,1280]{1,0:T(8,128)(2,1)S(1)}, bf16[176,1280]{1,0:T(8,128)(2,1)S(1)}, u32[]{:S(2)}, u32[]{:S(2)}) collective-permute-start(bf16[176,1280]{1,0:T(8,128)(2,1)S(1)} %copy-done.24), channel_id=1, source_target_pairs={{0,1},{1,0},{2,3},{3,2},{4,5},{5,4},{6,7},{7,6},{8,9},{9,8},{10,11... | collective-permute-start | bytes 1351688 | tf_op jit(solution)/shard_map/ppermute | solution.py:361
  59.7 9.9 %collective-permute-start.11 = (bf16[128,1280]{1,0:T(8,128)(2,1)S(1)}, bf16[128,1280]{1,0:T(8,128)(2,1)S(1)}, u32[]{:S(2)}, u32[]{:S(2)}) collective-permute-start(bf16[128,1280]{1,0:T(8,128)(2,1)S(1)} %slice.51), channel_id=1, source_target_pairs={{0,4},{1,5},{2,6},{3,7},{4,12},{5,13},{6,14},{7,15},{8,0},{9,1},{1... | collective-permute-start | bytes 983048 | tf_op jit(solution)/shard_map/ppermute | solution.py:361
  61.3 9.8 %collective-permute-start.10 = (bf16[128,1280]{1,0:T(8,128)(2,1)S(1)}, bf16[128,1280]{1,0:T(8,128)(2,1)S(1)}, u32[]{:S(2)}, u32[]{:S(2)}) collective-permute-start(bf16[128,1280]{1,0:T(8,128)(2,1)S(1)} %slice.50), channel_id=1, source_target_pairs={{0,8},{1,9},{2,10},{3,11},{4,0},{5,1},{6,2},{7,3},{8,16},{9,17},{1... | collective-permute-start | bytes 983048 | tf_op jit(solution)/shard_map/ppermute | solution.py:361
  76.3 21.1 %collective-permute-start.20 = (bf16[336,1280]{1,0:T(8,128)(2,1)S(1)}, bf16[336,1280]{1,0:T(8,128)(2,1)S(1)}, u32[]{:S(2)}, u32[]{:S(2)}) collective-permute-start(bf16[336,1280]{1,0:T(8,128)(2,1)S(1)} %pad_maximum_fusion.1), channel_id=1, source_target_pairs={{0,1},{1,0},{2,3},{3,2},{4,5},{5,4},{6,7},{7,6},{8,9},{9,8},{10,11... | collective-permute-start | bytes 2580488 | tf_op jit(solution)/shard_map/ppermute | solution.py:361
  98.3 24.0 %collective-permute-start.22 = (bf16[2048,1280]{1,0:T(8,128)(2,1)}, bf16[2048,1280]{1,0:T(8,128)(2,1)}, u32[]{:S(2)}, u32[]{:S(2)}) collective-permute-start(bf16[2048,1280]{1,0:T(8,128)(2,1)} %get-tuple-element.222.refs_0_), channel_id=1, source_target_pairs={{0,2},{1,3},{2,0},{3,1},{4,6},{5,7},{6,4},{7,5},{8,10},{9,11},{10,... | collective-permute-start | bytes 15728648 | tf_op jit(solution)/shard_map/ppermute | solution.py:361
  98.3 24.0 %all-to-all-start = ((bf16[16,80,256]{2,1,0:T(8,128)(2,1)}), bf16[16,80,256]{2,1,0:T(8,128)(2,1)S(1)}, u32[]{:S(2)}, u32[]{:S(2)}) async-start(bf16[16,80,256]{2,1,0:T(8,128)(2,1)} %get-tuple-element.219.refs_5_), calls=%async_computation | async-start | bytes 1310720 | tf_op jit(solution)/shard_map/all_to_all | solution.py:1034
  104.7 17.7 %collective-permute-start.21 = (bf16[336,1280]{1,0:T(8,128)(2,1)}, bf16[336,1280]{1,0:T(8,128)(2,1)S(1)}, u32[]{:S(2)}, u32[]{:S(2)}) collective-permute-start(bf16[336,1280]{1,0:T(8,128)(2,1)} %copy-done.61), channel_id=1, source_target_pairs={{0,2},{1,3},{2,0},{3,1},{4,6},{5,7},{6,4},{7,5},{8,10},{9,11},{10,... | collective-permute-start | bytes 2580488 | tf_op jit(solution)/shard_map/ppermute | solution.py:361
  105.2 15.4 %collective-permute-start.23 = (bf16[256,1280]{1,0:T(8,128)(2,1)}, bf16[256,1280]{1,0:T(8,128)(2,1)S(1)}, u32[]{:S(2)}, u32[]{:S(2)}) collective-permute-start(bf16[256,1280]{1,0:T(8,128)(2,1)} %bitcast.35), channel_id=1, source_target_pairs={{0,2},{1,3},{2,0},{3,1},{4,6},{5,7},{6,4},{7,5},{8,10},{9,11},{10,... | collective-permute-start | bytes 1966088 | tf_op jit(solution)/shard_map/ppermute | solution.py:361
  105.3 15.3 %collective-permute-start.24 = (bf16[224,1280]{1,0:T(8,128)(2,1)S(1)}, bf16[224,1280]{1,0:T(8,128)(2,1)S(1)}, u32[]{:S(2)}, u32[]{:S(2)}) collective-permute-start(bf16[224,1280]{1,0:T(8,128)(2,1)S(1)} %copy-done.23), channel_id=1, source_target_pairs={{0,1},{1,0},{2,3},{3,2},{4,5},{5,4},{6,7},{7,6},{8,9},{9,8},{10,11... | collective-permute-start | bytes 1720328 | tf_op jit(solution)/shard_map/ppermute | solution.py:361
  122.4 13.7 %collective-permute-start.25 = (bf16[160,1280]{1,0:T(8,128)(2,1)S(1)}, bf16[160,1280]{1,0:T(8,128)(2,1)}, u32[]{:S(2)}, u32[]{:S(2)}) collective-permute-start(bf16[160,1280]{1,0:T(8,128)(2,1)S(1)} %copy-done.27), channel_id=1, source_target_pairs={{0,1},{1,0},{2,3},{3,2},{4,5},{5,4},{6,7},{7,6},{8,9},{9,8},{10,11... | collective-permute-start | bytes 1228808 | tf_op jit(solution)/shard_map/ppermute | solution.py:361
  136.1 22.6 %all-to-all-start.1 = ((bf16[16,80,256]{2,1,0:T(8,128)(2,1)}), bf16[16,80,256]{2,1,0:T(8,128)(2,1)S(1)}, u32[]{:S(2)}, u32[]{:S(2)}) async-start(bf16[16,80,256]{2,1,0:T(8,128)(2,1)} %bitcast.31), calls=%async_computation.1 | async-start | bytes 1310720 | tf_op jit(solution)/shard_map/all_to_all | solution.py:1058
  142.7 15.1 %collective-permute-start.26 = (bf16[224,1280]{1,0:T(8,128)(2,1)S(1)}, bf16[224,1280]{1,0:T(8,128)(2,1)}, u32[]{:S(2)}, u32[]{:S(2)}) collective-permute-start(bf16[224,1280]{1,0:T(8,128)(2,1)S(1)} %copy-done.22), channel_id=1, source_target_pairs={{0,1},{1,0},{2,3},{3,2},{4,5},{5,4},{6,7},{7,6},{8,9},{9,8},{10,11... | collective-permute-start | bytes 1720328 | tf_op jit(solution)/shard_map/ppermute | solution.py:361
  158.7 35.5 %collective-permute-start.29 = (bf16[640,640]{1,0:T(8,128)(2,1)}, bf16[640,640]{1,0:T(8,128)(2,1)}, u32[]{:S(2)}, u32[]{:S(2)}) collective-permute-start(bf16[640,640]{1,0:T(8,128)(2,1)} %get-tuple-element.258), channel_id=1, source_target_pairs={{0,1},{1,0},{2,3},{3,2},{4,5},{5,4},{6,7},{7,6},{8,9},{9,8},{10,11... | collective-permute-start | bytes 2457608 | tf_op jit(solution)/shard_map/ppermute | solution.py:361
  159.8 34.5 %collective-permute-start.30 = (bf16[640,640]{1,0:T(8,128)(2,1)}, bf16[640,640]{1,0:T(8,128)(2,1)}, u32[]{:S(2)}, u32[]{:S(2)}) collective-permute-start(bf16[640,640]{1,0:T(8,128)(2,1)} %get-tuple-element.259), channel_id=1, source_target_pairs={{0,4},{1,5},{2,6},{3,7},{4,0},{5,1},{6,2},{7,3},{8,12},{9,13},{10,... | collective-permute-start | bytes 2457608 | tf_op jit(solution)/shard_map/ppermute | solution.py:361
  160.8 33.5 %collective-permute-start.31 = (bf16[640,640]{1,0:T(8,128)(2,1)}, bf16[640,640]{1,0:T(8,128)(2,1)}, u32[]{:S(2)}, u32[]{:S(2)}) collective-permute-start(bf16[640,640]{1,0:T(8,128)(2,1)} %get-tuple-element.260), channel_id=1, source_target_pairs={{0,8},{1,9},{2,10},{3,11},{4,12},{5,13},{6,14},{7,15},{8,0},{9,1},... | collective-permute-start | bytes 2457608 | tf_op jit(solution)/shard_map/ppermute | solution.py:361
  194.3 67.3 %all-to-all-start.2 = ((bf16[16,240,256]{2,1,0:T(8,128)(2,1)}), bf16[16,240,256]{2,1,0:T(8,128)(2,1)S(1)}, u32[]{:S(2)}, u32[]{:S(2)}) async-start(bf16[16,240,256]{2,1,0:T(8,128)(2,1)} %shard_map.231.grads), calls=%async_computation.2 | async-start | bytes 3932160 | tf_op jit(solution)/shard_map/all_to_all | solution.py:1113
  198.5 32.1 %collective-permute-start.32 = (bf16[352,1280]{1,0:T(8,128)(2,1)}, bf16[352,1280]{1,0:T(8,128)(2,1)S(1)}, u32[]{:S(2)}, u32[]{:S(2)}) collective-permute-start(bf16[352,1280]{1,0:T(8,128)(2,1)} %pad_maximum_fusion), channel_id=1, source_target_pairs={{0,1},{1,0},{2,3},{3,2},{4,5},{5,4},{6,7},{7,6},{8,9},{9,8},{10,11... | collective-permute-start | bytes 2703368 | tf_op jit(solution)/shard_map/ppermute | solution.py:361
  208.0 20.6 %collective-permute-start.33 = (bf16[256,640]{1,0:T(8,128)(2,1)}, bf16[256,640]{1,0:T(8,128)(2,1)S(1)}, u32[]{:S(2)}, u32[]{:S(2)}) collective-permute-start(bf16[256,640]{1,0:T(8,128)(2,1)} %get-tuple-element.280), channel_id=1, source_target_pairs={{0,1},{1,0},{2,3},{3,2},{4,5},{5,4},{6,7},{7,6},{8,9},{9,8},{10,11... | collective-permute-start | bytes 983048 | tf_op jit(solution)/shard_map/ppermute | solution.py:361
  213.4 18.3 %collective-permute-start.42 = (bf16[320,640]{1,0:T(8,128)(2,1)}, bf16[320,640]{1,0:T(8,128)(2,1)S(1)}, u32[]{:S(2)}, u32[]{:S(2)}) collective-permute-start(bf16[320,640]{1,0:T(8,128)(2,1)} %get-tuple-element.287), channel_id=1, source_target_pairs={{0,4},{1,5},{2,6},{3,7},{4,0},{5,1},{6,2},{7,3},{8,12},{9,13},{10,... | collective-permute-start | bytes 1228808 | tf_op jit(solution)/shard_map/ppermute | solution.py:361
  215.3 27.2 %collective-permute-start.43 = (bf16[320,640]{1,0:T(8,128)(2,1)}, bf16[320,640]{1,0:T(8,128)(2,1)S(1)}, u32[]{:S(2)}, u32[]{:S(2)}) collective-permute-start(bf16[320,640]{1,0:T(8,128)(2,1)} %get-tuple-element.288), channel_id=1, source_target_pairs={{0,8},{1,9},{2,10},{3,11},{4,12},{5,13},{6,14},{7,15},{8,0},{9,1},... | collective-permute-start | bytes 1228808 | tf_op jit(solution)/shard_map/ppermute | solution.py:361
  216.8 25.9 %collective-permute-start.44 = (bf16[320,640]{1,0:T(8,128)(2,1)}, bf16[320,640]{1,0:T(8,128)(2,1)S(1)}, u32[]{:S(2)}, u32[]{:S(2)}) collective-permute-start(bf16[320,640]{1,0:T(8,128)(2,1)} %get-tuple-element.289), channel_id=1, source_target_pairs={{0,1},{1,0},{2,3},{3,2},{4,5},{5,4},{6,7},{7,6},{8,9},{9,8},{10,11... | collective-permute-start | bytes 1228808 | tf_op jit(solution)/shard_map/ppermute | solution.py:361
  228.7 20.3 %collective-permute-start.39 = (bf16[256,640]{1,0:T(8,128)(2,1)S(1)}, bf16[256,640]{1,0:T(8,128)(2,1)S(1)}, u32[]{:S(2)}, u32[]{:S(2)}) collective-permute-start(bf16[256,640]{1,0:T(8,128)(2,1)S(1)} %add_convert_fusion.refs_0_), channel_id=1, source_target_pairs={{0,4},{1,5},{2,6},{3,7},{4,12},{5,13},{6,14},{7,15},{8,0},{9,1},{1... | collective-permute-start | bytes 983048 | tf_op jit(solution)/shard_map/ppermute | solution.py:361
  230.6 31.0 %collective-permute-start.37 = (bf16[352,1280]{1,0:T(8,128)(2,1)S(1)}, bf16[352,1280]{1,0:T(8,128)(2,1)}, u32[]{:S(2)}, u32[]{:S(2)}) collective-permute-start(bf16[352,1280]{1,0:T(8,128)(2,1)S(1)} %collective-permute-done.32.refs_6_), channel_id=1, source_target_pairs={{0,2},{1,3},{2,0},{3,1},{4,6},{5,7},{6,4},{7,5},{8,10},{9,11},{10,... | collective-permute-start | bytes 2703368 | tf_op jit(solution)/shard_map/ppermute | solution.py:361
  231.7 21.1 %collective-permute-start.35 = (bf16[160,1280]{1,0:T(8,128)(2,1)}, bf16[160,1280]{1,0:T(8,128)(2,1)S(1)}, u32[]{:S(2)}, u32[]{:S(2)}) collective-permute-start(bf16[160,1280]{1,0:T(8,128)(2,1)} %collective-permute-done.25.refs_4_), channel_id=1, source_target_pairs={{0,2},{1,3},{2,0},{3,1},{4,6},{5,7},{6,4},{7,5},{8,10},{9,11},{10,... | collective-permute-start | bytes 1228808 | tf_op jit(solution)/shard_map/ppermute | solution.py:361
  242.7 13.4 %collective-permute-start.34 = (bf16[224,1280]{1,0:T(8,128)(2,1)S(1)}, bf16[224,1280]{1,0:T(8,128)(2,1)S(1)}, u32[]{:S(2)}, u32[]{:S(2)}) collective-permute-start(bf16[224,1280]{1,0:T(8,128)(2,1)S(1)} %copy-done.19), channel_id=1, source_target_pairs={{0,2},{1,3},{2,0},{3,1},{4,6},{5,7},{6,4},{7,5},{8,10},{9,11},{10,... | collective-permute-start | bytes 1720328 | tf_op jit(solution)/shard_map/ppermute | solution.py:361
  265.1 35.9 %collective-permute-start.45 = (bf16[5,256,640]{2,1,0:T(8,128)(2,1)}, bf16[5,256,640]{2,1,0:T(8,128)(2,1)S(1)}, u32[]{:S(2)}, u32[]{:S(2)}) collective-permute-start(bf16[5,256,640]{2,1,0:T(8,128)(2,1)} %shard_map.236.near), channel_id=1, source_target_pairs={{0,2},{1,3},{2,0},{3,1},{4,6},{5,7},{6,4},{7,5},{8,10},{9,11},{10,... | collective-permute-start | bytes 4915208 | tf_op jit(solution)/shard_map/ppermute | solution.py:361
  266.9 17.2 %collective-permute-start.46 = (bf16[256,640]{1,0:T(8,128)(2,1)S(1)}, bf16[256,640]{1,0:T(8,128)(2,1)S(1)}, u32[]{:S(2)}, u32[]{:S(2)}) collective-permute-start(bf16[256,640]{1,0:T(8,128)(2,1)S(1)} %copy-done.36), channel_id=1, source_target_pairs={{0,8},{1,9},{2,10},{3,11},{4,0},{5,1},{6,2},{7,3},{8,16},{9,17},{1... | collective-permute-start | bytes 983048 | tf_op jit(solution)/shard_map/ppermute | solution.py:361
  267.2 16.9 %collective-permute-start.47 = (bf16[256,640]{1,0:T(8,128)(2,1)}, bf16[256,640]{1,0:T(8,128)(2,1)S(1)}, u32[]{:S(2)}, u32[]{:S(2)}) collective-permute-start(bf16[256,640]{1,0:T(8,128)(2,1)} %copy-done.33), channel_id=1, source_target_pairs={{0,4},{1,5},{2,6},{3,7},{4,12},{5,13},{6,14},{7,15},{8,0},{9,1},{1... | collective-permute-start | bytes 983048 | tf_op jit(solution)/shard_map/ppermute | solution.py:361
  286.2 14.8 %collective-permute-start.53 = (bf16[256,640]{1,0:T(8,128)(2,1)S(1)}, bf16[256,640]{1,0:T(8,128)(2,1)S(1)}, u32[]{:S(2)}, u32[]{:S(2)}) collective-permute-start(bf16[256,640]{1,0:T(8,128)(2,1)S(1)} %collective-permute-done.46.refs_0_), channel_id=1, source_target_pairs={{0,2},{1,3},{2,0},{3,1},{4,6},{5,7},{6,4},{7,5},{8,10},{9,11},{10,... | collective-permute-start | bytes 983048 | tf_op jit(solution)/shard_map/ppermute | solution.py:361
  286.2 14.9 %collective-permute-start.54 = (bf16[256,640]{1,0:T(8,128)(2,1)S(1)}, bf16[256,640]{1,0:T(8,128)(2,1)S(1)}, u32[]{:S(2)}, u32[]{:S(2)}) collective-permute-start(bf16[256,640]{1,0:T(8,128)(2,1)S(1)} %collective-permute-done.47.refs_1_), channel_id=1, source_target_pairs={{0,2},{1,3},{2,0},{3,1},{4,6},{5,7},{6,4},{7,5},{8,10},{9,11},{10,... | collective-permute-start | bytes 983048 | tf_op jit(solution)/shard_map/ppermute | solution.py:361
  286.7 16.6 %collective-permute-start.57 = (bf16[240,640]{1,0:T(8,128)(2,1)}, bf16[240,640]{1,0:T(8,128)(2,1)S(1)}, u32[]{:S(2)}, u32[]{:S(2)}) collective-permute-start(bf16[240,640]{1,0:T(8,128)(2,1)} %get-tuple-element.310), channel_id=1, source_target_pairs={{0,16},{1,17},{2,18},{3,19},{4,20},{5,21},{6,22},{7,23},{8,24},{9,... | collective-permute-start | bytes 921608 | tf_op jit(solution)/shard_map/ppermute | solution.py:361
  289.7 11.3 %collective-permute-start.51 = (bf16[128,640]{1,0:T(8,128)(2,1)S(1)}, bf16[128,640]{1,0:T(8,128)(2,1)S(1)}, u32[]{:S(2)}, u32[]{:S(2)}) collective-permute-start(bf16[128,640]{1,0:T(8,128)(2,1)S(1)} %slice.52), channel_id=1, source_target_pairs={{0,8},{1,9},{2,10},{3,11},{4,0},{5,1},{6,2},{7,3},{8,16},{9,17},{1... | collective-permute-start | bytes 491528 | tf_op jit(solution)/shard_map/ppermute | solution.py:361
  303.4 12.9 %collective-permute-start.59 = (bf16[240,640]{1,0:T(8,128)(2,1)S(1)}, bf16[240,640]{1,0:T(8,128)(2,1)S(1)}, u32[]{:S(2)}, u32[]{:S(2)}) collective-permute-start(bf16[240,640]{1,0:T(8,128)(2,1)S(1)} %add_convert_fusion.1.refs_0_), channel_id=1, source_target_pairs={{0,4},{1,5},{2,6},{3,7},{4,12},{5,13},{6,14},{7,15},{8,0},{9,1},{1... | collective-permute-start | bytes 921608 | tf_op jit(solution)/shard_map/ppermute | solution.py:361
  304.0 12.4 %collective-permute-start.58 = (bf16[240,640]{1,0:T(8,128)(2,1)S(1)}, bf16[240,640]{1,0:T(8,128)(2,1)S(1)}, u32[]{:S(2)}, u32[]{:S(2)}) collective-permute-start(bf16[240,640]{1,0:T(8,128)(2,1)S(1)} %add_convert_fusion.1.refs_0_), channel_id=1, source_target_pairs={{0,8},{1,9},{2,10},{3,11},{4,0},{5,1},{6,2},{7,3},{8,16},{9,17},{1... | collective-permute-start | bytes 921608 | tf_op jit(solution)/shard_map/ppermute | solution.py:361
  316.4 9.8 %collective-permute-start.60 = (bf16[240,640]{1,0:T(8,128)(2,1)S(1)}, bf16[240,640]{1,0:T(8,128)(2,1)S(1)}, u32[]{:S(2)}, u32[]{:S(2)}) collective-permute-start(bf16[240,640]{1,0:T(8,128)(2,1)S(1)} %collective-permute-done.58.refs_1_), channel_id=1, source_target_pairs={{0,8},{1,9},{2,10},{3,11},{4,0},{5,1},{6,2},{7,3},{8,16},{9,17},{1... | collective-permute-start | bytes 921608 | tf_op jit(solution)/shard_map/ppermute | solution.py:361
  331.0 10.7 %collective-permute-start.61 = (bf16[240,640]{1,0:T(8,128)(2,1)}, bf16[240,640]{1,0:T(8,128)(2,1)S(1)}, u32[]{:S(2)}, u32[]{:S(2)}) collective-permute-start(bf16[240,640]{1,0:T(8,128)(2,1)} %copy-done.41), channel_id=1, source_target_pairs={{0,8},{1,9},{2,10},{3,11},{4,0},{5,1},{6,2},{7,3},{8,16},{9,17},{1... | collective-permute-start | bytes 921608 | tf_op jit(solution)/shard_map/ppermute | solution.py:361
  332.7 9.6 %collective-permute-start.63 = (bf16[240,640]{1,0:T(8,128)(2,1)}, bf16[240,640]{1,0:T(8,128)(2,1)S(1)}, u32[]{:S(2)}, u32[]{:S(2)}) collective-permute-start(bf16[240,640]{1,0:T(8,128)(2,1)} %copy-done.42), channel_id=1, source_target_pairs={{0,4},{1,5},{2,6},{3,7},{4,12},{5,13},{6,14},{7,15},{8,0},{9,1},{1... | collective-permute-start | bytes 921608 | tf_op jit(solution)/shard_map/ppermute | solution.py:361
  (108 other events, 793.8 us)

commit v5 on v4

--- a/solution.py
+++ b/solution.py
@@ -610,8 +610,8 @@
         dv[...] = jnp.zeros_like(dv)
 
         def tile(masked, i, low, first, size):
-            keys = pl.ds(pl.multiple_of(j * BLOCK + low, BLOCK // 2), size)
-            here = pl.ds(pl.multiple_of(i * BLOCK + first, BLOCK // 2), BLOCK - first)
+            keys = pl.ds(pl.multiple_of(j * BLOCK + low, BLOCK // 4), size)
+            here = pl.ds(pl.multiple_of(i * BLOCK + first, BLOCK // 4), BLOCK - first)
             probs = jnp.exp(mm(k_n[keys, :], q_t[:, here]))
             if masked:
                 key_pos = j * BLOCK + low + key_at[:size, first:]
@@ -628,8 +628,8 @@
             tile(masked, i, 0, 0, BLOCK)
             return carry
 
-        tile(True, j, 0, 0, BLOCK // 2)
-        tile(True, j, BLOCK // 2, BLOCK // 2, BLOCK // 2)
+        for low in range(0, BLOCK, BLOCK // 4):
+            tile(True, j, low, low, BLOCK // 4)
         split = jnp.where((j + 1) * BLOCK <= length, j + 1, blocks)
         lax.fori_loop(j + 1, split, functools.partial(step, True), 0)
         lax.fori_loop(split, blocks, functools.partial(step, False), 0)
@@ -1092,7 +1092,6 @@
     came = travel(terms[3:], 0)
     kept = terms[:3]
     grad_out, direct_back[2] = after((grad_out, direct_back[2]), kept[0])
-    direct_back.append(send(after(chunks[6:], kept[0])[0], Y_SWAP))
     grads = call(
         backward_kernel,
         [((16, 3 * HEAD, rows), BF)],
@@ -1133,6 +1132,7 @@
     keep = after((keep,), kept[0])[0]
     summed = (keep + from_pair.astype(F32)).astype(BF)
     passed_back = [send(value, CORE_SWAP) for value in after(direct_back, summed)]
+    direct_back.append(send(after(chunks[6:], summed)[0], Y_SWAP))
 
     shard = ((half_width, width), F32)
     line = ((half_width,), F32)
@@ -1145,9 +1145,10 @@
     forth2, back2 = send(forth1, FORTH), send(back1, BACK)
     terms = halving(kept, after(came, forth1), 2)
     kept, came = terms[:3], travel(terms[3:], 2)
-    forth2, back2 = after((forth2, back2), kept[0], returned, *passed_back)
+    forth2, back2, direct_back[3] = after((forth2, back2, direct_back[3]), kept[0], returned, *passed_back)
+    passed_back.append(send(direct_back[3], CORE_SWAP))
     forth3, back3 = send(forth2, FORTH), send(back2, BACK)
-    near, near_partner = stacked([summed, forth1, back1, forth2, back2])
+    near, near_partner = stacked([*after((summed, forth1, back1, forth2, back2), *came)])
     terms = halving(kept, came, 3)
     far = send(terms[1], FAR_SWAP)
     forth3, back3 = after((forth3, back3), terms[0])

time: 362 us -> 361 us (level)
  starting transfers between devices: 74.8 us -> 81.2 us
  waiting for transfers between devices: 102 us -> 97 us
    ppermute x71, starting transfers between devices: 58.3 us -> 64.6 us  [send(): return lax.ppermute(value, AXES, moves)]
    ppermute x71, waiting for transfers between devices: 101 us -> 96 us  [send(): return lax.ppermute(value, AXES, moves)]
    unnamed x164 -> x154, local copies, waits for them, and re-layouts: 12.3 us -> 11.7 us
  transfers between devices with their start and end apart: 74 -> 74, of which waited for: 31 -> 32; matrix products, arithmetic and copies ran while one was open for 4% -> 4% of each run, Pallas kernels for 39% -> 39%
where the time goes in v5:
time: 361 us; the launch traced here: 355 us
  Pallas kernels  149 us (41%)
  waiting for transfers between devices  97 us (27%)
  starting transfers between devices  81.2 us (22%)
  local copies, waits for them, and re-layouts  22 us (6%)
    pallas_call x21, Pallas kernels, call(): pl.pallas_call(body, out_shape=[jax.ShapeDtypeStruct(shape, kind) for sha...  149 us
    ppermute x71, waiting for transfers between devices, send(): return lax.ppermute(value, AXES, moves)  96 us
    ppermute x71, starting transfers between devices, send(): return lax.ppermute(value, AXES, moves)  64.6 us
    unnamed x154, local copies, waits for them, and re-layouts  11.7 us
  transfers between devices with their start and end apart: 74, of which 32 were waited for; matrix products, arithmetic and copies ran while one was open for 4% of the time, Pallas kernels for 39%

profile of v5, /device:TPU:0, one launch (start us, length us, event | category | flops | bytes accessed | tf_op | source)
XLA Modules:
  0.0 355.2 jit_solution(15935411792072669729)
XLA Ops:
  0.6 3.0 collective-permute-start.1
  4.8 2.0 collective-permute-start.2
  11.2 5.1 %shard_map.221.refs_1_.refs_2_.own = bf16[496,640]{1,0:T(8,128)(2,1)} custom-call(s32[23]{0:T(128)} %concatenate.17.info, bf16[640,1280]{1,0:T(8,128)(2,1)} %refs_0_.3, bf16[640,1280]{1,0:T(8,128)(2,1)} %refs_1_.3, bf16[640,1280]{1,0:T(8,128)(2,1)} %refs_2_.3, bf16[1,640]{1,0:T(2,128)(2,1)} %broadcast_in_dim.20.gain_a.refs_8_, ...), custom_call_target="tpu_custom_call" | custom-call | flops 786432000 | bytes 4915200 | tf_op jit(solution)/shard_map/pallas_call | solution.py:375
  16.5 2.2 collective-permute-done.1.refs_1_
  28.5 1.8 constant_dynamic-slice_fusion.2
  32.2 5.7 %collective-permute-done.4.refs_1_ = bf16[256,1280]{1,0:T(8,128)(2,1)} collective-permute-done((bf16[256,1280]{1,0:T(8,128)(2,1)S(1)}, bf16[256,1280]{1,0:T(8,128)(2,1)}, u32[]{:S(2)}, u32[]{:S(2)}) %collective-permute-start.4) | collective-permute-done | bytes 655392 | tf_op jit(solution)/shard_map/ppermute | solution.py:361
  42.8 3.4 shard_map.222
  46.2 4.3 %shard_map.223 = (bf16[2048,1280]{1,0:T(8,128)(2,1)}, bf16[240,512]{1,0:T(8,128)(2,1)}, bf16[240,512]{1,0:T(8,128)(2,1)}) custom-call(s32[23]{0:T(128)} %concatenate.17.info, bf16[256,1280]{1,0:T(8,128)(2,1)} %collective-permute-done.refs_0_, bf16[256,1280]{1,0:T(8,128)(2,1)} %copy-done.20, ...), custom_call_target="tpu_custom_call", output_to_operand_aliasing={{0}: (6, {})} | custom-call | flops 629145600 | bytes 2621440 | tf_op jit(solution)/shard_map/pallas_call | solution.py:375
  50.5 4.3 %shard_map.224 = (bf16[2048,1280]{1,0:T(8,128)(2,1)}, bf16[240,512]{1,0:T(8,128)(2,1)}, bf16[240,512]{1,0:T(8,128)(2,1)}) custom-call(s32[23]{0:T(128)} %concatenate.17.info, bf16[256,1280]{1,0:T(8,128)(2,1)} %collective-permute-done.3.refs_0_, bf16[256,1280]{1,0:T(8,128)(2,1)} %collective-permute-done.4.refs_1_, ...), custom_call_target="tpu_custom_call", output_to_operand_aliasing={{0}: (6, {})} | custom-call | flops 629145600 | bytes 2621440 | tf_op jit(solution)/shard_map/pallas_call | solution.py:375
  62.1 4.3 %shard_map.225 = (bf16[2048,1280]{1,0:T(8,128)(2,1)}, bf16[240,512]{1,0:T(8,128)(2,1)}, bf16[240,512]{1,0:T(8,128)(2,1)}) custom-call(s32[23]{0:T(128)} %concatenate.17.info, bf16[256,1280]{1,0:T(8,128)(2,1)} %copy-done.7, bf16[256,1280]{1,0:T(8,128)(2,1)} %copy-done.8, ...), custom_call_target="tpu_custom_call", output_to_operand_aliasing={{0}: (6, {})} | custom-call | flops 629145600 | bytes 2621440 | tf_op jit(solution)/shard_map/pallas_call | solution.py:375
  66.4 3.2 collective-permute-done.11.refs_1_
  72.3 3.4 shard_map.226
  78.4 15.3 %shard_map.227 = (bf16[16,80,256]{2,1,0:T(8,128)(2,1)}, bf16[128,4096]{1,0:T(8,128)(2,1)}, bf16[4096,128]{1,0:T(8,128)(2,1)}) custom-call(s32[23]{0:T(128)} %concatenate.17.info, s32[32]{0:T(128)} %bitcast.32, bf16[240,256]{1,0:T(8,128)(2,1)} %get-tuple-element.231.refs_0_, bf16[240,512]{1,0:T(8,128)(2,1)} %get-tuple-element.232.refs_1_, ...), custom_call_target="tpu_custom_call" | custom-call | flops 8589934592 | bytes 1966080 | tf_op jit(solution)/shard_map/pallas_call | solution.py:375
  93.7 3.7 %collective-permute-done.20.refs_6_ = bf16[336,1280]{1,0:T(8,128)(2,1)S(1)} collective-permute-done((bf16[336,1280]{1,0:T(8,128)(2,1)S(1)}, bf16[336,1280]{1,0:T(8,128)(2,1)S(1)}, u32[]{:S(2)}, u32[]{:S(2)}) %collective-permute-start.20) | collective-permute-done | bytes 860192 | tf_op jit(solution)/shard_map/ppermute | solution.py:361
  98.3 6.3 %all-to-all-start = ((bf16[16,80,256]{2,1,0:T(8,128)(2,1)}), bf16[16,80,256]{2,1,0:T(8,128)(2,1)S(1)}, u32[]{:S(2)}, u32[]{:S(2)}) async-start(bf16[16,80,256]{2,1,0:T(8,128)(2,1)} %get-tuple-element.224.refs_5_), calls=%async_computation | async-start | bytes 1310720 | tf_op jit(solution)/shard_map/all_to_all | solution.py:1034
  106.8 4.0 %shard_map.228 = (bf16[80,4096]{1,0:T(8,128)(2,1)}, bf16[4096,128]{1,0:T(8,128)(2,1)}, bf16[4096,128]{1,0:T(8,128)(2,1)}) custom-call(s32[23]{0:T(128)} %concatenate.17.info, s32[32]{0:T(128)} %bitcast.33, bf16[240,256]{1,0:T(8,128)(2,1)} %get-tuple-element.231.refs_0_, bf16[240,512]{1,0:T(8,128)(2,1)} %get-tuple-element.232.refs_1_, ...), custom_call_target="tpu_custom_call" | custom-call | bytes 6291456 | tf_op jit(solution)/shard_map/pallas_call | solution.py:375
  110.8 9.8 %collective-permute-done.24.refs_3_ = bf16[224,1280]{1,0:T(8,128)(2,1)S(1)} collective-permute-done((bf16[224,1280]{1,0:T(8,128)(2,1)S(1)}, bf16[224,1280]{1,0:T(8,128)(2,1)S(1)}, u32[]{:S(2)}, u32[]{:S(2)}) %collective-permute-start.24) | collective-permute-done | bytes 573472 | tf_op jit(solution)/shard_map/ppermute | solution.py:361
  124.0 12.0 %shard_map.229 = (bf16[256,1280]{1,0:T(8,128)(2,1)}, f32[256,1280]{1,0:T(8,128)}, bf16[1280,256]{1,0:T(8,128)(2,1)}, bf16[3,256,1280]{2,1,0:T(8,128)(2,1)}, bf16[256,1280]{1,0:T(8,128)(2,1)}) custom-call(s32[23]{0:T(128)} %concatenate.17.info, bf16[256,1280]{1,0:T(8,128)(2,1)} %bitcast.25, bf16[256,1280]{1,0:T(8,128)(2,1)} %bitcast.36, ...), custom_call_target="tpu_custom_call" | custom-call | flops 5033164800 | bytes 9830400 | tf_op jit(solution)/shard_map/pallas_call | solution.py:375
  136.1 6.0 %all-to-all-start.1 = ((bf16[16,80,256]{2,1,0:T(8,128)(2,1)}), bf16[16,80,256]{2,1,0:T(8,128)(2,1)S(1)}, u32[]{:S(2)}, u32[]{:S(2)}) async-start(bf16[16,80,256]{2,1,0:T(8,128)(2,1)} %bitcast.31), calls=%async_computation.1 | async-start | bytes 1310720 | tf_op jit(solution)/shard_map/all_to_all | solution.py:1058
  146.1 8.0 %shard_map.230 = (bf16[640,640]{1,0:T(8,128)(2,1)}, bf16[640,640]{1,0:T(8,128)(2,1)}, bf16[640,640]{1,0:T(8,128)(2,1)}, bf16[640,640]{1,0:T(8,128)(2,1)}, bf16[6...) custom-call(s32[23]{0:T(128)} %concatenate.17.info, bf16[3,256,1280]{2,1,0:T(8,128)(2,1)} %get-tuple-element.257.own, ...), custom_call_target="tpu_custom_call" | custom-call | flops 2516582400 | bytes 9830400 | tf_op jit(solution)/shard_map/pallas_call | solution.py:375
  154.1 3.6 %collective-permute-done.26.refs_5_ = bf16[224,1280]{1,0:T(8,128)(2,1)} collective-permute-done((bf16[224,1280]{1,0:T(8,128)(2,1)S(1)}, bf16[224,1280]{1,0:T(8,128)(2,1)}, u32[]{:S(2)}, u32[]{:S(2)}) %collective-permute-start.26) | collective-permute-done | bytes 573472 | tf_op jit(solution)/shard_map/ppermute | solution.py:361
  160.7 2.1 collective-permute-start.31
  162.8 30.4 %shard_map.231.grads = bf16[16,240,256]{2,1,0:T(8,128)(2,1)} custom-call(s32[23]{0:T(128)} %concatenate.17.info, s32[32]{0:T(128)} %bitcast.34, bf16[128,4096]{1,0:T(8,128)(2,1)} %get-tuple-element.247.refs_0_, bf16[4096,128]{1,0:T(8,128)(2,1)} %get-tuple-element.248.refs_1_, bf16[80,4096]{1,0:T(8,128)(2,1)} %get-tuple-element.241.refs_2_, ...), custom_call_target="tpu_custom_call" | custom-call | flops 21474836480 | bytes 3932160 | tf_op jit(solution)/shard_map/pallas_call | solution.py:375
  194.1 4.2 %all-to-all-start.2 = ((bf16[16,240,256]{2,1,0:T(8,128)(2,1)}), bf16[16,240,256]{2,1,0:T(8,128)(2,1)S(1)}, u32[]{:S(2)}, u32[]{:S(2)}) async-start(bf16[16,240,256]{2,1,0:T(8,128)(2,1)} %shard_map.231.grads), calls=%async_computation.2 | async-start | bytes 3932160 | tf_op jit(solution)/shard_map/all_to_all | solution.py:1112
  198.3 8.4 %shard_map.232 = (f32[256,640]{1,0:T(8,128)}, bf16[256,640]{1,0:T(8,128)(2,1)}) custom-call(s32[23]{0:T(128)} %concatenate.17.info, bf16[16,240,256]{2,1,0:T(8,128)(2,1)} %shard_map.231.grads, bf16[496,640]{1,0:T(8,128)(2,1)} %shard_map.221.refs_1_.refs_2_.own, bf16[496,640]{1,0:T(8,128)(2,1)} %copy-done, bf16[2048,1280]{1,0:T(8,128)(2,1)} %get-tuple-element.227.refs_0_, ...), custom_call_target="tpu_custom_call" | custom-call | flops 2516582400 | bytes 10485760 | tf_op jit(solution)/shard_map/pallas_call | solution.py:375
  207.8 4.4 %shard_map.233 = (bf16[320,640]{1,0:T(8,128)(2,1)}, bf16[320,640]{1,0:T(8,128)(2,1)}, bf16[320,640]{1,0:T(8,128)(2,1)}, bf16[320,640]{1,0:T(8,128)(2,1)}, bf16[3...) custom-call(s32[23]{0:T(128)} %concatenate.17.info, bf16[640,640]{1,0:T(8,128)(2,1)} %get-tuple-element.261.refs_0_, ...), custom_call_target="tpu_custom_call" | custom-call | bytes 2457600 | tf_op jit(solution)/shard_map/pallas_call | solution.py:375
  212.2 1.9 collective-permute-start.38
  217.1 2.0 collective-permute-start.35
  220.1 11.4 %collective-permute-done.38.refs_3_ = bf16[320,640]{1,0:T(8,128)(2,1)S(1)} collective-permute-done((bf16[320,640]{1,0:T(8,128)(2,1)}, bf16[320,640]{1,0:T(8,128)(2,1)S(1)}, u32[]{:S(2)}, u32[]{:S(2)}) %collective-permute-start.38) | collective-permute-done | bytes 409632 | tf_op jit(solution)/shard_map/ppermute | solution.py:361
  231.5 3.8 %collective-permute-start.33 = (bf16[256,640]{1,0:T(8,128)(2,1)S(1)}, bf16[256,640]{1,0:T(8,128)(2,1)}, u32[]{:S(2)}, u32[]{:S(2)}) collective-permute-start(bf16[256,640]{1,0:T(8,128)(2,1)S(1)} %add_convert_fusion.refs_0_), channel_id=1, source_target_pairs={{0,8},{1,9},{2,10},{3,11},{4,0},{5,1},{6,2},{7,3},{8,16},{9,17},{1... | collective-permute-start | bytes 983048 | tf_op jit(solution)/shard_map/ppermute | solution.py:361
  235.3 7.0 %collective-permute-done.39.refs_4_ = bf16[320,640]{1,0:T(8,128)(2,1)S(1)} collective-permute-done((bf16[320,640]{1,0:T(8,128)(2,1)}, bf16[320,640]{1,0:T(8,128)(2,1)S(1)}, u32[]{:S(2)}, u32[]{:S(2)}) %collective-permute-start.39) | collective-permute-done | bytes 409632 | tf_op jit(solution)/shard_map/ppermute | solution.py:361
  242.8 6.0 %collective-permute-done.35.refs_2_ = bf16[256,640]{1,0:T(8,128)(2,1)S(1)} collective-permute-done((bf16[256,640]{1,0:T(8,128)(2,1)S(1)}, bf16[256,640]{1,0:T(8,128)(2,1)S(1)}, u32[]{:S(2)}, u32[]{:S(2)}) %collective-permute-start.35) | collective-permute-done | bytes 327712 | tf_op jit(solution)/shard_map/ppermute | solution.py:361
  250.8 3.4 collective-permute-start.34
  254.1 2.8 shard_map.234
  258.1 2.6 collective-permute-done.36.refs_4_
  262.6 3.5 collective-permute-done.45.refs_3_
  267.8 2.7 shard_map.236.near
  273.0 2.3 shard_map.237
  275.4 5.4 %collective-permute-done.49.refs_0_ = bf16[256,640]{1,0:T(8,128)(2,1)S(1)} collective-permute-done((bf16[256,640]{1,0:T(8,128)(2,1)}, bf16[256,640]{1,0:T(8,128)(2,1)S(1)}, u32[]{:S(2)}, u32[]{:S(2)}) %collective-permute-start.49) | collective-permute-done | bytes 327712 | tf_op jit(solution)/shard_map/ppermute | solution.py:361
  282.9 4.3 %collective-permute-done.52.refs_3_ = bf16[128,640]{1,0:T(8,128)(2,1)S(1)} collective-permute-done((bf16[128,640]{1,0:T(8,128)(2,1)S(1)}, bf16[128,640]{1,0:T(8,128)(2,1)S(1)}, u32[]{:S(2)}, u32[]{:S(2)}) %collective-permute-start.52) | collective-permute-done | bytes 163872 | tf_op jit(solution)/shard_map/ppermute | solution.py:361
  289.3 11.3 %shard_map.235 = bf16[256,1280]{1,0:T(8,128)(2,1)} custom-call(s32[23]{0:T(128)} %concatenate.17.info, bf16[256,1280]{1,0:T(8,128)(2,1)} %bitcast.26, bf16[16,240,256]{2,1,0:T(8,128)(2,1)} %copy-done.5, f32[256,1280]{1,0:T(8,128)} %get-tuple-element.267.grad_mid, bf16[496,640]{1,0:T(8,128)(2,1)} %shard_map.221.refs_1_.refs_2_.own, bf16[496,640]{1,0:T(8,128)(2,1)} %copy-done, ...), custom_call_target="tpu_custom_call" | custom-call | flops 2516582400 | bytes 9830400 | tf_op jit(solution)/shard_map/pallas_call | solution.py:375
  305.7 9.3 %shard_map.238 = (f32[640,1280]{1,0:T(8,128)}, f32[640,1280]{1,0:T(8,128)}, f32[640,1280]{1,0:T(8,128)}, f32[640]{0:T(1024)}, f32[1,80]{1,0:T(1,128)}) custom-call(s32[23]{0:T(128)} %concatenate.17.info, bf16[5,256,640]{2,1,0:T(8,128)(2,1)} %shard_map.236.near, bf16[5,256,640]{2,1,0:T(8,128)(2,1)} %copy-done.58, bf16[256,640]{1,0:T(8,128)(2,1)} %copy-done.55, ...), custom_call_target="tpu_custom_call" | custom-call | flops 3145728000 | bytes 9830400 | tf_op jit(solution)/shard_map/pallas_call | solution.py:375
  315.0 2.5 collective-permute-start.60
  317.7 7.2 %collective-permute-done.60.refs_3_ = bf16[240,640]{1,0:T(8,128)(2,1)S(1)} collective-permute-done((bf16[240,640]{1,0:T(8,128)(2,1)S(1)}, bf16[240,640]{1,0:T(8,128)(2,1)S(1)}, u32[]{:S(2)}, u32[]{:S(2)}) %collective-permute-start.60) | collective-permute-done | bytes 307232 | tf_op jit(solution)/shard_map/ppermute | solution.py:361
  327.0 2.6 shard_map.239.near
  334.3 6.0 %shard_map.240 = (f32[640,128]{1,0:T(8,128)}, f32[640,1280]{1,0:T(8,128)}, f32[640,1280]{1,0:T(8,128)}, f32[640,1280]{1,0:T(8,128)}) custom-call(s32[23]{0:T(128)} %concatenate.17.info, bf16[5,240,640]{2,1,0:T(8,128)(2,1)} %shard_map.239.near, bf16[5,240,640]{2,1,0:T(8,128)(2,1)} %copy-done.6, bf16[640,1280]{1,0:T(8,128)(2,1)} %refs_10_.1), custom_call_target="tpu_custom_call" | custom-call | bytes 9830400 | tf_op jit(solution)/shard_map/pallas_call | solution.py:375
  343.6 4.1 %collective-permute-done.65.refs_2_ = bf16[112,640]{1,0:T(8,128)(2,1)S(1)} collective-permute-done((bf16[112,640]{1,0:T(8,128)(2,1)S(1)}, bf16[112,640]{1,0:T(8,128)(2,1)S(1)}, u32[]{:S(2)}, u32[]{:S(2)}) %collective-permute-start.65) | collective-permute-done | bytes 143392 | tf_op jit(solution)/shard_map/ppermute | solution.py:361
  350.1 4.8 %shard_map.241 = (f32[640,1280]{1,0:T(8,128)}, f32[640,1280]{1,0:T(8,128)}, f32[640,1280]{1,0:T(8,128)}, f32[640]{0:T(1024)}) custom-call(s32[23]{0:T(128)} %concatenate.17.info, bf16[240,640]{1,0:T(8,128)(2,1)} %copy-done.16, bf16[240,640]{1,0:T(8,128)(2,1)} %copy-done.15, ...), custom_call_target="tpu_custom_call", output_to_operand_aliasing={{0}: (12, {}), {1}: (13, {}), {2}: (14, {})} | custom-call | bytes 9830400 | tf_op jit(solution)/shard_map/pallas_call | solution.py:375
  (300 shorter events, 84.8 us)
Async XLA Ops:
  0.6 18.0 %collective-permute-start.1 = (bf16[256,1280]{1,0:T(8,128)(2,1)}, bf16[256,1280]{1,0:T(8,128)(2,1)S(1)}, u32[]{:S(2)}, u32[]{:S(2)}) collective-permute-start(bf16[256,1280]{1,0:T(8,128)(2,1)} %bitcast.22), channel_id=1, source_target_pairs={{0,4},{1,5},{2,6},{3,7},{4,12},{5,13},{6,14},{7,15},{8,0},{9,1},{1... | collective-permute-start | bytes 1966088 | tf_op jit(solution)/shard_map/ppermute | solution.py:361
  3.6 16.5 %collective-permute-start = (bf16[256,1280]{1,0:T(8,128)(2,1)}, bf16[256,1280]{1,0:T(8,128)(2,1)}, u32[]{:S(2)}, u32[]{:S(2)}) collective-permute-start(bf16[256,1280]{1,0:T(8,128)(2,1)} %bitcast.23), channel_id=1, source_target_pairs={{0,8},{1,9},{2,10},{3,11},{4,0},{5,1},{6,2},{7,3},{8,16},{9,17},{1... | collective-permute-start | bytes 1966088 | tf_op jit(solution)/shard_map/ppermute | solution.py:361
  4.8 11.7 %collective-permute-start.2 = (bf16[128,1280]{1,0:T(8,128)(2,1)S(1)}, bf16[128,1280]{1,0:T(8,128)(2,1)}, u32[]{:S(2)}, u32[]{:S(2)}) collective-permute-start(bf16[128,1280]{1,0:T(8,128)(2,1)S(1)} %constant_dynamic-slice_fusion.9), channel_id=1, source_target_pairs={{0,1},{1,0},{2,3},{3,2},{4,5},{5,4},{6,7},{7,6},{8,9},{9,8},{10,11... | collective-permute-start | bytes 983048 | tf_op jit(solution)/shard_map/ppermute | solution.py:361
  16.3 15.8 %collective-permute-start.5 = (bf16[496,640]{1,0:T(8,128)(2,1)}, bf16[496,640]{1,0:T(8,128)(2,1)S(1)}, u32[]{:S(2)}, u32[]{:S(2)}) collective-permute-start(bf16[496,640]{1,0:T(8,128)(2,1)} %shard_map.221.refs_1_.refs_2_.own), channel_id=1, source_target_pairs={{0,1},{1,0},{2,3},{3,2},{4,5},{5,4},{6,7},{7,6},{8,9},{9,8},{10,11... | collective-permute-start | bytes 1904648 | tf_op jit(solution)/shard_map/ppermute | solution.py:361
  20.1 17.7 %collective-permute-start.3 = (bf16[256,1280]{1,0:T(8,128)(2,1)}, bf16[256,1280]{1,0:T(8,128)(2,1)}, u32[]{:S(2)}, u32[]{:S(2)}) collective-permute-start(bf16[256,1280]{1,0:T(8,128)(2,1)} %collective-permute-done.refs_0_), channel_id=1, source_target_pairs={{0,8},{1,9},{2,10},{3,11},{4,0},{5,1},{6,2},{7,3},{8,16},{9,17},{1... | collective-permute-start | bytes 1966088 | tf_op jit(solution)/shard_map/ppermute | solution.py:361
  20.6 11.6 %collective-permute-start.6 = (bf16[128,1280]{1,0:T(8,128)(2,1)}, bf16[128,1280]{1,0:T(8,128)(2,1)S(1)}, u32[]{:S(2)}, u32[]{:S(2)}) collective-permute-start(bf16[128,1280]{1,0:T(8,128)(2,1)} %collective-permute-done.2.refs_3_), channel_id=1, source_target_pairs={{0,2},{1,3},{2,0},{3,1},{4,6},{5,7},{6,4},{7,5},{8,10},{9,11},{10,... | collective-permute-start | bytes 983048 | tf_op jit(solution)/shard_map/ppermute | solution.py:361
  20.6 17.3 %collective-permute-start.4 = (bf16[256,1280]{1,0:T(8,128)(2,1)S(1)}, bf16[256,1280]{1,0:T(8,128)(2,1)}, u32[]{:S(2)}, u32[]{:S(2)}) collective-permute-start(bf16[256,1280]{1,0:T(8,128)(2,1)S(1)} %collective-permute-done.1.refs_1_), channel_id=1, source_target_pairs={{0,4},{1,5},{2,6},{3,7},{4,12},{5,13},{6,14},{7,15},{8,0},{9,1},{1... | collective-permute-start | bytes 1966088 | tf_op jit(solution)/shard_map/ppermute | solution.py:361
  37.8 20.2 %collective-permute-start.9 = (bf16[320,1280]{1,0:T(8,128)(2,1)}, bf16[320,1280]{1,0:T(8,128)(2,1)}, u32[]{:S(2)}, u32[]{:S(2)}) collective-permute-start(bf16[320,1280]{1,0:T(8,128)(2,1)} %pad_maximum_fusion.2), channel_id=1, source_target_pairs={{0,1},{1,0},{2,3},{3,2},{4,5},{5,4},{6,7},{7,6},{8,9},{9,8},{10,11... | collective-permute-start | bytes 2457608 | tf_op jit(solution)/shard_map/ppermute | solution.py:361
  39.5 16.3 %collective-permute-start.7 = (bf16[256,1280]{1,0:T(8,128)(2,1)}, bf16[256,1280]{1,0:T(8,128)(2,1)S(1)}, u32[]{:S(2)}, u32[]{:S(2)}) collective-permute-start(bf16[256,1280]{1,0:T(8,128)(2,1)} %collective-permute-done.3.refs_0_), channel_id=1, source_target_pairs={{0,8},{1,9},{2,10},{3,11},{4,0},{5,1},{6,2},{7,3},{8,16},{9,17},{1... | collective-permute-start | bytes 1966088 | tf_op jit(solution)/shard_map/ppermute | solution.py:361
  41.0 16.0 %collective-permute-start.8 = (bf16[256,1280]{1,0:T(8,128)(2,1)}, bf16[256,1280]{1,0:T(8,128)(2,1)S(1)}, u32[]{:S(2)}, u32[]{:S(2)}) collective-permute-start(bf16[256,1280]{1,0:T(8,128)(2,1)} %collective-permute-done.4.refs_1_), channel_id=1, source_target_pairs={{0,4},{1,5},{2,6},{3,7},{4,12},{5,13},{6,14},{7,15},{8,0},{9,1},{1... | collective-permute-start | bytes 1966088 | tf_op jit(solution)/shard_map/ppermute | solution.py:361
  58.0 13.1 %collective-permute-start.13 = (bf16[320,1280]{1,0:T(8,128)(2,1)}, bf16[320,1280]{1,0:T(8,128)(2,1)S(1)}, u32[]{:S(2)}, u32[]{:S(2)}) collective-permute-start(bf16[320,1280]{1,0:T(8,128)(2,1)} %collective-permute-done.9.refs_4_), channel_id=1, source_target_pairs={{0,2},{1,3},{2,0},{3,1},{4,6},{5,7},{6,4},{7,5},{8,10},{9,11},{10,... | collective-permute-start | bytes 2457608 | tf_op jit(solution)/shard_map/ppermute | solution.py:361
  58.0 13.1 %collective-permute-start.12 = (bf16[176,1280]{1,0:T(8,128)(2,1)S(1)}, bf16[176,1280]{1,0:T(8,128)(2,1)S(1)}, u32[]{:S(2)}, u32[]{:S(2)}) collective-permute-start(bf16[176,1280]{1,0:T(8,128)(2,1)S(1)} %copy-done.27), channel_id=1, source_target_pairs={{0,1},{1,0},{2,3},{3,2},{4,5},{5,4},{6,7},{7,6},{8,9},{9,8},{10,11... | collective-permute-start | bytes 1351688 | tf_op jit(solution)/shard_map/ppermute | solution.py:361
  59.7 9.9 %collective-permute-start.11 = (bf16[128,1280]{1,0:T(8,128)(2,1)S(1)}, bf16[128,1280]{1,0:T(8,128)(2,1)S(1)}, u32[]{:S(2)}, u32[]{:S(2)}) collective-permute-start(bf16[128,1280]{1,0:T(8,128)(2,1)S(1)} %slice.51), channel_id=1, source_target_pairs={{0,4},{1,5},{2,6},{3,7},{4,12},{5,13},{6,14},{7,15},{8,0},{9,1},{1... | collective-permute-start | bytes 983048 | tf_op jit(solution)/shard_map/ppermute | solution.py:361
  61.3 9.8 %collective-permute-start.10 = (bf16[128,1280]{1,0:T(8,128)(2,1)S(1)}, bf16[128,1280]{1,0:T(8,128)(2,1)S(1)}, u32[]{:S(2)}, u32[]{:S(2)}) collective-permute-start(bf16[128,1280]{1,0:T(8,128)(2,1)S(1)} %slice.50), channel_id=1, source_target_pairs={{0,8},{1,9},{2,10},{3,11},{4,0},{5,1},{6,2},{7,3},{8,16},{9,17},{1... | collective-permute-start | bytes 983048 | tf_op jit(solution)/shard_map/ppermute | solution.py:361
  76.3 21.1 %collective-permute-start.20 = (bf16[336,1280]{1,0:T(8,128)(2,1)S(1)}, bf16[336,1280]{1,0:T(8,128)(2,1)S(1)}, u32[]{:S(2)}, u32[]{:S(2)}) collective-permute-start(bf16[336,1280]{1,0:T(8,128)(2,1)S(1)} %pad_maximum_fusion.1), channel_id=1, source_target_pairs={{0,1},{1,0},{2,3},{3,2},{4,5},{5,4},{6,7},{7,6},{8,9},{9,8},{10,11... | collective-permute-start | bytes 2580488 | tf_op jit(solution)/shard_map/ppermute | solution.py:361
  98.3 24.1 %collective-permute-start.22 = (bf16[2048,1280]{1,0:T(8,128)(2,1)}, bf16[2048,1280]{1,0:T(8,128)(2,1)}, u32[]{:S(2)}, u32[]{:S(2)}) collective-permute-start(bf16[2048,1280]{1,0:T(8,128)(2,1)} %get-tuple-element.227.refs_0_), channel_id=1, source_target_pairs={{0,2},{1,3},{2,0},{3,1},{4,6},{5,7},{6,4},{7,5},{8,10},{9,11},{10,... | collective-permute-start | bytes 15728648 | tf_op jit(solution)/shard_map/ppermute | solution.py:361
  98.3 24.0 %all-to-all-start = ((bf16[16,80,256]{2,1,0:T(8,128)(2,1)}), bf16[16,80,256]{2,1,0:T(8,128)(2,1)S(1)}, u32[]{:S(2)}, u32[]{:S(2)}) async-start(bf16[16,80,256]{2,1,0:T(8,128)(2,1)} %get-tuple-element.224.refs_5_), calls=%async_computation | async-start | bytes 1310720 | tf_op jit(solution)/shard_map/all_to_all | solution.py:1034
  104.6 17.7 %collective-permute-start.21 = (bf16[336,1280]{1,0:T(8,128)(2,1)}, bf16[336,1280]{1,0:T(8,128)(2,1)S(1)}, u32[]{:S(2)}, u32[]{:S(2)}) collective-permute-start(bf16[336,1280]{1,0:T(8,128)(2,1)} %copy-done.59), channel_id=1, source_target_pairs={{0,2},{1,3},{2,0},{3,1},{4,6},{5,7},{6,4},{7,5},{8,10},{9,11},{10,... | collective-permute-start | bytes 2580488 | tf_op jit(solution)/shard_map/ppermute | solution.py:361
  105.2 15.4 %collective-permute-start.23 = (bf16[256,1280]{1,0:T(8,128)(2,1)}, bf16[256,1280]{1,0:T(8,128)(2,1)S(1)}, u32[]{:S(2)}, u32[]{:S(2)}) collective-permute-start(bf16[256,1280]{1,0:T(8,128)(2,1)} %bitcast.35), channel_id=1, source_target_pairs={{0,2},{1,3},{2,0},{3,1},{4,6},{5,7},{6,4},{7,5},{8,10},{9,11},{10,... | collective-permute-start | bytes 1966088 | tf_op jit(solution)/shard_map/ppermute | solution.py:361
  105.3 15.3 %collective-permute-start.24 = (bf16[224,1280]{1,0:T(8,128)(2,1)S(1)}, bf16[224,1280]{1,0:T(8,128)(2,1)S(1)}, u32[]{:S(2)}, u32[]{:S(2)}) collective-permute-start(bf16[224,1280]{1,0:T(8,128)(2,1)S(1)} %copy-done.26), channel_id=1, source_target_pairs={{0,1},{1,0},{2,3},{3,2},{4,5},{5,4},{6,7},{7,6},{8,9},{9,8},{10,11... | collective-permute-start | bytes 1720328 | tf_op jit(solution)/shard_map/ppermute | solution.py:361
  122.4 13.6 %collective-permute-start.25 = (bf16[160,1280]{1,0:T(8,128)(2,1)S(1)}, bf16[160,1280]{1,0:T(8,128)(2,1)}, u32[]{:S(2)}, u32[]{:S(2)}) collective-permute-start(bf16[160,1280]{1,0:T(8,128)(2,1)S(1)} %copy-done.30), channel_id=1, source_target_pairs={{0,1},{1,0},{2,3},{3,2},{4,5},{5,4},{6,7},{7,6},{8,9},{9,8},{10,11... | collective-permute-start | bytes 1228808 | tf_op jit(solution)/shard_map/ppermute | solution.py:361
  136.1 22.6 %all-to-all-start.1 = ((bf16[16,80,256]{2,1,0:T(8,128)(2,1)}), bf16[16,80,256]{2,1,0:T(8,128)(2,1)S(1)}, u32[]{:S(2)}, u32[]{:S(2)}) async-start(bf16[16,80,256]{2,1,0:T(8,128)(2,1)} %bitcast.31), calls=%async_computation.1 | async-start | bytes 1310720 | tf_op jit(solution)/shard_map/all_to_all | solution.py:1058
  142.7 15.1 %collective-permute-start.26 = (bf16[224,1280]{1,0:T(8,128)(2,1)S(1)}, bf16[224,1280]{1,0:T(8,128)(2,1)}, u32[]{:S(2)}, u32[]{:S(2)}) collective-permute-start(bf16[224,1280]{1,0:T(8,128)(2,1)S(1)} %copy-done.25), channel_id=1, source_target_pairs={{0,1},{1,0},{2,3},{3,2},{4,5},{5,4},{6,7},{7,6},{8,9},{9,8},{10,11... | collective-permute-start | bytes 1720328 | tf_op jit(solution)/shard_map/ppermute | solution.py:361
  158.7 34.5 %collective-permute-start.29 = (bf16[640,640]{1,0:T(8,128)(2,1)}, bf16[640,640]{1,0:T(8,128)(2,1)S(1)}, u32[]{:S(2)}, u32[]{:S(2)}) collective-permute-start(bf16[640,640]{1,0:T(8,128)(2,1)} %get-tuple-element.263), channel_id=1, source_target_pairs={{0,1},{1,0},{2,3},{3,2},{4,5},{5,4},{6,7},{7,6},{8,9},{9,8},{10,11... | collective-permute-start | bytes 2457608 | tf_op jit(solution)/shard_map/ppermute | solution.py:361
  159.7 33.5 %collective-permute-start.30 = (bf16[640,640]{1,0:T(8,128)(2,1)}, bf16[640,640]{1,0:T(8,128)(2,1)}, u32[]{:S(2)}, u32[]{:S(2)}) collective-permute-start(bf16[640,640]{1,0:T(8,128)(2,1)} %get-tuple-element.264), channel_id=1, source_target_pairs={{0,4},{1,5},{2,6},{3,7},{4,0},{5,1},{6,2},{7,3},{8,12},{9,13},{10,... | collective-permute-start | bytes 2457608 | tf_op jit(solution)/shard_map/ppermute | solution.py:361
  160.7 32.5 %collective-permute-start.31 = (bf16[640,640]{1,0:T(8,128)(2,1)}, bf16[640,640]{1,0:T(8,128)(2,1)}, u32[]{:S(2)}, u32[]{:S(2)}) collective-permute-start(bf16[640,640]{1,0:T(8,128)(2,1)} %get-tuple-element.265), channel_id=1, source_target_pairs={{0,8},{1,9},{2,10},{3,11},{4,12},{5,13},{6,14},{7,15},{8,0},{9,1},... | collective-permute-start | bytes 2457608 | tf_op jit(solution)/shard_map/ppermute | solution.py:361
  194.1 68.4 %all-to-all-start.2 = ((bf16[16,240,256]{2,1,0:T(8,128)(2,1)}), bf16[16,240,256]{2,1,0:T(8,128)(2,1)S(1)}, u32[]{:S(2)}, u32[]{:S(2)}) async-start(bf16[16,240,256]{2,1,0:T(8,128)(2,1)} %shard_map.231.grads), calls=%async_computation.2 | async-start | bytes 3932160 | tf_op jit(solution)/shard_map/all_to_all | solution.py:1112
  206.7 10.3 %collective-permute-start.32 = (bf16[256,640]{1,0:T(8,128)(2,1)}, bf16[256,640]{1,0:T(8,128)(2,1)S(1)}, u32[]{:S(2)}, u32[]{:S(2)}) collective-permute-start(bf16[256,640]{1,0:T(8,128)(2,1)} %get-tuple-element.283), channel_id=1, source_target_pairs={{0,1},{1,0},{2,3},{3,2},{4,5},{5,4},{6,7},{7,6},{8,9},{9,8},{10,11... | collective-permute-start | bytes 983048 | tf_op jit(solution)/shard_map/ppermute | solution.py:361
  212.2 19.2 %collective-permute-start.38 = (bf16[320,640]{1,0:T(8,128)(2,1)}, bf16[320,640]{1,0:T(8,128)(2,1)S(1)}, u32[]{:S(2)}, u32[]{:S(2)}) collective-permute-start(bf16[320,640]{1,0:T(8,128)(2,1)} %get-tuple-element.288), channel_id=1, source_target_pairs={{0,4},{1,5},{2,6},{3,7},{4,0},{5,1},{6,2},{7,3},{8,12},{9,13},{10,... | collective-permute-start | bytes 1228808 | tf_op jit(solution)/shard_map/ppermute | solution.py:361
  214.1 28.1 %collective-permute-start.39 = (bf16[320,640]{1,0:T(8,128)(2,1)}, bf16[320,640]{1,0:T(8,128)(2,1)S(1)}, u32[]{:S(2)}, u32[]{:S(2)}) collective-permute-start(bf16[320,640]{1,0:T(8,128)(2,1)} %get-tuple-element.289), channel_id=1, source_target_pairs={{0,8},{1,9},{2,10},{3,11},{4,12},{5,13},{6,14},{7,15},{8,0},{9,1},... | collective-permute-start | bytes 1228808 | tf_op jit(solution)/shard_map/ppermute | solution.py:361
  215.6 26.6 %collective-permute-start.40 = (bf16[320,640]{1,0:T(8,128)(2,1)}, bf16[320,640]{1,0:T(8,128)(2,1)S(1)}, u32[]{:S(2)}, u32[]{:S(2)}) collective-permute-start(bf16[320,640]{1,0:T(8,128)(2,1)} %get-tuple-element.290), channel_id=1, source_target_pairs={{0,1},{1,0},{2,3},{3,2},{4,5},{5,4},{6,7},{7,6},{8,9},{9,8},{10,11... | collective-permute-start | bytes 1228808 | tf_op jit(solution)/shard_map/ppermute | solution.py:361
  217.1 31.7 %collective-permute-start.35 = (bf16[256,640]{1,0:T(8,128)(2,1)S(1)}, bf16[256,640]{1,0:T(8,128)(2,1)S(1)}, u32[]{:S(2)}, u32[]{:S(2)}) collective-permute-start(bf16[256,640]{1,0:T(8,128)(2,1)S(1)} %add_convert_fusion.refs_0_), channel_id=1, source_target_pairs={{0,4},{1,5},{2,6},{3,7},{4,12},{5,13},{6,14},{7,15},{8,0},{9,1},{1... | collective-permute-start | bytes 983048 | tf_op jit(solution)/shard_map/ppermute | solution.py:361
  219.1 43.4 %collective-permute-start.37 = (bf16[352,1280]{1,0:T(8,128)(2,1)S(1)}, bf16[352,1280]{1,0:T(8,128)(2,1)S(1)}, u32[]{:S(2)}, u32[]{:S(2)}) collective-permute-start(bf16[352,1280]{1,0:T(8,128)(2,1)S(1)} %copy-done.13), channel_id=1, source_target_pairs={{0,1},{1,0},{2,3},{3,2},{4,5},{5,4},{6,7},{7,6},{8,9},{9,8},{10,11... | collective-permute-start | bytes 2703368 | tf_op jit(solution)/shard_map/ppermute | solution.py:361
  231.5 17.3 %collective-permute-start.33 = (bf16[256,640]{1,0:T(8,128)(2,1)S(1)}, bf16[256,640]{1,0:T(8,128)(2,1)}, u32[]{:S(2)}, u32[]{:S(2)}) collective-permute-start(bf16[256,640]{1,0:T(8,128)(2,1)S(1)} %add_convert_fusion.refs_0_), channel_id=1, source_target_pairs={{0,8},{1,9},{2,10},{3,11},{4,0},{5,1},{6,2},{7,3},{8,16},{9,17},{1... | collective-permute-start | bytes 983048 | tf_op jit(solution)/shard_map/ppermute | solution.py:361
  242.2 14.7 %collective-permute-start.41 = (bf16[224,1280]{1,0:T(8,128)(2,1)S(1)}, bf16[224,1280]{1,0:T(8,128)(2,1)S(1)}, u32[]{:S(2)}, u32[]{:S(2)}) collective-permute-start(bf16[224,1280]{1,0:T(8,128)(2,1)S(1)} %copy-done.22), channel_id=1, source_target_pairs={{0,2},{1,3},{2,0},{3,1},{4,6},{5,7},{6,4},{7,5},{8,10},{9,11},{10,... | collective-permute-start | bytes 1720328 | tf_op jit(solution)/shard_map/ppermute | solution.py:361
  242.3 14.8 %collective-permute-start.43 = (bf16[224,1280]{1,0:T(8,128)(2,1)}, bf16[224,1280]{1,0:T(8,128)(2,1)S(1)}, u32[]{:S(2)}, u32[]{:S(2)}) collective-permute-start(bf16[224,1280]{1,0:T(8,128)(2,1)} %collective-permute-done.26.refs_5_), channel_id=1, source_target_pairs={{0,2},{1,3},{2,0},{3,1},{4,6},{5,7},{6,4},{7,5},{8,10},{9,11},{10,... | collective-permute-start | bytes 1720328 | tf_op jit(solution)/shard_map/ppermute | solution.py:361
  248.8 12.0 %collective-permute-start.36 = (bf16[256,640]{1,0:T(8,128)(2,1)S(1)}, bf16[256,640]{1,0:T(8,128)(2,1)S(1)}, u32[]{:S(2)}, u32[]{:S(2)}) collective-permute-start(bf16[256,640]{1,0:T(8,128)(2,1)S(1)} %collective-permute-done.35.refs_2_), channel_id=1, source_target_pairs={{0,4},{1,5},{2,6},{3,7},{4,12},{5,13},{6,14},{7,15},{8,0},{9,1},{1... | collective-permute-start | bytes 983048 | tf_op jit(solution)/shard_map/ppermute | solution.py:361
  250.8 11.7 %collective-permute-start.34 = (bf16[256,640]{1,0:T(8,128)(2,1)}, bf16[256,640]{1,0:T(8,128)(2,1)}, u32[]{:S(2)}, u32[]{:S(2)}) collective-permute-start(bf16[256,640]{1,0:T(8,128)(2,1)} %collective-permute-done.33.refs_1_), channel_id=1, source_target_pairs={{0,8},{1,9},{2,10},{3,11},{4,0},{5,1},{6,2},{7,3},{8,16},{9,17},{1... | collective-permute-start | bytes 983048 | tf_op jit(solution)/shard_map/ppermute | solution.py:361
  270.5 30.2 %collective-permute-start.48 = (bf16[5,256,640]{2,1,0:T(8,128)(2,1)}, bf16[5,256,640]{2,1,0:T(8,128)(2,1)S(1)}, u32[]{:S(2)}, u32[]{:S(2)}) collective-permute-start(bf16[5,256,640]{2,1,0:T(8,128)(2,1)} %shard_map.236.near), channel_id=1, source_target_pairs={{0,2},{1,3},{2,0},{3,1},{4,6},{5,7},{6,4},{7,5},{8,10},{9,11},{10,... | collective-permute-start | bytes 4915208 | tf_op jit(solution)/shard_map/ppermute | solution.py:361
  270.5 17.0 %collective-permute-start.44 = (bf16[352,1280]{1,0:T(8,128)(2,1)S(1)}, bf16[352,1280]{1,0:T(8,128)(2,1)S(1)}, u32[]{:S(2)}, u32[]{:S(2)}) collective-permute-start(bf16[352,1280]{1,0:T(8,128)(2,1)S(1)} %collective-permute-done.37.refs_6_), channel_id=1, source_target_pairs={{0,2},{1,3},{2,0},{3,1},{4,6},{5,7},{6,4},{7,5},{8,10},{9,11},{10,... | collective-permute-start | bytes 2703368 | tf_op jit(solution)/shard_map/ppermute | solution.py:361
  282.4 18.2 %collective-permute-start.53 = (bf16[256,640]{1,0:T(8,128)(2,1)S(1)}, bf16[256,640]{1,0:T(8,128)(2,1)S(1)}, u32[]{:S(2)}, u32[]{:S(2)}) collective-permute-start(bf16[256,640]{1,0:T(8,128)(2,1)S(1)} %collective-permute-done.49.refs_0_), channel_id=1, source_target_pairs={{0,2},{1,3},{2,0},{3,1},{4,6},{5,7},{6,4},{7,5},{8,10},{9,11},{10,... | collective-permute-start | bytes 983048 | tf_op jit(solution)/shard_map/ppermute | solution.py:361
  282.4 18.2 %collective-permute-start.54 = (bf16[256,640]{1,0:T(8,128)(2,1)S(1)}, bf16[256,640]{1,0:T(8,128)(2,1)S(1)}, u32[]{:S(2)}, u32[]{:S(2)}) collective-permute-start(bf16[256,640]{1,0:T(8,128)(2,1)S(1)} %collective-permute-done.50.refs_1_), channel_id=1, source_target_pairs={{0,2},{1,3},{2,0},{3,1},{4,6},{5,7},{6,4},{7,5},{8,10},{9,11},{10,... | collective-permute-start | bytes 983048 | tf_op jit(solution)/shard_map/ppermute | solution.py:361
  287.3 14.6 %collective-permute-start.57 = (bf16[240,640]{1,0:T(8,128)(2,1)}, bf16[240,640]{1,0:T(8,128)(2,1)S(1)}, u32[]{:S(2)}, u32[]{:S(2)}) collective-permute-start(bf16[240,640]{1,0:T(8,128)(2,1)} %get-tuple-element.320), channel_id=1, source_target_pairs={{0,16},{1,17},{2,18},{3,19},{4,20},{5,21},{6,22},{7,23},{8,24},{9,... | collective-permute-start | bytes 921608 | tf_op jit(solution)/shard_map/ppermute | solution.py:361
  287.5 13.1 %collective-permute-start.51 = (bf16[128,640]{1,0:T(8,128)(2,1)S(1)}, bf16[128,640]{1,0:T(8,128)(2,1)S(1)}, u32[]{:S(2)}, u32[]{:S(2)}) collective-permute-start(bf16[128,640]{1,0:T(8,128)(2,1)S(1)} %slice.52), channel_id=1, source_target_pairs={{0,8},{1,9},{2,10},{3,11},{4,0},{5,1},{6,2},{7,3},{8,16},{9,17},{1... | collective-permute-start | bytes 491528 | tf_op jit(solution)/shard_map/ppermute | solution.py:361
  301.9 13.1 %collective-permute-start.59 = (bf16[240,640]{1,0:T(8,128)(2,1)S(1)}, bf16[240,640]{1,0:T(8,128)(2,1)S(1)}, u32[]{:S(2)}, u32[]{:S(2)}) collective-permute-start(bf16[240,640]{1,0:T(8,128)(2,1)S(1)} %add_convert_fusion.1.refs_0_), channel_id=1, source_target_pairs={{0,4},{1,5},{2,6},{3,7},{4,12},{5,13},{6,14},{7,15},{8,0},{9,1},{1... | collective-permute-start | bytes 921608 | tf_op jit(solution)/shard_map/ppermute | solution.py:361
  303.6 11.4 %collective-permute-start.58 = (bf16[240,640]{1,0:T(8,128)(2,1)S(1)}, bf16[240,640]{1,0:T(8,128)(2,1)S(1)}, u32[]{:S(2)}, u32[]{:S(2)}) collective-permute-start(bf16[240,640]{1,0:T(8,128)(2,1)S(1)} %add_convert_fusion.1.refs_0_), channel_id=1, source_target_pairs={{0,8},{1,9},{2,10},{3,11},{4,0},{5,1},{6,2},{7,3},{8,16},{9,17},{1... | collective-permute-start | bytes 921608 | tf_op jit(solution)/shard_map/ppermute | solution.py:361
  315.0 9.9 %collective-permute-start.60 = (bf16[240,640]{1,0:T(8,128)(2,1)S(1)}, bf16[240,640]{1,0:T(8,128)(2,1)S(1)}, u32[]{:S(2)}, u32[]{:S(2)}) collective-permute-start(bf16[240,640]{1,0:T(8,128)(2,1)S(1)} %collective-permute-done.58.refs_1_), channel_id=1, source_target_pairs={{0,8},{1,9},{2,10},{3,11},{4,0},{5,1},{6,2},{7,3},{8,16},{9,17},{1... | collective-permute-start | bytes 921608 | tf_op jit(solution)/shard_map/ppermute | solution.py:361
  329.6 10.7 %collective-permute-start.61 = (bf16[240,640]{1,0:T(8,128)(2,1)}, bf16[240,640]{1,0:T(8,128)(2,1)S(1)}, u32[]{:S(2)}, u32[]{:S(2)}) collective-permute-start(bf16[240,640]{1,0:T(8,128)(2,1)} %copy-done.42), channel_id=1, source_target_pairs={{0,8},{1,9},{2,10},{3,11},{4,0},{5,1},{6,2},{7,3},{8,16},{9,17},{1... | collective-permute-start | bytes 921608 | tf_op jit(solution)/shard_map/ppermute | solution.py:361
  (103 other events, 758.8 us)

commit v6 on v4

--- a/solution.py
+++ b/solution.py
@@ -822,9 +822,8 @@
     return copies
 
 
-def spread_kernel(info, near, near_partner, expand, sums, *refs):
-    outs, (blocks, sems) = refs[:3], refs[3:]
-    pieces = [stack.at[at] for stack in (near, near_partner) for at in range(5)]
+def spread_kernel(info, *refs):
+    pieces, (expand, sums), outs, (blocks, sems) = refs[:10], refs[10:12], refs[12:15], refs[15:]
     sums[...] = jnp.zeros_like(sums)
     arrive(scatter(info, pieces, 0, blocks, sems, outs, expand, sums))
 
@@ -1185,11 +1184,12 @@
     forth1, back1 = after((forth1, back1), grad_query)
     forth2, back2 = send(forth1, FORTH), send(back1, BACK)
     forth3, back3 = send(forth2, FORTH), send(back2, BACK)
-    near, near_partner = stacked([piece, forth1, back1, forth2, back2])
+    near = [piece, forth1, back1, forth2, back2]
+    near_partner = [send(value, CORE_SWAP) for value in near]
     partial_out = call(
         spread_kernel,
         [((half_width, 128), F32), shard, shard, shard],
-        [info, near, near_partner, w_expand],
+        [info, *near, *near_partner, w_expand],
         smem=1,
         out_anys=(1, 2, 3),
         scratch=[pltpu.VMEM((30, PART, half_width), F32), pltpu.SemaphoreType.DMA((30,))],

time: 362 us -> 359 us (level)
    pallas_call x21 -> x20, Pallas kernels: 151 us -> 148 us  [call(): pl.pallas_call(body, out_shape=[jax.ShapeDtypeStruct(shape, kind) for sha...]
    ppermute x71 -> x75, waiting for transfers between devices: 101 us -> 99.9 us  [send(): return lax.ppermute(value, AXES, moves)]
    ppermute x71 -> x75, starting transfers between devices: 58.3 us -> 59 us  [send(): return lax.ppermute(value, AXES, moves)]
    unnamed x164 -> x172, local copies, waits for them, and re-layouts: 12.3 us -> 11.9 us
  transfers between devices with their start and end apart: 74 -> 78, of which waited for: 31 -> 31; matrix products, arithmetic and copies ran while one was open for 4% -> 4% of each run, Pallas kernels for 39% -> 40%
where the time goes in v6:
time: 359 us; the launch traced here: 353 us
  Pallas kernels  148 us (41%)
  waiting for transfers between devices  101 us (28%)
  starting transfers between devices  75.5 us (21%)
  local copies, waits for them, and re-layouts  22.1 us (6%)
    pallas_call x20, Pallas kernels, call(): pl.pallas_call(body, out_shape=[jax.ShapeDtypeStruct(shape, kind) for sha...  148 us
    ppermute x75, waiting for transfers between devices, send(): return lax.ppermute(value, AXES, moves)  99.9 us
    ppermute x75, starting transfers between devices, send(): return lax.ppermute(value, AXES, moves)  59 us
    unnamed x172, local copies, waits for them, and re-layouts  11.9 us
  transfers between devices with their start and end apart: 78, of which 31 were waited for; matrix products, arithmetic and copies ran while one was open for 4% of the time, Pallas kernels for 40%

profile of v6, /device:TPU:0, one launch (start us, length us, event | category | flops | bytes accessed | tf_op | source)
XLA Modules:
  0.0 353.1 jit_solution(9870890318909912729)
XLA Ops:
  0.6 3.0 collective-permute-start.1
  4.8 2.0 collective-permute-start.2
  11.2 5.2 %shard_map.221.refs_1_.refs_2_.own = bf16[496,640]{1,0:T(8,128)(2,1)} custom-call(s32[23]{0:T(128)} %concatenate.17.info, bf16[640,1280]{1,0:T(8,128)(2,1)} %refs_0_.3, bf16[640,1280]{1,0:T(8,128)(2,1)} %refs_1_.3, bf16[640,1280]{1,0:T(8,128)(2,1)} %refs_2_.3, bf16[1,640]{1,0:T(2,128)(2,1)} %broadcast_in_dim.20.gain_a.refs_8_, ...), custom_call_target="tpu_custom_call" | custom-call | flops 786432000 | bytes 4915200 | tf_op jit(solution)/shard_map/pallas_call | solution.py:375
  16.5 2.2 collective-permute-done.1.refs_1_
  28.5 1.8 constant_dynamic-slice_fusion.2
  32.2 5.7 %collective-permute-done.4.refs_1_ = bf16[256,1280]{1,0:T(8,128)(2,1)} collective-permute-done((bf16[256,1280]{1,0:T(8,128)(2,1)S(1)}, bf16[256,1280]{1,0:T(8,128)(2,1)}, u32[]{:S(2)}, u32[]{:S(2)}) %collective-permute-start.4) | collective-permute-done | bytes 655392 | tf_op jit(solution)/shard_map/ppermute | solution.py:361
  42.8 3.4 shard_map.222
  46.2 4.2 %shard_map.223 = (bf16[2048,1280]{1,0:T(8,128)(2,1)}, bf16[240,512]{1,0:T(8,128)(2,1)}, bf16[240,512]{1,0:T(8,128)(2,1)}) custom-call(s32[23]{0:T(128)} %concatenate.17.info, bf16[256,1280]{1,0:T(8,128)(2,1)} %collective-permute-done.refs_0_, bf16[256,1280]{1,0:T(8,128)(2,1)} %copy-done.16, ...), custom_call_target="tpu_custom_call", output_to_operand_aliasing={{0}: (6, {})} | custom-call | flops 629145600 | bytes 2621440 | tf_op jit(solution)/shard_map/pallas_call | solution.py:375
  50.5 4.2 %shard_map.224 = (bf16[2048,1280]{1,0:T(8,128)(2,1)}, bf16[240,512]{1,0:T(8,128)(2,1)}, bf16[240,512]{1,0:T(8,128)(2,1)}) custom-call(s32[23]{0:T(128)} %concatenate.17.info, bf16[256,1280]{1,0:T(8,128)(2,1)} %collective-permute-done.3.refs_0_, bf16[256,1280]{1,0:T(8,128)(2,1)} %collective-permute-done.4.refs_1_, ...), custom_call_target="tpu_custom_call", output_to_operand_aliasing={{0}: (6, {})} | custom-call | flops 629145600 | bytes 2621440 | tf_op jit(solution)/shard_map/pallas_call | solution.py:375
  62.1 4.3 %shard_map.225 = (bf16[2048,1280]{1,0:T(8,128)(2,1)}, bf16[240,512]{1,0:T(8,128)(2,1)}, bf16[240,512]{1,0:T(8,128)(2,1)}) custom-call(s32[23]{0:T(128)} %concatenate.17.info, bf16[256,1280]{1,0:T(8,128)(2,1)} %copy-done.6, bf16[256,1280]{1,0:T(8,128)(2,1)} %copy-done.7, ...), custom_call_target="tpu_custom_call", output_to_operand_aliasing={{0}: (6, {})} | custom-call | flops 629145600 | bytes 2621440 | tf_op jit(solution)/shard_map/pallas_call | solution.py:375
  66.4 3.2 collective-permute-done.11.refs_1_
  72.3 3.5 shard_map.226
  78.4 15.3 %shard_map.227 = (bf16[16,80,256]{2,1,0:T(8,128)(2,1)}, bf16[128,4096]{1,0:T(8,128)(2,1)}, bf16[4096,128]{1,0:T(8,128)(2,1)}) custom-call(s32[23]{0:T(128)} %concatenate.17.info, s32[32]{0:T(128)} %bitcast.32, bf16[240,256]{1,0:T(8,128)(2,1)} %get-tuple-element.226.refs_0_, bf16[240,512]{1,0:T(8,128)(2,1)} %get-tuple-element.227.refs_1_, ...), custom_call_target="tpu_custom_call" | custom-call | flops 8589934592 | bytes 1966080 | tf_op jit(solution)/shard_map/pallas_call | solution.py:375
  93.7 3.7 %collective-permute-done.20.refs_6_ = bf16[336,1280]{1,0:T(8,128)(2,1)S(1)} collective-permute-done((bf16[336,1280]{1,0:T(8,128)(2,1)S(1)}, bf16[336,1280]{1,0:T(8,128)(2,1)S(1)}, u32[]{:S(2)}, u32[]{:S(2)}) %collective-permute-start.20) | collective-permute-done | bytes 860192 | tf_op jit(solution)/shard_map/ppermute | solution.py:361
  98.3 6.3 %all-to-all-start = ((bf16[16,80,256]{2,1,0:T(8,128)(2,1)}), bf16[16,80,256]{2,1,0:T(8,128)(2,1)S(1)}, u32[]{:S(2)}, u32[]{:S(2)}) async-start(bf16[16,80,256]{2,1,0:T(8,128)(2,1)} %get-tuple-element.219.refs_5_), calls=%async_computation | async-start | bytes 1310720 | tf_op jit(solution)/shard_map/all_to_all | solution.py:1033
  106.8 4.0 %shard_map.228 = (bf16[80,4096]{1,0:T(8,128)(2,1)}, bf16[4096,128]{1,0:T(8,128)(2,1)}, bf16[4096,128]{1,0:T(8,128)(2,1)}) custom-call(s32[23]{0:T(128)} %concatenate.17.info, s32[32]{0:T(128)} %bitcast.33, bf16[240,256]{1,0:T(8,128)(2,1)} %get-tuple-element.226.refs_0_, bf16[240,512]{1,0:T(8,128)(2,1)} %get-tuple-element.227.refs_1_, ...), custom_call_target="tpu_custom_call" | custom-call | bytes 6291456 | tf_op jit(solution)/shard_map/pallas_call | solution.py:375
  110.8 9.8 %collective-permute-done.24.refs_3_ = bf16[224,1280]{1,0:T(8,128)(2,1)S(1)} collective-permute-done((bf16[224,1280]{1,0:T(8,128)(2,1)S(1)}, bf16[224,1280]{1,0:T(8,128)(2,1)S(1)}, u32[]{:S(2)}, u32[]{:S(2)}) %collective-permute-start.24) | collective-permute-done | bytes 573472 | tf_op jit(solution)/shard_map/ppermute | solution.py:361
  123.9 12.1 %shard_map.229 = (bf16[256,1280]{1,0:T(8,128)(2,1)}, f32[256,1280]{1,0:T(8,128)}, bf16[1280,256]{1,0:T(8,128)(2,1)}, bf16[3,256,1280]{2,1,0:T(8,128)(2,1)}, bf16[256,1280]{1,0:T(8,128)(2,1)}) custom-call(s32[23]{0:T(128)} %concatenate.17.info, bf16[256,1280]{1,0:T(8,128)(2,1)} %bitcast.25, bf16[256,1280]{1,0:T(8,128)(2,1)} %bitcast.36, ...), custom_call_target="tpu_custom_call" | custom-call | flops 5033164800 | bytes 9830400 | tf_op jit(solution)/shard_map/pallas_call | solution.py:375
  136.1 6.0 %all-to-all-start.1 = ((bf16[16,80,256]{2,1,0:T(8,128)(2,1)}), bf16[16,80,256]{2,1,0:T(8,128)(2,1)S(1)}, u32[]{:S(2)}, u32[]{:S(2)}) async-start(bf16[16,80,256]{2,1,0:T(8,128)(2,1)} %bitcast.31), calls=%async_computation.1 | async-start | bytes 1310720 | tf_op jit(solution)/shard_map/all_to_all | solution.py:1057
  146.1 8.1 %shard_map.230 = (bf16[640,640]{1,0:T(8,128)(2,1)}, bf16[640,640]{1,0:T(8,128)(2,1)}, bf16[640,640]{1,0:T(8,128)(2,1)}, bf16[640,640]{1,0:T(8,128)(2,1)}, bf16[6...) custom-call(s32[23]{0:T(128)} %concatenate.17.info, bf16[3,256,1280]{2,1,0:T(8,128)(2,1)} %get-tuple-element.252.own, ...), custom_call_target="tpu_custom_call" | custom-call | flops 2516582400 | bytes 9830400 | tf_op jit(solution)/shard_map/pallas_call | solution.py:375
  154.2 3.6 %collective-permute-done.26.refs_5_ = bf16[224,1280]{1,0:T(8,128)(2,1)} collective-permute-done((bf16[224,1280]{1,0:T(8,128)(2,1)S(1)}, bf16[224,1280]{1,0:T(8,128)(2,1)}, u32[]{:S(2)}, u32[]{:S(2)}) %collective-permute-start.26) | collective-permute-done | bytes 573472 | tf_op jit(solution)/shard_map/ppermute | solution.py:361
  160.7 2.1 collective-permute-start.31
  162.8 31.4 %shard_map.231.grads = bf16[16,240,256]{2,1,0:T(8,128)(2,1)} custom-call(s32[23]{0:T(128)} %concatenate.17.info, s32[32]{0:T(128)} %bitcast.34, bf16[128,4096]{1,0:T(8,128)(2,1)} %get-tuple-element.242.refs_0_, bf16[4096,128]{1,0:T(8,128)(2,1)} %get-tuple-element.243.refs_1_, bf16[80,4096]{1,0:T(8,128)(2,1)} %get-tuple-element.236.refs_2_, ...), custom_call_target="tpu_custom_call" | custom-call | flops 21474836480 | bytes 3932160 | tf_op jit(solution)/shard_map/pallas_call | solution.py:375
  194.2 4.2 %all-to-all-start.2 = ((bf16[16,240,256]{2,1,0:T(8,128)(2,1)}), bf16[16,240,256]{2,1,0:T(8,128)(2,1)S(1)}, u32[]{:S(2)}, u32[]{:S(2)}) async-start(bf16[16,240,256]{2,1,0:T(8,128)(2,1)} %shard_map.231.grads), calls=%async_computation.2 | async-start | bytes 3932160 | tf_op jit(solution)/shard_map/all_to_all | solution.py:1112
  199.5 8.4 %shard_map.232 = (f32[256,640]{1,0:T(8,128)}, bf16[256,640]{1,0:T(8,128)(2,1)}) custom-call(s32[23]{0:T(128)} %concatenate.17.info, bf16[16,240,256]{2,1,0:T(8,128)(2,1)} %shard_map.231.grads, bf16[496,640]{1,0:T(8,128)(2,1)} %shard_map.221.refs_1_.refs_2_.own, bf16[496,640]{1,0:T(8,128)(2,1)} %copy-done, bf16[2048,1280]{1,0:T(8,128)(2,1)} %get-tuple-element.222.refs_0_, ...), custom_call_target="tpu_custom_call" | custom-call | flops 2516582400 | bytes 10485760 | tf_op jit(solution)/shard_map/pallas_call | solution.py:375
  209.0 4.4 %shard_map.233 = (bf16[320,640]{1,0:T(8,128)(2,1)}, bf16[320,640]{1,0:T(8,128)(2,1)}, bf16[320,640]{1,0:T(8,128)(2,1)}, bf16[320,640]{1,0:T(8,128)(2,1)}, bf16[3...) custom-call(s32[23]{0:T(128)} %concatenate.17.info, bf16[640,640]{1,0:T(8,128)(2,1)} %get-tuple-element.256.refs_0_, ...), custom_call_target="tpu_custom_call" | custom-call | bytes 2457600 | tf_op jit(solution)/shard_map/pallas_call | solution.py:375
  213.4 1.9 collective-permute-start.42
  217.7 10.8 %collective-permute-done.33 = bf16[256,640]{1,0:T(8,128)(2,1)S(1)} collective-permute-done((bf16[256,640]{1,0:T(8,128)(2,1)}, bf16[256,640]{1,0:T(8,128)(2,1)S(1)}, u32[]{:S(2)}, u32[]{:S(2)}) %collective-permute-start.33) | collective-permute-done | bytes 327712 | tf_op jit(solution)/shard_map/ppermute | solution.py:361
  228.6 1.9 collective-permute-start.39
  231.6 10.8 %collective-permute-done.43.refs_4_ = bf16[320,640]{1,0:T(8,128)(2,1)S(1)} collective-permute-done((bf16[320,640]{1,0:T(8,128)(2,1)}, bf16[320,640]{1,0:T(8,128)(2,1)S(1)}, u32[]{:S(2)}, u32[]{:S(2)}) %collective-permute-start.43) | collective-permute-done | bytes 409632 | tf_op jit(solution)/shard_map/ppermute | solution.py:361
  242.7 6.3 %collective-permute-done.39.refs_2_ = bf16[256,640]{1,0:T(8,128)(2,1)S(1)} collective-permute-done((bf16[256,640]{1,0:T(8,128)(2,1)S(1)}, bf16[256,640]{1,0:T(8,128)(2,1)S(1)}, u32[]{:S(2)}, u32[]{:S(2)}) %collective-permute-start.39) | collective-permute-done | bytes 327712 | tf_op jit(solution)/shard_map/ppermute | solution.py:361
  248.9 2.2 collective-permute-done.38.refs_1_
  253.2 2.8 shard_map.235
  256.0 4.7 %collective-permute-done.41.refs_4_ = bf16[256,640]{1,0:T(8,128)(2,1)S(1)} collective-permute-done((bf16[256,640]{1,0:T(8,128)(2,1)S(1)}, bf16[256,640]{1,0:T(8,128)(2,1)S(1)}, u32[]{:S(2)}, u32[]{:S(2)}) %collective-permute-start.41) | collective-permute-done | bytes 327712 | tf_op jit(solution)/shard_map/ppermute | solution.py:361
  261.6 3.4 shard_map.236.near
  269.9 3.1 collective-permute-done.48.refs_3_
  275.5 5.5 %collective-permute-done.50.refs_5_ = bf16[160,640]{1,0:T(8,128)(2,1)S(1)} collective-permute-done((bf16[160,640]{1,0:T(8,128)(2,1)S(1)}, bf16[160,640]{1,0:T(8,128)(2,1)S(1)}, u32[]{:S(2)}, u32[]{:S(2)}) %collective-permute-start.50) | collective-permute-done | bytes 204832 | tf_op jit(solution)/shard_map/ppermute | solution.py:361
  281.7 2.4 shard_map.237
  284.1 2.0 collective-permute-start.52
  286.7 2.9 collective-permute-done.52.refs_3_
  289.6 11.3 %shard_map.234 = bf16[256,1280]{1,0:T(8,128)(2,1)} custom-call(s32[23]{0:T(128)} %concatenate.17.info, bf16[256,1280]{1,0:T(8,128)(2,1)} %bitcast.26, bf16[16,240,256]{2,1,0:T(8,128)(2,1)} %copy-done.5, f32[256,1280]{1,0:T(8,128)} %get-tuple-element.262.grad_mid, bf16[496,640]{1,0:T(8,128)(2,1)} %shard_map.221.refs_1_.refs_2_.own, bf16[496,640]{1,0:T(8,128)(2,1)} %copy-done, ...), custom_call_target="tpu_custom_call" | custom-call | flops 2516582400 | bytes 9830400 | tf_op jit(solution)/shard_map/pallas_call | solution.py:375
  304.0 2.3 collective-permute-start.58
  307.1 9.3 %shard_map.238 = (f32[640,1280]{1,0:T(8,128)}, f32[640,1280]{1,0:T(8,128)}, f32[640,1280]{1,0:T(8,128)}, f32[640]{0:T(1024)}, f32[1,80]{1,0:T(1,128)}) custom-call(s32[23]{0:T(128)} %concatenate.17.info, bf16[5,256,640]{2,1,0:T(8,128)(2,1)} %shard_map.236.near, bf16[5,256,640]{2,1,0:T(8,128)(2,1)} %copy-done.64, bf16[256,640]{1,0:T(8,128)(2,1)} %copy-done.61, ...), custom_call_target="tpu_custom_call" | custom-call | flops 3145728000 | bytes 9830400 | tf_op jit(solution)/shard_map/pallas_call | solution.py:375
  316.4 2.5 collective-permute-start.60
  319.6 6.6 %collective-permute-done.60.refs_3_ = bf16[240,640]{1,0:T(8,128)(2,1)S(1)} collective-permute-done((bf16[240,640]{1,0:T(8,128)(2,1)S(1)}, bf16[240,640]{1,0:T(8,128)(2,1)S(1)}, u32[]{:S(2)}, u32[]{:S(2)}) %collective-permute-start.60) | collective-permute-done | bytes 307232 | tf_op jit(solution)/shard_map/ppermute | solution.py:361
  331.3 6.0 %shard_map.239 = (f32[640,128]{1,0:T(8,128)}, f32[640,1280]{1,0:T(8,128)}, f32[640,1280]{1,0:T(8,128)}, f32[640,1280]{1,0:T(8,128)}) custom-call(s32[23]{0:T(128)} %concatenate.17.info, bf16[240,640]{1,0:T(8,128)(2,1)} %copy-done.9, bf16[240,640]{1,0:T(8,128)(2,1)} %copy-done.38, bf16[240,640]{1,0:T(8,128)(2,1)} %copy-done.37, bf16[240,640]{1,0:T(8,128)(2,1)} %copy-done.39, ...), custom_call_target="tpu_custom_call" | custom-call | bytes 9830400 | tf_op jit(solution)/shard_map/pallas_call | solution.py:375
  341.4 3.7 %collective-permute-done.69.refs_2_ = bf16[112,640]{1,0:T(8,128)(2,1)S(1)} collective-permute-done((bf16[112,640]{1,0:T(8,128)(2,1)S(1)}, bf16[112,640]{1,0:T(8,128)(2,1)S(1)}, u32[]{:S(2)}, u32[]{:S(2)}) %collective-permute-start.69) | collective-permute-done | bytes 143392 | tf_op jit(solution)/shard_map/ppermute | solution.py:361
  347.8 4.8 %shard_map.240 = (f32[640,1280]{1,0:T(8,128)}, f32[640,1280]{1,0:T(8,128)}, f32[640,1280]{1,0:T(8,128)}, f32[640]{0:T(1024)}) custom-call(s32[23]{0:T(128)} %concatenate.17.info, bf16[240,640]{1,0:T(8,128)(2,1)} %copy-done.12, bf16[240,640]{1,0:T(8,128)(2,1)} %copy-done.11, ...), custom_call_target="tpu_custom_call", output_to_operand_aliasing={{0}: (12, {}), {1}: (13, {}), {2}: (14, {})} | custom-call | bytes 9830400 | tf_op jit(solution)/shard_map/pallas_call | solution.py:375
  (325 shorter events, 81.1 us)
Async XLA Ops:
  0.6 18.0 %collective-permute-start.1 = (bf16[256,1280]{1,0:T(8,128)(2,1)}, bf16[256,1280]{1,0:T(8,128)(2,1)S(1)}, u32[]{:S(2)}, u32[]{:S(2)}) collective-permute-start(bf16[256,1280]{1,0:T(8,128)(2,1)} %bitcast.22), channel_id=1, source_target_pairs={{0,4},{1,5},{2,6},{3,7},{4,12},{5,13},{6,14},{7,15},{8,0},{9,1},{1... | collective-permute-start | bytes 1966088 | tf_op jit(solution)/shard_map/ppermute | solution.py:361
  3.6 16.5 %collective-permute-start = (bf16[256,1280]{1,0:T(8,128)(2,1)}, bf16[256,1280]{1,0:T(8,128)(2,1)}, u32[]{:S(2)}, u32[]{:S(2)}) collective-permute-start(bf16[256,1280]{1,0:T(8,128)(2,1)} %bitcast.23), channel_id=1, source_target_pairs={{0,8},{1,9},{2,10},{3,11},{4,0},{5,1},{6,2},{7,3},{8,16},{9,17},{1... | collective-permute-start | bytes 1966088 | tf_op jit(solution)/shard_map/ppermute | solution.py:361
  4.8 11.7 %collective-permute-start.2 = (bf16[128,1280]{1,0:T(8,128)(2,1)S(1)}, bf16[128,1280]{1,0:T(8,128)(2,1)}, u32[]{:S(2)}, u32[]{:S(2)}) collective-permute-start(bf16[128,1280]{1,0:T(8,128)(2,1)S(1)} %constant_dynamic-slice_fusion.9), channel_id=1, source_target_pairs={{0,1},{1,0},{2,3},{3,2},{4,5},{5,4},{6,7},{7,6},{8,9},{9,8},{10,11... | collective-permute-start | bytes 983048 | tf_op jit(solution)/shard_map/ppermute | solution.py:361
  16.4 15.8 %collective-permute-start.5 = (bf16[496,640]{1,0:T(8,128)(2,1)}, bf16[496,640]{1,0:T(8,128)(2,1)S(1)}, u32[]{:S(2)}, u32[]{:S(2)}) collective-permute-start(bf16[496,640]{1,0:T(8,128)(2,1)} %shard_map.221.refs_1_.refs_2_.own), channel_id=1, source_target_pairs={{0,1},{1,0},{2,3},{3,2},{4,5},{5,4},{6,7},{7,6},{8,9},{9,8},{10,11... | collective-permute-start | bytes 1904648 | tf_op jit(solution)/shard_map/ppermute | solution.py:361
  20.1 17.7 %collective-permute-start.3 = (bf16[256,1280]{1,0:T(8,128)(2,1)}, bf16[256,1280]{1,0:T(8,128)(2,1)}, u32[]{:S(2)}, u32[]{:S(2)}) collective-permute-start(bf16[256,1280]{1,0:T(8,128)(2,1)} %collective-permute-done.refs_0_), channel_id=1, source_target_pairs={{0,8},{1,9},{2,10},{3,11},{4,0},{5,1},{6,2},{7,3},{8,16},{9,17},{1... | collective-permute-start | bytes 1966088 | tf_op jit(solution)/shard_map/ppermute | solution.py:361
  20.6 11.6 %collective-permute-start.6 = (bf16[128,1280]{1,0:T(8,128)(2,1)}, bf16[128,1280]{1,0:T(8,128)(2,1)S(1)}, u32[]{:S(2)}, u32[]{:S(2)}) collective-permute-start(bf16[128,1280]{1,0:T(8,128)(2,1)} %collective-permute-done.2.refs_3_), channel_id=1, source_target_pairs={{0,2},{1,3},{2,0},{3,1},{4,6},{5,7},{6,4},{7,5},{8,10},{9,11},{10,... | collective-permute-start | bytes 983048 | tf_op jit(solution)/shard_map/ppermute | solution.py:361
  20.6 17.3 %collective-permute-start.4 = (bf16[256,1280]{1,0:T(8,128)(2,1)S(1)}, bf16[256,1280]{1,0:T(8,128)(2,1)}, u32[]{:S(2)}, u32[]{:S(2)}) collective-permute-start(bf16[256,1280]{1,0:T(8,128)(2,1)S(1)} %collective-permute-done.1.refs_1_), channel_id=1, source_target_pairs={{0,4},{1,5},{2,6},{3,7},{4,12},{5,13},{6,14},{7,15},{8,0},{9,1},{1... | collective-permute-start | bytes 1966088 | tf_op jit(solution)/shard_map/ppermute | solution.py:361
  37.8 20.2 %collective-permute-start.9 = (bf16[320,1280]{1,0:T(8,128)(2,1)}, bf16[320,1280]{1,0:T(8,128)(2,1)}, u32[]{:S(2)}, u32[]{:S(2)}) collective-permute-start(bf16[320,1280]{1,0:T(8,128)(2,1)} %pad_maximum_fusion.2), channel_id=1, source_target_pairs={{0,1},{1,0},{2,3},{3,2},{4,5},{5,4},{6,7},{7,6},{8,9},{9,8},{10,11... | collective-permute-start | bytes 2457608 | tf_op jit(solution)/shard_map/ppermute | solution.py:361
  39.5 16.3 %collective-permute-start.7 = (bf16[256,1280]{1,0:T(8,128)(2,1)}, bf16[256,1280]{1,0:T(8,128)(2,1)S(1)}, u32[]{:S(2)}, u32[]{:S(2)}) collective-permute-start(bf16[256,1280]{1,0:T(8,128)(2,1)} %collective-permute-done.3.refs_0_), channel_id=1, source_target_pairs={{0,8},{1,9},{2,10},{3,11},{4,0},{5,1},{6,2},{7,3},{8,16},{9,17},{1... | collective-permute-start | bytes 1966088 | tf_op jit(solution)/shard_map/ppermute | solution.py:361
  41.0 16.0 %collective-permute-start.8 = (bf16[256,1280]{1,0:T(8,128)(2,1)}, bf16[256,1280]{1,0:T(8,128)(2,1)S(1)}, u32[]{:S(2)}, u32[]{:S(2)}) collective-permute-start(bf16[256,1280]{1,0:T(8,128)(2,1)} %collective-permute-done.4.refs_1_), channel_id=1, source_target_pairs={{0,4},{1,5},{2,6},{3,7},{4,12},{5,13},{6,14},{7,15},{8,0},{9,1},{1... | collective-permute-start | bytes 1966088 | tf_op jit(solution)/shard_map/ppermute | solution.py:361
  58.0 13.1 %collective-permute-start.13 = (bf16[320,1280]{1,0:T(8,128)(2,1)}, bf16[320,1280]{1,0:T(8,128)(2,1)S(1)}, u32[]{:S(2)}, u32[]{:S(2)}) collective-permute-start(bf16[320,1280]{1,0:T(8,128)(2,1)} %collective-permute-done.9.refs_4_), channel_id=1, source_target_pairs={{0,2},{1,3},{2,0},{3,1},{4,6},{5,7},{6,4},{7,5},{8,10},{9,11},{10,... | collective-permute-start | bytes 2457608 | tf_op jit(solution)/shard_map/ppermute | solution.py:361
  58.0 13.1 %collective-permute-start.12 = (bf16[176,1280]{1,0:T(8,128)(2,1)S(1)}, bf16[176,1280]{1,0:T(8,128)(2,1)S(1)}, u32[]{:S(2)}, u32[]{:S(2)}) collective-permute-start(bf16[176,1280]{1,0:T(8,128)(2,1)S(1)} %copy-done.23), channel_id=1, source_target_pairs={{0,1},{1,0},{2,3},{3,2},{4,5},{5,4},{6,7},{7,6},{8,9},{9,8},{10,11... | collective-permute-start | bytes 1351688 | tf_op jit(solution)/shard_map/ppermute | solution.py:361
  59.7 9.9 %collective-permute-start.11 = (bf16[128,1280]{1,0:T(8,128)(2,1)S(1)}, bf16[128,1280]{1,0:T(8,128)(2,1)S(1)}, u32[]{:S(2)}, u32[]{:S(2)}) collective-permute-start(bf16[128,1280]{1,0:T(8,128)(2,1)S(1)} %slice.51), channel_id=1, source_target_pairs={{0,4},{1,5},{2,6},{3,7},{4,12},{5,13},{6,14},{7,15},{8,0},{9,1},{1... | collective-permute-start | bytes 983048 | tf_op jit(solution)/shard_map/ppermute | solution.py:361
  61.3 9.8 %collective-permute-start.10 = (bf16[128,1280]{1,0:T(8,128)(2,1)S(1)}, bf16[128,1280]{1,0:T(8,128)(2,1)S(1)}, u32[]{:S(2)}, u32[]{:S(2)}) collective-permute-start(bf16[128,1280]{1,0:T(8,128)(2,1)S(1)} %slice.50), channel_id=1, source_target_pairs={{0,8},{1,9},{2,10},{3,11},{4,0},{5,1},{6,2},{7,3},{8,16},{9,17},{1... | collective-permute-start | bytes 983048 | tf_op jit(solution)/shard_map/ppermute | solution.py:361
  76.3 21.1 %collective-permute-start.20 = (bf16[336,1280]{1,0:T(8,128)(2,1)S(1)}, bf16[336,1280]{1,0:T(8,128)(2,1)S(1)}, u32[]{:S(2)}, u32[]{:S(2)}) collective-permute-start(bf16[336,1280]{1,0:T(8,128)(2,1)S(1)} %pad_maximum_fusion.1), channel_id=1, source_target_pairs={{0,1},{1,0},{2,3},{3,2},{4,5},{5,4},{6,7},{7,6},{8,9},{9,8},{10,11... | collective-permute-start | bytes 2580488 | tf_op jit(solution)/shard_map/ppermute | solution.py:361
  98.3 24.0 %collective-permute-start.22 = (bf16[2048,1280]{1,0:T(8,128)(2,1)}, bf16[2048,1280]{1,0:T(8,128)(2,1)}, u32[]{:S(2)}, u32[]{:S(2)}) collective-permute-start(bf16[2048,1280]{1,0:T(8,128)(2,1)} %get-tuple-element.222.refs_0_), channel_id=1, source_target_pairs={{0,2},{1,3},{2,0},{3,1},{4,6},{5,7},{6,4},{7,5},{8,10},{9,11},{10,... | collective-permute-start | bytes 15728648 | tf_op jit(solution)/shard_map/ppermute | solution.py:361
  98.3 24.0 %all-to-all-start = ((bf16[16,80,256]{2,1,0:T(8,128)(2,1)}), bf16[16,80,256]{2,1,0:T(8,128)(2,1)S(1)}, u32[]{:S(2)}, u32[]{:S(2)}) async-start(bf16[16,80,256]{2,1,0:T(8,128)(2,1)} %get-tuple-element.219.refs_5_), calls=%async_computation | async-start | bytes 1310720 | tf_op jit(solution)/shard_map/all_to_all | solution.py:1033
  104.7 17.6 %collective-permute-start.21 = (bf16[336,1280]{1,0:T(8,128)(2,1)}, bf16[336,1280]{1,0:T(8,128)(2,1)S(1)}, u32[]{:S(2)}, u32[]{:S(2)}) collective-permute-start(bf16[336,1280]{1,0:T(8,128)(2,1)} %copy-done.65), channel_id=1, source_target_pairs={{0,2},{1,3},{2,0},{3,1},{4,6},{5,7},{6,4},{7,5},{8,10},{9,11},{10,... | collective-permute-start | bytes 2580488 | tf_op jit(solution)/shard_map/ppermute | solution.py:361
  105.2 15.4 %collective-permute-start.23 = (bf16[256,1280]{1,0:T(8,128)(2,1)}, bf16[256,1280]{1,0:T(8,128)(2,1)S(1)}, u32[]{:S(2)}, u32[]{:S(2)}) collective-permute-start(bf16[256,1280]{1,0:T(8,128)(2,1)} %bitcast.35), channel_id=1, source_target_pairs={{0,2},{1,3},{2,0},{3,1},{4,6},{5,7},{6,4},{7,5},{8,10},{9,11},{10,... | collective-permute-start | bytes 1966088 | tf_op jit(solution)/shard_map/ppermute | solution.py:361
  105.3 15.3 %collective-permute-start.24 = (bf16[224,1280]{1,0:T(8,128)(2,1)S(1)}, bf16[224,1280]{1,0:T(8,128)(2,1)S(1)}, u32[]{:S(2)}, u32[]{:S(2)}) collective-permute-start(bf16[224,1280]{1,0:T(8,128)(2,1)S(1)} %copy-done.22), channel_id=1, source_target_pairs={{0,1},{1,0},{2,3},{3,2},{4,5},{5,4},{6,7},{7,6},{8,9},{9,8},{10,11... | collective-permute-start | bytes 1720328 | tf_op jit(solution)/shard_map/ppermute | solution.py:361
  122.3 13.7 %collective-permute-start.25 = (bf16[160,1280]{1,0:T(8,128)(2,1)S(1)}, bf16[160,1280]{1,0:T(8,128)(2,1)}, u32[]{:S(2)}, u32[]{:S(2)}) collective-permute-start(bf16[160,1280]{1,0:T(8,128)(2,1)S(1)} %copy-done.26), channel_id=1, source_target_pairs={{0,1},{1,0},{2,3},{3,2},{4,5},{5,4},{6,7},{7,6},{8,9},{9,8},{10,11... | collective-permute-start | bytes 1228808 | tf_op jit(solution)/shard_map/ppermute | solution.py:361
  136.1 22.6 %all-to-all-start.1 = ((bf16[16,80,256]{2,1,0:T(8,128)(2,1)}), bf16[16,80,256]{2,1,0:T(8,128)(2,1)S(1)}, u32[]{:S(2)}, u32[]{:S(2)}) async-start(bf16[16,80,256]{2,1,0:T(8,128)(2,1)} %bitcast.31), calls=%async_computation.1 | async-start | bytes 1310720 | tf_op jit(solution)/shard_map/all_to_all | solution.py:1057
  142.7 15.1 %collective-permute-start.26 = (bf16[224,1280]{1,0:T(8,128)(2,1)S(1)}, bf16[224,1280]{1,0:T(8,128)(2,1)}, u32[]{:S(2)}, u32[]{:S(2)}) collective-permute-start(bf16[224,1280]{1,0:T(8,128)(2,1)S(1)} %copy-done.21), channel_id=1, source_target_pairs={{0,1},{1,0},{2,3},{3,2},{4,5},{5,4},{6,7},{7,6},{8,9},{9,8},{10,11... | collective-permute-start | bytes 1720328 | tf_op jit(solution)/shard_map/ppermute | solution.py:361
  158.7 35.5 %collective-permute-start.29 = (bf16[640,640]{1,0:T(8,128)(2,1)}, bf16[640,640]{1,0:T(8,128)(2,1)}, u32[]{:S(2)}, u32[]{:S(2)}) collective-permute-start(bf16[640,640]{1,0:T(8,128)(2,1)} %get-tuple-element.258), channel_id=1, source_target_pairs={{0,1},{1,0},{2,3},{3,2},{4,5},{5,4},{6,7},{7,6},{8,9},{9,8},{10,11... | collective-permute-start | bytes 2457608 | tf_op jit(solution)/shard_map/ppermute | solution.py:361
  159.7 34.5 %collective-permute-start.30 = (bf16[640,640]{1,0:T(8,128)(2,1)}, bf16[640,640]{1,0:T(8,128)(2,1)}, u32[]{:S(2)}, u32[]{:S(2)}) collective-permute-start(bf16[640,640]{1,0:T(8,128)(2,1)} %get-tuple-element.259), channel_id=1, source_target_pairs={{0,4},{1,5},{2,6},{3,7},{4,0},{5,1},{6,2},{7,3},{8,12},{9,13},{10,... | collective-permute-start | bytes 2457608 | tf_op jit(solution)/shard_map/ppermute | solution.py:361
  160.7 33.5 %collective-permute-start.31 = (bf16[640,640]{1,0:T(8,128)(2,1)}, bf16[640,640]{1,0:T(8,128)(2,1)}, u32[]{:S(2)}, u32[]{:S(2)}) collective-permute-start(bf16[640,640]{1,0:T(8,128)(2,1)} %get-tuple-element.260), channel_id=1, source_target_pairs={{0,8},{1,9},{2,10},{3,11},{4,12},{5,13},{6,14},{7,15},{8,0},{9,1},... | collective-permute-start | bytes 2457608 | tf_op jit(solution)/shard_map/ppermute | solution.py:361
  194.2 67.3 %all-to-all-start.2 = ((bf16[16,240,256]{2,1,0:T(8,128)(2,1)}), bf16[16,240,256]{2,1,0:T(8,128)(2,1)S(1)}, u32[]{:S(2)}, u32[]{:S(2)}) async-start(bf16[16,240,256]{2,1,0:T(8,128)(2,1)} %shard_map.231.grads), calls=%async_computation.2 | async-start | bytes 3932160 | tf_op jit(solution)/shard_map/all_to_all | solution.py:1112
  198.4 32.1 %collective-permute-start.32 = (bf16[352,1280]{1,0:T(8,128)(2,1)}, bf16[352,1280]{1,0:T(8,128)(2,1)S(1)}, u32[]{:S(2)}, u32[]{:S(2)}) collective-permute-start(bf16[352,1280]{1,0:T(8,128)(2,1)} %pad_maximum_fusion), channel_id=1, source_target_pairs={{0,1},{1,0},{2,3},{3,2},{4,5},{5,4},{6,7},{7,6},{8,9},{9,8},{10,11... | collective-permute-start | bytes 2703368 | tf_op jit(solution)/shard_map/ppermute | solution.py:361
  207.9 20.6 %collective-permute-start.33 = (bf16[256,640]{1,0:T(8,128)(2,1)}, bf16[256,640]{1,0:T(8,128)(2,1)S(1)}, u32[]{:S(2)}, u32[]{:S(2)}) collective-permute-start(bf16[256,640]{1,0:T(8,128)(2,1)} %get-tuple-element.280), channel_id=1, source_target_pairs={{0,1},{1,0},{2,3},{3,2},{4,5},{5,4},{6,7},{7,6},{8,9},{9,8},{10,11... | collective-permute-start | bytes 983048 | tf_op jit(solution)/shard_map/ppermute | solution.py:361
  213.4 18.2 %collective-permute-start.42 = (bf16[320,640]{1,0:T(8,128)(2,1)}, bf16[320,640]{1,0:T(8,128)(2,1)S(1)}, u32[]{:S(2)}, u32[]{:S(2)}) collective-permute-start(bf16[320,640]{1,0:T(8,128)(2,1)} %get-tuple-element.287), channel_id=1, source_target_pairs={{0,4},{1,5},{2,6},{3,7},{4,0},{5,1},{6,2},{7,3},{8,12},{9,13},{10,... | collective-permute-start | bytes 1228808 | tf_op jit(solution)/shard_map/ppermute | solution.py:361
  215.2 27.1 %collective-permute-start.43 = (bf16[320,640]{1,0:T(8,128)(2,1)}, bf16[320,640]{1,0:T(8,128)(2,1)S(1)}, u32[]{:S(2)}, u32[]{:S(2)}) collective-permute-start(bf16[320,640]{1,0:T(8,128)(2,1)} %get-tuple-element.288), channel_id=1, source_target_pairs={{0,8},{1,9},{2,10},{3,11},{4,12},{5,13},{6,14},{7,15},{8,0},{9,1},... | collective-permute-start | bytes 1228808 | tf_op jit(solution)/shard_map/ppermute | solution.py:361
  216.7 25.9 %collective-permute-start.44 = (bf16[320,640]{1,0:T(8,128)(2,1)}, bf16[320,640]{1,0:T(8,128)(2,1)S(1)}, u32[]{:S(2)}, u32[]{:S(2)}) collective-permute-start(bf16[320,640]{1,0:T(8,128)(2,1)} %get-tuple-element.289), channel_id=1, source_target_pairs={{0,1},{1,0},{2,3},{3,2},{4,5},{5,4},{6,7},{7,6},{8,9},{9,8},{10,11... | collective-permute-start | bytes 1228808 | tf_op jit(solution)/shard_map/ppermute | solution.py:361
  228.6 20.3 %collective-permute-start.39 = (bf16[256,640]{1,0:T(8,128)(2,1)S(1)}, bf16[256,640]{1,0:T(8,128)(2,1)S(1)}, u32[]{:S(2)}, u32[]{:S(2)}) collective-permute-start(bf16[256,640]{1,0:T(8,128)(2,1)S(1)} %add_convert_fusion.refs_0_), channel_id=1, source_target_pairs={{0,4},{1,5},{2,6},{3,7},{4,12},{5,13},{6,14},{7,15},{8,0},{9,1},{1... | collective-permute-start | bytes 983048 | tf_op jit(solution)/shard_map/ppermute | solution.py:361
  230.5 31.0 %collective-permute-start.37 = (bf16[352,1280]{1,0:T(8,128)(2,1)S(1)}, bf16[352,1280]{1,0:T(8,128)(2,1)}, u32[]{:S(2)}, u32[]{:S(2)}) collective-permute-start(bf16[352,1280]{1,0:T(8,128)(2,1)S(1)} %collective-permute-done.32.refs_6_), channel_id=1, source_target_pairs={{0,2},{1,3},{2,0},{3,1},{4,6},{5,7},{6,4},{7,5},{8,10},{9,11},{10,... | collective-permute-start | bytes 2703368 | tf_op jit(solution)/shard_map/ppermute | solution.py:361
  231.6 21.1 %collective-permute-start.35 = (bf16[160,1280]{1,0:T(8,128)(2,1)}, bf16[160,1280]{1,0:T(8,128)(2,1)S(1)}, u32[]{:S(2)}, u32[]{:S(2)}) collective-permute-start(bf16[160,1280]{1,0:T(8,128)(2,1)} %collective-permute-done.25.refs_4_), channel_id=1, source_target_pairs={{0,2},{1,3},{2,0},{3,1},{4,6},{5,7},{6,4},{7,5},{8,10},{9,11},{10,... | collective-permute-start | bytes 1228808 | tf_op jit(solution)/shard_map/ppermute | solution.py:361
  242.6 13.4 %collective-permute-start.34 = (bf16[224,1280]{1,0:T(8,128)(2,1)S(1)}, bf16[224,1280]{1,0:T(8,128)(2,1)S(1)}, u32[]{:S(2)}, u32[]{:S(2)}) collective-permute-start(bf16[224,1280]{1,0:T(8,128)(2,1)S(1)} %copy-done.18), channel_id=1, source_target_pairs={{0,2},{1,3},{2,0},{3,1},{4,6},{5,7},{6,4},{7,5},{8,10},{9,11},{10,... | collective-permute-start | bytes 1720328 | tf_op jit(solution)/shard_map/ppermute | solution.py:361
  265.1 36.0 %collective-permute-start.45 = (bf16[5,256,640]{2,1,0:T(8,128)(2,1)}, bf16[5,256,640]{2,1,0:T(8,128)(2,1)S(1)}, u32[]{:S(2)}, u32[]{:S(2)}) collective-permute-start(bf16[5,256,640]{2,1,0:T(8,128)(2,1)} %shard_map.236.near), channel_id=1, source_target_pairs={{0,2},{1,3},{2,0},{3,1},{4,6},{5,7},{6,4},{7,5},{8,10},{9,11},{10,... | collective-permute-start | bytes 4915208 | tf_op jit(solution)/shard_map/ppermute | solution.py:361
  266.8 17.2 %collective-permute-start.46 = (bf16[256,640]{1,0:T(8,128)(2,1)S(1)}, bf16[256,640]{1,0:T(8,128)(2,1)S(1)}, u32[]{:S(2)}, u32[]{:S(2)}) collective-permute-start(bf16[256,640]{1,0:T(8,128)(2,1)S(1)} %copy-done.35), channel_id=1, source_target_pairs={{0,8},{1,9},{2,10},{3,11},{4,0},{5,1},{6,2},{7,3},{8,16},{9,17},{1... | collective-permute-start | bytes 983048 | tf_op jit(solution)/shard_map/ppermute | solution.py:361
  267.2 16.9 %collective-permute-start.47 = (bf16[256,640]{1,0:T(8,128)(2,1)}, bf16[256,640]{1,0:T(8,128)(2,1)S(1)}, u32[]{:S(2)}, u32[]{:S(2)}) collective-permute-start(bf16[256,640]{1,0:T(8,128)(2,1)} %copy-done.32), channel_id=1, source_target_pairs={{0,4},{1,5},{2,6},{3,7},{4,12},{5,13},{6,14},{7,15},{8,0},{9,1},{1... | collective-permute-start | bytes 983048 | tf_op jit(solution)/shard_map/ppermute | solution.py:361
  286.1 14.8 %collective-permute-start.53 = (bf16[256,640]{1,0:T(8,128)(2,1)S(1)}, bf16[256,640]{1,0:T(8,128)(2,1)S(1)}, u32[]{:S(2)}, u32[]{:S(2)}) collective-permute-start(bf16[256,640]{1,0:T(8,128)(2,1)S(1)} %collective-permute-done.46.refs_0_), channel_id=1, source_target_pairs={{0,2},{1,3},{2,0},{3,1},{4,6},{5,7},{6,4},{7,5},{8,10},{9,11},{10,... | collective-permute-start | bytes 983048 | tf_op jit(solution)/shard_map/ppermute | solution.py:361
  286.1 14.9 %collective-permute-start.54 = (bf16[256,640]{1,0:T(8,128)(2,1)S(1)}, bf16[256,640]{1,0:T(8,128)(2,1)S(1)}, u32[]{:S(2)}, u32[]{:S(2)}) collective-permute-start(bf16[256,640]{1,0:T(8,128)(2,1)S(1)} %collective-permute-done.47.refs_1_), channel_id=1, source_target_pairs={{0,2},{1,3},{2,0},{3,1},{4,6},{5,7},{6,4},{7,5},{8,10},{9,11},{10,... | collective-permute-start | bytes 983048 | tf_op jit(solution)/shard_map/ppermute | solution.py:361
  286.6 16.6 %collective-permute-start.57 = (bf16[240,640]{1,0:T(8,128)(2,1)}, bf16[240,640]{1,0:T(8,128)(2,1)S(1)}, u32[]{:S(2)}, u32[]{:S(2)}) collective-permute-start(bf16[240,640]{1,0:T(8,128)(2,1)} %get-tuple-element.310), channel_id=1, source_target_pairs={{0,16},{1,17},{2,18},{3,19},{4,20},{5,21},{6,22},{7,23},{8,24},{9,... | collective-permute-start | bytes 921608 | tf_op jit(solution)/shard_map/ppermute | solution.py:361
  289.6 11.3 %collective-permute-start.51 = (bf16[128,640]{1,0:T(8,128)(2,1)S(1)}, bf16[128,640]{1,0:T(8,128)(2,1)S(1)}, u32[]{:S(2)}, u32[]{:S(2)}) collective-permute-start(bf16[128,640]{1,0:T(8,128)(2,1)S(1)} %slice.52), channel_id=1, source_target_pairs={{0,8},{1,9},{2,10},{3,11},{4,0},{5,1},{6,2},{7,3},{8,16},{9,17},{1... | collective-permute-start | bytes 491528 | tf_op jit(solution)/shard_map/ppermute | solution.py:361
  303.4 13.0 %collective-permute-start.59 = (bf16[240,640]{1,0:T(8,128)(2,1)S(1)}, bf16[240,640]{1,0:T(8,128)(2,1)S(1)}, u32[]{:S(2)}, u32[]{:S(2)}) collective-permute-start(bf16[240,640]{1,0:T(8,128)(2,1)S(1)} %add_convert_fusion.1.refs_0_), channel_id=1, source_target_pairs={{0,4},{1,5},{2,6},{3,7},{4,12},{5,13},{6,14},{7,15},{8,0},{9,1},{1... | collective-permute-start | bytes 921608 | tf_op jit(solution)/shard_map/ppermute | solution.py:361
  304.0 12.4 %collective-permute-start.58 = (bf16[240,640]{1,0:T(8,128)(2,1)S(1)}, bf16[240,640]{1,0:T(8,128)(2,1)S(1)}, u32[]{:S(2)}, u32[]{:S(2)}) collective-permute-start(bf16[240,640]{1,0:T(8,128)(2,1)S(1)} %add_convert_fusion.1.refs_0_), channel_id=1, source_target_pairs={{0,8},{1,9},{2,10},{3,11},{4,0},{5,1},{6,2},{7,3},{8,16},{9,17},{1... | collective-permute-start | bytes 921608 | tf_op jit(solution)/shard_map/ppermute | solution.py:361
  316.4 9.7 %collective-permute-start.60 = (bf16[240,640]{1,0:T(8,128)(2,1)S(1)}, bf16[240,640]{1,0:T(8,128)(2,1)S(1)}, u32[]{:S(2)}, u32[]{:S(2)}) collective-permute-start(bf16[240,640]{1,0:T(8,128)(2,1)S(1)} %collective-permute-done.58.refs_1_), channel_id=1, source_target_pairs={{0,8},{1,9},{2,10},{3,11},{4,0},{5,1},{6,2},{7,3},{8,16},{9,17},{1... | collective-permute-start | bytes 921608 | tf_op jit(solution)/shard_map/ppermute | solution.py:361
  319.0 10.4 %collective-permute-start.65 = (bf16[240,640]{1,0:T(8,128)(2,1)S(1)}, bf16[240,640]{1,0:T(8,128)(2,1)S(1)}, u32[]{:S(2)}, u32[]{:S(2)}) collective-permute-start(bf16[240,640]{1,0:T(8,128)(2,1)S(1)} %collective-permute-done.58.refs_1_), channel_id=1, source_target_pairs={{0,2},{1,3},{2,0},{3,1},{4,6},{5,7},{6,4},{7,5},{8,10},{9,11},{10,... | collective-permute-start | bytes 921608 | tf_op jit(solution)/shard_map/ppermute | solution.py:361
  319.5 10.3 %collective-permute-start.66 = (bf16[240,640]{1,0:T(8,128)(2,1)S(1)}, bf16[240,640]{1,0:T(8,128)(2,1)S(1)}, u32[]{:S(2)}, u32[]{:S(2)}) collective-permute-start(bf16[240,640]{1,0:T(8,128)(2,1)S(1)} %collective-permute-done.59.refs_2_), channel_id=1, source_target_pairs={{0,2},{1,3},{2,0},{3,1},{4,6},{5,7},{6,4},{7,5},{8,10},{9,11},{10,... | collective-permute-start | bytes 921608 | tf_op jit(solution)/shard_map/ppermute | solution.py:361
  (116 other events, 839.4 us)
